TPU v7x, 32 devices: a whole 2x2x4 slice. The times are simulated.
32 devices in a mesh: dp: 2 (over core), ctx: 4 (over z), head: 4 (over y, x).
Axes of the slice: x: 2, y: 2, z: 4, core: 2. Of those that a mesh axis runs over, the one named last changes fastest.
Arguments:
- queries: bfloat16 [2, 4096, 2048], P('dp', 'ctx', 'head'), may hold values from -6 to 6
- keys_raw: bfloat16 [2, 4096, 2048], P('dp', 'ctx', 'head'), may hold values from -0.625 to 0.625
- values: bfloat16 [2, 4096, 2048], P('dp', 'ctx', 'head'), may hold values from -6 to 6
- gates: float32 [2, 16, 4096], P('dp', 'head', 'ctx'), as said below
- lengths: int32 [2, 16], P('dp'), may hold values from 1 to 2048, 4096 in all within a row
- key_gain: float32 [16, 128], P('head'), may hold values from 0.1 to 1.9
- cotangent: bfloat16 [2, 4096, 2048], P('dp', 'ctx', 'head'), may hold values from -6 to 6
Outputs:
- attended: bfloat16 [2, 4096, 2048], P('dp', 'ctx', 'head')
- grad_queries: bfloat16 [2, 4096, 2048], P('dp', 'ctx', 'head')
- grad_keys: bfloat16 [2, 4096, 2048], P('dp', 'ctx', 'head')
- grad_values: bfloat16 [2, 4096, 2048], P('dp', 'ctx', 'head')
- grad_gates: float32 [2, 16, 4096], P('dp', 'head', 'ctx')
- grad_gain: float32 [16, 128], P('head', 'dp')
Inputs may be any that keep to these rules, and one draw needn't show every extreme that they name: Each row of lengths gives its documents in packing order and sums to 4096. `gates`: every entry is negative.
All inputs are finite; a program needn't handle non-finite values.
Results may differ from a plain program's by a relative error of at most 0.009.
Values sent between devices are 32-bit elements; how exact they have to be, the bound alone decides.
No kernel may reach another device: no remote copies, remote signals or barrier semaphores. Data moves between devices by JAX's collectives and lax.ppermute only.
A program may use at most 128 MiB of HBM per device.

v0:
```python
import jax
import jax.numpy as jnp
from jax import lax
from jax.sharding import PartitionSpec as P

BLOCK = 512


PRECISE = lax.Precision.HIGHEST


def passed_along(value, axis, steps):
    count = lax.axis_size(axis)
    first, last = (max(0, -steps), min(count, count - steps))
    return lax.ppermute(value, axis, [(source, source + steps) for source in range(first, last)])


def start_flags(doc_lengths, first_pos, num_rows):
    starts = jnp.cumsum(doc_lengths, dtype=jnp.int32) - doc_lengths
    positions = first_pos + jnp.arange(num_rows, dtype=jnp.int32)
    matches = jnp.any(positions[:, None] == starts[None, :], axis=1)
    return matches.astype(jnp.float32)


def make_step(key_gain, head_width):
    q_scale = head_width ** (-0.5)

    def block_step(carried, inputs):
        q_block, k_block, v_block, gate_block, flag_block = inputs
        k_bf = (k_block.astype(jnp.float32) * key_gain[None]).astype(jnp.bfloat16)
        q_float = q_block.astype(jnp.float32) * q_scale
        k_float = lax.optimization_barrier(k_bf).astype(jnp.float32)
        v_float = v_block.astype(jnp.float32)
        segment = jnp.cumsum(flag_block)
        positions = jnp.arange(flag_block.shape[0])
        same_doc = (segment[:, None] == segment[None, :]) & (
            positions[:, None] >= positions[None, :]
        )
        cum_decay = jnp.cumsum(gate_block, axis=1)
        exponent = cum_decay[:, :, None] - cum_decay[:, None, :]
        decays = jnp.where(same_doc[None], jnp.exp(jnp.where(same_doc[None], exponent, 0.0)), 0.0)
        scores = jnp.einsum("thd,shd->hts", q_block, k_bf, preferred_element_type=jnp.float32)
        weights = (scores * q_scale * decays).astype(jnp.bfloat16)
        within = jnp.einsum("hts,she->the", weights, v_block, preferred_element_type=jnp.float32)
        opened = (segment == 0).astype(cum_decay.dtype)
        carry_in = jnp.exp(cum_decay) * opened[None, :]
        across = (
            jnp.einsum("thd,hde->the", q_float, carried, precision=PRECISE) * carry_in.T[:, :, None]
        )
        tail_mask = (segment == segment[-1]).astype(cum_decay.dtype)
        to_end = jnp.exp(cum_decay[:, -1:] - cum_decay) * tail_mask[None, :]
        written = jnp.einsum(
            "shd,she->hde", k_float * to_end.T[:, :, None], v_float, precision=PRECISE
        )
        end_state = carried * carry_in[:, -1][:, None, None] + written
        return (end_state, within + across)

    return block_step


def run_blocks(q_rows, k_rows, v_rows, gate_rows, flags, key_gain, start_state):
    num_rows = q_rows.shape[0]
    head_count = key_gain.shape[0]
    head_width = key_gain.shape[1]
    num_blocks = num_rows // BLOCK

    def to_blocks(tensor):
        return tensor.reshape(num_blocks, BLOCK, head_count, head_width)

    gate_blocks = gate_rows.reshape(head_count, num_blocks, BLOCK).transpose(1, 0, 2)
    flag_blocks = flags.reshape(num_blocks, BLOCK)
    end_state, outputs = lax.scan(
        jax.checkpoint(make_step(key_gain, head_width)),
        start_state,
        (to_blocks(q_rows), to_blocks(k_rows), to_blocks(v_rows), gate_blocks, flag_blocks),
    )
    return (outputs.reshape(num_rows, head_count * head_width), end_state)


def shards(queries, keys_raw, values, gates, lengths, key_gain, cotangent):
    tok_rows = queries.shape[1]
    head_count = key_gain.shape[0]
    head_width = key_gain.shape[1]
    flags = start_flags(lengths[0], lax.axis_index("ctx") * tok_rows, tok_rows)
    q_rows, k_rows, v_rows, gate_rows = (queries[0], keys_raw[0], values[0], gates[0])
    segment = jnp.cumsum(flags)
    opened = (segment == 0).astype(jnp.float32)
    tail_mask = (segment == segment[-1]).astype(jnp.float32)
    cum_decay = jnp.cumsum(gate_rows, axis=1)
    shard_decay = jnp.exp(cum_decay[:, -1]) * opened[-1]
    to_end = jnp.exp(cum_decay[:, -1:] - cum_decay) * tail_mask[None, :]
    k_bf = (
        k_rows.reshape(tok_rows, head_count, head_width).astype(jnp.float32) * key_gain[None]
    ).astype(jnp.bfloat16)
    k_float = lax.optimization_barrier(k_bf).astype(jnp.float32)
    v_float = v_rows.reshape(tok_rows, head_count, head_width).astype(jnp.float32)
    local_end = jnp.einsum(
        "shd,she->hde", k_float * to_end.T[:, :, None], v_float, precision=PRECISE
    )
    ctx_size = lax.axis_size("ctx")

    def relay_forward(step_index, incoming):
        return passed_along(shard_decay[:, None, None] * incoming + local_end, "ctx", 1)

    state_in = lax.fori_loop(0, ctx_size - 1, relay_forward, jnp.zeros_like(local_end))

    def forward(q_part, k_part, v_part, gate_part, gain_part):
        return run_blocks(q_part, k_part, v_part, gate_part, flags, gain_part, state_in)

    (primal, end_state), pullback = jax.vjp(forward, q_rows, k_rows, v_rows, gate_rows, key_gain)
    factor = jnp.exp(cum_decay) * opened[None, :]
    weighted = (
        q_rows.reshape(tok_rows, head_count, head_width).astype(jnp.float32)
        * head_width ** (-0.5)
        * factor.T[:, :, None]
    )
    cot_float = cotangent[0].astype(jnp.float32)
    local_grad = jnp.einsum(
        "thd,the->hde",
        weighted,
        cot_float.reshape(tok_rows, head_count, head_width),
        precision=PRECISE,
    )

    def relay_back(step_index, incoming):
        return passed_along(shard_decay[:, None, None] * incoming + local_grad, "ctx", -1)

    later_grad = lax.fori_loop(0, ctx_size - 1, relay_back, jnp.zeros_like(local_grad))
    grad_q, grad_k, grad_v, grad_a, gain_term = pullback((cot_float, later_grad))
    gain_total = lax.psum(gain_term, "ctx")
    grad_gain = lax.psum_scatter(gain_total, "dp", scatter_dimension=1, tiled=True)
    return (
        primal.astype(jnp.bfloat16)[None],
        grad_q[None],
        grad_k[None],
        grad_v[None],
        grad_a[None],
        grad_gain,
    )


def solution(mesh):
    placed = (
        P("dp", "ctx", "head"),
        P("dp", "ctx", "head"),
        P("dp", "ctx", "head"),
        P("dp", "head", "ctx"),
        P("dp", None),
        P("head", None),
        P("dp", "ctx", "head"),
    )
    return jax.shard_map(
        shards,
        mesh=mesh,
        in_specs=placed,
        out_specs=(
            P("dp", "ctx", "head"),
            P("dp", "ctx", "head"),
            P("dp", "ctx", "head"),
            P("dp", "ctx", "head"),
            P("dp", "head", "ctx"),
            P("head", "dp"),
        ),
        check_vma=False,
    )
```

profile of v0, /device:TPU:0, one launch (start us, length us, event | category | flops | bytes accessed | tf_op | source)
XLA Modules:
  0.0 240.2 jit_solution(14776636399371960728)
XLA Ops:
  37.1 28.1 %while.62 = (s32[]{:T(128)}, f32[4,128,128]{2,1,0:T(8,128)S(1)}, f32[4]{0:T(128)S(1)}, f32[4,128,128]{2,1,0:T(8,128)S(1)}, s32[]{:T(128)}) while((s32[]{:T(128)}, f32[4,128,128]{2,1,0:T(8,128)S(1)}, f32[4]{0:T(128)S(1)}, f32[4,128,128]{2,1,0:T(8,128)S(1)}, s32[]{:T(128)}) %tuple.140), condition=%wide.region_7.8_spmd, body=%wide.region_6.7_spmd.sunk | while | flops 131074 | bytes 1835125 | solution.py:105
  37.2 4.9 %collective-permute-start = (f32[4,128,128]{2,1,0:T(8,128)S(1)}, f32[4,128,128]{2,1,0:T(8,128)S(1)}, u32[]{:S(2)}, u32[]{:S(2)}) collective-permute-start(f32[4,128,128]{2,1,0:T(8,128)S(1)} %multiply_add_fusion.4), channel_id=1, source_target_pairs={{0,4},{4,8},{8,12},{1,5},{5,9},{9,13},{2,6},{6,10},{10,14},{3,7},{... | collective-permute-start | bytes 786440 | tf_op jit(solution)/shard_map/while/body/eval_jaxpr/ppermute | solution.py:15
  42.1 5.5 %collective-permute-done = f32[4,128,128]{2,1,0:T(8,128)S(1)} collective-permute-done((f32[4,128,128]{2,1,0:T(8,128)S(1)}, f32[4,128,128]{2,1,0:T(8,128)S(1)}, u32[]{:S(2)}, u32[]{:S(2)}) %collective-permute-start) | collective-permute-done | bytes 262176 | tf_op jit(solution)/shard_map/while/body/eval_jaxpr/ppermute | solution.py:15
  47.7 4.4 %collective-permute-start = (f32[4,128,128]{2,1,0:T(8,128)S(1)}, f32[4,128,128]{2,1,0:T(8,128)S(1)}, u32[]{:S(2)}, u32[]{:S(2)}) collective-permute-start(f32[4,128,128]{2,1,0:T(8,128)S(1)} %multiply_add_fusion.4), channel_id=1, source_target_pairs={{0,4},{4,8},{8,12},{1,5},{5,9},{9,13},{2,6},{6,10},{10,14},{3,7},{... | collective-permute-start | bytes 786440 | tf_op jit(solution)/shard_map/while/body/eval_jaxpr/ppermute | solution.py:15
  52.2 4.7 %collective-permute-done = f32[4,128,128]{2,1,0:T(8,128)S(1)} collective-permute-done((f32[4,128,128]{2,1,0:T(8,128)S(1)}, f32[4,128,128]{2,1,0:T(8,128)S(1)}, u32[]{:S(2)}, u32[]{:S(2)}) %collective-permute-start) | collective-permute-done | bytes 262176 | tf_op jit(solution)/shard_map/while/body/eval_jaxpr/ppermute | solution.py:15
  56.9 4.4 %collective-permute-start = (f32[4,128,128]{2,1,0:T(8,128)S(1)}, f32[4,128,128]{2,1,0:T(8,128)S(1)}, u32[]{:S(2)}, u32[]{:S(2)}) collective-permute-start(f32[4,128,128]{2,1,0:T(8,128)S(1)} %multiply_add_fusion.4), channel_id=1, source_target_pairs={{0,4},{4,8},{8,12},{1,5},{5,9},{9,13},{2,6},{6,10},{10,14},{3,7},{... | collective-permute-start | bytes 786440 | tf_op jit(solution)/shard_map/while/body/eval_jaxpr/ppermute | solution.py:15
  61.3 3.9 %collective-permute-done = f32[4,128,128]{2,1,0:T(8,128)S(1)} collective-permute-done((f32[4,128,128]{2,1,0:T(8,128)S(1)}, f32[4,128,128]{2,1,0:T(8,128)S(1)}, u32[]{:S(2)}, u32[]{:S(2)}) %collective-permute-start) | collective-permute-done | bytes 262176 | tf_op jit(solution)/shard_map/while/body/eval_jaxpr/ppermute | solution.py:15
  65.2 27.3 %while.64 = (s32[]{:T(128)}, f32[4,128,128]{2,1,0:T(8,128)S(1)}, bf16[2,512,4,128]{1,3,2,0:T(8,128)(2,1)}, f32[2,4,128,128]{3,2,1,0:T(8,128)}, f32[2,4,512]{2,1,...) while((s32[]{:T(128)}, f32[4,128,128]{2,1,0:T(8,128)S(1)}, ...), condition=%wide.region_13.14_spmd.clone, body=%wide.region_8.13_spmd.clone.sunk | while | flops 1352081408 | bytes 9343697 | solution.py:72
  68.5 3.3 %fusion.191 = f32[512,4,128]{0,2,1:T(8,128)S(1)} fusion(bf16[512,4,128]{2,0,1:T(8,128)(2,1)S(1)} %fusion.189, f32[4,512]{1,0:T(4,128)S(1)} %bitcast.353, pred[512,512]{1,0:T(8,128)(4,1)S(1)} %fusion.190, bf16[2,512,4,128]{3,1,2,0:T(8,128)(2,1)} %get-tuple-element.1136, s32[]{:T(128)S(6)} %copy.332, bf16[2,512,4,128]{3,1,2,0:T(8,128)(2,1)} %get-tuple-element.1135), kind=kOutput, calls=%fused_computation.5.clone.1 | convolution fusion | flops 543162368 | bytes 2900992 | tf_op jit(solution)/shard_map/jvp()/while/body/eval_jaxpr/hts,she->the/dot_general | solution.py:44
  82.2 3.3 %fusion.191 = f32[512,4,128]{0,2,1:T(8,128)S(1)} fusion(bf16[512,4,128]{2,0,1:T(8,128)(2,1)S(1)} %fusion.189, f32[4,512]{1,0:T(4,128)S(1)} %bitcast.353, pred[512,512]{1,0:T(8,128)(4,1)S(1)} %fusion.190, bf16[2,512,4,128]{3,1,2,0:T(8,128)(2,1)} %get-tuple-element.1136, s32[]{:T(128)S(6)} %copy.332, bf16[2,512,4,128]{3,1,2,0:T(8,128)(2,1)} %get-tuple-element.1135), kind=kOutput, calls=%fused_computation.5.clone.1 | convolution fusion | flops 543162368 | bytes 2900992 | tf_op jit(solution)/shard_map/jvp()/while/body/eval_jaxpr/hts,she->the/dot_general | solution.py:44
  95.6 26.3 %while.63 = (s32[]{:T(128)}, f32[4,128,128]{2,1,0:T(8,128)S(1)}, f32[4]{0:T(128)S(1)}, f32[4,128,128]{2,1,0:T(8,128)S(1)}, s32[]{:T(128)}) while((s32[]{:T(128)}, f32[4,128,128]{2,1,0:T(8,128)S(1)}, f32[4]{0:T(128)S(1)}, f32[4,128,128]{2,1,0:T(8,128)S(1)}, s32[]{:T(128)}) %tuple.160), condition=%wide.region_15.16_spmd, body=%wide.region_14.15_spmd.sunk | while | flops 131074 | bytes 1835125 | solution.py:128
  97.1 7.4 %collective-permute-done.1 = f32[4,128,128]{2,1,0:T(8,128)S(1)} collective-permute-done((f32[4,128,128]{2,1,0:T(8,128)S(1)}, f32[4,128,128]{2,1,0:T(8,128)S(1)}, u32[]{:S(2)}, u32[]{:S(2)}) %collective-permute-start.1) | collective-permute-done | bytes 262176 | tf_op jit(solution)/shard_map/while/body/eval_jaxpr/ppermute | solution.py:15
  105.9 7.4 %collective-permute-done.1 = f32[4,128,128]{2,1,0:T(8,128)S(1)} collective-permute-done((f32[4,128,128]{2,1,0:T(8,128)S(1)}, f32[4,128,128]{2,1,0:T(8,128)S(1)}, u32[]{:S(2)}, u32[]{:S(2)}) %collective-permute-start.1) | collective-permute-done | bytes 262176 | tf_op jit(solution)/shard_map/while/body/eval_jaxpr/ppermute | solution.py:15
  114.7 7.2 %collective-permute-done.1 = f32[4,128,128]{2,1,0:T(8,128)S(1)} collective-permute-done((f32[4,128,128]{2,1,0:T(8,128)S(1)}, f32[4,128,128]{2,1,0:T(8,128)S(1)}, u32[]{:S(2)}, u32[]{:S(2)}) %collective-permute-start.1) | collective-permute-done | bytes 262176 | tf_op jit(solution)/shard_map/while/body/eval_jaxpr/ppermute | solution.py:15
  125.7 85.2 %while.65 = (s32[]{:T(128)}, f32[4,128]{1,0:T(4,128)S(1)}, f32[4,128,128]{2,1,0:T(8,128)S(1)}, bf16[2,512,4,128]{3,2,1,0:T(4,128)(2,1)}, bf16[2,512,4,128]{3,2,1...) while((s32[]{:T(128)}, f32[4,128]{1,0:T(4,128)S(1)}, ...), condition=%wide.region_30.31_spmd.clone, body=%wide.region_16.30_spmd.clone.sunk | while | flops 3394863616 | bytes 116524784 | solution.py:72
  141.8 3.2 %fusion.214 = (bf16[1,512,4,128]{3,1,2,0:T(8,128)(2,1)}, f32[4,128]{1,0:T(4,128)S(1)}) fusion(f32[4,128]{1,0:T(4,128)S(1)} %get-tuple-element.1066, bf16[512,4,128]{2,0,1:T(8,128)(2,1)S(1)} %copy-done.2, bf16[512,4,128]{2,0,1:T(8,128)(2,1)S(1)} %get-tuple-element.1073, bf16[512,4,128]{2,0,1:T(8,128)(2,1)S(1)} %dynamic-slice_bitcast_fusion.11, ...), kind=kOutput, calls=%fused_computation.112.clone.1 | convolution fusion | flops 276823552 | bytes 4468736 | tf_op jit(solution)/shard_map/transpose(jvp())/while/body/eval_jaxpr/checkpoint/thd,shd->hts/dot_general | solution.py:42
  145.0 3.8 %fusion.220 = bf16[4,128,512]{2,1,0:T(8,128)(2,1)S(1)} fusion(f32[4,512,512]{2,1,0:T(8,128)} %copy-done, f32[4,512]{1,0:T(4,128)S(1)} %bitcast.351, pred[512,512]{1,0:T(8,128)(4,1)S(1)} %fusion.212, f32[512,4,128]{0,2,1:T(8,128)S(1)} %bitcast.337), kind=kOutput, calls=%fused_computation.83.clone.1 | convolution fusion | flops 274726912 | bytes 6037504 | tf_op jit(solution)/shard_map/transpose(jvp())/while/body/eval_jaxpr/checkpoint/hts,she->the/dot_general | solution.py:44
  154.0 3.3 %fusion.218 = bf16[4,512,128]{2,1,0:T(8,128)(2,1)S(1)} fusion(bf16[512,4,128]{2,0,1:T(8,128)(2,1)S(1)} %fusion.209, bf16[4,512,512]{2,1,0:T(8,128)(2,1)} %copy-done.21, f32[4,512]{1,0:T(4,128)S(1)} %bitcast.352, pred[512,512]{1,0:T(8,128)(4,1)S(1)} %fusion.212), kind=kOutput, calls=%fused_computation.87.clone.1 | convolution fusion | flops 274989056 | bytes 3416064 | tf_op jit(solution)/shard_map/transpose(jvp())/while/body/eval_jaxpr/checkpoint/thd,shd->hts/dot_general | solution.py:42
  162.8 5.0 %reduce-window.150 = f32[4,4,128]{2,1,0:T(4,128)S(1)} reduce-window(f32[4,4,128]{2,1,0:T(4,128)S(1)} %reshape.625, f32[]{:T(128)} %constant.150.clone.1..sunk.1), window={size=1x1x128 pad=0_0x0_0x0_127}, to_apply=%region_28.28 | reduce-window | flops 260096 | bytes 16388 | tf_op jit(solution)/shard_map/reduce-window.60
  184.4 3.2 %fusion.214 = (bf16[1,512,4,128]{3,1,2,0:T(8,128)(2,1)}, f32[4,128]{1,0:T(4,128)S(1)}) fusion(f32[4,128]{1,0:T(4,128)S(1)} %get-tuple-element.1066, bf16[512,4,128]{2,0,1:T(8,128)(2,1)S(1)} %copy-done.2, bf16[512,4,128]{2,0,1:T(8,128)(2,1)S(1)} %get-tuple-element.1073, bf16[512,4,128]{2,0,1:T(8,128)(2,1)S(1)} %dynamic-slice_bitcast_fusion.11, ...), kind=kOutput, calls=%fused_computation.112.clone.1 | convolution fusion | flops 276823552 | bytes 4468736 | tf_op jit(solution)/shard_map/transpose(jvp())/while/body/eval_jaxpr/checkpoint/thd,shd->hts/dot_general | solution.py:42
  187.7 3.8 %fusion.220 = bf16[4,128,512]{2,1,0:T(8,128)(2,1)S(1)} fusion(f32[4,512,512]{2,1,0:T(8,128)} %copy-done, f32[4,512]{1,0:T(4,128)S(1)} %bitcast.351, pred[512,512]{1,0:T(8,128)(4,1)S(1)} %fusion.212, f32[512,4,128]{0,2,1:T(8,128)S(1)} %bitcast.337), kind=kOutput, calls=%fused_computation.83.clone.1 | convolution fusion | flops 274726912 | bytes 6037504 | tf_op jit(solution)/shard_map/transpose(jvp())/while/body/eval_jaxpr/checkpoint/hts,she->the/dot_general | solution.py:44
  196.7 3.3 %fusion.218 = bf16[4,512,128]{2,1,0:T(8,128)(2,1)S(1)} fusion(bf16[512,4,128]{2,0,1:T(8,128)(2,1)S(1)} %fusion.209, bf16[4,512,512]{2,1,0:T(8,128)(2,1)} %copy-done.21, f32[4,512]{1,0:T(4,128)S(1)} %bitcast.352, pred[512,512]{1,0:T(8,128)(4,1)S(1)} %fusion.212), kind=kOutput, calls=%fused_computation.87.clone.1 | convolution fusion | flops 274989056 | bytes 3416064 | tf_op jit(solution)/shard_map/transpose(jvp())/while/body/eval_jaxpr/checkpoint/thd,shd->hts/dot_general | solution.py:42
  205.4 5.0 %reduce-window.150 = f32[4,4,128]{2,1,0:T(4,128)S(1)} reduce-window(f32[4,4,128]{2,1,0:T(4,128)S(1)} %reshape.625, f32[]{:T(128)} %constant.150.clone.1..sunk.1), window={size=1x1x128 pad=0_0x0_0x0_127}, to_apply=%region_28.28 | reduce-window | flops 260096 | bytes 16388 | tf_op jit(solution)/shard_map/reduce-window.60
  220.9 12.4 %psum.8 = f32[4,64]{1,0:T(4,128)} all-reduce(f32[4,64]{1,0:T(4,128)S(1)} %copy.251), channel_id=1, replica_groups=mesh['dp'=2,'ctx'=4,'head'=4] {'ctx'}, use_global_device_ids=true, to_apply=%region_31.32 | all-reduce | flops 256 | bytes 2048 | tf_op jit(solution)/shard_map/psum | solution.py:130
  (278 shorter events, 125.5 us)
Async XLA Ops:
  7.2 212.9 %reduce-scatter.4.cloned.1.call-start = ((), (), s32[]{:S(2)}) async-start(), calls=%async_computation.1 | async-start | bytes 98304
  7.2 8.0 %copy-start.7 = (bf16[1,1024,512]{2,1,0:T(8,128)(2,1)S(1)}, bf16[1,1024,512]{2,1,0:T(8,128)(2,1)}, u32[]{:S(2)}) copy-start(bf16[1,1024,512]{2,1,0:T(8,128)(2,1)} %param.15) | copy-start | bytes 3145732
  16.4 6.5 %copy-start.20 = (s32[1,16]{1,0:T(1,128)S(1)}, s32[1,16]{1,0:T(1,128)}, u32[]{:S(2)}) copy-start(s32[1,16]{1,0:T(1,128)} %param.19) | copy-start | bytes 196
  16.4 8.1 %copy-start.17 = (f32[1,4,1024]{2,1,0:T(4,128)S(1)}, f32[1,4,1024]{2,1,0:T(4,128)}, u32[]{:S(2)}) copy-start(f32[1,4,1024]{2,1,0:T(4,128)} %param.18) | copy-start | bytes 49156
  16.4 9.8 %copy-start.18 = (f32[4,128]{1,0:T(4,128)S(1)}, f32[4,128]{1,0:T(4,128)}, u32[]{:S(2)}) copy-start(f32[4,128]{1,0:T(4,128)} %param.20) | copy-start | bytes 6148
  27.3 8.3 %copy-start.15 = (bf16[1024,4,128]{2,1,0:T(4,128)(2,1)S(1)}, bf16[1024,4,128]{2,1,0:T(4,128)(2,1)}, u32[]{:S(2)}) copy-start(bf16[1024,4,128]{2,1,0:T(4,128)(2,1)} %reshape_squeeze.17) | copy-start | bytes 3145732
  28.7 7.0 %copy-start.16 = (bf16[1024,4,128]{0,2,1:T(8,128)(2,1)S(1)}, bf16[1024,4,128]{0,2,1:T(8,128)(2,1)}, u32[]{:S(2)}) copy-start(bf16[1024,4,128]{0,2,1:T(8,128)(2,1)} %multiply_convert_fusion.6) | copy-start | bytes 3145732
  37.2 10.5 %collective-permute-start = (f32[4,128,128]{2,1,0:T(8,128)S(1)}, f32[4,128,128]{2,1,0:T(8,128)S(1)}, u32[]{:S(2)}, u32[]{:S(2)}) collective-permute-start(f32[4,128,128]{2,1,0:T(8,128)S(1)} %multiply_add_fusion.4), channel_id=1, source_target_pairs={{0,4},{4,8},{8,12},{1,5},{5,9},{9,13},{2,6},{6,10},{10,14},{3,7},{... | collective-permute-start | bytes 786440 | tf_op jit(solution)/shard_map/while/body/eval_jaxpr/ppermute | solution.py:15
  47.7 9.1 %collective-permute-start = (f32[4,128,128]{2,1,0:T(8,128)S(1)}, f32[4,128,128]{2,1,0:T(8,128)S(1)}, u32[]{:S(2)}, u32[]{:S(2)}) collective-permute-start(f32[4,128,128]{2,1,0:T(8,128)S(1)} %multiply_add_fusion.4), channel_id=1, source_target_pairs={{0,4},{4,8},{8,12},{1,5},{5,9},{9,13},{2,6},{6,10},{10,14},{3,7},{... | collective-permute-start | bytes 786440 | tf_op jit(solution)/shard_map/while/body/eval_jaxpr/ppermute | solution.py:15
  56.9 8.3 %collective-permute-start = (f32[4,128,128]{2,1,0:T(8,128)S(1)}, f32[4,128,128]{2,1,0:T(8,128)S(1)}, u32[]{:S(2)}, u32[]{:S(2)}) collective-permute-start(f32[4,128,128]{2,1,0:T(8,128)S(1)} %multiply_add_fusion.4), channel_id=1, source_target_pairs={{0,4},{4,8},{8,12},{1,5},{5,9},{9,13},{2,6},{6,10},{10,14},{3,7},{... | collective-permute-start | bytes 786440 | tf_op jit(solution)/shard_map/while/body/eval_jaxpr/ppermute | solution.py:15
  95.8 8.7 %collective-permute-start.1 = (f32[4,128,128]{2,1,0:T(8,128)S(1)}, f32[4,128,128]{2,1,0:T(8,128)S(1)}, u32[]{:S(2)}, u32[]{:S(2)}) collective-permute-start(f32[4,128,128]{2,1,0:T(8,128)S(1)} %multiply_add_fusion.5), channel_id=1, source_target_pairs={{4,0},{8,4},{12,8},{5,1},{9,5},{13,9},{6,2},{10,6},{14,10},{7,3},{... | collective-permute-start | bytes 786440 | tf_op jit(solution)/shard_map/while/body/eval_jaxpr/ppermute | solution.py:15
  104.6 8.7 %collective-permute-start.1 = (f32[4,128,128]{2,1,0:T(8,128)S(1)}, f32[4,128,128]{2,1,0:T(8,128)S(1)}, u32[]{:S(2)}, u32[]{:S(2)}) collective-permute-start(f32[4,128,128]{2,1,0:T(8,128)S(1)} %multiply_add_fusion.5), channel_id=1, source_target_pairs={{4,0},{8,4},{12,8},{5,1},{9,5},{13,9},{6,2},{10,6},{14,10},{7,3},{... | collective-permute-start | bytes 786440 | tf_op jit(solution)/shard_map/while/body/eval_jaxpr/ppermute | solution.py:15
  113.4 8.5 %collective-permute-start.1 = (f32[4,128,128]{2,1,0:T(8,128)S(1)}, f32[4,128,128]{2,1,0:T(8,128)S(1)}, u32[]{:S(2)}, u32[]{:S(2)}) collective-permute-start(f32[4,128,128]{2,1,0:T(8,128)S(1)} %multiply_add_fusion.5), channel_id=1, source_target_pairs={{4,0},{8,4},{12,8},{5,1},{9,5},{13,9},{6,2},{10,6},{14,10},{7,3},{... | collective-permute-start | bytes 786440 | tf_op jit(solution)/shard_map/while/body/eval_jaxpr/ppermute | solution.py:15
  131.4 7.9 %copy-start.1 = (bf16[512,4,128]{2,0,1:T(8,128)(2,1)S(1)}, bf16[512,4,128]{2,0,1:T(8,128)(2,1)}, u32[]{:S(2)}) copy-start(bf16[512,4,128]{2,0,1:T(8,128)(2,1)} %dynamic-slice_bitcast_fusion.13) | copy-start | bytes 1572868 | tf_op jit(solution)/shard_map/transpose(jvp())/while
  154.0 5.2 %copy-start.6 = (bf16[1,512,4,128]{3,1,2,0:T(8,128)(2,1)S(1)}, bf16[1,512,4,128]{3,1,2,0:T(8,128)(2,1)}, u32[]{:S(2)}) copy-start(bf16[1,512,4,128]{3,1,2,0:T(8,128)(2,1)} %get-tuple-element.1084) | copy-start | bytes 1572868 | tf_op jit(solution)/shard_map/transpose(jvp())/while
  154.0 5.2 %copy-start.8 = (bf16[2,512,4,128]{3,2,1,0:T(4,128)(2,1)S(1)}, bf16[2,512,4,128]{3,2,1,0:T(4,128)(2,1)}, u32[]{:S(2)}) copy-start(bf16[2,512,4,128]{3,2,1,0:T(4,128)(2,1)} %get-tuple-element.1175) | copy-start | bytes 3145732 | tf_op jit(solution)/shard_map/transpose(jvp())/while
  159.3 9.0 %copy-start.4 = (bf16[2,512,4,128]{3,1,2,0:T(8,128)(2,1)S(1)}, bf16[2,512,4,128]{3,1,2,0:T(8,128)(2,1)}, u32[]{:S(2)}) copy-start(bf16[2,512,4,128]{3,1,2,0:T(8,128)(2,1)} %copy-done.3) | copy-start | bytes 3145732 | tf_op jit(solution)/shard_map/transpose(jvp())/while
  174.0 7.9 %copy-start.1 = (bf16[512,4,128]{2,0,1:T(8,128)(2,1)S(1)}, bf16[512,4,128]{2,0,1:T(8,128)(2,1)}, u32[]{:S(2)}) copy-start(bf16[512,4,128]{2,0,1:T(8,128)(2,1)} %dynamic-slice_bitcast_fusion.13) | copy-start | bytes 1572868 | tf_op jit(solution)/shard_map/transpose(jvp())/while
  196.6 5.2 %copy-start.6 = (bf16[1,512,4,128]{3,1,2,0:T(8,128)(2,1)S(1)}, bf16[1,512,4,128]{3,1,2,0:T(8,128)(2,1)}, u32[]{:S(2)}) copy-start(bf16[1,512,4,128]{3,1,2,0:T(8,128)(2,1)} %get-tuple-element.1084) | copy-start | bytes 1572868 | tf_op jit(solution)/shard_map/transpose(jvp())/while
  201.9 9.1 %copy-start.4 = (bf16[2,512,4,128]{3,1,2,0:T(8,128)(2,1)S(1)}, bf16[2,512,4,128]{3,1,2,0:T(8,128)(2,1)}, u32[]{:S(2)}) copy-start(bf16[2,512,4,128]{3,1,2,0:T(8,128)(2,1)} %copy-done.3) | copy-start | bytes 3145732 | tf_op jit(solution)/shard_map/transpose(jvp())/while
  210.9 7.9 %copy-start.19 = (f32[2,4,512]{2,1,0:T(4,128)}, f32[2,4,512]{2,1,0:T(4,128)S(1)}, u32[]{:S(2)}) copy-start(f32[2,4,512]{2,1,0:T(4,128)S(1)} %get-tuple-element.489) | copy-start | bytes 49156
  210.9 5.5 %copy-start.10 = (bf16[2,512,4,128]{3,2,1,0:T(4,128)(2,1)S(1)}, bf16[2,512,4,128]{3,2,1,0:T(4,128)(2,1)}, u32[]{:S(2)}) copy-start(bf16[2,512,4,128]{3,2,1,0:T(4,128)(2,1)} %get-tuple-element.486) | copy-start | bytes 3145732
  211.0 6.7 %copy-start.13 = (bf16[2,512,4,128]{3,2,1,0:T(4,128)(2,1)S(1)}, bf16[2,512,4,128]{3,2,1,0:T(4,128)(2,1)}, u32[]{:S(2)}) copy-start(bf16[2,512,4,128]{3,2,1,0:T(4,128)(2,1)} %get-tuple-element.487) | copy-start | bytes 3145732
  211.7 7.1 %copy-start.14 = (bf16[2,512,4,128]{3,2,1,0:T(4,128)(2,1)S(1)}, bf16[2,512,4,128]{3,2,1,0:T(4,128)(2,1)}, u32[]{:S(2)}) copy-start(bf16[2,512,4,128]{3,2,1,0:T(4,128)(2,1)} %get-tuple-element.488) | copy-start | bytes 3145732
  (17 other events, 58.1 us)
Sparse Core Ops, SparseCore 0:
  211.8 8.1 reduce-scatter.3
where the time goes:
time: 241 us; the launch traced here: 240 us
  matrix products  65.1 us (27%)
  local copies, waits for them, and re-layouts  63.2 us (26%)
  waiting for transfers between devices  36.2 us (15%)
  other arithmetic  30.5 us (13%)
  starting transfers between devices  17.7 us (7%)
  between operations  14.2 us (6%)
  blocking collectives  12.4 us (5%)
    ppermute x6, waiting for transfers between devices, passed_along(): lax.ppermute(value, axis, [(source, source + steps) for source in range(f...  36.2 us
    another operation x27, other arithmetic  19.4 us
    dot_general x6, matrix products, block_step(): jnp.einsum('hts,she->the', weights, v_block, preferred_element_type=jnp.f...  19.2 us
    ppermute x6, starting transfers between devices, passed_along(): lax.ppermute(value, axis, [(source, source + steps) for source in range(f...  17.6 us
    dot_general x8, matrix products, block_step(): jnp.einsum('thd,hde->the', q_float, carried, precision=PRECISE)  15.6 us
    dot_general x6, matrix products, block_step(): jnp.einsum('thd,shd->hts', q_block, k_bf, preferred_element_type=jnp.floa...  14.5 us
    psum x1, blocking collectives, shards(): gain_total = lax.psum(gain_term, 'ctx')  12.4 us
    dot_general x6, matrix products, block_step(): jnp.einsum('shd,she->hde', k_float * to_end.T[:, :, None], v_float, preci...  11.3 us
  transfers between devices with their start and end apart: 7, of which 6 were waited for; matrix products, arithmetic and copies ran while one was open for 3% of the time, Pallas kernels for 0%

commit v1 on v0

v1 whole, which is shorter than its diff:
```python
import functools

import jax
import jax.numpy as jnp
from jax import lax
from jax.experimental import pallas as pl
from jax.experimental.pallas import tpu as pltpu
from jax.sharding import PartitionSpec as P

CHUNK = 128
PRECISE = lax.Precision.HIGHEST
F32 = jnp.float32
BF16 = jnp.bfloat16


def dot_nn(a, b, precision=None):
    return lax.dot_general(
        a, b, (((1,), (0,)), ((), ())), precision=precision, preferred_element_type=F32
    )


def dot_nt(a, b):
    return lax.dot_general(a, b, (((1,), (1,)), ((), ())), preferred_element_type=F32)


def dot_tn(a, b):
    return lax.dot_general(a, b, (((0,), (0,)), ((), ())), preferred_element_type=F32)


def iota(shape, dim):
    return lax.broadcasted_iota(jnp.int32, shape, dim)


def upper(strict):
    rows, columns = iota((CHUNK, CHUNK), 0), iota((CHUNK, CHUNK), 1)
    return ((rows < columns) if strict else (rows <= columns)).astype(F32)


def lower(strict):
    rows, columns = iota((CHUNK, CHUNK), 0), iota((CHUNK, CHUNK), 1)
    return ((rows > columns) if strict else (rows >= columns)).astype(F32)


def decay_tables(lengths_ref, ctx_ref, gates_ref, spread, cum_ref, chunk_fac_ref, shard_fac_ref):
    rows = cum_ref.shape[0]
    num_chunks = rows // 8
    tokens = num_chunks * CHUNK
    for chunk in range(num_chunks):
        part = gates_ref[0, :, chunk * CHUNK : (chunk + 1) * CHUNK]
        spread[chunk * 8 : chunk * 8 + 4, :] = part
        spread[chunk * 8 + 4 : chunk * 8 + 8, :] = part
    gates = spread[...]
    prefix = dot_nn(gates, upper(False), PRECISE)
    suffix = dot_nn(gates, lower(True), PRECISE)
    totals = jnp.broadcast_to(prefix[:, CHUNK - 1 : CHUNK], (rows, CHUNK))
    row_a, row_b = iota((rows, rows), 0), iota((rows, rows), 1)
    same = (row_a % 8) == (row_b % 8)
    before = dot_nn((same & (row_b // 8 < row_a // 8)).astype(F32), totals, PRECISE)
    after = dot_nn((same & (row_b // 8 > row_a // 8)).astype(F32), totals, PRECISE)

    first = ctx_ref[0] * tokens
    chunk_first = first + (iota((rows, CHUNK), 0) // 8) * CHUNK
    positions = chunk_first + iota((rows, CHUNK), 1)
    segment = jnp.zeros((rows, CHUNK), jnp.int32)
    segment_before = jnp.zeros((rows, CHUNK), jnp.int32)
    segment_last = jnp.zeros((rows, CHUNK), jnp.int32)
    shard_before = jnp.int32(0)
    shard_last = jnp.int32(0)
    start = jnp.int32(0)
    for doc in range(lengths_ref.shape[1]):
        segment += (positions >= start).astype(jnp.int32)
        segment_before += (chunk_first > start).astype(jnp.int32)
        segment_last += (chunk_first + (CHUNK - 1) >= start).astype(jnp.int32)
        shard_before += (first > start).astype(jnp.int32)
        shard_last += (first + (tokens - 1) >= start).astype(jnp.int32)
        start += lengths_ref[0, doc]
    is_start = iota((rows, CHUNK), 0) % 8 < 4
    cum_ref[...] = jnp.where(is_start, prefix, segment.astype(F32))
    exponent = jnp.minimum(jnp.where(is_start, prefix, suffix), 0.0)
    keep = segment == jnp.where(is_start, segment_before, segment_last)
    chunk_fac_ref[...] = jnp.where(keep, jnp.exp(exponent), 0.0)
    exponent = jnp.minimum(jnp.where(is_start, prefix + before, suffix + after), 0.0)
    keep = segment == jnp.where(is_start, shard_before, shard_last)
    shard_fac_ref[...] = jnp.where(keep, jnp.exp(exponent), 0.0)


def ends_kernel(
    head_width, lengths_ref, ctx_ref, gates_ref, q_ref, k_ref, v_ref, cot_ref,
    cum_ref, chunk_fac_ref, shard_fac_ref, end_ref, grad_ref, spread,
):
    step = pl.program_id(0)
    heads = end_ref.shape[0]
    block = q_ref.shape[1]
    chunks = block // CHUNK

    @pl.when(step == 0)
    def _():
        decay_tables(
            lengths_ref, ctx_ref, gates_ref, spread, cum_ref, chunk_fac_ref, shard_fac_ref
        )
        end_ref[...] = jnp.zeros_like(end_ref)
        grad_ref[...] = jnp.zeros_like(grad_ref)

    columns = []
    for chunk in range(chunks):
        at = pl.multiple_of((step * chunks + chunk) * 8, 8)
        columns.append(jnp.transpose(shard_fac_ref[pl.ds(at, 8), :]))
    factors = jnp.concatenate(columns, axis=0)
    for head in range(heads):
        lanes = slice(head * head_width, (head + 1) * head_width)
        k_part = (k_ref[0, :, lanes].astype(F32) * factors[:, 4 + head : 5 + head]).astype(BF16)
        q_part = (
            q_ref[0, :, lanes].astype(F32)
            * (factors[:, head : head + 1] * head_width ** (-0.5))
        ).astype(BF16)
        end_ref[head] += dot_tn(k_part, v_ref[0, :, lanes])
        grad_ref[head] += dot_tn(q_part, cot_ref[0, :, lanes])


def local_kernel(
    head_width, q_ref, k_ref, v_ref, cot_ref, gain_ref, cum_ref, fac_ref,
    out_ref, dq_ref, dk_ref, dv_ref, dgate_ref, dgain_ref, leaving, state,
):
    heads = state.shape[0]
    num_chunks = leaving.shape[0]
    scale = head_width ** (-0.5)

    def lanes_of(head):
        return slice(head * head_width, (head + 1) * head_width)

    state[...] = jnp.zeros_like(state)

    def backward(index, carry):
        chunk = num_chunks - 1 - index
        rows = pl.ds(pl.multiple_of(chunk * CHUNK, CHUNK), CHUNK)
        fac = fac_ref[pl.ds(pl.multiple_of(chunk * 8, 8), 8), :]
        columns = jnp.transpose(fac)
        for head in range(heads):
            lanes = lanes_of(head)
            leaving[chunk, head] = state[head].astype(BF16)
            q_part = (
                q_ref[0, rows, lanes].astype(F32) * (columns[:, head : head + 1] * scale)
            ).astype(BF16)
            added = dot_tn(q_part, cot_ref[0, rows, lanes])
            state[head] = state[head] * fac[head : head + 1, CHUNK - 1 : CHUNK] + added
        return carry

    lax.fori_loop(0, num_chunks, backward, 0)
    state[...] = jnp.zeros_like(state)
    dgain_ref[...] = jnp.zeros_like(dgain_ref)

    def forward(chunk, carry):
        rows = pl.ds(pl.multiple_of(chunk * CHUNK, CHUNK), CHUNK)
        fac = fac_ref[pl.ds(pl.multiple_of(chunk * 8, 8), 8), :]
        cum = cum_ref[pl.ds(pl.multiple_of(chunk * 8, 8), 8), :]
        fac_columns = jnp.transpose(fac)
        cum_columns = jnp.transpose(cum)
        same = (cum_columns[:, 4:5] == cum[4:5, :]) & (
            iota((CHUNK, CHUNK), 0) >= iota((CHUNK, CHUNK), 1)
        )
        lane = iota((CHUNK, 8), 1)
        sums = jnp.zeros((CHUNK, 8), F32)
        column_sums, constants = [], []
        for head in range(heads):
            lanes = lanes_of(head)
            q, v, cot = q_ref[0, rows, lanes], v_ref[0, rows, lanes], cot_ref[0, rows, lanes]
            k_raw = k_ref[0, rows, lanes].astype(F32)
            gain = gain_ref[head : head + 1, :]
            k = (k_raw * gain).astype(BF16)
            from_start = fac_columns[:, head : head + 1] * scale
            to_end = fac_columns[:, 4 + head : 5 + head]
            exponent = jnp.minimum(cum_columns[:, head : head + 1] - cum[head : head + 1, :], 0.0)
            decays = jnp.where(same, jnp.exp(exponent) * scale, 0.0)
            grad_weights = dot_nt(cot, v)
            weights = dot_nt(q, k) * decays
            paired = weights * grad_weights
            weights = weights.astype(BF16)
            grad_scores = (grad_weights * decays).astype(BF16)
            held = state[head]
            entering = held.astype(BF16)
            later = leaving[chunk, head]
            across = dot_nn(q, entering) * from_start
            out_ref[0, rows, lanes] = (dot_nn(weights, v) + across).astype(BF16)
            dq_ref[0, rows, lanes] = (
                dot_nn(grad_scores, k) + dot_nt(cot, entering) * from_start
            ).astype(BF16)
            written = dot_nn(k, later) * to_end
            dv_ref[0, rows, lanes] = (dot_tn(weights, cot) + written).astype(BF16)
            grad_k = dot_tn(grad_scores, q) + dot_nt(v, later) * to_end
            dk_ref[0, rows, lanes] = (grad_k * gain).astype(BF16)
            dgain_ref[head : head + 1, :] += jnp.sum(grad_k * k_raw, axis=0, keepdims=True)
            queried = jnp.sum(across * cot.astype(F32) + paired, axis=1, keepdims=True)
            kept = jnp.sum(written * v.astype(F32), axis=1, keepdims=True)
            sums = jnp.where(lane == head, queried, jnp.where(lane == 4 + head, kept, sums))
            column_sums.append(jnp.sum(paired, axis=0, keepdims=True))
            decay = fac[head : head + 1, CHUNK - 1 : CHUNK]
            constants.append(
                jnp.sum(held * later.astype(F32), axis=(0, 1), keepdims=True) * decay
            )
            state[head] = held * decay + dot_tn((k.astype(F32) * to_end).astype(BF16), v)
        sum_rows = jnp.transpose(sums)
        by_query = sum_rows[0:4] - jnp.concatenate(column_sums, axis=0)
        dgate_ref[0, :, rows] = (
            dot_nn(by_query, lower(False), PRECISE)
            + dot_nn(sum_rows[4:8], upper(True), PRECISE)
            + jnp.concatenate(constants, axis=0)
        )
        return carry

    lax.fori_loop(0, num_chunks, forward, 0)


def merge_kernel(
    head_width, q_ref, k_ref, v_ref, cot_ref, gain_ref, fac_ref, state_ref, later_ref,
    out_in, dq_in, dk_in, dv_in, dgate_in,
    out_ref, dq_ref, dk_ref, dv_ref, dgate_ref, entering, leaving, sums_scr,
):
    step = pl.program_id(0)
    heads = entering.shape[0]
    block = q_ref.shape[1]
    chunks = block // CHUNK
    rows_all = fac_ref.shape[0]
    num_chunks = rows_all // 8
    scale = head_width ** (-0.5)

    @pl.when(step == 0)
    def _():
        gain_columns = jnp.transpose(jnp.concatenate([gain_ref[...], gain_ref[...]], axis=0))
        for head in range(heads):
            entering[head] = (state_ref[head] * scale).astype(BF16)
            leaving[head] = (later_ref[head] * gain_columns[:, head : head + 1]).astype(BF16)

    for chunk in range(chunks):
        at = pl.multiple_of((step * chunks + chunk) * 8, 8)
        columns = jnp.transpose(fac_ref[pl.ds(at, 8), :])
        rows = slice(chunk * CHUNK, (chunk + 1) * CHUNK)
        lane = iota((CHUNK, 8), 1)
        sums = jnp.zeros((CHUNK, 8), F32)
        for head in range(heads):
            lanes = slice(head * head_width, (head + 1) * head_width)
            q, k = q_ref[0, rows, lanes], k_ref[0, rows, lanes]
            v, cot = v_ref[0, rows, lanes], cot_ref[0, rows, lanes]
            from_start, to_end = columns[:, head : head + 1], columns[:, 4 + head : 5 + head]
            across = dot_nn(q, entering[head]) * from_start
            out_ref[0, rows, lanes] = (out_in[0, rows, lanes].astype(F32) + across).astype(BF16)
            dq_ref[0, rows, lanes] = (
                dq_in[0, rows, lanes].astype(F32) + dot_nt(cot, entering[head]) * from_start
            ).astype(BF16)
            written = dot_nn(k, leaving[head]) * to_end
            dv_ref[0, rows, lanes] = (dv_in[0, rows, lanes].astype(F32) + written).astype(BF16)
            dk_ref[0, rows, lanes] = (
                dk_in[0, rows, lanes].astype(F32) + dot_nt(v, leaving[head]) * to_end
            ).astype(BF16)
            queried = jnp.sum(across * cot.astype(F32), axis=1, keepdims=True)
            kept = jnp.sum(written * v.astype(F32), axis=1, keepdims=True)
            sums = jnp.where(lane == head, queried, jnp.where(lane == 4 + head, kept, sums))
        sums_scr[pl.ds(at, 8), :] = jnp.transpose(sums)

    @pl.when(step == pl.num_programs(0) - 1)
    def _():
        sums = sums_scr[...]
        by_query = dot_nn(sums, lower(False), PRECISE)
        by_key = dot_nn(sums, upper(True), PRECISE)
        last = fac_ref[(num_chunks - 1) * 8 : num_chunks * 8, CHUNK - 1 : CHUNK]
        constants = []
        for head in range(heads):
            product = jnp.sum(state_ref[head] * later_ref[head], axis=(0, 1), keepdims=True)
            constants.append(product * last[head : head + 1])
        base = jnp.concatenate(constants, axis=0)
        for chunk in range(num_chunks):
            lanes = slice(chunk * CHUNK, (chunk + 1) * CHUNK)
            dgate_ref[0, :, lanes] = (
                dgate_in[0, :, lanes]
                + by_query[chunk * 8 : chunk * 8 + 4]
                + by_key[chunk * 8 + 4 : chunk * 8 + 8]
                + base
            )
            if chunk < num_chunks - 1:
                base = base + jnp.sum(
                    sums[chunk * 8 + 4 : chunk * 8 + 8], axis=1, keepdims=True
                )
        tail = jnp.zeros((heads, 1), F32)
        for chunk in range(num_chunks - 2, -1, -1):
            lanes = slice(chunk * CHUNK, (chunk + 1) * CHUNK)
            tail = tail + jnp.sum(
                sums[(chunk + 1) * 8 : (chunk + 1) * 8 + 4], axis=1, keepdims=True
            )
            dgate_ref[0, :, lanes] += tail


def shards(queries, keys_raw, values, gates, lengths, key_gain, cotangent):
    tokens = queries.shape[1]
    width = queries.shape[2]
    heads, head_width = key_gain.shape
    num_chunks = tokens // CHUNK
    rows = num_chunks * 8
    block = min(256, tokens)
    steps = tokens // block
    ctx = lax.axis_index("ctx")
    count = lax.axis_size("ctx")
    streams = (queries, keys_raw, values, cotangent)
    stream_spec = pl.BlockSpec((1, block, width), lambda i: (0, i, 0))
    wide = jax.ShapeDtypeStruct(queries.shape, BF16)

    def whole(array):
        zeros = (0,) * len(array.shape)
        return pl.BlockSpec(array.shape, lambda *_: zeros)

    smem = pl.BlockSpec(memory_space=pltpu.SMEM)
    vmem = pl.BlockSpec(memory_space=pltpu.VMEM)
    table = jax.ShapeDtypeStruct((rows, CHUNK), F32)
    states = jax.ShapeDtypeStruct((heads, head_width, head_width), F32)
    product = 2 * tokens * width * head_width

    cum, chunk_fac, shard_fac, end_raw, local_grad = pl.pallas_call(
        functools.partial(ends_kernel, head_width),
        grid=(steps,),
        in_specs=[smem, smem, whole(gates)] + [stream_spec] * 4,
        out_specs=[whole(table)] * 3 + [whole(states)] * 2,
        out_shape=[table] * 3 + [states] * 2,
        scratch_shapes=[pltpu.VMEM((rows, CHUNK), F32)],
        compiler_params=pltpu.CompilerParams(vmem_limit_bytes=32 << 20),
        cost_estimate=pl.CostEstimate(
            flops=2 * product, bytes_accessed=8 * tokens * width, transcendentals=0
        ),
        name="shard_ends",
    )(lengths, jnp.reshape(ctx, (1,)).astype(jnp.int32), gates, *streams)

    out, dq, dk, dv, dgate, dgain = pl.pallas_call(
        functools.partial(local_kernel, head_width),
        in_specs=[vmem] * 7,
        out_specs=[vmem] * 6,
        out_shape=[wide] * 4
        + [
            jax.ShapeDtypeStruct(gates.shape, F32),
            jax.ShapeDtypeStruct((heads, head_width), F32),
        ],
        scratch_shapes=[
            pltpu.VMEM((num_chunks, heads, head_width, head_width), BF16),
            pltpu.VMEM((heads, head_width, head_width), F32),
        ],
        compiler_params=pltpu.CompilerParams(vmem_limit_bytes=32 << 20),
        cost_estimate=pl.CostEstimate(
            flops=12 * product, bytes_accessed=16 * tokens * width, transcendentals=0
        ),
        name="local_part",
    )(*streams, key_gain, cum, chunk_fac)

    local_end = end_raw * key_gain[:, :, None]
    decay = shard_fac[rows - 8 : rows - 8 + heads, CHUNK - 1][:, None, None]
    state_in = jnp.zeros_like(local_end)
    grad_in = jnp.zeros_like(local_end)
    arrived = None
    for hop in range(count - 1):
        sent = jnp.where(ctx == hop, local_end, local_grad)
        if arrived is not None:
            sent = sent + decay * arrived
        arrived = lax.ppermute(
            sent, "ctx", [(hop, hop + 1), (count - 1 - hop, count - 2 - hop)]
        )
        state_in = jnp.where(ctx == hop + 1, arrived, state_in)
        grad_in = jnp.where(ctx == count - 2 - hop, arrived, grad_in)

    gain_term = dgain + jnp.sum(grad_in * end_raw, axis=2)
    half = head_width // lax.axis_size("dp")
    dp = lax.axis_index("dp")
    away = jnp.where(dp == 0, gain_term[:, half:], gain_term[:, :half])
    kept = jnp.where(dp == 0, gain_term[:, :half], gain_term[:, half:])
    grad_gain = kept + lax.ppermute(away, "dp", [(0, 1), (1, 0)])
    reach = 1
    while reach < count:
        grad_gain = grad_gain + lax.ppermute(
            grad_gain, "ctx", [(i, i ^ reach) for i in range(count)]
        )
        reach *= 2

    merged = pl.pallas_call(
        functools.partial(merge_kernel, head_width),
        grid=(steps,),
        in_specs=[stream_spec] * 4
        + [whole(key_gain), whole(table), whole(states), whole(states)]
        + [stream_spec] * 4
        + [whole(gates)],
        out_specs=[stream_spec] * 4 + [whole(gates)],
        out_shape=[wide] * 4 + [jax.ShapeDtypeStruct(gates.shape, F32)],
        scratch_shapes=[
            pltpu.VMEM((heads, head_width, head_width), BF16),
            pltpu.VMEM((heads, head_width, head_width), BF16),
            pltpu.VMEM((rows, CHUNK), F32),
        ],
        compiler_params=pltpu.CompilerParams(vmem_limit_bytes=32 << 20),
        cost_estimate=pl.CostEstimate(
            flops=4 * product, bytes_accessed=24 * tokens * width, transcendentals=0
        ),
        name="merge_incoming",
    )(*streams, key_gain, shard_fac, state_in, grad_in, out, dq, dk, dv, dgate)
    return (*merged, grad_gain)


def solution(mesh):
    wide = P("dp", "ctx", "head")
    narrow = P("dp", "head", "ctx")
    return jax.shard_map(
        shards,
        mesh=mesh,
        in_specs=(wide, wide, wide, narrow, P("dp", None), P("head", None), wide),
        out_specs=(wide, wide, wide, wide, narrow, P("head", "dp")),
        check_vma=False,
    )
```

time: 241 us -> 75.3 us (0.31)
  matrix products: 65.1 us -> 0 us
  local copies, waits for them, and re-layouts: 63.2 us -> 8.39 us
  Pallas kernels: 0 us -> 28.9 us
  waiting for transfers between devices: 36.2 us -> 7.69 us
  other arithmetic: 30.5 us -> 6.6 us
  between operations: 14.2 us -> 0.8 us
  blocking collectives: 12.4 us -> 0 us
  starting transfers between devices: 17.7 us -> 22.4 us
    dot_general x28 -> x0, matrix products: 65.1 us -> none  [the longest x6 19.2 us: block_step(): jnp.einsum('hts,she->the', weights, v_block, preferred_element_type=jnp.f...]
    pallas_call x0 -> x3, Pallas kernels: none -> 28.9 us  [the longest x1 17.1 us: shards(): pl.pallas_call(functools.partial(local_kernel, head_width), in_specs=[vme...]
    ppermute x6, waiting for transfers between devices: 36.2 us -> 7.69 us  [the longest x3 4.98 us: shards(): lax.ppermute(sent, 'ctx', [(hop, hop + 1), (count - 1 - hop, count - 2 -...]
    another operation x27 -> x0, other arithmetic: 19.4 us -> none
    another operation x36 -> x0, local copies, waits for them, and re-layouts: 13.5 us -> none
    psum x1 -> x0, blocking collectives: 12.4 us -> none  [shards(): gain_total = lax.psum(gain_term, 'ctx')]
    convert_element_type x6 -> x0, local copies, waits for them, and re-layouts: 10.7 us -> none  [the longest x2 4.72 us: shards(): primal.astype(jnp.bfloat16)[None]]
    squeeze x10 -> x0, local copies, waits for them, and re-layouts: 10.3 us -> none  [run_blocks(): lax.scan(jax.checkpoint(make_step(key_gain, head_width)), start_state, (t...]
  transfers between devices with their start and end apart: 7 -> 6, of which waited for: 6 -> 3; matrix products, arithmetic and copies ran while one was open for 3% -> 0% of each run, Pallas kernels for 0% -> 32%
where the time goes in v1:
time: 75.3 us; the launch traced here: 74.8 us
  Pallas kernels  28.9 us (38%)
  starting transfers between devices  22.4 us (30%)
  local copies, waits for them, and re-layouts  8.39 us (11%)
  waiting for transfers between devices  7.69 us (10%)
  other arithmetic  6.6 us (9%)
  between operations  0.8 us (1%)
    pallas_call x1, Pallas kernels, shards(): pl.pallas_call(functools.partial(local_kernel, head_width), in_specs=[vme...  17.1 us
    ppermute x2, starting transfers between devices, shards(): lax.ppermute(grad_gain, 'ctx', [(i, i ^ reach) for i in range(count)])  14.1 us
    ppermute x3, starting transfers between devices, shards(): lax.ppermute(sent, 'ctx', [(hop, hop + 1), (count - 1 - hop, count - 2 -...  8.25 us
    unnamed x24, local copies, waits for them, and re-layouts  8.2 us
    pallas_call x1, Pallas kernels, shards(): pl.pallas_call(functools.partial(merge_kernel, head_width), grid=(steps,)...  7.01 us
    ppermute x3, waiting for transfers between devices, shards(): lax.ppermute(sent, 'ctx', [(hop, hop + 1), (count - 1 - hop, count - 2 -...  4.98 us
    pallas_call x1, Pallas kernels, shards(): pl.pallas_call(functools.partial(ends_kernel, head_width), grid=(steps,),...  4.86 us
    add x2, other arithmetic, shards(): sent = sent + decay * arrived  3.75 us
  transfers between devices with their start and end apart: 6, of which 3 were waited for; matrix products, arithmetic and copies ran while one was open for 0% of the time, Pallas kernels for 32%

profile of v1, /device:TPU:0, one launch (start us, length us, event | category | flops | bytes accessed | tf_op | source)
XLA Modules:
  0.0 74.8 jit_solution(877414128899567257)
XLA Ops:
  0.7 0.6 copy-done.11
  1.3 1.2 %copy-done = bf16[1,1024,512]{2,1,0:T(8,128)(2,1)S(1)} copy-done((bf16[1,1024,512]{2,1,0:T(8,128)(2,1)S(1)}, bf16[1,1024,512]{2,1,0:T(8,128)(2,1)}, u32[]{:S(2)}) %copy-start) | copy-done | bytes 1048600
  2.5 1.2 %copy-done.2 = bf16[1,1024,512]{2,1,0:T(8,128)(2,1)S(1)} copy-done((bf16[1,1024,512]{2,1,0:T(8,128)(2,1)S(1)}, bf16[1,1024,512]{2,1,0:T(8,128)(2,1)}, u32[]{:S(2)}) %copy-start.2) | copy-done | bytes 1048600
  3.7 1.2 %copy-done.4 = bf16[1,1024,512]{2,1,0:T(8,128)(2,1)S(1)} copy-done((bf16[1,1024,512]{2,1,0:T(8,128)(2,1)S(1)}, bf16[1,1024,512]{2,1,0:T(8,128)(2,1)}, u32[]{:S(2)}) %copy-start.4) | copy-done | bytes 1048600
  5.0 1.2 %copy-done.6 = bf16[1,1024,512]{2,1,0:T(8,128)(2,1)S(1)} copy-done((bf16[1,1024,512]{2,1,0:T(8,128)(2,1)S(1)}, bf16[1,1024,512]{2,1,0:T(8,128)(2,1)}, u32[]{:S(2)}) %copy-start.6) | copy-done | bytes 1048600
  6.2 0.7 copy-done.10
  6.9 4.9 %shard_ends.1 = (f32[64,128]{1,0:T(8,128)S(1)}, f32[64,128]{1,0:T(8,128)S(1)}, f32[64,128]{1,0:T(8,128)S(1)}, f32[4,128,128]{2,1,0:T(8,128)S(1)}, f32[4,128,128]{2,1,0:T(8,128)S(1)}) custom-call(s32[1,16]{1,0:T(1,128)S(1)} %copy-done.11, s32[1]{0:T(128)} %bitcast.ctx_ref, f32[1,4,1024]{2,1,0:T(4,128)S(1)} %copy-done.10, bf16[1,1024,512]{2,1,0:T(8,128)(2,1)S(1)} %copy-done, ...), custom_call_target="tpu_custom_call" | custom-call | flops 268435456 | bytes 4194304 | tf_op jit(solution)/shard_map/shard_ends/pallas_call | solution.py:315
  11.8 0.7 copy-done.9
  12.5 0.8 %multiply_select_fusion = f32[4,128,128]{2,1,0:T(8,128)} fusion(f32[4,128,128]{2,1,0:T(8,128)S(1)} %get-tuple-element.24, f32[4,128,128]{2,1,0:T(8,128)S(1)} %get-tuple-element.23, f32[4,128]{1,0:T(4,128)S(1)} %copy-done.9, pred[]{:T(512)S(6)} %eq.24), kind=kLoop, calls=%fused_computation.5 | loop fusion | flops 131072 | bytes 788481 | tf_op jit(solution)/shard_map/jit(_where)/select_n | solution.py:355
  13.3 5.6 %collective-permute-start = (f32[4,128,128]{2,1,0:T(8,128)}, f32[4,128,128]{2,1,0:T(8,128)}, u32[]{:S(2)}, u32[]{:S(2)}) collective-permute-start(f32[4,128,128]{2,1,0:T(8,128)} %multiply_select_fusion), channel_id=1, source_target_pairs={{0,4},{12,8},{1,5},{13,9},{2,6},{14,10},{3,7},{15,11},{16,20},{28,... | collective-permute-start | bytes 786440 | tf_op jit(solution)/shard_map/ppermute | solution.py:358
  19.2 5.0 %collective-permute-done = f32[4,128,128]{2,1,0:T(8,128)} collective-permute-done((f32[4,128,128]{2,1,0:T(8,128)}, f32[4,128,128]{2,1,0:T(8,128)}, u32[]{:S(2)}, u32[]{:S(2)}) %collective-permute-start) | collective-permute-done | bytes 262176 | tf_op jit(solution)/shard_map/ppermute | solution.py:358
  24.1 1.9 %multiply_add_fusion.1 = f32[4,128,128]{2,1,0:T(8,128)} fusion(f32[4,128,128]{2,1,0:T(8,128)} %collective-permute-done, f32[4,128,128]{2,1,0:T(8,128)} %copy-done.8, f32[4,128,128]{2,1,0:T(8,128)S(1)} %get-tuple-element.23, f32[4]{0:T(128)S(1)} %slice_reduce_fusion, f32[4,128]{1,0:T(4,128)S(1)} %copy-done.9, pred[]{:T(512)S(6)} %eq.23), kind=kLoop, calls=%fused_computation.4 | loop fusion | flops 262144 | bytes 1050641 | tf_op jit(solution)/shard_map/add | solution.py:357
  26.0 1.4 %collective-permute-start.1 = (f32[4,128,128]{2,1,0:T(8,128)}, f32[4,128,128]{2,1,0:T(8,128)}, u32[]{:S(2)}, u32[]{:S(2)}) collective-permute-start(f32[4,128,128]{2,1,0:T(8,128)} %multiply_add_fusion.1), channel_id=1, source_target_pairs={{4,8},{8,4},{5,9},{9,5},{6,10},{10,6},{7,11},{11,7},{20,24},{24,20... | collective-permute-start | bytes 786440 | tf_op jit(solution)/shard_map/ppermute | solution.py:358
  27.4 1.9 %multiply_add_fusion = f32[4,128,128]{2,1,0:T(8,128)} fusion(f32[4,128,128]{2,1,0:T(8,128)} %collective-permute-done.1, f32[4,128,128]{2,1,0:T(8,128)} %copy-done.8, f32[4,128,128]{2,1,0:T(8,128)S(1)} %get-tuple-element.23, f32[4]{0:T(128)S(1)} %slice_reduce_fusion, f32[4,128]{1,0:T(4,128)S(1)} %copy-done.9, pred[]{:T(512)S(6)} %eq.22), kind=kLoop, calls=%fused_computation.3 | loop fusion | flops 262144 | bytes 1050641 | tf_op jit(solution)/shard_map/add | solution.py:357
  29.2 1.3 %collective-permute-start.2 = (f32[4,128,128]{2,1,0:T(8,128)}, f32[4,128,128]{2,1,0:T(8,128)}, u32[]{:S(2)}, u32[]{:S(2)}) collective-permute-start(f32[4,128,128]{2,1,0:T(8,128)} %multiply_add_fusion), channel_id=1, source_target_pairs={{8,12},{4,0},{9,13},{5,1},{10,14},{6,2},{11,15},{7,3},{24,28},{20,... | collective-permute-start | bytes 786440 | tf_op jit(solution)/shard_map/ppermute | solution.py:358
  30.6 1.2 %copy-done.7 = bf16[1,1024,512]{2,1,0:T(8,128)(2,1)S(1)} copy-done((bf16[1,1024,512]{2,1,0:T(8,128)(2,1)S(1)}, bf16[1,1024,512]{2,1,0:T(8,128)(2,1)}, u32[]{:S(2)}) %copy-start.7) | copy-done | bytes 1048600
  31.8 17.1 %local_part.1 = (bf16[1,1024,512]{2,1,0:T(8,128)(2,1)S(1)}, bf16[1,1024,512]{2,1,0:T(8,128)(2,1)S(1)}, bf16[1,1024,512]{2,1,0:T(8,128)(2,1)S(1)}, bf16[1,1024,51...) custom-call(bf16[1,1024,512]{2,1,0:T(8,128)(2,1)S(1)} %copy-done.1, ...), custom_call_target="tpu_custom_call" | custom-call | flops 1610612736 | bytes 8388608 | tf_op jit(solution)/shard_map/local_part/pallas_call | solution.py:329
  48.9 1.3 %multiply_reduce_fusion = (f32[4,128]{1,0:T(4,128)S(1)}, f32[4,128,128]{2,1,0:T(8,128)S(1)}, f32[4,128,128]{2,1,0:T(8,128)S(1)}) fusion(f32[4,128,128]{2,1,0:T(8,128)S(1)} %get-tuple-element.23, f32[4,128,128]{2,1,0:T(8,128)} %collective-permute-done.2, f32[4,128,128]{2,1,0:T(8,128)} %collective-permute-done.1, f32[4,128,128]{2,1,0:T(8,128)} %collective-permute-done, ...), kind=kLoop, calls=%fused_computation | loop fusion | flops 523776 | bytes 1574916 | tf_op jit(solution)/shard_map/reduce_sum | solution.py:364
  50.3 1.1 %collective-permute-done.3 = f32[4,64]{1,0:T(4,128)S(1)} collective-permute-done((f32[4,64]{1,0:T(4,128)S(1)}, f32[4,64]{1,0:T(4,128)S(1)}, u32[]{:S(2)}, u32[]{:S(2)}) %collective-permute-start.3) | collective-permute-done | bytes 1056 | tf_op jit(solution)/shard_map/ppermute | solution.py:369
  51.5 11.1 %collective-permute-start.4 = (f32[4,64]{1,0:T(4,128)S(1)}, f32[4,64]{1,0:T(4,128)S(1)}, u32[]{:S(2)}, u32[]{:S(2)}) collective-permute-start(f32[4,64]{1,0:T(4,128)S(1)} %select_add_fusion), channel_id=1, source_target_pairs={{0,4},{4,0},{8,12},{12,8},{1,5},{5,1},{9,13},{13,9},{2,6},{6,2},{1... | collective-permute-start | bytes 3080 | tf_op jit(solution)/shard_map/ppermute | solution.py:372
  62.6 1.6 %collective-permute-done.4 = f32[4,64]{1,0:T(4,128)S(1)} collective-permute-done((f32[4,64]{1,0:T(4,128)S(1)}, f32[4,64]{1,0:T(4,128)S(1)}, u32[]{:S(2)}, u32[]{:S(2)}) %collective-permute-start.4) | collective-permute-done | bytes 1056 | tf_op jit(solution)/shard_map/ppermute | solution.py:372
  64.2 3.0 %collective-permute-start.5 = (f32[4,64]{1,0:T(4,128)S(1)}, f32[4,64]{1,0:T(4,128)S(1)}, u32[]{:S(2)}, u32[]{:S(2)}) collective-permute-start(f32[4,64]{1,0:T(4,128)S(1)} %add.22), channel_id=1, source_target_pairs={{0,8},{4,12},{8,0},{12,4},{1,9},{5,13},{9,1},{13,5},{2,10},{6,14},... | collective-permute-start | bytes 3080 | tf_op jit(solution)/shard_map/ppermute | solution.py:372
  67.2 7.0 %merge_incoming.1 = (bf16[1,1024,512]{2,1,0:T(8,128)(2,1)}, bf16[1,1024,512]{2,1,0:T(8,128)(2,1)}, bf16[1,1024,512]{2,1,0:T(8,128)(2,1)}, bf16[1,1024,512]{2,1,0:T(8,128)(2,1)}, f32[1,4,1024]{2,1,0:T(4,128)}) custom-call(bf16[1,1024,512]{2,1,0:T(8,128)(2,1)S(1)} %copy-done.1, bf16[1,1024,512]{2,1,0:T(8,128)(2,1)S(1)} %copy-done.3, ...), custom_call_target="tpu_custom_call" | custom-call | flops 536870912 | bytes 12582912 | tf_op jit(solution)/shard_map/merge_incoming/pallas_call | solution.py:377
  74.2 0.6 add.23
  (25 shorter events, 0.4 us)
Async XLA Ops:
  0.6 0.7 copy-start.11
  1.3 1.2 %copy-start = (bf16[1,1024,512]{2,1,0:T(8,128)(2,1)S(1)}, bf16[1,1024,512]{2,1,0:T(8,128)(2,1)}, u32[]{:S(2)}) copy-start(bf16[1,1024,512]{2,1,0:T(8,128)(2,1)} %q_ref.5) | copy-start | bytes 3145732
  2.5 1.2 %copy-start.2 = (bf16[1,1024,512]{2,1,0:T(8,128)(2,1)S(1)}, bf16[1,1024,512]{2,1,0:T(8,128)(2,1)}, u32[]{:S(2)}) copy-start(bf16[1,1024,512]{2,1,0:T(8,128)(2,1)} %k_ref.5) | copy-start | bytes 3145732
  3.7 1.2 %copy-start.4 = (bf16[1,1024,512]{2,1,0:T(8,128)(2,1)S(1)}, bf16[1,1024,512]{2,1,0:T(8,128)(2,1)}, u32[]{:S(2)}) copy-start(bf16[1,1024,512]{2,1,0:T(8,128)(2,1)} %v_ref.5) | copy-start | bytes 3145732
  5.0 1.2 %copy-start.6 = (bf16[1,1024,512]{2,1,0:T(8,128)(2,1)S(1)}, bf16[1,1024,512]{2,1,0:T(8,128)(2,1)}, u32[]{:S(2)}) copy-start(bf16[1,1024,512]{2,1,0:T(8,128)(2,1)} %cot_ref.5) | copy-start | bytes 3145732
  6.2 0.7 copy-start.10
  6.9 23.6 %copy-start.5 = (bf16[1,1024,512]{2,1,0:T(8,128)(2,1)S(1)}, bf16[1,1024,512]{2,1,0:T(8,128)(2,1)}, u32[]{:S(2)}) copy-start(bf16[1,1024,512]{2,1,0:T(8,128)(2,1)} %v_ref.5) | copy-start | bytes 3145732
  11.8 1.6 %copy-start.8 = (f32[4,128,128]{2,1,0:T(8,128)}, f32[4,128,128]{2,1,0:T(8,128)S(1)}, u32[]{:S(2)}) copy-start(f32[4,128,128]{2,1,0:T(8,128)S(1)} %get-tuple-element.24) | copy-start | bytes 786436
  11.8 0.7 copy-start.9
  13.3 10.8 %collective-permute-start = (f32[4,128,128]{2,1,0:T(8,128)}, f32[4,128,128]{2,1,0:T(8,128)}, u32[]{:S(2)}, u32[]{:S(2)}) collective-permute-start(f32[4,128,128]{2,1,0:T(8,128)} %multiply_select_fusion), channel_id=1, source_target_pairs={{0,4},{12,8},{1,5},{13,9},{2,6},{14,10},{3,7},{15,11},{16,20},{28,... | collective-permute-start | bytes 786440 | tf_op jit(solution)/shard_map/ppermute | solution.py:358
  19.2 11.4 %copy-start.1 = (bf16[1,1024,512]{2,1,0:T(8,128)(2,1)S(1)}, bf16[1,1024,512]{2,1,0:T(8,128)(2,1)}, u32[]{:S(2)}) copy-start(bf16[1,1024,512]{2,1,0:T(8,128)(2,1)} %q_ref.5) | copy-start | bytes 3145732
  19.2 11.4 %copy-start.3 = (bf16[1,1024,512]{2,1,0:T(8,128)(2,1)S(1)}, bf16[1,1024,512]{2,1,0:T(8,128)(2,1)}, u32[]{:S(2)}) copy-start(bf16[1,1024,512]{2,1,0:T(8,128)(2,1)} %k_ref.5) | copy-start | bytes 3145732
  26.0 1.4 %collective-permute-start.1 = (f32[4,128,128]{2,1,0:T(8,128)}, f32[4,128,128]{2,1,0:T(8,128)}, u32[]{:S(2)}, u32[]{:S(2)}) collective-permute-start(f32[4,128,128]{2,1,0:T(8,128)} %multiply_add_fusion.1), channel_id=1, source_target_pairs={{4,8},{8,4},{5,9},{9,5},{6,10},{10,6},{7,11},{11,7},{20,24},{24,20... | collective-permute-start | bytes 786440 | tf_op jit(solution)/shard_map/ppermute | solution.py:358
  29.2 19.7 %collective-permute-start.2 = (f32[4,128,128]{2,1,0:T(8,128)}, f32[4,128,128]{2,1,0:T(8,128)}, u32[]{:S(2)}, u32[]{:S(2)}) collective-permute-start(f32[4,128,128]{2,1,0:T(8,128)} %multiply_add_fusion), channel_id=1, source_target_pairs={{8,12},{4,0},{9,13},{5,1},{10,14},{6,2},{11,15},{7,3},{24,28},{20,... | collective-permute-start | bytes 786440 | tf_op jit(solution)/shard_map/ppermute | solution.py:358
  30.6 1.2 %copy-start.7 = (bf16[1,1024,512]{2,1,0:T(8,128)(2,1)S(1)}, bf16[1,1024,512]{2,1,0:T(8,128)(2,1)}, u32[]{:S(2)}) copy-start(bf16[1,1024,512]{2,1,0:T(8,128)(2,1)} %cot_ref.5) | copy-start | bytes 3145732
  50.3 1.2 %collective-permute-start.3 = (f32[4,64]{1,0:T(4,128)S(1)}, f32[4,64]{1,0:T(4,128)S(1)}, u32[]{:S(2)}, u32[]{:S(2)}) collective-permute-start(f32[4,64]{1,0:T(4,128)S(1)} %slice_select_fusion), channel_id=1, source_target_pairs={{0,16},{16,0},{1,17},{17,1},{2,18},{18,2},{3,19},{19,3},{4,20},{20... | collective-permute-start | bytes 3080 | tf_op jit(solution)/shard_map/ppermute | solution.py:369
  51.5 12.7 %collective-permute-start.4 = (f32[4,64]{1,0:T(4,128)S(1)}, f32[4,64]{1,0:T(4,128)S(1)}, u32[]{:S(2)}, u32[]{:S(2)}) collective-permute-start(f32[4,64]{1,0:T(4,128)S(1)} %select_add_fusion), channel_id=1, source_target_pairs={{0,4},{4,0},{8,12},{12,8},{1,5},{5,1},{9,13},{13,9},{2,6},{6,2},{1... | collective-permute-start | bytes 3080 | tf_op jit(solution)/shard_map/ppermute | solution.py:372
  64.2 10.1 %collective-permute-start.5 = (f32[4,64]{1,0:T(4,128)S(1)}, f32[4,64]{1,0:T(4,128)S(1)}, u32[]{:S(2)}, u32[]{:S(2)}) collective-permute-start(f32[4,64]{1,0:T(4,128)S(1)} %add.22), channel_id=1, source_target_pairs={{0,8},{4,12},{8,0},{12,4},{1,9},{5,13},{9,1},{13,5},{2,10},{6,14},... | collective-permute-start | bytes 3080 | tf_op jit(solution)/shard_map/ppermute | solution.py:372

commit v2 on v1

v2 whole, which is shorter than its diff:
```python
import functools
import math

import jax
import jax.numpy as jnp
from jax import lax
from jax.experimental import pallas as pl
from jax.experimental.pallas import tpu as pltpu
from jax.sharding import PartitionSpec as P

CHUNK = 128
PARTS = 2
PRECISE = lax.Precision.HIGHEST
F32 = jnp.float32
BF16 = jnp.bfloat16
LOG2E = math.log2(math.e)


def dot_nn(a, b, precision=None):
    return lax.dot_general(
        a, b, (((1,), (0,)), ((), ())), precision=precision, preferred_element_type=F32
    )


def dot_nt(a, b):
    return lax.dot_general(a, b, (((1,), (1,)), ((), ())), preferred_element_type=F32)


def dot_tn(a, b):
    return lax.dot_general(a, b, (((0,), (0,)), ((), ())), preferred_element_type=F32)


def iota(shape, dim):
    return lax.broadcasted_iota(jnp.int32, shape, dim)


def total_of(array):
    return jnp.sum(jnp.sum(array, axis=0, keepdims=True), axis=1, keepdims=True)


def later_sums(column):
    kept = iota((CHUNK, CHUNK), 0) >= iota((CHUNK, CHUNK), 1)
    return jnp.sum(jnp.where(kept, column, 0.0), axis=0, keepdims=True)


def decay_tables(lengths_ref, ctx_ref, gates_ref, spread, cum_ref, chunk_fac_ref, shard_fac_ref):
    rows = cum_ref.shape[0]
    num_chunks = rows // 8
    tokens = num_chunks * CHUNK
    for chunk in range(num_chunks):
        part = gates_ref[0, :, chunk * CHUNK : (chunk + 1) * CHUNK]
        spread[chunk * 8 : chunk * 8 + 4, :] = part
        spread[chunk * 8 + 4 : chunk * 8 + 8, :] = part
    gates = spread[...] * LOG2E
    lane_a, lane_b = iota((CHUNK, CHUNK), 0), iota((CHUNK, CHUNK), 1)
    prefix = dot_nn(gates, (lane_a <= lane_b).astype(F32), PRECISE)
    suffix = dot_nn(gates, (lane_a > lane_b).astype(F32), PRECISE)
    totals = jnp.broadcast_to(prefix[:, CHUNK - 1 : CHUNK], (rows, CHUNK))
    row_a, row_b = iota((rows, rows), 0), iota((rows, rows), 1)
    same = (row_a % 8) == (row_b % 8)
    outside = ((row_a % 8 < 4) & (row_b // 8 < row_a // 8)) | (
        (row_a % 8 >= 4) & (row_b // 8 > row_a // 8)
    )
    others = dot_nn((same & outside).astype(F32), totals, PRECISE)

    first = ctx_ref[0] * tokens
    chunk_first = first + (iota((rows, CHUNK), 0) // 8) * CHUNK
    positions = chunk_first + iota((rows, CHUNK), 1)
    from_start = iota((rows, CHUNK), 0) % 8 < 4
    chunk_anchor = jnp.where(from_start, chunk_first - 1, chunk_first + (CHUNK - 1))
    segment = jnp.zeros((rows, CHUNK), F32)
    chunk_segment = jnp.zeros((rows, CHUNK), F32)
    shard_before = jnp.float32(0)
    shard_last = jnp.float32(0)
    start = jnp.int32(0)
    for doc in range(lengths_ref.shape[1]):
        segment += jnp.where(positions >= start, 1.0, 0.0)
        chunk_segment += jnp.where(chunk_anchor >= start, 1.0, 0.0)
        shard_before += jnp.where(first > start, 1.0, 0.0)
        shard_last += jnp.where(first + (tokens - 1) >= start, 1.0, 0.0)
        start += lengths_ref[0, doc]
    cum_ref[...] = jnp.where(from_start, prefix, segment)
    exponent = jnp.where(from_start, prefix, suffix)
    chunk_fac_ref[...] = jnp.where(
        segment == chunk_segment, jnp.exp2(jnp.minimum(exponent, 0.0)), 0.0
    )
    keep = segment == jnp.where(from_start, shard_before, shard_last)
    shard_fac_ref[...] = jnp.where(keep, jnp.exp2(jnp.minimum(exponent + others, 0.0)), 0.0)


def ends_kernel(head_width, part, half_ctx, *refs):
    if part == 0:
        (lengths_ref, ctx_ref, gates_ref, q_ref, k_ref, v_ref, cot_ref,
         near_ref, far_ref, decay_ref, cum_ref, chunk_fac_ref, shard_fac_ref,
         end_scr, grad_scr, spread) = refs
    else:
        (ctx_ref, shard_fac_ref, q_ref, k_ref, v_ref, cot_ref,
         near_ref, far_ref, decay_ref, end_scr, grad_scr) = refs
    step = pl.program_id(0)
    heads = near_ref.shape[0]
    block = q_ref.shape[1]
    chunks = block // CHUNK
    rows = shard_fac_ref.shape[0]

    @pl.when(step == 0)
    def _():
        if part == 0:
            decay_tables(
                lengths_ref, ctx_ref, gates_ref, spread, cum_ref, chunk_fac_ref, shard_fac_ref
            )
        for head in range(heads):
            row = rows - 8 + part * heads + head
            decay_ref[head] = jnp.broadcast_to(
                shard_fac_ref[row : row + 1, CHUNK - 1 : CHUNK], (1, head_width)
            )
        end_scr[...] = jnp.zeros_like(end_scr)
        grad_scr[...] = jnp.zeros_like(grad_scr)

    columns = []
    for chunk in range(chunks):
        at = pl.multiple_of((step * chunks + chunk) * 8, 8)
        columns.append(jnp.transpose(shard_fac_ref[pl.ds(at, 8), :]))
    factors = jnp.concatenate(columns, axis=0)
    for head in range(heads):
        lanes = slice(head * head_width, (head + 1) * head_width)
        row = part * heads + head
        k_part = (k_ref[0, :, lanes].astype(F32) * factors[:, 4 + row : 5 + row]).astype(BF16)
        q_part = (
            q_ref[0, :, lanes].astype(F32) * (factors[:, row : row + 1] * head_width ** (-0.5))
        ).astype(BF16)
        end_scr[head] += dot_tn(k_part, v_ref[0, :, lanes])
        grad_scr[head] += dot_tn(q_part, cot_ref[0, :, lanes])

    @pl.when(step == pl.num_programs(0) - 1)
    def _():
        low = ctx_ref[0] < half_ctx
        end, grad = end_scr[...], grad_scr[...]
        near_ref[...] = jnp.where(low, end, grad)
        far_ref[...] = jnp.where(low, grad, end)


def local_kernel(
    head_width, part, q_ref, k_ref, v_ref, cot_ref, gain_ref, cum_ref, fac_ref,
    out_ref, dq_ref, dk_ref, dv_ref, dgate_ref, dgain_ref, leaving, state,
):
    heads = state.shape[0]
    num_chunks = leaving.shape[0]
    scale = head_width ** (-0.5)
    unroll = 2 if num_chunks % 2 == 0 else 1

    def lanes_of(head):
        return slice((part * heads + head) * head_width, (part * heads + head + 1) * head_width)

    def own_lanes(head):
        return slice(head * head_width, (head + 1) * head_width)

    def backward(chunk):
        rows = pl.ds(pl.multiple_of(chunk * CHUNK, CHUNK), CHUNK)
        fac = fac_ref[pl.ds(pl.multiple_of(chunk * 8, 8), 8), :]
        columns = jnp.transpose(fac) * scale
        for head in range(heads):
            row = part * heads + head
            lanes = lanes_of(head)
            held = state[head]
            leaving[chunk, head] = held.astype(BF16)
            q_part = (q_ref[0, rows, lanes].astype(F32) * columns[:, row : row + 1]).astype(BF16)
            added = dot_tn(q_part, cot_ref[0, rows, lanes])
            state[head] = held * fac[row : row + 1, CHUNK - 1 : CHUNK] + added

    def forward(chunk):
        rows = pl.ds(pl.multiple_of(chunk * CHUNK, CHUNK), CHUNK)
        fac = fac_ref[pl.ds(pl.multiple_of(chunk * 8, 8), 8), :]
        cum = cum_ref[pl.ds(pl.multiple_of(chunk * 8, 8), 8), :]
        fac_columns = jnp.transpose(fac)
        cum_columns = jnp.transpose(cum)
        same = (cum_columns[:, 4:5] == cum[4:5, :]) & (
            iota((CHUNK, CHUNK), 0) >= iota((CHUNK, CHUNK), 1)
        )
        limit = jnp.where(same, math.log2(scale), -1e30)
        cum_columns = cum_columns + math.log2(scale)
        for head in range(heads):
            row = part * heads + head
            lanes, own = lanes_of(head), own_lanes(head)
            q, v, cot = q_ref[0, rows, lanes], v_ref[0, rows, lanes], cot_ref[0, rows, lanes]
            k_raw = k_ref[0, rows, lanes].astype(F32)
            gain = gain_ref[row : row + 1, :]
            k_wide = k_raw * gain
            k = k_wide.astype(BF16)
            from_start = fac_columns[:, row : row + 1] * scale
            to_end = fac_columns[:, 4 + row : 5 + row]
            decays = jnp.exp2(
                jnp.minimum(cum_columns[:, row : row + 1] - cum[row : row + 1, :], limit)
            )
            held = state[head]
            entering = held.astype(BF16)
            later = leaving[chunk, head]
            by_cot = dot_nt(cot, jnp.concatenate([v, entering], axis=0))
            weights = (dot_nt(q, k) * decays).astype(BF16)
            grad_scores = (by_cot[:, :CHUNK] * decays).astype(BF16)
            q_decayed = (q.astype(F32) * from_start).astype(BF16)
            k_decayed = (k_wide * to_end).astype(BF16)
            out = dot_nn(
                jnp.concatenate([weights, q_decayed], axis=1),
                jnp.concatenate([v, entering], axis=0),
            )
            out_ref[0, rows, own] = out.astype(BF16)
            dq_ref[0, rows, own] = (
                dot_nn(grad_scores, k) + by_cot[:, CHUNK:] * from_start
            ).astype(BF16)
            dv = dot_nn(
                jnp.concatenate([jnp.transpose(weights), k_decayed], axis=1),
                jnp.concatenate([cot, later], axis=0),
            )
            dv_ref[0, rows, own] = dv.astype(BF16)
            grad_k = dot_tn(grad_scores, q) + dot_nt(v, later) * to_end
            dk_ref[0, rows, own] = (grad_k * gain).astype(BF16)
            dgain_ref[head : head + 1, :] += jnp.sum(grad_k * k_raw, axis=0, keepdims=True)
            new_state = held * fac[row : row + 1, CHUNK - 1 : CHUNK] + dot_tn(k_decayed, v)
            state[head] = new_state
            balance = jnp.sum(
                out * cot.astype(F32) - dv * v.astype(F32), axis=1, keepdims=True
            )
            dgate_ref[0, head : head + 1, rows] = later_sums(balance) + total_of(
                new_state * later.astype(F32)
            )

    state[...] = jnp.zeros_like(state)

    def backward_group(index, carry):
        for offset in range(unroll):
            backward(num_chunks - 1 - (index * unroll + offset))
        return carry

    lax.fori_loop(0, num_chunks // unroll, backward_group, 0)
    state[...] = jnp.zeros_like(state)
    dgain_ref[...] = jnp.zeros_like(dgain_ref)

    def forward_group(index, carry):
        for offset in range(unroll):
            forward(index * unroll + offset)
        return carry

    lax.fori_loop(0, num_chunks // unroll, forward_group, 0)


def merge_kernel(head_width, part, half_ctx, *refs):
    (ctx_ref, q_ref, k_ref, v_ref, cot_ref, gain_ref, fac_ref, first_ref, second_ref, last_ref,
     out_in, dq_in, dk_in, dv_in, dgate_in) = refs[:15]
    refs = refs[15:]
    if part > 0:
        before_ref, refs = refs[0], refs[5:]
    out_ref, dq_ref, dk_ref, dv_ref, dgate_ref, entering, leaving, sums_scr, tot_scr = refs
    step = pl.program_id(0)
    heads = first_ref.shape[0]
    block = q_ref.shape[1]
    chunks = block // CHUNK
    num_chunks = fac_ref.shape[0] // 8
    scale = head_width ** (-0.5)

    def arrived(head):
        low = ctx_ref[0] < half_ctx
        first, second = first_ref[head], second_ref[head] + last_ref[head]
        return jnp.where(low, first, second), jnp.where(low, second, first)

    @pl.when(step == 0)
    def _():
        gain_columns = jnp.transpose(jnp.concatenate([gain_ref[...], gain_ref[...]], axis=0))
        entering[...] = jnp.zeros_like(entering)
        leaving[...] = jnp.zeros_like(leaving)
        for head in range(heads):
            row = part * heads + head
            own = slice(head * head_width, (head + 1) * head_width)
            gain = gain_columns[:, row : row + 1]
            state, later = arrived(head)
            entering[own, own] = (state * (gain * scale)).astype(BF16)
            leaving[own, own] = (later * gain).astype(BF16)

    for chunk in range(chunks):
        number = step * chunks + chunk
        columns = jnp.transpose(fac_ref[pl.ds(pl.multiple_of(number * 8, 8), 8), :])
        rows = slice(chunk * CHUNK, (chunk + 1) * CHUNK)
        across_all = dot_nn(q_ref[0, rows, :], entering[...])
        dq_all = dot_nt(cot_ref[0, rows, :], entering[...])
        written_all = dot_nn(k_ref[0, rows, :], leaving[...])
        dk_all = dot_nt(v_ref[0, rows, :], leaving[...])
        for head in range(heads):
            row = part * heads + head
            lanes = slice(head * head_width, (head + 1) * head_width)
            from_start, to_end = columns[:, row : row + 1], columns[:, 4 + row : 5 + row]
            across = across_all[:, lanes] * from_start
            written = written_all[:, lanes] * to_end
            out_ref[0, rows, lanes] = (out_in[0, rows, lanes].astype(F32) + across).astype(BF16)
            dq_ref[0, rows, lanes] = (
                dq_in[0, rows, lanes].astype(F32) + dq_all[:, lanes] * from_start
            ).astype(BF16)
            dv_ref[0, rows, lanes] = (dv_in[0, rows, lanes].astype(F32) + written).astype(BF16)
            dk_ref[0, rows, lanes] = (
                dk_in[0, rows, lanes].astype(F32) + dk_all[:, lanes] * to_end
            ).astype(BF16)
            kept = written * v_ref[0, rows, lanes].astype(F32)
            balance = jnp.sum(
                across * cot_ref[0, rows, lanes].astype(F32) - kept, axis=1, keepdims=True
            )
            sums_scr[number, head : head + 1, :] = later_sums(balance)
            tot_scr[number, head : head + 1, :] = jnp.sum(kept, axis=0, keepdims=True)

    @pl.when(step == pl.num_programs(0) - 1)
    def _():
        last = fac_ref[(num_chunks - 1) * 8 : num_chunks * 8, CHUNK - 1 : CHUNK]
        kept = tot_scr[0]
        for chunk in range(1, num_chunks):
            kept = kept + tot_scr[chunk]
        base = jnp.sum(kept, axis=1, keepdims=True)
        constants = []
        for head in range(heads):
            row = part * heads + head
            state, later = arrived(head)
            gain_columns = jnp.transpose(
                jnp.concatenate([gain_ref[...], gain_ref[...]], axis=0)
            )
            product = total_of(state * later * gain_columns[:, row : row + 1])
            constants.append(product * last[row : row + 1])
        base = base[:heads] + jnp.concatenate(constants, axis=0)
        if part > 0:
            dgate_ref[0, : part * heads, :] = before_ref[0]
        own = slice(part * heads, (part + 1) * heads)
        for chunk in range(num_chunks - 1, -1, -1):
            lanes = slice(chunk * CHUNK, (chunk + 1) * CHUNK)
            sums = sums_scr[chunk, :heads, :]
            dgate_ref[0, own, lanes] = dgate_in[0, :, lanes] + sums + base
            base = base + sums[:, 0:1]


def shards(queries, keys_raw, values, gates, lengths, key_gain, cotangent):
    tokens, width = queries.shape[1:]
    all_heads, head_width = key_gain.shape
    heads = all_heads // PARTS
    part_width = width // PARTS
    num_chunks = tokens // CHUNK
    rows = num_chunks * 8
    block = min(512, tokens)
    steps = tokens // block
    ctx = lax.axis_index("ctx")
    count = lax.axis_size("ctx")
    middle = count // 2 - 1
    streams = (queries, keys_raw, values, cotangent)
    ctx_scalar = jnp.reshape(ctx, (1,)).astype(jnp.int32)

    def stream_spec(part):
        return pl.BlockSpec((1, block, part_width), lambda i: (0, i, part))

    def whole(array):
        zeros = (0,) * len(array.shape)
        return pl.BlockSpec(array.shape, lambda *_: zeros)

    def shape_of(*shape, dtype=F32):
        return jax.ShapeDtypeStruct(shape, dtype)

    smem = pl.BlockSpec(memory_space=pltpu.SMEM)
    vmem = pl.BlockSpec(memory_space=pltpu.VMEM)
    table = shape_of(rows, CHUNK)
    states = shape_of(heads, head_width, head_width)
    decays = shape_of(heads, 1, head_width)
    part_gates = shape_of(1, heads, tokens)
    product = 2 * tokens * part_width * head_width

    def ends(part, *tables):
        specs = [smem, smem, whole(gates)] if part == 0 else [smem, whole(table)]
        outs = [states, states, decays] + ([table] * 3 if part == 0 else [])
        scratch = [pltpu.VMEM(states.shape, F32)] * 2
        if part == 0:
            scratch.append(pltpu.VMEM((rows, CHUNK), F32))
        return pl.pallas_call(
            functools.partial(ends_kernel, head_width, part, count // 2),
            grid=(steps,),
            in_specs=specs + [stream_spec(part)] * 4,
            out_specs=[whole(out) for out in outs],
            out_shape=outs,
            scratch_shapes=scratch,
            compiler_params=pltpu.CompilerParams(vmem_limit_bytes=56 << 20),
            cost_estimate=pl.CostEstimate(
                flops=2 * product, bytes_accessed=8 * tokens * part_width, transcendentals=0
            ),
            name=f"shard_ends_{part}",
        )(*tables, *streams)

    def local(part, arrays, gain, cum, fac):
        wide = shape_of(1, tokens, part_width, dtype=BF16)
        return pl.pallas_call(
            functools.partial(local_kernel, head_width, part),
            in_specs=[vmem] * 7,
            out_specs=[vmem] * 6,
            out_shape=[wide] * 4 + [part_gates, shape_of(heads, head_width)],
            scratch_shapes=[
                pltpu.VMEM((num_chunks, heads, head_width, head_width), BF16),
                pltpu.VMEM((heads, head_width, head_width), F32),
            ],
            compiler_params=pltpu.CompilerParams(vmem_limit_bytes=24 << 20),
            cost_estimate=pl.CostEstimate(
                flops=12 * product, bytes_accessed=16 * tokens * part_width, transcendentals=0
            ),
            name=f"local_{part}",
        )(*arrays, gain, cum, fac)

    def merge(part, arrivals, locals_, done):
        own_spec = pl.BlockSpec((1, block, part_width), lambda i: (0, i, 0))
        full_gates = shape_of(1, (part + 1) * heads, tokens)
        extra, extra_specs, aliases = [], [], {}
        if part > 0:
            extra = [done[4]] + list(done[:4])
            extra_specs = [whole(done[4])] + [pl.BlockSpec(memory_space=pl.ANY)] * 4
            aliases = {16 + i: i for i in range(4)}
        return pl.pallas_call(
            functools.partial(merge_kernel, head_width, part, count // 2),
            grid=(steps,),
            in_specs=[smem]
            + [stream_spec(part)] * 4
            + [whole(key_gain), whole(table)]
            + [whole(states)] * 3
            + [own_spec] * 4
            + [whole(part_gates)]
            + extra_specs,
            out_specs=[stream_spec(part)] * 4 + [whole(full_gates)],
            out_shape=[shape_of(1, tokens, width, dtype=BF16)] * 4 + [full_gates],
            scratch_shapes=[
                pltpu.VMEM((part_width, part_width), BF16),
                pltpu.VMEM((part_width, part_width), BF16),
                pltpu.VMEM((num_chunks, 8, CHUNK), F32),
                pltpu.VMEM((num_chunks, 8, CHUNK), F32),
            ],
            input_output_aliases=aliases,
            compiler_params=pltpu.CompilerParams(vmem_limit_bytes=24 << 20),
            cost_estimate=pl.CostEstimate(
                flops=4 * product, bytes_accessed=24 * tokens * part_width, transcendentals=0
            ),
            name=f"merge_{part}",
        )(ctx_scalar, *streams, key_gain, shard_fac, *arrivals, *locals_, *extra)

    near, far, decay = [None] * PARTS, [None] * PARTS, [None] * PARTS
    near[0], far[0], decay[0], cum, chunk_fac, shard_fac = ends(0, lengths, ctx_scalar, gates)
    sent = [[] for _ in range(PARTS)]
    arrived = [[] for _ in range(PARTS)]
    local_parts = [None] * PARTS

    def send(part, hop):
        payload = near[part] if hop <= middle else far[part]
        if hop > 0:
            payload = payload + decay[part] * arrived[part][-1]
        sent[part].append(payload)
        arrived[part].append(
            lax.ppermute(
                payload, "ctx", [(hop, hop + 1), (count - 1 - hop, count - 2 - hop)]
            )
        )

    for part in range(PARTS):
        if part > 0:
            near[part], far[part], decay[part] = ends(part, ctx_scalar, shard_fac)
        send(part, 0)
    for hop in range(count - 1):
        if hop < PARTS:
            local_cum = cum
            if hop > 0:
                local_cum, _ = lax.optimization_barrier((cum, arrived[0][hop - 1]))
            local_parts[hop] = list(local(hop, streams, key_gain, local_cum, chunk_fac))
            if hop + 1 < count - 1:
                local_parts[hop][5], arrived[0][-1] = lax.optimization_barrier(
                    (local_parts[hop][5], arrived[0][-1])
                )
        if hop + 1 < count - 1:
            for part in range(PARTS):
                send(part, hop + 1)

    terms = []
    for part in range(PARTS):
        crossed = jnp.sum(sent[part][middle] * arrived[part][middle], axis=2)
        term = local_parts[part][5] + jnp.where(ctx == middle, crossed, 0.0)
        if middle > 0:
            term = term + jnp.sum(sum(arrived[part][:middle]) * far[part], axis=2)
        terms.append(term)
    gain_term = jnp.concatenate(terms, axis=0)
    half = head_width // lax.axis_size("dp")
    dp = lax.axis_index("dp")
    away = jnp.where(dp == 0, gain_term[:, half:], gain_term[:, :half])
    kept = jnp.where(dp == 0, gain_term[:, :half], gain_term[:, half:])
    grad_gain = kept + lax.ppermute(away, "dp", [(0, 1), (1, 0)])
    reach = 1
    while reach < count:
        grad_gain = grad_gain + lax.ppermute(
            grad_gain, "ctx", [(i, i ^ reach) for i in range(count)]
        )
        reach *= 2

    done = None
    for part in range(PARTS):
        zeros = jnp.zeros(states.shape, F32)
        first = sum(arrived[part][:middle], zeros) if middle != 1 else arrived[part][0]
        second = sum(arrived[part][middle:-1], zeros) if middle != 1 else arrived[part][1]
        done = merge(part, (first, second, arrived[part][-1]), local_parts[part][:5], done)
    return (*done, grad_gain)


def solution(mesh):
    wide = P("dp", "ctx", "head")
    narrow = P("dp", "head", "ctx")
    return jax.shard_map(
        shards,
        mesh=mesh,
        in_specs=(wide, wide, wide, narrow, P("dp", None), P("head", None), wide),
        out_specs=(wide, wide, wide, wide, narrow, P("head", "dp")),
        check_vma=False,
    )
```

time: 75.3 us -> 61.4 us (0.82)
  starting transfers between devices: 22.4 us -> 14.8 us
  other arithmetic: 6.6 us -> 1.1 us
  local copies, waits for them, and re-layouts: 8.39 us -> 3.26 us
  Pallas kernels: 28.9 us -> 31.4 us
  waiting for transfers between devices: 7.69 us -> 9.52 us
    ppermute x2, starting transfers between devices: 14.1 us -> 4.44 us  [shards(): lax.ppermute(grad_gain, 'ctx', [(i, i ^ reach) for i in range(count)])]
    ppermute x2, waiting for transfers between devices: 1.56 us -> 9.5 us  [shards(): lax.ppermute(grad_gain, 'ctx', [(i, i ^ reach) for i in range(count)])]
    ppermute x3 -> x6, waiting for transfers between devices: 4.98 us -> 0.02 us  [send(): lax.ppermute(payload, 'ctx', [(hop, hop + 1), (count - 1 - hop, count - 2...]
    unnamed x24 -> x30, local copies, waits for them, and re-layouts: 8.2 us -> 3.26 us
    add x3 -> x4, other arithmetic: 3.75 us -> 0.06 us  [the longest x2 0.04 us: send(): payload = payload + decay[part] * arrived[part][-1]]
    pallas_call x3 -> x6, Pallas kernels: 28.9 us -> 31.4 us  [the longest x2 14.6 us: local(): pl.pallas_call(functools.partial(local_kernel, head_width, part), in_spec...]
    ppermute x3 -> x6, starting transfers between devices: 8.25 us -> 10.4 us  [send(): lax.ppermute(payload, 'ctx', [(hop, hop + 1), (count - 1 - hop, count - 2...]
    ppermute x1, waiting for transfers between devices: 1.14 us -> 0.01 us  [shards(): grad_gain = kept + lax.ppermute(away, 'dp', [(0, 1), (1, 0)])]
  transfers between devices with their start and end apart: 6 -> 9, of which waited for: 3 -> 2; matrix products, arithmetic and copies ran while one was open for 0% -> 1% of each run, Pallas kernels for 32% -> 37%
where the time goes in v2:
time: 61.4 us; the launch traced here: 61 us
  Pallas kernels  31.4 us (51%)
  starting transfers between devices  14.8 us (24%)
  waiting for transfers between devices  9.52 us (16%)
  local copies, waits for them, and re-layouts  3.26 us (5%)
  other arithmetic  1.1 us (2%)
  between operations  0.91 us (1%)
    pallas_call x2, Pallas kernels, local(): pl.pallas_call(functools.partial(local_kernel, head_width, part), in_spec...  14.6 us
    ppermute x6, starting transfers between devices, send(): lax.ppermute(payload, 'ctx', [(hop, hop + 1), (count - 1 - hop, count - 2...  10.4 us
    ppermute x2, waiting for transfers between devices, shards(): lax.ppermute(grad_gain, 'ctx', [(i, i ^ reach) for i in range(count)])  9.5 us
    pallas_call x2, Pallas kernels, merge(): pl.pallas_call(functools.partial(merge_kernel, head_width, part, count //...  8.71 us
    pallas_call x2, Pallas kernels, ends(): pl.pallas_call(functools.partial(ends_kernel, head_width, part, count //...  8.05 us
    ppermute x2, starting transfers between devices, shards(): lax.ppermute(grad_gain, 'ctx', [(i, i ^ reach) for i in range(count)])  4.44 us
    unnamed x30, local copies, waits for them, and re-layouts  3.26 us
  transfers between devices with their start and end apart: 9, of which 2 were waited for; matrix products, arithmetic and copies ran while one was open for 1% of the time, Pallas kernels for 37%

profile of v2, /device:TPU:0, one launch (start us, length us, event | category | flops | bytes accessed | tf_op | source)
XLA Modules:
  0.0 61.0 jit_solution(7858358701826040974)
XLA Ops:
  0.6 4.3 %shard_ends_0.1 = (f32[2,128,128]{2,1,0:T(8,128)}, f32[2,128,128]{2,1,0:T(8,128)}, f32[2,1,128]{2,1,0:T(1,128)}, f32[64,128]{1,0:T(8,128)}, f32[64,128]{1,0:T(8,128)}, /*index=5*/f32[64,128]{1,0:T(8,128)}) custom-call(s32[1,16]{1,0:T(1,128)} %refs_0_.1, s32[1]{0:T(128)} %bitcast.refs_1_.refs_0_, f32[1,4,1024]{2,1,0:T(4,128)} %refs_2_.4, ...), custom_call_target="tpu_custom_call" | custom-call | flops 134217728 | bytes 2097152 | tf_op jit(solution)/shard_map/shard_ends_0/pallas_call | solution.py:373
  4.9 4.9 %collective-permute-start.3 = (f32[2,128,128]{2,1,0:T(8,128)}, f32[2,128,128]{2,1,0:T(8,128)S(1)}, u32[]{:S(2)}, u32[]{:S(2)}) collective-permute-start(f32[2,128,128]{2,1,0:T(8,128)} %get-tuple-element.49), channel_id=1, source_target_pairs={{0,4},{12,8},{1,5},{13,9},{2,6},{14,10},{3,7},{15,11},{16,20},{28,... | collective-permute-start | bytes 393224 | tf_op jit(solution)/shard_map/ppermute | solution.py:451
  9.9 3.8 %shard_ends_1.1 = (f32[2,128,128]{2,1,0:T(8,128)}, f32[2,128,128]{2,1,0:T(8,128)}, f32[2,1,128]{2,1,0:T(1,128)}) custom-call(s32[1]{0:T(128)} %bitcast.refs_1_.refs_0_, f32[64,128]{1,0:T(8,128)} %get-tuple-element.42.refs_1_.refs_6_, bf16[1,1024,512]{2,1,0:T(8,128)(2,1)} %refs_1_.3, bf16[1,1024,512]{2,1,0:T(8,128)(2,1)} %refs_2_.7, ...), custom_call_target="tpu_custom_call" | custom-call | flops 134217728 | bytes 2097152 | tf_op jit(solution)/shard_map/shard_ends_1/pallas_call | solution.py:373
  13.7 1.3 %collective-permute-start = (f32[2,128,128]{2,1,0:T(8,128)}, f32[2,128,128]{2,1,0:T(8,128)S(1)}, u32[]{:S(2)}, u32[]{:S(2)}) collective-permute-start(f32[2,128,128]{2,1,0:T(8,128)} %get-tuple-element.43), channel_id=1, source_target_pairs={{0,4},{12,8},{1,5},{13,9},{2,6},{14,10},{3,7},{15,11},{16,20},{28,... | collective-permute-start | bytes 393224 | tf_op jit(solution)/shard_map/ppermute | solution.py:451
  15.0 0.6 %copy-done.8 = f32[4,128]{1,0:T(4,128)S(1)} copy-done((f32[4,128]{1,0:T(4,128)S(1)}, f32[4,128]{1,0:T(4,128)}, u32[]{:S(2)}) %copy-start.8) | copy-done | bytes 2072
  15.7 1.2 %copy-done.3 = bf16[1,1024,512]{2,1,0:T(8,128)(2,1)S(1)} copy-done((bf16[1,1024,512]{2,1,0:T(8,128)(2,1)S(1)}, bf16[1,1024,512]{2,1,0:T(8,128)(2,1)}, u32[]{:S(2)}) %copy-start.3) | copy-done | bytes 1048600
  16.9 7.3 %local_0.1 = (bf16[1,1024,256]{2,1,0:T(8,128)(2,1)S(1)}, bf16[1,1024,256]{2,1,0:T(8,128)(2,1)S(1)}, bf16[1,1024,256]{2,1,0:T(8,128)(2,1)S(1)}, bf16[1,1024,256]{...) custom-call(bf16[1,1024,512]{2,1,0:T(8,128)(2,1)S(1)} %copy-done, ...), custom_call_target="tpu_custom_call" | custom-call | flops 805306368 | bytes 4194304 | tf_op jit(solution)/shard_map/local_0/pallas_call | solution.py:389
  24.2 0.7 %copy-done.14 = f32[2,1,128]{2,1,0:T(1,128)S(1)} copy-done((f32[2,1,128]{2,1,0:T(1,128)S(1)}, f32[2,1,128]{2,1,0:T(1,128)}, u32[]{:S(2)}) %copy-start.14) | copy-done | bytes 1048
  24.9 0.8 %collective-permute-start.4 = (f32[2,128,128]{2,1,0:T(8,128)S(1)}, f32[2,128,128]{2,1,0:T(8,128)S(1)}, u32[]{:S(2)}, u32[]{:S(2)}) collective-permute-start(f32[2,128,128]{2,1,0:T(8,128)S(1)} %multiply_add_fusion.1), channel_id=1, source_target_pairs={{4,8},{8,4},{5,9},{9,5},{6,10},{10,6},{7,11},{11,7},{20,24},{24,20... | collective-permute-start | bytes 393224 | tf_op jit(solution)/shard_map/ppermute | solution.py:451
  25.8 0.6 %copy-done.13 = f32[2,1,128]{2,1,0:T(1,128)S(1)} copy-done((f32[2,1,128]{2,1,0:T(1,128)S(1)}, f32[2,1,128]{2,1,0:T(1,128)}, u32[]{:S(2)}) %copy-start.13) | copy-done | bytes 1048
  26.4 0.8 %collective-permute-start.1 = (f32[2,128,128]{2,1,0:T(8,128)S(1)}, f32[2,128,128]{2,1,0:T(8,128)S(1)}, u32[]{:S(2)}, u32[]{:S(2)}) collective-permute-start(f32[2,128,128]{2,1,0:T(8,128)S(1)} %multiply_add_fusion.3), channel_id=1, source_target_pairs={{4,8},{8,4},{5,9},{9,5},{6,10},{10,6},{7,11},{11,7},{20,24},{24,20... | collective-permute-start | bytes 393224 | tf_op jit(solution)/shard_map/ppermute | solution.py:451
  27.3 7.3 %local_1.1 = (bf16[1,1024,256]{2,1,0:T(8,128)(2,1)S(1)}, bf16[1,1024,256]{2,1,0:T(8,128)(2,1)S(1)}, bf16[1,1024,256]{2,1,0:T(8,128)(2,1)S(1)}, bf16[1,1024,256]{...) custom-call(bf16[1,1024,512]{2,1,0:T(8,128)(2,1)S(1)} %copy-done, ...), custom_call_target="tpu_custom_call" | custom-call | flops 805306368 | bytes 4194304 | tf_op jit(solution)/shard_map/local_1/pallas_call | solution.py:389
  34.6 0.2 multiply_reduce_fusion.3
  34.8 0.2 multiply_reduce_fusion.1
  35.1 1.3 %collective-permute-start.2 = (f32[2,128,128]{2,1,0:T(8,128)S(1)}, f32[2,128,128]{2,1,0:T(8,128)S(1)}, u32[]{:S(2)}, u32[]{:S(2)}) collective-permute-start(f32[2,128,128]{2,1,0:T(8,128)S(1)} %get-tuple-element.82), channel_id=1, source_target_pairs={{8,12},{4,0},{9,13},{5,1},{10,14},{6,2},{11,15},{7,3},{24,28},{20,... | collective-permute-start | bytes 393224 | tf_op jit(solution)/shard_map/ppermute | solution.py:451
  36.4 1.3 %collective-permute-start.5 = (f32[2,128,128]{2,1,0:T(8,128)S(1)}, f32[2,128,128]{2,1,0:T(8,128)S(1)}, u32[]{:S(2)}, u32[]{:S(2)}) collective-permute-start(f32[2,128,128]{2,1,0:T(8,128)S(1)} %get-tuple-element.79), channel_id=1, source_target_pairs={{8,12},{4,0},{9,13},{5,1},{10,14},{6,2},{11,15},{7,3},{24,28},{20,... | collective-permute-start | bytes 393224 | tf_op jit(solution)/shard_map/ppermute | solution.py:451
  37.7 0.1 select_add_fusion
  37.8 3.9 %collective-permute-start.7 = (f32[4,64]{1,0:T(4,128)S(1)}, f32[4,64]{1,0:T(4,128)S(1)}, u32[]{:S(2)}, u32[]{:S(2)}) collective-permute-start(f32[4,64]{1,0:T(4,128)S(1)} %select_add_fusion), channel_id=1, source_target_pairs={{0,4},{4,0},{8,12},{12,8},{1,5},{5,1},{9,13},{13,9},{2,6},{6,2},{1... | collective-permute-start | bytes 3080 | tf_op jit(solution)/shard_map/ppermute | solution.py:489
  41.7 5.6 %collective-permute-done.7 = f32[4,64]{1,0:T(4,128)S(1)} collective-permute-done((f32[4,64]{1,0:T(4,128)S(1)}, f32[4,64]{1,0:T(4,128)S(1)}, u32[]{:S(2)}, u32[]{:S(2)}) %collective-permute-start.7) | collective-permute-done | bytes 1056 | tf_op jit(solution)/shard_map/ppermute | solution.py:489
  47.2 0.6 collective-permute-start.8
  47.8 3.9 %collective-permute-done.8 = f32[4,64]{1,0:T(4,128)S(1)} collective-permute-done((f32[4,64]{1,0:T(4,128)S(1)}, f32[4,64]{1,0:T(4,128)S(1)}, u32[]{:S(2)}, u32[]{:S(2)}) %collective-permute-start.8) | collective-permute-done | bytes 1056 | tf_op jit(solution)/shard_map/ppermute | solution.py:489
  51.7 0.6 add.43
  52.3 4.4 %merge_0.1 = (bf16[1,1024,512]{2,1,0:T(8,128)(2,1)}, bf16[1,1024,512]{2,1,0:T(8,128)(2,1)}, bf16[1,1024,512]{2,1,0:T(8,128)(2,1)}, bf16[1,1024,512]{2,1,0:T(8,128)(2,1)}, f32[1,2,1024]{2,1,0:T(2,128)S(1)}) custom-call(s32[1]{0:T(128)} %bitcast.refs_1_.refs_0_, bf16[1,1024,512]{2,1,0:T(8,128)(2,1)S(1)} %copy-done, bf16[1,1024,512]{2,1,0:T(8,128)(2,1)S(1)} %copy-done.1, ...), custom_call_target="tpu_custom_call" | custom-call | flops 268435456 | bytes 6291456 | tf_op jit(solution)/shard_map/merge_0/pallas_call | solution.py:413
  56.7 4.4 %merge_1.1 = (bf16[1,1024,512]{2,1,0:T(8,128)(2,1)}, bf16[1,1024,512]{2,1,0:T(8,128)(2,1)}, bf16[1,1024,512]{2,1,0:T(8,128)(2,1)}, bf16[1,1024,512]{2,1,0:T(8,128)(2,1)}, f32[1,4,1024]{2,1,0:T(4,128)}) custom-call(s32[1]{0:T(128)} %bitcast.refs_1_.refs_0_, ...), custom_call_target="tpu_custom_call", output_to_operand_aliasing={{0}: (16, {}), {1}: (17, {}), {2}: (18, {}), {3}: (19, {})} | custom-call | flops 268435456 | bytes 6291456 | tf_op jit(solution)/shard_map/merge_1/pallas_call | solution.py:413
  (41 shorter events, 0.3 us)
Async XLA Ops:
  4.9 19.3 %collective-permute-start.3 = (f32[2,128,128]{2,1,0:T(8,128)}, f32[2,128,128]{2,1,0:T(8,128)S(1)}, u32[]{:S(2)}, u32[]{:S(2)}) collective-permute-start(f32[2,128,128]{2,1,0:T(8,128)} %get-tuple-element.49), channel_id=1, source_target_pairs={{0,4},{12,8},{1,5},{13,9},{2,6},{14,10},{3,7},{15,11},{16,20},{28,... | collective-permute-start | bytes 393224 | tf_op jit(solution)/shard_map/ppermute | solution.py:451
  9.9 5.1 %copy-start = (bf16[1,1024,512]{2,1,0:T(8,128)(2,1)S(1)}, bf16[1,1024,512]{2,1,0:T(8,128)(2,1)}, u32[]{:S(2)}) copy-start(bf16[1,1024,512]{2,1,0:T(8,128)(2,1)} %refs_1_.3) | copy-start | bytes 3145732
  9.9 5.1 %copy-start.1 = (bf16[1,1024,512]{2,1,0:T(8,128)(2,1)S(1)}, bf16[1,1024,512]{2,1,0:T(8,128)(2,1)}, u32[]{:S(2)}) copy-start(bf16[1,1024,512]{2,1,0:T(8,128)(2,1)} %refs_2_.7) | copy-start | bytes 3145732
  9.9 5.1 %copy-start.2 = (bf16[1,1024,512]{2,1,0:T(8,128)(2,1)S(1)}, bf16[1,1024,512]{2,1,0:T(8,128)(2,1)}, u32[]{:S(2)}) copy-start(bf16[1,1024,512]{2,1,0:T(8,128)(2,1)} %refs_3_.7) | copy-start | bytes 3145732
  9.9 5.1 %copy-start.6 = (f32[64,128]{1,0:T(8,128)S(1)}, f32[64,128]{1,0:T(8,128)}, u32[]{:S(2)}) copy-start(f32[64,128]{1,0:T(8,128)} %get-tuple-element.51.cum_ref) | copy-start | bytes 98308
  9.9 5.1 %copy-start.7 = (f32[64,128]{1,0:T(8,128)S(1)}, f32[64,128]{1,0:T(8,128)}, u32[]{:S(2)}) copy-start(f32[64,128]{1,0:T(8,128)} %get-tuple-element.47.fac_ref) | copy-start | bytes 98308
  13.7 12.0 %collective-permute-start = (f32[2,128,128]{2,1,0:T(8,128)}, f32[2,128,128]{2,1,0:T(8,128)S(1)}, u32[]{:S(2)}, u32[]{:S(2)}) collective-permute-start(f32[2,128,128]{2,1,0:T(8,128)} %get-tuple-element.43), channel_id=1, source_target_pairs={{0,4},{12,8},{1,5},{13,9},{2,6},{14,10},{3,7},{15,11},{16,20},{28,... | collective-permute-start | bytes 393224 | tf_op jit(solution)/shard_map/ppermute | solution.py:451
  15.0 0.7 %copy-start.8 = (f32[4,128]{1,0:T(4,128)S(1)}, f32[4,128]{1,0:T(4,128)}, u32[]{:S(2)}) copy-start(f32[4,128]{1,0:T(4,128)} %refs_5_.7) | copy-start | bytes 6148
  15.7 1.2 %copy-start.3 = (bf16[1,1024,512]{2,1,0:T(8,128)(2,1)S(1)}, bf16[1,1024,512]{2,1,0:T(8,128)(2,1)}, u32[]{:S(2)}) copy-start(bf16[1,1024,512]{2,1,0:T(8,128)(2,1)} %refs_4_.7) | copy-start | bytes 3145732
  16.9 7.3 %copy-start.11 = (f32[2,128,128]{2,1,0:T(8,128)S(1)}, f32[2,128,128]{2,1,0:T(8,128)}, u32[]{:S(2)}) copy-start(f32[2,128,128]{2,1,0:T(8,128)} %get-tuple-element.49) | copy-start | bytes 393220
  24.2 0.7 %copy-start.14 = (f32[2,1,128]{2,1,0:T(1,128)S(1)}, f32[2,1,128]{2,1,0:T(1,128)}, u32[]{:S(2)}) copy-start(f32[2,1,128]{2,1,0:T(1,128)} %get-tuple-element.58) | copy-start | bytes 3076
  24.9 0.9 %copy-start.12 = (f32[2,128,128]{2,1,0:T(8,128)S(1)}, f32[2,128,128]{2,1,0:T(8,128)}, u32[]{:S(2)}) copy-start(f32[2,128,128]{2,1,0:T(8,128)} %get-tuple-element.43) | copy-start | bytes 393220
  24.9 9.7 %collective-permute-start.4 = (f32[2,128,128]{2,1,0:T(8,128)S(1)}, f32[2,128,128]{2,1,0:T(8,128)S(1)}, u32[]{:S(2)}, u32[]{:S(2)}) collective-permute-start(f32[2,128,128]{2,1,0:T(8,128)S(1)} %multiply_add_fusion.1), channel_id=1, source_target_pairs={{4,8},{8,4},{5,9},{9,5},{6,10},{10,6},{7,11},{11,7},{20,24},{24,20... | collective-permute-start | bytes 393224 | tf_op jit(solution)/shard_map/ppermute | solution.py:451
  25.7 0.7 %copy-start.13 = (f32[2,1,128]{2,1,0:T(1,128)S(1)}, f32[2,1,128]{2,1,0:T(1,128)}, u32[]{:S(2)}) copy-start(f32[2,1,128]{2,1,0:T(1,128)} %get-tuple-element.44) | copy-start | bytes 3076
  26.4 8.2 %copy-start.10 = (f32[2,128,128]{2,1,0:T(8,128)S(1)}, f32[2,128,128]{2,1,0:T(8,128)}, u32[]{:S(2)}) copy-start(f32[2,128,128]{2,1,0:T(8,128)} %get-tuple-element.60) | copy-start | bytes 393220
  26.4 8.3 %collective-permute-start.1 = (f32[2,128,128]{2,1,0:T(8,128)S(1)}, f32[2,128,128]{2,1,0:T(8,128)S(1)}, u32[]{:S(2)}, u32[]{:S(2)}) collective-permute-start(f32[2,128,128]{2,1,0:T(8,128)S(1)} %multiply_add_fusion.3), channel_id=1, source_target_pairs={{4,8},{8,4},{5,9},{9,5},{6,10},{10,6},{7,11},{11,7},{20,24},{24,20... | collective-permute-start | bytes 393224 | tf_op jit(solution)/shard_map/ppermute | solution.py:451
  27.3 7.5 %copy-start.9 = (f32[2,128,128]{2,1,0:T(8,128)S(1)}, f32[2,128,128]{2,1,0:T(8,128)}, u32[]{:S(2)}) copy-start(f32[2,128,128]{2,1,0:T(8,128)} %get-tuple-element.45) | copy-start | bytes 393220
  34.6 17.7 %copy-start.4 = (bf16[1,1024,512]{2,1,0:T(8,128)(2,1)S(1)}, bf16[1,1024,512]{2,1,0:T(8,128)(2,1)}, u32[]{:S(2)}) copy-start(bf16[1,1024,512]{2,1,0:T(8,128)(2,1)} %refs_4_.7) | copy-start | bytes 3145732
  34.9 17.4 %copy-start.5 = (f32[64,128]{1,0:T(8,128)S(1)}, f32[64,128]{1,0:T(8,128)}, u32[]{:S(2)}) copy-start(f32[64,128]{1,0:T(8,128)} %get-tuple-element.42.refs_1_.refs_6_) | copy-start | bytes 98308
  35.1 2.6 %collective-permute-start.6 = (f32[4,64]{1,0:T(4,128)S(1)}, f32[4,64]{1,0:T(4,128)S(1)}, u32[]{:S(2)}, u32[]{:S(2)}) collective-permute-start(f32[4,64]{1,0:T(4,128)S(1)} %slice_select_fusion), channel_id=1, source_target_pairs={{0,16},{16,0},{1,17},{17,1},{2,18},{18,2},{3,19},{19,3},{4,20},{20... | collective-permute-start | bytes 3080 | tf_op jit(solution)/shard_map/ppermute | solution.py:486
  35.1 21.6 %collective-permute-start.2 = (f32[2,128,128]{2,1,0:T(8,128)S(1)}, f32[2,128,128]{2,1,0:T(8,128)S(1)}, u32[]{:S(2)}, u32[]{:S(2)}) collective-permute-start(f32[2,128,128]{2,1,0:T(8,128)S(1)} %get-tuple-element.82), channel_id=1, source_target_pairs={{8,12},{4,0},{9,13},{5,1},{10,14},{6,2},{11,15},{7,3},{24,28},{20,... | collective-permute-start | bytes 393224 | tf_op jit(solution)/shard_map/ppermute | solution.py:451
  36.4 15.9 %collective-permute-start.5 = (f32[2,128,128]{2,1,0:T(8,128)S(1)}, f32[2,128,128]{2,1,0:T(8,128)S(1)}, u32[]{:S(2)}, u32[]{:S(2)}) collective-permute-start(f32[2,128,128]{2,1,0:T(8,128)S(1)} %get-tuple-element.79), channel_id=1, source_target_pairs={{8,12},{4,0},{9,13},{5,1},{10,14},{6,2},{11,15},{7,3},{24,28},{20,... | collective-permute-start | bytes 393224 | tf_op jit(solution)/shard_map/ppermute | solution.py:451
  37.8 9.5 %collective-permute-start.7 = (f32[4,64]{1,0:T(4,128)S(1)}, f32[4,64]{1,0:T(4,128)S(1)}, u32[]{:S(2)}, u32[]{:S(2)}) collective-permute-start(f32[4,64]{1,0:T(4,128)S(1)} %select_add_fusion), channel_id=1, source_target_pairs={{0,4},{4,0},{8,12},{12,8},{1,5},{5,1},{9,13},{13,9},{2,6},{6,2},{1... | collective-permute-start | bytes 3080 | tf_op jit(solution)/shard_map/ppermute | solution.py:489
  47.2 4.5 %collective-permute-start.8 = (f32[4,64]{1,0:T(4,128)S(1)}, f32[4,64]{1,0:T(4,128)S(1)}, u32[]{:S(2)}, u32[]{:S(2)}) collective-permute-start(f32[4,64]{1,0:T(4,128)S(1)} %add.42), channel_id=1, source_target_pairs={{0,8},{4,12},{8,0},{12,4},{1,9},{5,13},{9,1},{13,5},{2,10},{6,14},... | collective-permute-start | bytes 3080 | tf_op jit(solution)/shard_map/ppermute | solution.py:489

commit v3 on v2

--- a/solution.py
+++ b/solution.py
@@ -10,6 +10,7 @@
 
 CHUNK = 128
 PARTS = 2
+UNROLL = 4
 PRECISE = lax.Precision.HIGHEST
 F32 = jnp.float32
 BF16 = jnp.bfloat16
@@ -116,20 +117,26 @@
         end_scr[...] = jnp.zeros_like(end_scr)
         grad_scr[...] = jnp.zeros_like(grad_scr)
 
-    columns = []
+    factors = []
     for chunk in range(chunks):
         at = pl.multiple_of((step * chunks + chunk) * 8, 8)
-        columns.append(jnp.transpose(shard_fac_ref[pl.ds(at, 8), :]))
-    factors = jnp.concatenate(columns, axis=0)
+        factors.append(shard_fac_ref[pl.ds(at, 8), :])
+
+    def turned(ref, lanes, row, scale):
+        pieces = []
+        for chunk in range(chunks):
+            rows_here = slice(chunk * CHUNK, (chunk + 1) * CHUNK)
+            piece = jnp.transpose(ref[0, rows_here, lanes]).astype(F32)
+            pieces.append((piece * (factors[chunk][row : row + 1, :] * scale)).astype(BF16))
+        return jnp.concatenate(pieces, axis=1)
+
     for head in range(heads):
         lanes = slice(head * head_width, (head + 1) * head_width)
         row = part * heads + head
-        k_part = (k_ref[0, :, lanes].astype(F32) * factors[:, 4 + row : 5 + row]).astype(BF16)
-        q_part = (
-            q_ref[0, :, lanes].astype(F32) * (factors[:, row : row + 1] * head_width ** (-0.5))
-        ).astype(BF16)
-        end_scr[head] += dot_tn(k_part, v_ref[0, :, lanes])
-        grad_scr[head] += dot_tn(q_part, cot_ref[0, :, lanes])
+        end_scr[head] += dot_nn(turned(k_ref, lanes, 4 + row, 1.0), v_ref[0, :, lanes])
+        grad_scr[head] += dot_nn(
+            turned(q_ref, lanes, row, head_width ** (-0.5)), cot_ref[0, :, lanes]
+        )
 
     @pl.when(step == pl.num_programs(0) - 1)
     def _():
@@ -146,7 +153,7 @@
     heads = state.shape[0]
     num_chunks = leaving.shape[0]
     scale = head_width ** (-0.5)
-    unroll = 2 if num_chunks % 2 == 0 else 1
+    unroll = math.gcd(num_chunks, UNROLL)
 
     def lanes_of(head):
         return slice((part * heads + head) * head_width, (part * heads + head + 1) * head_width)
@@ -154,81 +161,120 @@
     def own_lanes(head):
         return slice(head * head_width, (head + 1) * head_width)
 
-    def backward(chunk):
-        rows = pl.ds(pl.multiple_of(chunk * CHUNK, CHUNK), CHUNK)
-        fac = fac_ref[pl.ds(pl.multiple_of(chunk * 8, 8), 8), :]
-        columns = jnp.transpose(fac) * scale
-        for head in range(heads):
-            row = part * heads + head
-            lanes = lanes_of(head)
+    def rows_of(chunk):
+        return pl.ds(pl.multiple_of(chunk * CHUNK, CHUNK), CHUNK)
+
+    def table(ref, chunk):
+        return ref[pl.ds(pl.multiple_of(chunk * 8, 8), 8), :]
+
+    pairs = [(at, head) for at in range(unroll) for head in range(heads)]
+
+    def backward(chunks):
+        facs = [table(fac_ref, chunk) for chunk in chunks]
+        added = {}
+        for at, head in pairs:
+            row = part * heads + head
+            rows, lanes = rows_of(chunks[at]), lanes_of(head)
+            turned = jnp.transpose(q_ref[0, rows, lanes]).astype(F32)
+            turned = (turned * (facs[at][row : row + 1, :] * scale)).astype(BF16)
+            added[at, head] = dot_nn(turned, cot_ref[0, rows, lanes])
+        for head in range(heads):
+            row = part * heads + head
             held = state[head]
-            leaving[chunk, head] = held.astype(BF16)
-            q_part = (q_ref[0, rows, lanes].astype(F32) * columns[:, row : row + 1]).astype(BF16)
-            added = dot_tn(q_part, cot_ref[0, rows, lanes])
-            state[head] = held * fac[row : row + 1, CHUNK - 1 : CHUNK] + added
-
-    def forward(chunk):
-        rows = pl.ds(pl.multiple_of(chunk * CHUNK, CHUNK), CHUNK)
-        fac = fac_ref[pl.ds(pl.multiple_of(chunk * 8, 8), 8), :]
-        cum = cum_ref[pl.ds(pl.multiple_of(chunk * 8, 8), 8), :]
-        fac_columns = jnp.transpose(fac)
-        cum_columns = jnp.transpose(cum)
-        same = (cum_columns[:, 4:5] == cum[4:5, :]) & (
-            iota((CHUNK, CHUNK), 0) >= iota((CHUNK, CHUNK), 1)
-        )
-        limit = jnp.where(same, math.log2(scale), -1e30)
-        cum_columns = cum_columns + math.log2(scale)
-        for head in range(heads):
-            row = part * heads + head
-            lanes, own = lanes_of(head), own_lanes(head)
-            q, v, cot = q_ref[0, rows, lanes], v_ref[0, rows, lanes], cot_ref[0, rows, lanes]
-            k_raw = k_ref[0, rows, lanes].astype(F32)
-            gain = gain_ref[row : row + 1, :]
-            k_wide = k_raw * gain
-            k = k_wide.astype(BF16)
-            from_start = fac_columns[:, row : row + 1] * scale
-            to_end = fac_columns[:, 4 + row : 5 + row]
+            for at in range(unroll):
+                leaving[chunks[at], head] = held.astype(BF16)
+                held = held * facs[at][row : row + 1, CHUNK - 1 : CHUNK] + added[at, head]
+            state[head] = held
+
+    def forward(chunks):
+        facs = [table(fac_ref, chunk) for chunk in chunks]
+        cums = [table(cum_ref, chunk) for chunk in chunks]
+        fac_columns = [jnp.transpose(fac) for fac in facs]
+        cum_columns = [jnp.transpose(cum) for cum in cums]
+        causal = iota((CHUNK, CHUNK), 0) >= iota((CHUNK, CHUNK), 1)
+        limits = [
+            jnp.where((columns[:, 4:5] == cum[4:5, :]) & causal, math.log2(scale), -1e30)
+            for columns, cum in zip(cum_columns, cums)
+        ]
+        cum_columns = [columns + math.log2(scale) for columns in cum_columns]
+        q, k, v, cot, k_raw, k_decayed, q_decayed, later = ({} for _ in range(8))
+        from_start, to_end, added, held, entering = ({} for _ in range(5))
+        for key in pairs:
+            at, head = key
+            row = part * heads + head
+            rows, lanes = rows_of(chunks[at]), lanes_of(head)
+            q[key], v[key], cot[key] = q_ref[0, rows, lanes], v_ref[0, rows, lanes], cot_ref[0, rows, lanes]
+            later[key] = leaving[chunks[at], head]
+            k_raw[key] = k_ref[0, rows, lanes].astype(F32)
+            k_wide = k_raw[key] * gain_ref[row : row + 1, :]
+            k[key] = k_wide.astype(BF16)
+            from_start[key] = fac_columns[at][:, row : row + 1] * scale
+            to_end[key] = fac_columns[at][:, 4 + row : 5 + row]
+            k_decayed[key] = (k_wide * to_end[key]).astype(BF16)
+            q_decayed[key] = (q[key].astype(F32) * from_start[key]).astype(BF16)
+            added[key] = dot_tn(k_decayed[key], v[key])
+        for head in range(heads):
+            row = part * heads + head
+            now = state[head]
+            for at in range(unroll):
+                held[at, head] = now
+                entering[at, head] = now.astype(BF16)
+                now = now * facs[at][row : row + 1, CHUNK - 1 : CHUNK] + added[at, head]
+            held[unroll, head] = now
+            state[head] = now
+        by_cot, scores, written = {}, {}, {}
+        for key in pairs:
+            by_cot[key] = dot_nt(cot[key], jnp.concatenate([v[key], entering[key]], axis=0))
+            scores[key] = dot_nt(q[key], k[key])
+            written[key] = dot_nt(v[key], later[key])
+        weights, grad_scores = {}, {}
+        for key in pairs:
+            at, head = key
+            row = part * heads + head
             decays = jnp.exp2(
-                jnp.minimum(cum_columns[:, row : row + 1] - cum[row : row + 1, :], limit)
-            )
-            held = state[head]
-            entering = held.astype(BF16)
-            later = leaving[chunk, head]
-            by_cot = dot_nt(cot, jnp.concatenate([v, entering], axis=0))
-            weights = (dot_nt(q, k) * decays).astype(BF16)
-            grad_scores = (by_cot[:, :CHUNK] * decays).astype(BF16)
-            q_decayed = (q.astype(F32) * from_start).astype(BF16)
-            k_decayed = (k_wide * to_end).astype(BF16)
-            out = dot_nn(
-                jnp.concatenate([weights, q_decayed], axis=1),
-                jnp.concatenate([v, entering], axis=0),
-            )
-            out_ref[0, rows, own] = out.astype(BF16)
-            dq_ref[0, rows, own] = (
-                dot_nn(grad_scores, k) + by_cot[:, CHUNK:] * from_start
-            ).astype(BF16)
-            dv = dot_nn(
-                jnp.concatenate([jnp.transpose(weights), k_decayed], axis=1),
-                jnp.concatenate([cot, later], axis=0),
-            )
-            dv_ref[0, rows, own] = dv.astype(BF16)
-            grad_k = dot_tn(grad_scores, q) + dot_nt(v, later) * to_end
-            dk_ref[0, rows, own] = (grad_k * gain).astype(BF16)
-            dgain_ref[head : head + 1, :] += jnp.sum(grad_k * k_raw, axis=0, keepdims=True)
-            new_state = held * fac[row : row + 1, CHUNK - 1 : CHUNK] + dot_tn(k_decayed, v)
-            state[head] = new_state
+                jnp.minimum(cum_columns[at][:, row : row + 1] - cums[at][row : row + 1, :], limits[at])
+            )
+            weights[key] = (scores[key] * decays).astype(BF16)
+            grad_scores[key] = (by_cot[key][:, :CHUNK] * decays).astype(BF16)
+        out, dq, dk, dv = {}, {}, {}, {}
+        for key in pairs:
+            out[key] = dot_nn(
+                jnp.concatenate([weights[key], q_decayed[key]], axis=1),
+                jnp.concatenate([v[key], entering[key]], axis=0),
+            )
+            dv[key] = dot_nn(
+                jnp.concatenate([jnp.transpose(weights[key]), k_decayed[key]], axis=1),
+                jnp.concatenate([cot[key], later[key]], axis=0),
+            )
+            dq[key] = dot_nn(grad_scores[key], k[key]) + by_cot[key][:, CHUNK:] * from_start[key]
+            dk[key] = dot_tn(grad_scores[key], q[key]) + written[key] * to_end[key]
+        gate_rows, gain_rows = {}, {}
+        for key in pairs:
+            at, head = key
             balance = jnp.sum(
-                out * cot.astype(F32) - dv * v.astype(F32), axis=1, keepdims=True
-            )
-            dgate_ref[0, head : head + 1, rows] = later_sums(balance) + total_of(
-                new_state * later.astype(F32)
-            )
+                out[key] * cot[key].astype(F32) - dv[key] * v[key].astype(F32),
+                axis=1, keepdims=True,
+            )
+            gate_rows[key] = later_sums(balance) + total_of(
+                held[at + 1, head] * later[key].astype(F32)
+            )
+            gain_rows[key] = jnp.sum(dk[key] * k_raw[key], axis=0, keepdims=True)
+        for key in pairs:
+            at, head = key
+            row = part * heads + head
+            rows, own = rows_of(chunks[at]), own_lanes(head)
+            out_ref[0, rows, own] = out[key].astype(BF16)
+            dq_ref[0, rows, own] = dq[key].astype(BF16)
+            dv_ref[0, rows, own] = dv[key].astype(BF16)
+            dk_ref[0, rows, own] = (dk[key] * gain_ref[row : row + 1, :]).astype(BF16)
+            dgate_ref[0, head : head + 1, rows] = gate_rows[key]
+        for head in range(heads):
+            dgain_ref[head : head + 1, :] += sum(gain_rows[at, head] for at in range(unroll))
 
     state[...] = jnp.zeros_like(state)
 
     def backward_group(index, carry):
-        for offset in range(unroll):
-            backward(num_chunks - 1 - (index * unroll + offset))
+        backward([num_chunks - 1 - (index * unroll + at) for at in range(unroll)])
         return carry
 
     lax.fori_loop(0, num_chunks // unroll, backward_group, 0)
@@ -236,8 +282,7 @@
     dgain_ref[...] = jnp.zeros_like(dgain_ref)
 
     def forward_group(index, carry):
-        for offset in range(unroll):
-            forward(index * unroll + offset)
+        forward([index * unroll + at for at in range(unroll)])
         return carry
 
     lax.fori_loop(0, num_chunks // unroll, forward_group, 0)
@@ -275,34 +320,52 @@
             entering[own, own] = (state * (gain * scale)).astype(BF16)
             leaving[own, own] = (later * gain).astype(BF16)
 
+    products, results = [], {}
+    for chunk in range(chunks):
+        rows = slice(chunk * CHUNK, (chunk + 1) * CHUNK)
+        products.append(
+            (
+                dot_nn(q_ref[0, rows, :], entering[...]),
+                dot_nt(cot_ref[0, rows, :], entering[...]),
+                dot_nn(k_ref[0, rows, :], leaving[...]),
+                dot_nt(v_ref[0, rows, :], leaving[...]),
+            )
+        )
     for chunk in range(chunks):
         number = step * chunks + chunk
         columns = jnp.transpose(fac_ref[pl.ds(pl.multiple_of(number * 8, 8), 8), :])
         rows = slice(chunk * CHUNK, (chunk + 1) * CHUNK)
-        across_all = dot_nn(q_ref[0, rows, :], entering[...])
-        dq_all = dot_nt(cot_ref[0, rows, :], entering[...])
-        written_all = dot_nn(k_ref[0, rows, :], leaving[...])
-        dk_all = dot_nt(v_ref[0, rows, :], leaving[...])
         for head in range(heads):
             row = part * heads + head
             lanes = slice(head * head_width, (head + 1) * head_width)
             from_start, to_end = columns[:, row : row + 1], columns[:, 4 + row : 5 + row]
+            across_all, dq_all, written_all, dk_all = products[chunk]
             across = across_all[:, lanes] * from_start
             written = written_all[:, lanes] * to_end
-            out_ref[0, rows, lanes] = (out_in[0, rows, lanes].astype(F32) + across).astype(BF16)
-            dq_ref[0, rows, lanes] = (
-                dq_in[0, rows, lanes].astype(F32) + dq_all[:, lanes] * from_start
-            ).astype(BF16)
-            dv_ref[0, rows, lanes] = (dv_in[0, rows, lanes].astype(F32) + written).astype(BF16)
-            dk_ref[0, rows, lanes] = (
-                dk_in[0, rows, lanes].astype(F32) + dk_all[:, lanes] * to_end
-            ).astype(BF16)
             kept = written * v_ref[0, rows, lanes].astype(F32)
             balance = jnp.sum(
                 across * cot_ref[0, rows, lanes].astype(F32) - kept, axis=1, keepdims=True
             )
-            sums_scr[number, head : head + 1, :] = later_sums(balance)
-            tot_scr[number, head : head + 1, :] = jnp.sum(kept, axis=0, keepdims=True)
+            results[chunk, head] = (
+                (out_in[0, rows, lanes].astype(F32) + across).astype(BF16),
+                (dq_in[0, rows, lanes].astype(F32) + dq_all[:, lanes] * from_start).astype(BF16),
+                (dk_in[0, rows, lanes].astype(F32) + dk_all[:, lanes] * to_end).astype(BF16),
+                (dv_in[0, rows, lanes].astype(F32) + written).astype(BF16),
+                later_sums(balance),
+                jnp.sum(kept, axis=0, keepdims=True),
+            )
+    for chunk in range(chunks):
+        number = step * chunks + chunk
+        rows = slice(chunk * CHUNK, (chunk + 1) * CHUNK)
+        for head in range(heads):
+            lanes = slice(head * head_width, (head + 1) * head_width)
+            out, dq, dk, dv, sums, kept = results[chunk, head]
+            out_ref[0, rows, lanes] = out
+            dq_ref[0, rows, lanes] = dq
+            dk_ref[0, rows, lanes] = dk
+            dv_ref[0, rows, lanes] = dv
+            sums_scr[number, head : head + 1, :] = sums
+            tot_scr[number, head : head + 1, :] = kept
 
     @pl.when(step == pl.num_programs(0) - 1)
     def _():
@@ -338,7 +401,7 @@
     part_width = width // PARTS
     num_chunks = tokens // CHUNK
     rows = num_chunks * 8
-    block = min(512, tokens)
+    block = min(256, tokens)
     steps = tokens // block
     ctx = lax.axis_index("ctx")
     count = lax.axis_size("ctx")
@@ -484,19 +547,25 @@
     away = jnp.where(dp == 0, gain_term[:, half:], gain_term[:, :half])
     kept = jnp.where(dp == 0, gain_term[:, :half], gain_term[:, half:])
     grad_gain = kept + lax.ppermute(away, "dp", [(0, 1), (1, 0)])
-    reach = 1
+
+    done, reach = None, 1
+    for part in range(PARTS):
+        others = jnp.zeros_like(grad_gain)
+        if reach < count:
+            others = lax.ppermute(grad_gain, "ctx", [(i, i ^ reach) for i in range(count)])
+            reach *= 2
+        zeros = jnp.zeros(states.shape, F32)
+        first = sum(arrived[part][:middle], zeros) if middle != 1 else arrived[part][0]
+        second = sum(arrived[part][middle:-1], zeros) if middle != 1 else arrived[part][1]
+        done = list(merge(part, (first, second, arrived[part][-1]), local_parts[part][:5], done))
+        if part < PARTS - 1:
+            done[4], others = lax.optimization_barrier((done[4], others))
+        grad_gain = grad_gain + others
     while reach < count:
         grad_gain = grad_gain + lax.ppermute(
             grad_gain, "ctx", [(i, i ^ reach) for i in range(count)]
         )
         reach *= 2
-
-    done = None
-    for part in range(PARTS):
-        zeros = jnp.zeros(states.shape, F32)
-        first = sum(arrived[part][:middle], zeros) if middle != 1 else arrived[part][0]
-        second = sum(arrived[part][middle:-1], zeros) if middle != 1 else arrived[part][1]
-        done = merge(part, (first, second, arrived[part][-1]), local_parts[part][:5], done)
     return (*done, grad_gain)
 
 

time: 61.4 us -> 50.7 us (0.83)
  waiting for transfers between devices: 9.52 us -> 2.94 us
  Pallas kernels: 31.4 us -> 27.1 us
    ppermute x2, waiting for transfers between devices: 9.5 us -> 0.01 us  [shards(): lax.ppermute(grad_gain, 'ctx', [(i, i ^ reach) for i in range(count)])]
    pallas_call x2, Pallas kernels: 14.6 us -> 9.43 us  [local(): pl.pallas_call(functools.partial(local_kernel, head_width, part), in_spec...]
    ppermute x6, waiting for transfers between devices: 0.02 us -> 2.94 us  [send(): lax.ppermute(payload, 'ctx', [(hop, hop + 1), (count - 1 - hop, count - 2...]
  transfers between devices with their start and end apart: 9 -> 9, of which waited for: 2 -> 1; matrix products, arithmetic and copies ran while one was open for 1% -> 1% of each run, Pallas kernels for 37% -> 45%
where the time goes in v3:
time: 50.7 us; the launch traced here: 50.3 us
  Pallas kernels  27.1 us (53%)
  starting transfers between devices  14.9 us (29%)
  local copies, waits for them, and re-layouts  3.26 us (6%)
  waiting for transfers between devices  2.94 us (6%)
  other arithmetic  1.1 us (2%)
  between operations  0.97 us (2%)
    ppermute x6, starting transfers between devices, send(): lax.ppermute(payload, 'ctx', [(hop, hop + 1), (count - 1 - hop, count - 2...  10.4 us
    pallas_call x2, Pallas kernels, local(): pl.pallas_call(functools.partial(local_kernel, head_width, part), in_spec...  9.43 us
    pallas_call x2, Pallas kernels, merge(): pl.pallas_call(functools.partial(merge_kernel, head_width, part, count //...  9.14 us
    pallas_call x2, Pallas kernels, ends(): pl.pallas_call(functools.partial(ends_kernel, head_width, part, count //...  8.52 us
    ppermute x2, starting transfers between devices, shards(): lax.ppermute(grad_gain, 'ctx', [(i, i ^ reach) for i in range(count)])  4.51 us
    unnamed x30, local copies, waits for them, and re-layouts  3.26 us
    ppermute x6, waiting for transfers between devices, send(): lax.ppermute(payload, 'ctx', [(hop, hop + 1), (count - 1 - hop, count - 2...  2.94 us
  transfers between devices with their start and end apart: 9, of which 1 were waited for; matrix products, arithmetic and copies ran while one was open for 1% of the time, Pallas kernels for 45%

profile of v3, /device:TPU:0, one launch (start us, length us, event | category | flops | bytes accessed | tf_op | source)
XLA Modules:
  0.0 50.3 jit_solution(726579175537034810)
XLA Ops:
  0.6 4.5 %shard_ends_0.1 = (f32[2,128,128]{2,1,0:T(8,128)}, f32[2,128,128]{2,1,0:T(8,128)}, f32[2,1,128]{2,1,0:T(1,128)}, f32[64,128]{1,0:T(8,128)}, f32[64,128]{1,0:T(8,128)}, /*index=5*/f32[64,128]{1,0:T(8,128)}) custom-call(s32[1,16]{1,0:T(1,128)} %refs_0_.1, s32[1]{0:T(128)} %bitcast.refs_1_.refs_0_, f32[1,4,1024]{2,1,0:T(4,128)} %refs_2_.4, ...), custom_call_target="tpu_custom_call" | custom-call | flops 134217728 | bytes 2097152 | tf_op jit(solution)/shard_map/shard_ends_0/pallas_call | solution.py:436
  5.1 4.9 %collective-permute-start.3 = (f32[2,128,128]{2,1,0:T(8,128)}, f32[2,128,128]{2,1,0:T(8,128)S(1)}, u32[]{:S(2)}, u32[]{:S(2)}) collective-permute-start(f32[2,128,128]{2,1,0:T(8,128)} %get-tuple-element.51), channel_id=1, source_target_pairs={{0,4},{12,8},{1,5},{13,9},{2,6},{14,10},{3,7},{15,11},{16,20},{28,... | collective-permute-start | bytes 393224 | tf_op jit(solution)/shard_map/ppermute | solution.py:514
  10.1 4.0 %shard_ends_1.1 = (f32[2,128,128]{2,1,0:T(8,128)}, f32[2,128,128]{2,1,0:T(8,128)}, f32[2,1,128]{2,1,0:T(1,128)}) custom-call(s32[1]{0:T(128)} %bitcast.refs_1_.refs_0_, f32[64,128]{1,0:T(8,128)} %get-tuple-element.44.refs_1_.refs_6_, bf16[1,1024,512]{2,1,0:T(8,128)(2,1)} %refs_1_.3, bf16[1,1024,512]{2,1,0:T(8,128)(2,1)} %refs_2_.7, ...), custom_call_target="tpu_custom_call" | custom-call | flops 134217728 | bytes 2097152 | tf_op jit(solution)/shard_map/shard_ends_1/pallas_call | solution.py:436
  14.1 1.3 %collective-permute-start = (f32[2,128,128]{2,1,0:T(8,128)}, f32[2,128,128]{2,1,0:T(8,128)S(1)}, u32[]{:S(2)}, u32[]{:S(2)}) collective-permute-start(f32[2,128,128]{2,1,0:T(8,128)} %get-tuple-element.45), channel_id=1, source_target_pairs={{0,4},{12,8},{1,5},{13,9},{2,6},{14,10},{3,7},{15,11},{16,20},{28,... | collective-permute-start | bytes 393224 | tf_op jit(solution)/shard_map/ppermute | solution.py:514
  15.5 0.6 %copy-done.8 = f32[4,128]{1,0:T(4,128)S(1)} copy-done((f32[4,128]{1,0:T(4,128)S(1)}, f32[4,128]{1,0:T(4,128)}, u32[]{:S(2)}) %copy-start.8) | copy-done | bytes 2072
  16.1 1.2 %copy-done.3 = bf16[1,1024,512]{2,1,0:T(8,128)(2,1)S(1)} copy-done((bf16[1,1024,512]{2,1,0:T(8,128)(2,1)S(1)}, bf16[1,1024,512]{2,1,0:T(8,128)(2,1)}, u32[]{:S(2)}) %copy-start.3) | copy-done | bytes 1048600
  17.4 4.7 %local_0.1 = (bf16[1,1024,256]{2,1,0:T(8,128)(2,1)S(1)}, bf16[1,1024,256]{2,1,0:T(8,128)(2,1)S(1)}, bf16[1,1024,256]{2,1,0:T(8,128)(2,1)S(1)}, bf16[1,1024,256]{...) custom-call(bf16[1,1024,512]{2,1,0:T(8,128)(2,1)S(1)} %copy-done, ...), custom_call_target="tpu_custom_call" | custom-call | flops 805306368 | bytes 4194304 | tf_op jit(solution)/shard_map/local_0/pallas_call | solution.py:452
  22.1 0.7 %copy-done.14 = f32[2,1,128]{2,1,0:T(1,128)S(1)} copy-done((f32[2,1,128]{2,1,0:T(1,128)S(1)}, f32[2,1,128]{2,1,0:T(1,128)}, u32[]{:S(2)}) %copy-start.14) | copy-done | bytes 1048
  22.8 0.8 %collective-permute-start.4 = (f32[2,128,128]{2,1,0:T(8,128)S(1)}, f32[2,128,128]{2,1,0:T(8,128)S(1)}, u32[]{:S(2)}, u32[]{:S(2)}) collective-permute-start(f32[2,128,128]{2,1,0:T(8,128)S(1)} %multiply_add_fusion.1), channel_id=1, source_target_pairs={{4,8},{8,4},{5,9},{9,5},{6,10},{10,6},{7,11},{11,7},{20,24},{24,20... | collective-permute-start | bytes 393224 | tf_op jit(solution)/shard_map/ppermute | solution.py:514
  23.7 0.6 %copy-done.13 = f32[2,1,128]{2,1,0:T(1,128)S(1)} copy-done((f32[2,1,128]{2,1,0:T(1,128)S(1)}, f32[2,1,128]{2,1,0:T(1,128)}, u32[]{:S(2)}) %copy-start.13) | copy-done | bytes 1048
  24.3 0.8 %collective-permute-start.1 = (f32[2,128,128]{2,1,0:T(8,128)S(1)}, f32[2,128,128]{2,1,0:T(8,128)S(1)}, u32[]{:S(2)}, u32[]{:S(2)}) collective-permute-start(f32[2,128,128]{2,1,0:T(8,128)S(1)} %multiply_add_fusion.3), channel_id=1, source_target_pairs={{4,8},{8,4},{5,9},{9,5},{6,10},{10,6},{7,11},{11,7},{20,24},{24,20... | collective-permute-start | bytes 393224 | tf_op jit(solution)/shard_map/ppermute | solution.py:514
  25.1 4.7 %local_1.1 = (bf16[1,1024,256]{2,1,0:T(8,128)(2,1)S(1)}, bf16[1,1024,256]{2,1,0:T(8,128)(2,1)S(1)}, bf16[1,1024,256]{2,1,0:T(8,128)(2,1)S(1)}, bf16[1,1024,256]{...) custom-call(bf16[1,1024,512]{2,1,0:T(8,128)(2,1)S(1)} %copy-done, ...), custom_call_target="tpu_custom_call" | custom-call | flops 805306368 | bytes 4194304 | tf_op jit(solution)/shard_map/local_1/pallas_call | solution.py:452
  29.9 0.2 multiply_reduce_fusion.3
  30.1 0.2 multiply_reduce_fusion.1
  30.3 0.1 slice_select_fusion
  30.4 1.3 %collective-permute-start.5 = (f32[2,128,128]{2,1,0:T(8,128)S(1)}, f32[2,128,128]{2,1,0:T(8,128)S(1)}, u32[]{:S(2)}, u32[]{:S(2)}) collective-permute-start(f32[2,128,128]{2,1,0:T(8,128)S(1)} %get-tuple-element.83), channel_id=1, source_target_pairs={{8,12},{4,0},{9,13},{5,1},{10,14},{6,2},{11,15},{7,3},{24,28},{20,... | collective-permute-start | bytes 393224 | tf_op jit(solution)/shard_map/ppermute | solution.py:514
  31.7 1.3 %collective-permute-start.2 = (f32[2,128,128]{2,1,0:T(8,128)S(1)}, f32[2,128,128]{2,1,0:T(8,128)S(1)}, u32[]{:S(2)}, u32[]{:S(2)}) collective-permute-start(f32[2,128,128]{2,1,0:T(8,128)S(1)} %get-tuple-element.86), channel_id=1, source_target_pairs={{8,12},{4,0},{9,13},{5,1},{10,14},{6,2},{11,15},{7,3},{24,28},{20,... | collective-permute-start | bytes 393224 | tf_op jit(solution)/shard_map/ppermute | solution.py:514
  33.0 0.1 select_add_fusion
  33.1 3.9 %collective-permute-start.7 = (f32[4,64]{1,0:T(4,128)S(1)}, f32[4,64]{1,0:T(4,128)S(1)}, u32[]{:S(2)}, u32[]{:S(2)}) collective-permute-start(f32[4,64]{1,0:T(4,128)S(1)} %select_add_fusion), channel_id=1, source_target_pairs={{0,4},{4,0},{8,12},{12,8},{1,5},{5,1},{9,13},{13,9},{2,6},{6,2},{1... | collective-permute-start | bytes 3080 | tf_op jit(solution)/shard_map/ppermute | solution.py:555
  37.0 2.9 %collective-permute-done.5.refs_9_ = f32[2,128,128]{2,1,0:T(8,128)S(1)} collective-permute-done((f32[2,128,128]{2,1,0:T(8,128)S(1)}, f32[2,128,128]{2,1,0:T(8,128)S(1)}, u32[]{:S(2)}, u32[]{:S(2)}) %collective-permute-start.5) | collective-permute-done | bytes 131104 | tf_op jit(solution)/shard_map/ppermute | solution.py:514
  39.9 4.6 %merge_0.1 = (bf16[1,1024,512]{2,1,0:T(8,128)(2,1)}, bf16[1,1024,512]{2,1,0:T(8,128)(2,1)}, bf16[1,1024,512]{2,1,0:T(8,128)(2,1)}, bf16[1,1024,512]{2,1,0:T(8,128)(2,1)}, f32[1,2,1024]{2,1,0:T(2,128)S(1)}) custom-call(s32[1]{0:T(128)} %bitcast.refs_1_.refs_0_, bf16[1,1024,512]{2,1,0:T(8,128)(2,1)S(1)} %copy-done, bf16[1,1024,512]{2,1,0:T(8,128)(2,1)S(1)} %copy-done.1, ...), custom_call_target="tpu_custom_call" | custom-call | flops 268435456 | bytes 6291456 | tf_op jit(solution)/shard_map/merge_0/pallas_call | solution.py:476
  44.5 0.6 %collective-permute-start.8 = (f32[4,64]{1,0:T(4,128)S(1)}, f32[4,64]{1,0:T(4,128)S(1)}, u32[]{:S(2)}, u32[]{:S(2)}) collective-permute-start(f32[4,64]{1,0:T(4,128)S(1)} %add.42), channel_id=1, source_target_pairs={{0,8},{4,12},{8,0},{12,4},{1,9},{5,13},{9,1},{13,5},{2,10},{6,14},... | collective-permute-start | bytes 3080 | tf_op jit(solution)/shard_map/ppermute | solution.py:555
  45.1 4.6 %merge_1.1 = (bf16[1,1024,512]{2,1,0:T(8,128)(2,1)}, bf16[1,1024,512]{2,1,0:T(8,128)(2,1)}, bf16[1,1024,512]{2,1,0:T(8,128)(2,1)}, bf16[1,1024,512]{2,1,0:T(8,128)(2,1)}, f32[1,4,1024]{2,1,0:T(4,128)}) custom-call(s32[1]{0:T(128)} %bitcast.refs_1_.refs_0_, ...), custom_call_target="tpu_custom_call", output_to_operand_aliasing={{0}: (16, {}), {1}: (17, {}), {2}: (18, {}), {3}: (19, {})} | custom-call | flops 268435456 | bytes 6291456 | tf_op jit(solution)/shard_map/merge_1/pallas_call | solution.py:476
  49.7 0.6 %add.43 = f32[4,64]{1,0:T(4,128)} add(f32[4,64]{1,0:T(4,128)S(1)} %add.42, f32[4,64]{1,0:T(4,128)S(1)} %collective-permute-done.8) | non-fusion elementwise | flops 256 | bytes 3072 | tf_op jit(solution)/shard_map/add | solution.py:563
  (41 shorter events, 0.2 us)
Async XLA Ops:
  5.1 16.9 %collective-permute-start.3 = (f32[2,128,128]{2,1,0:T(8,128)}, f32[2,128,128]{2,1,0:T(8,128)S(1)}, u32[]{:S(2)}, u32[]{:S(2)}) collective-permute-start(f32[2,128,128]{2,1,0:T(8,128)} %get-tuple-element.51), channel_id=1, source_target_pairs={{0,4},{12,8},{1,5},{13,9},{2,6},{14,10},{3,7},{15,11},{16,20},{28,... | collective-permute-start | bytes 393224 | tf_op jit(solution)/shard_map/ppermute | solution.py:514
  10.0 5.4 %copy-start = (bf16[1,1024,512]{2,1,0:T(8,128)(2,1)S(1)}, bf16[1,1024,512]{2,1,0:T(8,128)(2,1)}, u32[]{:S(2)}) copy-start(bf16[1,1024,512]{2,1,0:T(8,128)(2,1)} %refs_1_.3) | copy-start | bytes 3145732
  10.1 5.4 %copy-start.1 = (bf16[1,1024,512]{2,1,0:T(8,128)(2,1)S(1)}, bf16[1,1024,512]{2,1,0:T(8,128)(2,1)}, u32[]{:S(2)}) copy-start(bf16[1,1024,512]{2,1,0:T(8,128)(2,1)} %refs_2_.7) | copy-start | bytes 3145732
  10.1 5.4 %copy-start.2 = (bf16[1,1024,512]{2,1,0:T(8,128)(2,1)S(1)}, bf16[1,1024,512]{2,1,0:T(8,128)(2,1)}, u32[]{:S(2)}) copy-start(bf16[1,1024,512]{2,1,0:T(8,128)(2,1)} %refs_3_.7) | copy-start | bytes 3145732
  10.1 5.4 %copy-start.6 = (f32[64,128]{1,0:T(8,128)S(1)}, f32[64,128]{1,0:T(8,128)}, u32[]{:S(2)}) copy-start(f32[64,128]{1,0:T(8,128)} %get-tuple-element.53.cum_ref) | copy-start | bytes 98308
  10.1 5.4 %copy-start.7 = (f32[64,128]{1,0:T(8,128)S(1)}, f32[64,128]{1,0:T(8,128)}, u32[]{:S(2)}) copy-start(f32[64,128]{1,0:T(8,128)} %get-tuple-element.49.fac_ref) | copy-start | bytes 98308
  14.1 9.4 %collective-permute-start = (f32[2,128,128]{2,1,0:T(8,128)}, f32[2,128,128]{2,1,0:T(8,128)S(1)}, u32[]{:S(2)}, u32[]{:S(2)}) collective-permute-start(f32[2,128,128]{2,1,0:T(8,128)} %get-tuple-element.45), channel_id=1, source_target_pairs={{0,4},{12,8},{1,5},{13,9},{2,6},{14,10},{3,7},{15,11},{16,20},{28,... | collective-permute-start | bytes 393224 | tf_op jit(solution)/shard_map/ppermute | solution.py:514
  15.4 0.7 %copy-start.8 = (f32[4,128]{1,0:T(4,128)S(1)}, f32[4,128]{1,0:T(4,128)}, u32[]{:S(2)}) copy-start(f32[4,128]{1,0:T(4,128)} %refs_5_.7) | copy-start | bytes 6148
  16.1 1.2 %copy-start.3 = (bf16[1,1024,512]{2,1,0:T(8,128)(2,1)S(1)}, bf16[1,1024,512]{2,1,0:T(8,128)(2,1)}, u32[]{:S(2)}) copy-start(bf16[1,1024,512]{2,1,0:T(8,128)(2,1)} %refs_4_.7) | copy-start | bytes 3145732
  17.4 4.7 %copy-start.11 = (f32[2,128,128]{2,1,0:T(8,128)S(1)}, f32[2,128,128]{2,1,0:T(8,128)}, u32[]{:S(2)}) copy-start(f32[2,128,128]{2,1,0:T(8,128)} %get-tuple-element.51) | copy-start | bytes 393220
  22.1 0.7 %copy-start.14 = (f32[2,1,128]{2,1,0:T(1,128)S(1)}, f32[2,1,128]{2,1,0:T(1,128)}, u32[]{:S(2)}) copy-start(f32[2,1,128]{2,1,0:T(1,128)} %get-tuple-element.60) | copy-start | bytes 3076
  22.7 0.9 %copy-start.12 = (f32[2,128,128]{2,1,0:T(8,128)S(1)}, f32[2,128,128]{2,1,0:T(8,128)}, u32[]{:S(2)}) copy-start(f32[2,128,128]{2,1,0:T(8,128)} %get-tuple-element.45) | copy-start | bytes 393220
  22.8 7.1 %collective-permute-start.4 = (f32[2,128,128]{2,1,0:T(8,128)S(1)}, f32[2,128,128]{2,1,0:T(8,128)S(1)}, u32[]{:S(2)}, u32[]{:S(2)}) collective-permute-start(f32[2,128,128]{2,1,0:T(8,128)S(1)} %multiply_add_fusion.1), channel_id=1, source_target_pairs={{4,8},{8,4},{5,9},{9,5},{6,10},{10,6},{7,11},{11,7},{20,24},{24,20... | collective-permute-start | bytes 393224 | tf_op jit(solution)/shard_map/ppermute | solution.py:514
  23.6 0.7 %copy-start.13 = (f32[2,1,128]{2,1,0:T(1,128)S(1)}, f32[2,1,128]{2,1,0:T(1,128)}, u32[]{:S(2)}) copy-start(f32[2,1,128]{2,1,0:T(1,128)} %get-tuple-element.46) | copy-start | bytes 3076
  24.3 5.6 %copy-start.10 = (f32[2,128,128]{2,1,0:T(8,128)S(1)}, f32[2,128,128]{2,1,0:T(8,128)}, u32[]{:S(2)}) copy-start(f32[2,128,128]{2,1,0:T(8,128)} %get-tuple-element.62) | copy-start | bytes 393220
  24.3 5.8 %collective-permute-start.1 = (f32[2,128,128]{2,1,0:T(8,128)S(1)}, f32[2,128,128]{2,1,0:T(8,128)S(1)}, u32[]{:S(2)}, u32[]{:S(2)}) collective-permute-start(f32[2,128,128]{2,1,0:T(8,128)S(1)} %multiply_add_fusion.3), channel_id=1, source_target_pairs={{4,8},{8,4},{5,9},{9,5},{6,10},{10,6},{7,11},{11,7},{20,24},{24,20... | collective-permute-start | bytes 393224 | tf_op jit(solution)/shard_map/ppermute | solution.py:514
  25.1 5.0 %copy-start.9 = (f32[2,128,128]{2,1,0:T(8,128)S(1)}, f32[2,128,128]{2,1,0:T(8,128)}, u32[]{:S(2)}) copy-start(f32[2,128,128]{2,1,0:T(8,128)} %get-tuple-element.47) | copy-start | bytes 393220
  29.9 10.0 %copy-start.4 = (bf16[1,1024,512]{2,1,0:T(8,128)(2,1)S(1)}, bf16[1,1024,512]{2,1,0:T(8,128)(2,1)}, u32[]{:S(2)}) copy-start(bf16[1,1024,512]{2,1,0:T(8,128)(2,1)} %refs_4_.7) | copy-start | bytes 3145732
  30.3 9.6 %copy-start.5 = (f32[64,128]{1,0:T(8,128)S(1)}, f32[64,128]{1,0:T(8,128)}, u32[]{:S(2)}) copy-start(f32[64,128]{1,0:T(8,128)} %get-tuple-element.44.refs_1_.refs_6_) | copy-start | bytes 98308
  30.4 2.6 %collective-permute-start.6 = (f32[4,64]{1,0:T(4,128)S(1)}, f32[4,64]{1,0:T(4,128)S(1)}, u32[]{:S(2)}, u32[]{:S(2)}) collective-permute-start(f32[4,64]{1,0:T(4,128)S(1)} %slice_select_fusion), channel_id=1, source_target_pairs={{0,16},{16,0},{1,17},{17,1},{2,18},{18,2},{3,19},{19,3},{4,20},{20... | collective-permute-start | bytes 3080 | tf_op jit(solution)/shard_map/ppermute | solution.py:549
  30.4 9.5 %collective-permute-start.5 = (f32[2,128,128]{2,1,0:T(8,128)S(1)}, f32[2,128,128]{2,1,0:T(8,128)S(1)}, u32[]{:S(2)}, u32[]{:S(2)}) collective-permute-start(f32[2,128,128]{2,1,0:T(8,128)S(1)} %get-tuple-element.83), channel_id=1, source_target_pairs={{8,12},{4,0},{9,13},{5,1},{10,14},{6,2},{11,15},{7,3},{24,28},{20,... | collective-permute-start | bytes 393224 | tf_op jit(solution)/shard_map/ppermute | solution.py:514
  31.7 13.4 %collective-permute-start.2 = (f32[2,128,128]{2,1,0:T(8,128)S(1)}, f32[2,128,128]{2,1,0:T(8,128)S(1)}, u32[]{:S(2)}, u32[]{:S(2)}) collective-permute-start(f32[2,128,128]{2,1,0:T(8,128)S(1)} %get-tuple-element.86), channel_id=1, source_target_pairs={{8,12},{4,0},{9,13},{5,1},{10,14},{6,2},{11,15},{7,3},{24,28},{20,... | collective-permute-start | bytes 393224 | tf_op jit(solution)/shard_map/ppermute | solution.py:514
  33.1 11.4 %collective-permute-start.7 = (f32[4,64]{1,0:T(4,128)S(1)}, f32[4,64]{1,0:T(4,128)S(1)}, u32[]{:S(2)}, u32[]{:S(2)}) collective-permute-start(f32[4,64]{1,0:T(4,128)S(1)} %select_add_fusion), channel_id=1, source_target_pairs={{0,4},{4,0},{8,12},{12,8},{1,5},{5,1},{9,13},{13,9},{2,6},{6,2},{1... | collective-permute-start | bytes 3080 | tf_op jit(solution)/shard_map/ppermute | solution.py:555
  44.5 5.2 %collective-permute-start.8 = (f32[4,64]{1,0:T(4,128)S(1)}, f32[4,64]{1,0:T(4,128)S(1)}, u32[]{:S(2)}, u32[]{:S(2)}) collective-permute-start(f32[4,64]{1,0:T(4,128)S(1)} %add.42), channel_id=1, source_target_pairs={{0,8},{4,12},{8,0},{12,4},{1,9},{5,13},{9,1},{13,5},{2,10},{6,14},... | collective-permute-start | bytes 3080 | tf_op jit(solution)/shard_map/ppermute | solution.py:555

commit v4 on v3

--- a/solution.py
+++ b/solution.py
@@ -89,61 +89,70 @@
     shard_fac_ref[...] = jnp.where(keep, jnp.exp2(jnp.minimum(exponent + others, 0.0)), 0.0)
 
 
-def ends_kernel(head_width, part, half_ctx, *refs):
-    if part == 0:
-        (lengths_ref, ctx_ref, gates_ref, q_ref, k_ref, v_ref, cot_ref,
-         near_ref, far_ref, decay_ref, cum_ref, chunk_fac_ref, shard_fac_ref,
-         end_scr, grad_scr, spread) = refs
-    else:
-        (ctx_ref, shard_fac_ref, q_ref, k_ref, v_ref, cot_ref,
-         near_ref, far_ref, decay_ref, end_scr, grad_scr) = refs
-    step = pl.program_id(0)
-    heads = near_ref.shape[0]
-    block = q_ref.shape[1]
+def ends_kernel(head_width, half_ctx, *refs):
+    lengths_ref, ctx_ref, gates_ref = refs[:3]
+    sources, targets = refs[3:7], refs[7:11]
+    near_refs, far_refs, decay_refs = (
+        refs[11 + i * PARTS : 11 + (i + 1) * PARTS] for i in range(3)
+    )
+    cum_ref, chunk_fac_ref, shard_fac_ref, spread, sems = refs[11 + 3 * PARTS :]
+    q_ref, k_ref, v_ref, cot_ref = targets
+    heads = near_refs[0].shape[0]
+    rows = shard_fac_ref.shape[0]
+    steps = sems.shape[0]
+    block = q_ref.shape[1] // steps
     chunks = block // CHUNK
-    rows = shard_fac_ref.shape[0]
-
-    @pl.when(step == 0)
-    def _():
-        if part == 0:
-            decay_tables(
-                lengths_ref, ctx_ref, gates_ref, spread, cum_ref, chunk_fac_ref, shard_fac_ref
-            )
+
+    def copies(step):
+        at = pl.ds(step * block, block)
+        return [
+            pltpu.make_async_copy(source.at[:, at, :], target.at[:, at, :], sems.at[step, i])
+            for i, (source, target) in enumerate(zip(sources, targets))
+        ]
+
+    for step in range(steps):
+        for i, copy in enumerate(copies(step)):
+            copy.start(priority=i % 2)
+    decay_tables(lengths_ref, ctx_ref, gates_ref, spread, cum_ref, chunk_fac_ref, shard_fac_ref)
+    for part in range(PARTS):
         for head in range(heads):
             row = rows - 8 + part * heads + head
-            decay_ref[head] = jnp.broadcast_to(
+            decay_refs[part][head] = jnp.broadcast_to(
                 shard_fac_ref[row : row + 1, CHUNK - 1 : CHUNK], (1, head_width)
             )
-        end_scr[...] = jnp.zeros_like(end_scr)
-        grad_scr[...] = jnp.zeros_like(grad_scr)
-
-    factors = []
-    for chunk in range(chunks):
-        at = pl.multiple_of((step * chunks + chunk) * 8, 8)
-        factors.append(shard_fac_ref[pl.ds(at, 8), :])
-
-    def turned(ref, lanes, row, scale):
+
+    def turned(ref, step, row, scale):
         pieces = []
-        for chunk in range(chunks):
-            rows_here = slice(chunk * CHUNK, (chunk + 1) * CHUNK)
-            piece = jnp.transpose(ref[0, rows_here, lanes]).astype(F32)
-            pieces.append((piece * (factors[chunk][row : row + 1, :] * scale)).astype(BF16))
+        head = row % 4
+        for chunk in range(step * chunks, (step + 1) * chunks):
+            factor = shard_fac_ref[chunk * 8 + row : chunk * 8 + row + 1, :]
+            piece = jnp.transpose(
+                ref[
+                    0,
+                    chunk * CHUNK : (chunk + 1) * CHUNK,
+                    head * head_width : (head + 1) * head_width,
+                ]
+            )
+            pieces.append((piece.astype(F32) * (factor * scale)).astype(BF16))
         return jnp.concatenate(pieces, axis=1)
 
-    for head in range(heads):
-        lanes = slice(head * head_width, (head + 1) * head_width)
-        row = part * heads + head
-        end_scr[head] += dot_nn(turned(k_ref, lanes, 4 + row, 1.0), v_ref[0, :, lanes])
-        grad_scr[head] += dot_nn(
-            turned(q_ref, lanes, row, head_width ** (-0.5)), cot_ref[0, :, lanes]
-        )
-
-    @pl.when(step == pl.num_programs(0) - 1)
-    def _():
-        low = ctx_ref[0] < half_ctx
-        end, grad = end_scr[...], grad_scr[...]
-        near_ref[...] = jnp.where(low, end, grad)
-        far_ref[...] = jnp.where(low, grad, end)
+    ends, grads = {}, {}
+    for step in range(steps):
+        for copy in copies(step):
+            copy.wait()
+        at = slice(step * block, (step + 1) * block)
+        for row in range(PARTS * heads):
+            lanes = slice(row * head_width, (row + 1) * head_width)
+            end = dot_nn(turned(k_ref, step, 4 + row, 1.0), v_ref[0, at, lanes])
+            grad = dot_nn(turned(q_ref, step, row, head_width ** (-0.5)), cot_ref[0, at, lanes])
+            ends[row] = ends[row] + end if step else end
+            grads[row] = grads[row] + grad if step else grad
+    low = ctx_ref[0] < half_ctx
+    for part in range(PARTS):
+        for head in range(heads):
+            row = part * heads + head
+            near_refs[part][head] = jnp.where(low, ends[row], grads[row])
+            far_refs[part][head] = jnp.where(low, grads[row], ends[row])
 
 
 def local_kernel(
@@ -297,7 +306,7 @@
     out_ref, dq_ref, dk_ref, dv_ref, dgate_ref, entering, leaving, sums_scr, tot_scr = refs
     step = pl.program_id(0)
     heads = first_ref.shape[0]
-    block = q_ref.shape[1]
+    block = out_ref.shape[1]
     chunks = block // CHUNK
     num_chunks = fac_ref.shape[0] // 8
     scale = head_width ** (-0.5)
@@ -321,30 +330,36 @@
             leaving[own, own] = (later * gain).astype(BF16)
 
     products, results = [], {}
+    group = slice(part * heads * head_width, (part + 1) * heads * head_width)
+
+    def rows_of(chunk):
+        return pl.ds(pl.multiple_of(step * block + chunk * CHUNK, CHUNK), CHUNK)
+
     for chunk in range(chunks):
-        rows = slice(chunk * CHUNK, (chunk + 1) * CHUNK)
+        rows = rows_of(chunk)
         products.append(
             (
-                dot_nn(q_ref[0, rows, :], entering[...]),
-                dot_nt(cot_ref[0, rows, :], entering[...]),
-                dot_nn(k_ref[0, rows, :], leaving[...]),
-                dot_nt(v_ref[0, rows, :], leaving[...]),
+                dot_nn(q_ref[0, rows, group], entering[...]),
+                dot_nt(cot_ref[0, rows, group], entering[...]),
+                dot_nn(k_ref[0, rows, group], leaving[...]),
+                dot_nt(v_ref[0, rows, group], leaving[...]),
             )
         )
     for chunk in range(chunks):
         number = step * chunks + chunk
         columns = jnp.transpose(fac_ref[pl.ds(pl.multiple_of(number * 8, 8), 8), :])
-        rows = slice(chunk * CHUNK, (chunk + 1) * CHUNK)
+        rows = rows_of(chunk)
         for head in range(heads):
             row = part * heads + head
             lanes = slice(head * head_width, (head + 1) * head_width)
+            wide = slice(row * head_width, (row + 1) * head_width)
             from_start, to_end = columns[:, row : row + 1], columns[:, 4 + row : 5 + row]
             across_all, dq_all, written_all, dk_all = products[chunk]
             across = across_all[:, lanes] * from_start
             written = written_all[:, lanes] * to_end
-            kept = written * v_ref[0, rows, lanes].astype(F32)
+            kept = written * v_ref[0, rows, wide].astype(F32)
             balance = jnp.sum(
-                across * cot_ref[0, rows, lanes].astype(F32) - kept, axis=1, keepdims=True
+                across * cot_ref[0, rows, wide].astype(F32) - kept, axis=1, keepdims=True
             )
             results[chunk, head] = (
                 (out_in[0, rows, lanes].astype(F32) + across).astype(BF16),
@@ -406,7 +421,6 @@
     ctx = lax.axis_index("ctx")
     count = lax.axis_size("ctx")
     middle = count // 2 - 1
-    streams = (queries, keys_raw, values, cotangent)
     ctx_scalar = jnp.reshape(ctx, (1,)).astype(jnp.int32)
 
     def stream_spec(part):
@@ -427,25 +441,24 @@
     part_gates = shape_of(1, heads, tokens)
     product = 2 * tokens * part_width * head_width
 
-    def ends(part, *tables):
-        specs = [smem, smem, whole(gates)] if part == 0 else [smem, whole(table)]
-        outs = [states, states, decays] + ([table] * 3 if part == 0 else [])
-        scratch = [pltpu.VMEM(states.shape, F32)] * 2
-        if part == 0:
-            scratch.append(pltpu.VMEM((rows, CHUNK), F32))
+    def ends():
+        held = shape_of(1, tokens, width, dtype=BF16)
+        outs = [held] * 4 + [states] * (2 * PARTS) + [decays] * PARTS + [table] * 3
         return pl.pallas_call(
-            functools.partial(ends_kernel, head_width, part, count // 2),
-            grid=(steps,),
-            in_specs=specs + [stream_spec(part)] * 4,
-            out_specs=[whole(out) for out in outs],
+            functools.partial(ends_kernel, head_width, count // 2),
+            in_specs=[smem, smem, vmem] + [pl.BlockSpec(memory_space=pltpu.HBM)] * 4,
+            out_specs=[vmem] * len(outs),
             out_shape=outs,
-            scratch_shapes=scratch,
+            scratch_shapes=[
+                pltpu.VMEM((rows, CHUNK), F32),
+                pltpu.SemaphoreType.DMA((steps, 4)),
+            ],
             compiler_params=pltpu.CompilerParams(vmem_limit_bytes=56 << 20),
             cost_estimate=pl.CostEstimate(
-                flops=2 * product, bytes_accessed=8 * tokens * part_width, transcendentals=0
+                flops=2 * product * PARTS, bytes_accessed=8 * tokens * width, transcendentals=0
             ),
-            name=f"shard_ends_{part}",
-        )(*tables, *streams)
+            name="shard_ends",
+        )(lengths, ctx_scalar, gates, queries, keys_raw, values, cotangent)
 
     def local(part, arrays, gain, cum, fac):
         wide = shape_of(1, tokens, part_width, dtype=BF16)
@@ -466,23 +479,16 @@
         )(*arrays, gain, cum, fac)
 
     def merge(part, arrivals, locals_, done):
-        own_spec = pl.BlockSpec((1, block, part_width), lambda i: (0, i, 0))
         full_gates = shape_of(1, (part + 1) * heads, tokens)
         extra, extra_specs, aliases = [], [], {}
         if part > 0:
             extra = [done[4]] + list(done[:4])
-            extra_specs = [whole(done[4])] + [pl.BlockSpec(memory_space=pl.ANY)] * 4
+            extra_specs = [vmem] + [pl.BlockSpec(memory_space=pl.ANY)] * 4
             aliases = {16 + i: i for i in range(4)}
         return pl.pallas_call(
             functools.partial(merge_kernel, head_width, part, count // 2),
             grid=(steps,),
-            in_specs=[smem]
-            + [stream_spec(part)] * 4
-            + [whole(key_gain), whole(table)]
-            + [whole(states)] * 3
-            + [own_spec] * 4
-            + [whole(part_gates)]
-            + extra_specs,
+            in_specs=[smem] + [vmem] * 14 + extra_specs,
             out_specs=[stream_spec(part)] * 4 + [whole(full_gates)],
             out_shape=[shape_of(1, tokens, width, dtype=BF16)] * 4 + [full_gates],
             scratch_shapes=[
@@ -499,8 +505,10 @@
             name=f"merge_{part}",
         )(ctx_scalar, *streams, key_gain, shard_fac, *arrivals, *locals_, *extra)
 
-    near, far, decay = [None] * PARTS, [None] * PARTS, [None] * PARTS
-    near[0], far[0], decay[0], cum, chunk_fac, shard_fac = ends(0, lengths, ctx_scalar, gates)
+    results = ends()
+    streams, results = results[:4], results[4:]
+    near, far, decay = (results[i * PARTS : (i + 1) * PARTS] for i in range(3))
+    cum, chunk_fac, shard_fac = results[3 * PARTS :]
     sent = [[] for _ in range(PARTS)]
     arrived = [[] for _ in range(PARTS)]
     local_parts = [None] * PARTS
@@ -517,8 +525,6 @@
         )
 
     for part in range(PARTS):
-        if part > 0:
-            near[part], far[part], decay[part] = ends(part, ctx_scalar, shard_fac)
         send(part, 0)
     for hop in range(count - 1):
         if hop < PARTS:

time: 50.7 us -> 53 us (1.045)
  local copies, waits for them, and re-layouts: 3.26 us -> 8.46 us
  Pallas kernels: 27.1 us -> 24 us
    unnamed x30, local copies, waits for them, and re-layouts: 3.26 us -> 8.46 us
    pallas_call x2 -> x1, Pallas kernels: 8.52 us -> 5.98 us  [ends(): pl.pallas_call(functools.partial(ends_kernel, head_width, count // 2), in...]
  transfers between devices with their start and end apart: 9 -> 9, of which waited for: 1 -> 1; matrix products, arithmetic and copies ran while one was open for 1% -> 1% of each run, Pallas kernels for 45% -> 34%
where the time goes in v4:
time: 53 us; the launch traced here: 52.4 us
  Pallas kernels  24 us (45%)
  starting transfers between devices  14.9 us (28%)
  local copies, waits for them, and re-layouts  8.46 us (16%)
  waiting for transfers between devices  2.94 us (6%)
  other arithmetic  1.12 us (2%)
  between operations  0.91 us (2%)
    ppermute x6, starting transfers between devices, send(): lax.ppermute(payload, 'ctx', [(hop, hop + 1), (count - 1 - hop, count - 2...  10.4 us
    pallas_call x2, Pallas kernels, local(): pl.pallas_call(functools.partial(local_kernel, head_width, part), in_spec...  9.44 us
    pallas_call x2, Pallas kernels, merge(): pl.pallas_call(functools.partial(merge_kernel, head_width, part, count //...  8.63 us
    unnamed x30, local copies, waits for them, and re-layouts  8.46 us
    pallas_call x1, Pallas kernels, ends(): pl.pallas_call(functools.partial(ends_kernel, head_width, count // 2), in...  5.98 us
    ppermute x2, starting transfers between devices, shards(): lax.ppermute(grad_gain, 'ctx', [(i, i ^ reach) for i in range(count)])  4.5 us
    ppermute x6, waiting for transfers between devices, send(): lax.ppermute(payload, 'ctx', [(hop, hop + 1), (count - 1 - hop, count - 2...  2.94 us
  transfers between devices with their start and end apart: 9, of which 1 were waited for; matrix products, arithmetic and copies ran while one was open for 1% of the time, Pallas kernels for 34%

profile of v4, /device:TPU:0, one launch (start us, length us, event | category | flops | bytes accessed | tf_op | source)
XLA Modules:
  0.0 52.4 jit_solution(16617622281559181171)
XLA Ops:
  0.6 6.0 %shard_ends.1 = (bf16[1,1024,512]{2,1,0:T(8,128)(2,1)}, bf16[1,1024,512]{2,1,0:T(8,128)(2,1)}, bf16[1,1024,512]{2,1,0:T(8,128)(2,1)}, bf16[1,1024,512]{2,1,0:T(8...) custom-call(s32[1,16]{1,0:T(1,128)} %refs_0_.1, ...), custom_call_target="tpu_custom_call" | custom-call | flops 268435456 | bytes 4194304 | tf_op jit(solution)/shard_map/shard_ends/pallas_call | solution.py:447
  6.6 4.9 %collective-permute-start.3 = (f32[2,128,128]{2,1,0:T(8,128)}, f32[2,128,128]{2,1,0:T(8,128)S(1)}, u32[]{:S(2)}, u32[]{:S(2)}) collective-permute-start(f32[2,128,128]{2,1,0:T(8,128)} %get-tuple-element.59), channel_id=1, source_target_pairs={{0,4},{12,8},{1,5},{13,9},{2,6},{14,10},{3,7},{15,11},{16,20},{28,... | collective-permute-start | bytes 393224 | tf_op jit(solution)/shard_map/ppermute | solution.py:522
  11.6 1.3 %collective-permute-start = (f32[2,128,128]{2,1,0:T(8,128)}, f32[2,128,128]{2,1,0:T(8,128)S(1)}, u32[]{:S(2)}, u32[]{:S(2)}) collective-permute-start(f32[2,128,128]{2,1,0:T(8,128)} %get-tuple-element.53), channel_id=1, source_target_pairs={{0,4},{12,8},{1,5},{13,9},{2,6},{14,10},{3,7},{15,11},{16,20},{28,... | collective-permute-start | bytes 393224 | tf_op jit(solution)/shard_map/ppermute | solution.py:522
  12.9 0.7 %copy-done.8 = f32[4,128]{1,0:T(4,128)S(1)} copy-done((f32[4,128]{1,0:T(4,128)S(1)}, f32[4,128]{1,0:T(4,128)}, u32[]{:S(2)}) %copy-start.8) | copy-done | bytes 2072
  13.6 1.2 %copy-done = bf16[1,1024,512]{2,1,0:T(8,128)(2,1)S(1)} copy-done((bf16[1,1024,512]{2,1,0:T(8,128)(2,1)S(1)}, bf16[1,1024,512]{2,1,0:T(8,128)(2,1)}, u32[]{:S(2)}) %copy-start) | copy-done | bytes 1048600
  14.8 1.2 %copy-done.2 = bf16[1,1024,512]{2,1,0:T(8,128)(2,1)S(1)} copy-done((bf16[1,1024,512]{2,1,0:T(8,128)(2,1)S(1)}, bf16[1,1024,512]{2,1,0:T(8,128)(2,1)}, u32[]{:S(2)}) %copy-start.2) | copy-done | bytes 1048600
  16.0 1.2 %copy-done.3 = bf16[1,1024,512]{2,1,0:T(8,128)(2,1)S(1)} copy-done((bf16[1,1024,512]{2,1,0:T(8,128)(2,1)S(1)}, bf16[1,1024,512]{2,1,0:T(8,128)(2,1)}, u32[]{:S(2)}) %copy-start.3) | copy-done | bytes 1048600
  17.3 1.2 %copy-done.4 = bf16[1,1024,512]{2,1,0:T(8,128)(2,1)S(1)} copy-done((bf16[1,1024,512]{2,1,0:T(8,128)(2,1)S(1)}, bf16[1,1024,512]{2,1,0:T(8,128)(2,1)}, u32[]{:S(2)}) %copy-start.4) | copy-done | bytes 1048600
  18.5 0.8 %copy-done.6 = f32[64,128]{1,0:T(8,128)S(1)} copy-done((f32[64,128]{1,0:T(8,128)S(1)}, f32[64,128]{1,0:T(8,128)}, u32[]{:S(2)}) %copy-start.6) | copy-done | bytes 32792
  19.2 0.8 %copy-done.7 = f32[64,128]{1,0:T(8,128)S(1)} copy-done((f32[64,128]{1,0:T(8,128)S(1)}, f32[64,128]{1,0:T(8,128)}, u32[]{:S(2)}) %copy-start.7) | copy-done | bytes 32792
  20.0 4.7 %local_0.1 = (bf16[1,1024,256]{2,1,0:T(8,128)(2,1)S(1)}, bf16[1,1024,256]{2,1,0:T(8,128)(2,1)S(1)}, bf16[1,1024,256]{2,1,0:T(8,128)(2,1)S(1)}, bf16[1,1024,256]{...) custom-call(bf16[1,1024,512]{2,1,0:T(8,128)(2,1)S(1)} %copy-done, ...), custom_call_target="tpu_custom_call" | custom-call | flops 805306368 | bytes 4194304 | tf_op jit(solution)/shard_map/local_0/pallas_call | solution.py:465
  24.7 0.7 %copy-done.14 = f32[2,1,128]{2,1,0:T(1,128)S(1)} copy-done((f32[2,1,128]{2,1,0:T(1,128)S(1)}, f32[2,1,128]{2,1,0:T(1,128)}, u32[]{:S(2)}) %copy-start.14) | copy-done | bytes 1048
  25.4 0.8 %collective-permute-start.4 = (f32[2,128,128]{2,1,0:T(8,128)S(1)}, f32[2,128,128]{2,1,0:T(8,128)S(1)}, u32[]{:S(2)}, u32[]{:S(2)}) collective-permute-start(f32[2,128,128]{2,1,0:T(8,128)S(1)} %multiply_add_fusion.1), channel_id=1, source_target_pairs={{4,8},{8,4},{5,9},{9,5},{6,10},{10,6},{7,11},{11,7},{20,24},{24,20... | collective-permute-start | bytes 393224 | tf_op jit(solution)/shard_map/ppermute | solution.py:522
  26.3 0.6 %copy-done.13 = f32[2,1,128]{2,1,0:T(1,128)S(1)} copy-done((f32[2,1,128]{2,1,0:T(1,128)S(1)}, f32[2,1,128]{2,1,0:T(1,128)}, u32[]{:S(2)}) %copy-start.13) | copy-done | bytes 1048
  27.0 0.8 %collective-permute-start.1 = (f32[2,128,128]{2,1,0:T(8,128)S(1)}, f32[2,128,128]{2,1,0:T(8,128)S(1)}, u32[]{:S(2)}, u32[]{:S(2)}) collective-permute-start(f32[2,128,128]{2,1,0:T(8,128)S(1)} %multiply_add_fusion.3), channel_id=1, source_target_pairs={{4,8},{8,4},{5,9},{9,5},{6,10},{10,6},{7,11},{11,7},{20,24},{24,20... | collective-permute-start | bytes 393224 | tf_op jit(solution)/shard_map/ppermute | solution.py:522
  27.8 4.7 %local_1.1 = (bf16[1,1024,256]{2,1,0:T(8,128)(2,1)S(1)}, bf16[1,1024,256]{2,1,0:T(8,128)(2,1)S(1)}, bf16[1,1024,256]{2,1,0:T(8,128)(2,1)S(1)}, bf16[1,1024,256]{...) custom-call(bf16[1,1024,512]{2,1,0:T(8,128)(2,1)S(1)} %copy-done, ...), custom_call_target="tpu_custom_call" | custom-call | flops 805306368 | bytes 4194304 | tf_op jit(solution)/shard_map/local_1/pallas_call | solution.py:465
  33.0 1.3 %collective-permute-start.5 = (f32[2,128,128]{2,1,0:T(8,128)S(1)}, f32[2,128,128]{2,1,0:T(8,128)S(1)}, u32[]{:S(2)}, u32[]{:S(2)}) collective-permute-start(f32[2,128,128]{2,1,0:T(8,128)S(1)} %get-tuple-element.91), channel_id=1, source_target_pairs={{8,12},{4,0},{9,13},{5,1},{10,14},{6,2},{11,15},{7,3},{24,28},{20,... | collective-permute-start | bytes 393224 | tf_op jit(solution)/shard_map/ppermute | solution.py:522
  34.3 1.3 %collective-permute-start.2 = (f32[2,128,128]{2,1,0:T(8,128)S(1)}, f32[2,128,128]{2,1,0:T(8,128)S(1)}, u32[]{:S(2)}, u32[]{:S(2)}) collective-permute-start(f32[2,128,128]{2,1,0:T(8,128)S(1)} %get-tuple-element.94), channel_id=1, source_target_pairs={{8,12},{4,0},{9,13},{5,1},{10,14},{6,2},{11,15},{7,3},{24,28},{20,... | collective-permute-start | bytes 393224 | tf_op jit(solution)/shard_map/ppermute | solution.py:522
  35.7 3.9 %collective-permute-start.7 = (f32[4,64]{1,0:T(4,128)S(1)}, f32[4,64]{1,0:T(4,128)S(1)}, u32[]{:S(2)}, u32[]{:S(2)}) collective-permute-start(f32[4,64]{1,0:T(4,128)S(1)} %select_add_fusion), channel_id=1, source_target_pairs={{0,4},{4,0},{8,12},{12,8},{1,5},{5,1},{9,13},{13,9},{2,6},{6,2},{1... | collective-permute-start | bytes 3080 | tf_op jit(solution)/shard_map/ppermute | solution.py:561
  39.6 2.9 %collective-permute-done.5.refs_9_ = f32[2,128,128]{2,1,0:T(8,128)S(1)} collective-permute-done((f32[2,128,128]{2,1,0:T(8,128)S(1)}, f32[2,128,128]{2,1,0:T(8,128)S(1)}, u32[]{:S(2)}, u32[]{:S(2)}) %collective-permute-start.5) | collective-permute-done | bytes 131104 | tf_op jit(solution)/shard_map/ppermute | solution.py:522
  42.5 4.3 %merge_0.1 = (bf16[1,1024,512]{2,1,0:T(8,128)(2,1)}, bf16[1,1024,512]{2,1,0:T(8,128)(2,1)}, bf16[1,1024,512]{2,1,0:T(8,128)(2,1)}, bf16[1,1024,512]{2,1,0:T(8,128)(2,1)}, f32[1,2,1024]{2,1,0:T(2,128)S(1)}) custom-call(s32[1]{0:T(128)} %bitcast.refs_1_.refs_0_, bf16[1,1024,512]{2,1,0:T(8,128)(2,1)S(1)} %copy-done.1, bf16[1,1024,512]{2,1,0:T(8,128)(2,1)S(1)} %copy-done.2, ...), custom_call_target="tpu_custom_call" | custom-call | flops 268435456 | bytes 6291456 | tf_op jit(solution)/shard_map/merge_0/pallas_call | solution.py:488
  46.9 0.6 %collective-permute-start.8 = (f32[4,64]{1,0:T(4,128)S(1)}, f32[4,64]{1,0:T(4,128)S(1)}, u32[]{:S(2)}, u32[]{:S(2)}) collective-permute-start(f32[4,64]{1,0:T(4,128)S(1)} %add.42), channel_id=1, source_target_pairs={{0,8},{4,12},{8,0},{12,4},{1,9},{5,13},{9,1},{13,5},{2,10},{6,14},... | collective-permute-start | bytes 3080 | tf_op jit(solution)/shard_map/ppermute | solution.py:561
  47.5 4.3 %merge_1.1 = (bf16[1,1024,512]{2,1,0:T(8,128)(2,1)}, bf16[1,1024,512]{2,1,0:T(8,128)(2,1)}, bf16[1,1024,512]{2,1,0:T(8,128)(2,1)}, bf16[1,1024,512]{2,1,0:T(8,128)(2,1)}, f32[1,4,1024]{2,1,0:T(4,128)}) custom-call(s32[1]{0:T(128)} %bitcast.refs_1_.refs_0_, ...), custom_call_target="tpu_custom_call", output_to_operand_aliasing={{0}: (16, {}), {1}: (17, {}), {2}: (18, {}), {3}: (19, {})} | custom-call | flops 268435456 | bytes 6291456 | tf_op jit(solution)/shard_map/merge_1/pallas_call | solution.py:488
  51.8 0.6 %add.43 = f32[4,64]{1,0:T(4,128)} add(f32[4,64]{1,0:T(4,128)S(1)} %add.42, f32[4,64]{1,0:T(4,128)S(1)} %collective-permute-done.8) | non-fusion elementwise | flops 256 | bytes 3072 | tf_op jit(solution)/shard_map/add | solution.py:569
  (40 shorter events, 0.7 us)
Async XLA Ops:
  6.6 18.1 %collective-permute-start.3 = (f32[2,128,128]{2,1,0:T(8,128)}, f32[2,128,128]{2,1,0:T(8,128)S(1)}, u32[]{:S(2)}, u32[]{:S(2)}) collective-permute-start(f32[2,128,128]{2,1,0:T(8,128)} %get-tuple-element.59), channel_id=1, source_target_pairs={{0,4},{12,8},{1,5},{13,9},{2,6},{14,10},{3,7},{15,11},{16,20},{28,... | collective-permute-start | bytes 393224 | tf_op jit(solution)/shard_map/ppermute | solution.py:522
  11.6 14.6 %collective-permute-start = (f32[2,128,128]{2,1,0:T(8,128)}, f32[2,128,128]{2,1,0:T(8,128)S(1)}, u32[]{:S(2)}, u32[]{:S(2)}) collective-permute-start(f32[2,128,128]{2,1,0:T(8,128)} %get-tuple-element.53), channel_id=1, source_target_pairs={{0,4},{12,8},{1,5},{13,9},{2,6},{14,10},{3,7},{15,11},{16,20},{28,... | collective-permute-start | bytes 393224 | tf_op jit(solution)/shard_map/ppermute | solution.py:522
  12.9 0.7 %copy-start.8 = (f32[4,128]{1,0:T(4,128)S(1)}, f32[4,128]{1,0:T(4,128)}, u32[]{:S(2)}) copy-start(f32[4,128]{1,0:T(4,128)} %refs_5_.5) | copy-start | bytes 6148
  13.6 1.2 %copy-start = (bf16[1,1024,512]{2,1,0:T(8,128)(2,1)S(1)}, bf16[1,1024,512]{2,1,0:T(8,128)(2,1)}, u32[]{:S(2)}) copy-start(bf16[1,1024,512]{2,1,0:T(8,128)(2,1)} %get-tuple-element.48.q_ref.refs_1_) | copy-start | bytes 3145732
  14.8 1.2 %copy-start.2 = (bf16[1,1024,512]{2,1,0:T(8,128)(2,1)S(1)}, bf16[1,1024,512]{2,1,0:T(8,128)(2,1)}, u32[]{:S(2)}) copy-start(bf16[1,1024,512]{2,1,0:T(8,128)(2,1)} %get-tuple-element.49.k_ref.refs_2_) | copy-start | bytes 3145732
  16.0 1.2 %copy-start.3 = (bf16[1,1024,512]{2,1,0:T(8,128)(2,1)S(1)}, bf16[1,1024,512]{2,1,0:T(8,128)(2,1)}, u32[]{:S(2)}) copy-start(bf16[1,1024,512]{2,1,0:T(8,128)(2,1)} %get-tuple-element.50.v_ref.refs_3_) | copy-start | bytes 3145732
  17.2 1.2 %copy-start.4 = (bf16[1,1024,512]{2,1,0:T(8,128)(2,1)S(1)}, bf16[1,1024,512]{2,1,0:T(8,128)(2,1)}, u32[]{:S(2)}) copy-start(bf16[1,1024,512]{2,1,0:T(8,128)(2,1)} %get-tuple-element.51.cot_ref.refs_4_) | copy-start | bytes 3145732
  18.5 0.8 %copy-start.6 = (f32[64,128]{1,0:T(8,128)S(1)}, f32[64,128]{1,0:T(8,128)}, u32[]{:S(2)}) copy-start(f32[64,128]{1,0:T(8,128)} %get-tuple-element.61.cum_ref) | copy-start | bytes 98308
  19.2 0.8 %copy-start.7 = (f32[64,128]{1,0:T(8,128)S(1)}, f32[64,128]{1,0:T(8,128)}, u32[]{:S(2)}) copy-start(f32[64,128]{1,0:T(8,128)} %get-tuple-element.57.fac_ref) | copy-start | bytes 98308
  20.0 4.7 %copy-start.12 = (f32[2,128,128]{2,1,0:T(8,128)S(1)}, f32[2,128,128]{2,1,0:T(8,128)}, u32[]{:S(2)}) copy-start(f32[2,128,128]{2,1,0:T(8,128)} %get-tuple-element.59) | copy-start | bytes 393220
  24.7 0.7 %copy-start.14 = (f32[2,1,128]{2,1,0:T(1,128)S(1)}, f32[2,1,128]{2,1,0:T(1,128)}, u32[]{:S(2)}) copy-start(f32[2,1,128]{2,1,0:T(1,128)} %get-tuple-element.68) | copy-start | bytes 3076
  25.4 0.9 %copy-start.11 = (f32[2,128,128]{2,1,0:T(8,128)S(1)}, f32[2,128,128]{2,1,0:T(8,128)}, u32[]{:S(2)}) copy-start(f32[2,128,128]{2,1,0:T(8,128)} %get-tuple-element.53) | copy-start | bytes 393220
  25.4 7.1 %collective-permute-start.4 = (f32[2,128,128]{2,1,0:T(8,128)S(1)}, f32[2,128,128]{2,1,0:T(8,128)S(1)}, u32[]{:S(2)}, u32[]{:S(2)}) collective-permute-start(f32[2,128,128]{2,1,0:T(8,128)S(1)} %multiply_add_fusion.1), channel_id=1, source_target_pairs={{4,8},{8,4},{5,9},{9,5},{6,10},{10,6},{7,11},{11,7},{20,24},{24,20... | collective-permute-start | bytes 393224 | tf_op jit(solution)/shard_map/ppermute | solution.py:522
  26.2 0.7 %copy-start.13 = (f32[2,1,128]{2,1,0:T(1,128)S(1)}, f32[2,1,128]{2,1,0:T(1,128)}, u32[]{:S(2)}) copy-start(f32[2,1,128]{2,1,0:T(1,128)} %get-tuple-element.54) | copy-start | bytes 3076
  26.9 5.6 %copy-start.10 = (f32[2,128,128]{2,1,0:T(8,128)S(1)}, f32[2,128,128]{2,1,0:T(8,128)}, u32[]{:S(2)}) copy-start(f32[2,128,128]{2,1,0:T(8,128)} %get-tuple-element.70) | copy-start | bytes 393220
  27.0 5.8 %collective-permute-start.1 = (f32[2,128,128]{2,1,0:T(8,128)S(1)}, f32[2,128,128]{2,1,0:T(8,128)S(1)}, u32[]{:S(2)}, u32[]{:S(2)}) collective-permute-start(f32[2,128,128]{2,1,0:T(8,128)S(1)} %multiply_add_fusion.3), channel_id=1, source_target_pairs={{4,8},{8,4},{5,9},{9,5},{6,10},{10,6},{7,11},{11,7},{20,24},{24,20... | collective-permute-start | bytes 393224 | tf_op jit(solution)/shard_map/ppermute | solution.py:522
  27.8 5.0 %copy-start.9 = (f32[2,128,128]{2,1,0:T(8,128)S(1)}, f32[2,128,128]{2,1,0:T(8,128)}, u32[]{:S(2)}) copy-start(f32[2,128,128]{2,1,0:T(8,128)} %get-tuple-element.55) | copy-start | bytes 393220
  32.5 10.0 %copy-start.1 = (bf16[1,1024,512]{2,1,0:T(8,128)(2,1)S(1)}, bf16[1,1024,512]{2,1,0:T(8,128)(2,1)}, u32[]{:S(2)}) copy-start(bf16[1,1024,512]{2,1,0:T(8,128)(2,1)} %get-tuple-element.48.q_ref.refs_1_) | copy-start | bytes 3145732
  32.9 9.6 %copy-start.5 = (f32[64,128]{1,0:T(8,128)S(1)}, f32[64,128]{1,0:T(8,128)}, u32[]{:S(2)}) copy-start(f32[64,128]{1,0:T(8,128)} %get-tuple-element.52.refs_6_) | copy-start | bytes 98308
  33.0 2.6 %collective-permute-start.6 = (f32[4,64]{1,0:T(4,128)S(1)}, f32[4,64]{1,0:T(4,128)S(1)}, u32[]{:S(2)}, u32[]{:S(2)}) collective-permute-start(f32[4,64]{1,0:T(4,128)S(1)} %slice_select_fusion), channel_id=1, source_target_pairs={{0,16},{16,0},{1,17},{17,1},{2,18},{18,2},{3,19},{19,3},{4,20},{20... | collective-permute-start | bytes 3080 | tf_op jit(solution)/shard_map/ppermute | solution.py:555
  33.0 9.5 %collective-permute-start.5 = (f32[2,128,128]{2,1,0:T(8,128)S(1)}, f32[2,128,128]{2,1,0:T(8,128)S(1)}, u32[]{:S(2)}, u32[]{:S(2)}) collective-permute-start(f32[2,128,128]{2,1,0:T(8,128)S(1)} %get-tuple-element.91), channel_id=1, source_target_pairs={{8,12},{4,0},{9,13},{5,1},{10,14},{6,2},{11,15},{7,3},{24,28},{20,... | collective-permute-start | bytes 393224 | tf_op jit(solution)/shard_map/ppermute | solution.py:522
  34.3 13.2 %collective-permute-start.2 = (f32[2,128,128]{2,1,0:T(8,128)S(1)}, f32[2,128,128]{2,1,0:T(8,128)S(1)}, u32[]{:S(2)}, u32[]{:S(2)}) collective-permute-start(f32[2,128,128]{2,1,0:T(8,128)S(1)} %get-tuple-element.94), channel_id=1, source_target_pairs={{8,12},{4,0},{9,13},{5,1},{10,14},{6,2},{11,15},{7,3},{24,28},{20,... | collective-permute-start | bytes 393224 | tf_op jit(solution)/shard_map/ppermute | solution.py:522
  35.7 11.1 %collective-permute-start.7 = (f32[4,64]{1,0:T(4,128)S(1)}, f32[4,64]{1,0:T(4,128)S(1)}, u32[]{:S(2)}, u32[]{:S(2)}) collective-permute-start(f32[4,64]{1,0:T(4,128)S(1)} %select_add_fusion), channel_id=1, source_target_pairs={{0,4},{4,0},{8,12},{12,8},{1,5},{5,1},{9,13},{13,9},{2,6},{6,2},{1... | collective-permute-start | bytes 3080 | tf_op jit(solution)/shard_map/ppermute | solution.py:561
  46.9 4.9 %collective-permute-start.8 = (f32[4,64]{1,0:T(4,128)S(1)}, f32[4,64]{1,0:T(4,128)S(1)}, u32[]{:S(2)}, u32[]{:S(2)}) collective-permute-start(f32[4,64]{1,0:T(4,128)S(1)} %add.42), channel_id=1, source_target_pairs={{0,8},{4,12},{8,0},{12,4},{1,9},{5,13},{9,1},{13,5},{2,10},{6,14},... | collective-permute-start | bytes 3080 | tf_op jit(solution)/shard_map/ppermute | solution.py:561

commit v5 on v4

--- a/solution.py
+++ b/solution.py
@@ -303,110 +303,106 @@
     refs = refs[15:]
     if part > 0:
         before_ref, refs = refs[0], refs[5:]
-    out_ref, dq_ref, dk_ref, dv_ref, dgate_ref, entering, leaving, sums_scr, tot_scr = refs
-    step = pl.program_id(0)
+    targets, dgate_ref, staged, entering, leaving, sems = refs[:4], *refs[4:]
     heads = first_ref.shape[0]
-    block = out_ref.shape[1]
-    chunks = block // CHUNK
+    steps = sems.shape[0]
     num_chunks = fac_ref.shape[0] // 8
+    chunks = num_chunks // steps
+    block = chunks * CHUNK
     scale = head_width ** (-0.5)
+    group = slice(part * heads * head_width, (part + 1) * heads * head_width)
+    partials = (out_in, dq_in, dk_in, dv_in)
+
+    def copies(step):
+        at = pl.ds(step * block, block)
+        return [
+            pltpu.make_async_copy(
+                staged.at[i, at, :], target.at[0, at, group], sems.at[step, i]
+            )
+            for i, target in enumerate(targets)
+        ]
 
     def arrived(head):
         low = ctx_ref[0] < half_ctx
         first, second = first_ref[head], second_ref[head] + last_ref[head]
         return jnp.where(low, first, second), jnp.where(low, second, first)
 
-    @pl.when(step == 0)
-    def _():
-        gain_columns = jnp.transpose(jnp.concatenate([gain_ref[...], gain_ref[...]], axis=0))
-        entering[...] = jnp.zeros_like(entering)
-        leaving[...] = jnp.zeros_like(leaving)
-        for head in range(heads):
-            row = part * heads + head
-            own = slice(head * head_width, (head + 1) * head_width)
-            gain = gain_columns[:, row : row + 1]
-            state, later = arrived(head)
-            entering[own, own] = (state * (gain * scale)).astype(BF16)
-            leaving[own, own] = (later * gain).astype(BF16)
-
-    products, results = [], {}
-    group = slice(part * heads * head_width, (part + 1) * heads * head_width)
-
-    def rows_of(chunk):
-        return pl.ds(pl.multiple_of(step * block + chunk * CHUNK, CHUNK), CHUNK)
-
-    for chunk in range(chunks):
-        rows = rows_of(chunk)
-        products.append(
-            (
+    gain_columns = jnp.transpose(jnp.concatenate([gain_ref[...], gain_ref[...]], axis=0))
+    entering[...] = jnp.zeros_like(entering)
+    leaving[...] = jnp.zeros_like(leaving)
+    last = fac_ref[(num_chunks - 1) * 8 : num_chunks * 8, CHUNK - 1 : CHUNK]
+    constants = []
+    for head in range(heads):
+        row = part * heads + head
+        own = slice(head * head_width, (head + 1) * head_width)
+        gain = gain_columns[:, row : row + 1]
+        state, later = arrived(head)
+        state = state * gain
+        entering[own, own] = (state * scale).astype(BF16)
+        leaving[own, own] = (later * gain).astype(BF16)
+        constants.append(total_of(state * later) * last[row : row + 1])
+
+    gate_sums, kept_sums = {}, {}
+    for step in range(steps):
+        numbers = range(step * chunks, (step + 1) * chunks)
+        products, results = {}, {}
+        for number in numbers:
+            rows = slice(number * CHUNK, (number + 1) * CHUNK)
+            products[number] = (
                 dot_nn(q_ref[0, rows, group], entering[...]),
                 dot_nt(cot_ref[0, rows, group], entering[...]),
+                dot_nt(v_ref[0, rows, group], leaving[...]),
                 dot_nn(k_ref[0, rows, group], leaving[...]),
-                dot_nt(v_ref[0, rows, group], leaving[...]),
-            )
-        )
-    for chunk in range(chunks):
-        number = step * chunks + chunk
-        columns = jnp.transpose(fac_ref[pl.ds(pl.multiple_of(number * 8, 8), 8), :])
-        rows = rows_of(chunk)
-        for head in range(heads):
-            row = part * heads + head
-            lanes = slice(head * head_width, (head + 1) * head_width)
-            wide = slice(row * head_width, (row + 1) * head_width)
-            from_start, to_end = columns[:, row : row + 1], columns[:, 4 + row : 5 + row]
-            across_all, dq_all, written_all, dk_all = products[chunk]
-            across = across_all[:, lanes] * from_start
-            written = written_all[:, lanes] * to_end
-            kept = written * v_ref[0, rows, wide].astype(F32)
-            balance = jnp.sum(
-                across * cot_ref[0, rows, wide].astype(F32) - kept, axis=1, keepdims=True
-            )
-            results[chunk, head] = (
-                (out_in[0, rows, lanes].astype(F32) + across).astype(BF16),
-                (dq_in[0, rows, lanes].astype(F32) + dq_all[:, lanes] * from_start).astype(BF16),
-                (dk_in[0, rows, lanes].astype(F32) + dk_all[:, lanes] * to_end).astype(BF16),
-                (dv_in[0, rows, lanes].astype(F32) + written).astype(BF16),
-                later_sums(balance),
-                jnp.sum(kept, axis=0, keepdims=True),
-            )
-    for chunk in range(chunks):
-        number = step * chunks + chunk
-        rows = slice(chunk * CHUNK, (chunk + 1) * CHUNK)
-        for head in range(heads):
-            lanes = slice(head * head_width, (head + 1) * head_width)
-            out, dq, dk, dv, sums, kept = results[chunk, head]
-            out_ref[0, rows, lanes] = out
-            dq_ref[0, rows, lanes] = dq
-            dk_ref[0, rows, lanes] = dk
-            dv_ref[0, rows, lanes] = dv
-            sums_scr[number, head : head + 1, :] = sums
-            tot_scr[number, head : head + 1, :] = kept
-
-    @pl.when(step == pl.num_programs(0) - 1)
-    def _():
-        last = fac_ref[(num_chunks - 1) * 8 : num_chunks * 8, CHUNK - 1 : CHUNK]
-        kept = tot_scr[0]
-        for chunk in range(1, num_chunks):
-            kept = kept + tot_scr[chunk]
-        base = jnp.sum(kept, axis=1, keepdims=True)
-        constants = []
-        for head in range(heads):
-            row = part * heads + head
-            state, later = arrived(head)
-            gain_columns = jnp.transpose(
-                jnp.concatenate([gain_ref[...], gain_ref[...]], axis=0)
-            )
-            product = total_of(state * later * gain_columns[:, row : row + 1])
-            constants.append(product * last[row : row + 1])
-        base = base[:heads] + jnp.concatenate(constants, axis=0)
-        if part > 0:
-            dgate_ref[0, : part * heads, :] = before_ref[0]
-        own = slice(part * heads, (part + 1) * heads)
-        for chunk in range(num_chunks - 1, -1, -1):
-            lanes = slice(chunk * CHUNK, (chunk + 1) * CHUNK)
-            sums = sums_scr[chunk, :heads, :]
-            dgate_ref[0, own, lanes] = dgate_in[0, :, lanes] + sums + base
+            )
+        for number in numbers:
+            columns = jnp.transpose(fac_ref[number * 8 : number * 8 + 8, :])
+            rows = slice(number * CHUNK, (number + 1) * CHUNK)
+            for head in range(heads):
+                row = part * heads + head
+                lanes = slice(head * head_width, (head + 1) * head_width)
+                wide = slice(row * head_width, (row + 1) * head_width)
+                from_start, to_end = columns[:, row : row + 1], columns[:, 4 + row : 5 + row]
+                across, dq, dk, written = (
+                    product[:, lanes] * factor
+                    for product, factor in zip(
+                        products[number], (from_start, from_start, to_end, to_end)
+                    )
+                )
+                results[number, head] = [
+                    (partial[0, rows, lanes].astype(F32) + added).astype(BF16)
+                    for partial, added in zip(partials, (across, dq, dk, written))
+                ]
+                kept = written * v_ref[0, rows, wide].astype(F32)
+                balance = jnp.sum(
+                    across * cot_ref[0, rows, wide].astype(F32) - kept, axis=1, keepdims=True
+                )
+                gate_sums[number, head] = later_sums(balance)
+                kept_sums[number, head] = jnp.sum(kept, axis=0, keepdims=True)
+        for number in numbers:
+            rows = slice(number * CHUNK, (number + 1) * CHUNK)
+            for head in range(heads):
+                lanes = slice(head * head_width, (head + 1) * head_width)
+                for i in range(4):
+                    staged[i, rows, lanes] = results[number, head][i]
+        for i, copy in enumerate(copies(step)):
+            copy.start(priority=i % 2)
+
+    if part > 0:
+        dgate_ref[0, : part * heads, :] = before_ref[0]
+    for head in range(heads):
+        row = part * heads + head
+        kept = sum(kept_sums[number, head] for number in range(num_chunks))
+        base = jnp.sum(kept, axis=1, keepdims=True) + constants[head]
+        for number in range(num_chunks - 1, -1, -1):
+            lanes = slice(number * CHUNK, (number + 1) * CHUNK)
+            sums = gate_sums[number, head]
+            dgate_ref[0, row : row + 1, lanes] = (
+                dgate_in[0, head : head + 1, lanes] + sums + base
+            )
             base = base + sums[:, 0:1]
+    for step in range(steps):
+        for copy in copies(step):
+            copy.wait()
 
 
 def shards(queries, keys_raw, values, gates, lengths, key_gain, cotangent):
@@ -423,13 +419,6 @@
     middle = count // 2 - 1
     ctx_scalar = jnp.reshape(ctx, (1,)).astype(jnp.int32)
 
-    def stream_spec(part):
-        return pl.BlockSpec((1, block, part_width), lambda i: (0, i, part))
-
-    def whole(array):
-        zeros = (0,) * len(array.shape)
-        return pl.BlockSpec(array.shape, lambda *_: zeros)
-
     def shape_of(*shape, dtype=F32):
         return jax.ShapeDtypeStruct(shape, dtype)
 
@@ -453,7 +442,7 @@
                 pltpu.VMEM((rows, CHUNK), F32),
                 pltpu.SemaphoreType.DMA((steps, 4)),
             ],
-            compiler_params=pltpu.CompilerParams(vmem_limit_bytes=56 << 20),
+            compiler_params=pltpu.CompilerParams(vmem_limit_bytes=49 << 20),
             cost_estimate=pl.CostEstimate(
                 flops=2 * product * PARTS, bytes_accessed=8 * tokens * width, transcendentals=0
             ),
@@ -487,15 +476,14 @@
             aliases = {16 + i: i for i in range(4)}
         return pl.pallas_call(
             functools.partial(merge_kernel, head_width, part, count // 2),
-            grid=(steps,),
             in_specs=[smem] + [vmem] * 14 + extra_specs,
-            out_specs=[stream_spec(part)] * 4 + [whole(full_gates)],
+            out_specs=[pl.BlockSpec(memory_space=pl.ANY)] * 4 + [vmem],
             out_shape=[shape_of(1, tokens, width, dtype=BF16)] * 4 + [full_gates],
             scratch_shapes=[
+                pltpu.VMEM((4, tokens, part_width), BF16),
                 pltpu.VMEM((part_width, part_width), BF16),
                 pltpu.VMEM((part_width, part_width), BF16),
-                pltpu.VMEM((num_chunks, 8, CHUNK), F32),
-                pltpu.VMEM((num_chunks, 8, CHUNK), F32),
+                pltpu.SemaphoreType.DMA((steps, 4)),
             ],
             input_output_aliases=aliases,
             compiler_params=pltpu.CompilerParams(vmem_limit_bytes=24 << 20),

time: 53 us -> 49.7 us (0.938)
  local copies, waits for them, and re-layouts: 8.46 us -> 5.55 us
  Pallas kernels: 24 us -> 22.2 us
  other arithmetic: 1.12 us -> 2.91 us
    unnamed x30 -> x20, local copies, waits for them, and re-layouts: 8.46 us -> 5.55 us
    add x2, other arithmetic: 0.05 us -> 1.85 us  [send(): payload = payload + decay[part] * arrived[part][-1]]
    pallas_call x1, Pallas kernels: 5.98 us -> 4.74 us  [ends(): pl.pallas_call(functools.partial(ends_kernel, head_width, count // 2), in...]
    pallas_call x2, Pallas kernels: 8.63 us -> 8.03 us  [merge(): pl.pallas_call(functools.partial(merge_kernel, head_width, part, count //...]
  transfers between devices with their start and end apart: 9 -> 9, of which waited for: 1 -> 1; matrix products, arithmetic and copies ran while one was open for 1% -> 4% of each run, Pallas kernels for 34% -> 35%
where the time goes in v5:
time: 49.7 us; the launch traced here: 49.3 us
  Pallas kernels  22.2 us (45%)
  starting transfers between devices  14.8 us (30%)
  local copies, waits for them, and re-layouts  5.55 us (11%)
  waiting for transfers between devices  2.94 us (6%)
  other arithmetic  2.91 us (6%)
  between operations  0.91 us (2%)
    ppermute x6, starting transfers between devices, send(): lax.ppermute(payload, 'ctx', [(hop, hop + 1), (count - 1 - hop, count - 2...  10.3 us
    pallas_call x2, Pallas kernels, local(): pl.pallas_call(functools.partial(local_kernel, head_width, part), in_spec...  9.44 us
    pallas_call x2, Pallas kernels, merge(): pl.pallas_call(functools.partial(merge_kernel, head_width, part, count //...  8.03 us
    unnamed x20, local copies, waits for them, and re-layouts  5.55 us
    pallas_call x1, Pallas kernels, ends(): pl.pallas_call(functools.partial(ends_kernel, head_width, count // 2), in...  4.74 us
    ppermute x2, starting transfers between devices, shards(): lax.ppermute(grad_gain, 'ctx', [(i, i ^ reach) for i in range(count)])  4.51 us
    ppermute x6, waiting for transfers between devices, send(): lax.ppermute(payload, 'ctx', [(hop, hop + 1), (count - 1 - hop, count - 2...  2.94 us
    add x2, other arithmetic, send(): payload = payload + decay[part] * arrived[part][-1]  1.85 us
  transfers between devices with their start and end apart: 9, of which 1 were waited for; matrix products, arithmetic and copies ran while one was open for 4% of the time, Pallas kernels for 35%

profile of v5, /device:TPU:0, one launch (start us, length us, event | category | flops | bytes accessed | tf_op | source)
XLA Modules:
  0.0 49.3 jit_solution(13347129508785700901)
XLA Ops:
  0.6 0.6 %copy-done.9 = s32[1,16]{1,0:T(1,128)S(1)} copy-done((s32[1,16]{1,0:T(1,128)S(1)}, s32[1,16]{1,0:T(1,128)}, u32[]{:S(2)}) %copy-start.9) | copy-done | bytes 88
  1.3 0.7 %copy-done.8 = f32[1,4,1024]{2,1,0:T(4,128)S(1)} copy-done((f32[1,4,1024]{2,1,0:T(4,128)S(1)}, f32[1,4,1024]{2,1,0:T(4,128)}, u32[]{:S(2)}) %copy-start.8) | copy-done | bytes 16408
  2.0 4.7 %shard_ends.1 = (bf16[1,1024,512]{2,1,0:T(8,128)(2,1)S(1)}, bf16[1,1024,512]{2,1,0:T(8,128)(2,1)S(1)}, bf16[1,1024,512]{2,1,0:T(8,128)(2,1)S(1)}, bf16[1,1024,51...) custom-call(s32[1,16]{1,0:T(1,128)S(1)} %copy-done.9, ...), custom_call_target="tpu_custom_call" | custom-call | flops 268435456 | bytes 4194304 | tf_op jit(solution)/shard_map/shard_ends/pallas_call | solution.py:436
  6.8 1.0 %copy-done = bf16[1,1024,512]{2,1,0:T(8,128)(2,1)} copy-done((bf16[1,1024,512]{2,1,0:T(8,128)(2,1)}, bf16[1,1024,512]{2,1,0:T(8,128)(2,1)S(1)}, u32[]{:S(2)}) %copy-start) | copy-done | bytes 1048600
  7.7 0.7 %copy-done.3 = f32[2,128,128]{2,1,0:T(8,128)} copy-done((f32[2,128,128]{2,1,0:T(8,128)}, f32[2,128,128]{2,1,0:T(8,128)S(1)}, u32[]{:S(2)}) %copy-start.3) | copy-done | bytes 131096
  8.4 0.6 %copy-done.5 = f32[2,128,128]{2,1,0:T(8,128)} copy-done((f32[2,128,128]{2,1,0:T(8,128)}, f32[2,128,128]{2,1,0:T(8,128)S(1)}, u32[]{:S(2)}) %copy-start.5) | copy-done | bytes 131096
  9.0 4.9 %collective-permute-start.3 = (f32[2,128,128]{2,1,0:T(8,128)}, f32[2,128,128]{2,1,0:T(8,128)S(1)}, u32[]{:S(2)}, u32[]{:S(2)}) collective-permute-start(f32[2,128,128]{2,1,0:T(8,128)} %get-tuple-element.59), channel_id=1, source_target_pairs={{0,4},{12,8},{1,5},{13,9},{2,6},{14,10},{3,7},{15,11},{16,20},{28,... | collective-permute-start | bytes 393224 | tf_op jit(solution)/shard_map/ppermute | solution.py:510
  14.0 1.3 %collective-permute-start = (f32[2,128,128]{2,1,0:T(8,128)}, f32[2,128,128]{2,1,0:T(8,128)S(1)}, u32[]{:S(2)}, u32[]{:S(2)}) collective-permute-start(f32[2,128,128]{2,1,0:T(8,128)} %get-tuple-element.53), channel_id=1, source_target_pairs={{0,4},{12,8},{1,5},{13,9},{2,6},{14,10},{3,7},{15,11},{16,20},{28,... | collective-permute-start | bytes 393224 | tf_op jit(solution)/shard_map/ppermute | solution.py:510
  15.3 0.7 %copy-done.7 = f32[4,128]{1,0:T(4,128)S(1)} copy-done((f32[4,128]{1,0:T(4,128)S(1)}, f32[4,128]{1,0:T(4,128)}, u32[]{:S(2)}) %copy-start.7) | copy-done | bytes 2072
  16.0 1.2 %copy-done.1 = bf16[1,1024,512]{2,1,0:T(8,128)(2,1)S(1)} copy-done((bf16[1,1024,512]{2,1,0:T(8,128)(2,1)S(1)}, bf16[1,1024,512]{2,1,0:T(8,128)(2,1)}, u32[]{:S(2)}) %copy-start.1) | copy-done | bytes 1048600
  17.2 4.7 %local_0.1 = (bf16[1,1024,256]{2,1,0:T(8,128)(2,1)S(1)}, bf16[1,1024,256]{2,1,0:T(8,128)(2,1)S(1)}, bf16[1,1024,256]{2,1,0:T(8,128)(2,1)S(1)}, bf16[1,1024,256]{...) custom-call(bf16[1,1024,512]{2,1,0:T(8,128)(2,1)S(1)} %get-tuple-element.48.q_ref.refs_1_, ...), custom_call_target="tpu_custom_call" | custom-call | flops 805306368 | bytes 4194304 | tf_op jit(solution)/shard_map/local_0/pallas_call | solution.py:454
  21.9 0.9 %multiply_add_fusion.1 = f32[2,128,128]{2,1,0:T(8,128)S(1)} fusion(f32[2,128,128]{2,1,0:T(8,128)} %get-tuple-element.59, f32[2,128,128]{2,1,0:T(8,128)S(1)} %collective-permute-done.3.refs_7_, f32[2,128]{1,0:T(2,128)S(1)} %bitcast.5), kind=kLoop, calls=%fused_computation.5 | loop fusion | flops 65536 | bytes 394240 | tf_op jit(solution)/shard_map/add | solution.py:507
  22.8 0.7 %collective-permute-start.4 = (f32[2,128,128]{2,1,0:T(8,128)S(1)}, f32[2,128,128]{2,1,0:T(8,128)S(1)}, u32[]{:S(2)}, u32[]{:S(2)}) collective-permute-start(f32[2,128,128]{2,1,0:T(8,128)S(1)} %multiply_add_fusion.1), channel_id=1, source_target_pairs={{4,8},{8,4},{5,9},{9,5},{6,10},{10,6},{7,11},{11,7},{20,24},{24,20... | collective-permute-start | bytes 393224 | tf_op jit(solution)/shard_map/ppermute | solution.py:510
  23.5 0.9 %multiply_add_fusion.3 = f32[2,128,128]{2,1,0:T(8,128)S(1)} fusion(f32[2,128,128]{2,1,0:T(8,128)} %get-tuple-element.53, f32[2,128,128]{2,1,0:T(8,128)S(1)} %collective-permute-done.refs_7_, f32[2,128]{1,0:T(2,128)S(1)} %bitcast.3), kind=kLoop, calls=%fused_computation.7 | loop fusion | flops 65536 | bytes 394240 | tf_op jit(solution)/shard_map/add | solution.py:507
  24.4 0.8 %collective-permute-start.1 = (f32[2,128,128]{2,1,0:T(8,128)S(1)}, f32[2,128,128]{2,1,0:T(8,128)S(1)}, u32[]{:S(2)}, u32[]{:S(2)}) collective-permute-start(f32[2,128,128]{2,1,0:T(8,128)S(1)} %multiply_add_fusion.3), channel_id=1, source_target_pairs={{4,8},{8,4},{5,9},{9,5},{6,10},{10,6},{7,11},{11,7},{20,24},{24,20... | collective-permute-start | bytes 393224 | tf_op jit(solution)/shard_map/ppermute | solution.py:510
  25.3 4.7 %local_1.1 = (bf16[1,1024,256]{2,1,0:T(8,128)(2,1)S(1)}, bf16[1,1024,256]{2,1,0:T(8,128)(2,1)S(1)}, bf16[1,1024,256]{2,1,0:T(8,128)(2,1)S(1)}, bf16[1,1024,256]{...) custom-call(bf16[1,1024,512]{2,1,0:T(8,128)(2,1)S(1)} %get-tuple-element.48.q_ref.refs_1_, ...), custom_call_target="tpu_custom_call" | custom-call | flops 805306368 | bytes 4194304 | tf_op jit(solution)/shard_map/local_1/pallas_call | solution.py:454
  30.5 1.3 %collective-permute-start.5 = (f32[2,128,128]{2,1,0:T(8,128)S(1)}, f32[2,128,128]{2,1,0:T(8,128)S(1)}, u32[]{:S(2)}, u32[]{:S(2)}) collective-permute-start(f32[2,128,128]{2,1,0:T(8,128)S(1)} %get-tuple-element.91), channel_id=1, source_target_pairs={{8,12},{4,0},{9,13},{5,1},{10,14},{6,2},{11,15},{7,3},{24,28},{20,... | collective-permute-start | bytes 393224 | tf_op jit(solution)/shard_map/ppermute | solution.py:510
  31.8 1.3 %collective-permute-start.2 = (f32[2,128,128]{2,1,0:T(8,128)S(1)}, f32[2,128,128]{2,1,0:T(8,128)S(1)}, u32[]{:S(2)}, u32[]{:S(2)}) collective-permute-start(f32[2,128,128]{2,1,0:T(8,128)S(1)} %get-tuple-element.94), channel_id=1, source_target_pairs={{8,12},{4,0},{9,13},{5,1},{10,14},{6,2},{11,15},{7,3},{24,28},{20,... | collective-permute-start | bytes 393224 | tf_op jit(solution)/shard_map/ppermute | solution.py:510
  33.2 3.9 %collective-permute-start.7 = (f32[4,64]{1,0:T(4,128)S(1)}, f32[4,64]{1,0:T(4,128)S(1)}, u32[]{:S(2)}, u32[]{:S(2)}) collective-permute-start(f32[4,64]{1,0:T(4,128)S(1)} %select_add_fusion), channel_id=1, source_target_pairs={{0,4},{4,0},{8,12},{12,8},{1,5},{5,1},{9,13},{13,9},{2,6},{6,2},{1... | collective-permute-start | bytes 3080 | tf_op jit(solution)/shard_map/ppermute | solution.py:549
  37.1 2.9 %collective-permute-done.5.refs_9_ = f32[2,128,128]{2,1,0:T(8,128)S(1)} collective-permute-done((f32[2,128,128]{2,1,0:T(8,128)S(1)}, f32[2,128,128]{2,1,0:T(8,128)S(1)}, u32[]{:S(2)}, u32[]{:S(2)}) %collective-permute-start.5) | collective-permute-done | bytes 131104 | tf_op jit(solution)/shard_map/ppermute | solution.py:510
  40.0 3.8 %merge_0.1 = (bf16[1,1024,512]{2,1,0:T(8,128)(2,1)}, bf16[1,1024,512]{2,1,0:T(8,128)(2,1)}, bf16[1,1024,512]{2,1,0:T(8,128)(2,1)}, bf16[1,1024,512]{2,1,0:T(8,128)(2,1)}, f32[1,2,1024]{2,1,0:T(2,128)S(1)}) custom-call(s32[1]{0:T(128)} %bitcast.refs_1_.refs_0_, bf16[1,1024,512]{2,1,0:T(8,128)(2,1)S(1)} %get-tuple-element.48.q_ref.refs_1_, ...), custom_call_target="tpu_custom_call" | custom-call | flops 268435456 | bytes 6291456 | tf_op jit(solution)/shard_map/merge_0/pallas_call | solution.py:477
  43.8 0.6 %collective-permute-start.8 = (f32[4,64]{1,0:T(4,128)S(1)}, f32[4,64]{1,0:T(4,128)S(1)}, u32[]{:S(2)}, u32[]{:S(2)}) collective-permute-start(f32[4,64]{1,0:T(4,128)S(1)} %add.42), channel_id=1, source_target_pairs={{0,8},{4,12},{8,0},{12,4},{1,9},{5,13},{9,1},{13,5},{2,10},{6,14},... | collective-permute-start | bytes 3080 | tf_op jit(solution)/shard_map/ppermute | solution.py:549
  44.5 4.3 %merge_1.1 = (bf16[1,1024,512]{2,1,0:T(8,128)(2,1)}, bf16[1,1024,512]{2,1,0:T(8,128)(2,1)}, bf16[1,1024,512]{2,1,0:T(8,128)(2,1)}, bf16[1,1024,512]{2,1,0:T(8,128)(2,1)}, f32[1,4,1024]{2,1,0:T(4,128)}) custom-call(s32[1]{0:T(128)} %bitcast.refs_1_.refs_0_, ...), custom_call_target="tpu_custom_call", output_to_operand_aliasing={{0}: (16, {}), {1}: (17, {}), {2}: (18, {}), {3}: (19, {})} | custom-call | flops 268435456 | bytes 6291456 | tf_op jit(solution)/shard_map/merge_1/pallas_call | solution.py:477
  48.7 0.6 %add.43 = f32[4,64]{1,0:T(4,128)} add(f32[4,64]{1,0:T(4,128)S(1)} %add.42, f32[4,64]{1,0:T(4,128)S(1)} %collective-permute-done.8) | non-fusion elementwise | flops 256 | bytes 3072 | tf_op jit(solution)/shard_map/add | solution.py:557
  (30 shorter events, 0.5 us)
Async XLA Ops:
  0.6 0.7 %copy-start.9 = (s32[1,16]{1,0:T(1,128)S(1)}, s32[1,16]{1,0:T(1,128)}, u32[]{:S(2)}) copy-start(s32[1,16]{1,0:T(1,128)} %refs_0_.1) | copy-start | bytes 196
  1.3 0.7 %copy-start.8 = (f32[1,4,1024]{2,1,0:T(4,128)S(1)}, f32[1,4,1024]{2,1,0:T(4,128)}, u32[]{:S(2)}) copy-start(f32[1,4,1024]{2,1,0:T(4,128)} %refs_2_.1) | copy-start | bytes 49156
  6.8 1.0 %copy-start = (bf16[1,1024,512]{2,1,0:T(8,128)(2,1)}, bf16[1,1024,512]{2,1,0:T(8,128)(2,1)S(1)}, u32[]{:S(2)}) copy-start(bf16[1,1024,512]{2,1,0:T(8,128)(2,1)S(1)} %get-tuple-element.51.cot_ref.refs_4_) | copy-start | bytes 3145732
  7.7 0.7 %copy-start.3 = (f32[2,128,128]{2,1,0:T(8,128)}, f32[2,128,128]{2,1,0:T(8,128)S(1)}, u32[]{:S(2)}) copy-start(f32[2,128,128]{2,1,0:T(8,128)S(1)} %get-tuple-element.55) | copy-start | bytes 393220
  8.4 0.6 %copy-start.5 = (f32[2,128,128]{2,1,0:T(8,128)}, f32[2,128,128]{2,1,0:T(8,128)S(1)}, u32[]{:S(2)}) copy-start(f32[2,128,128]{2,1,0:T(8,128)S(1)} %get-tuple-element.70) | copy-start | bytes 393220
  9.0 12.9 %collective-permute-start.3 = (f32[2,128,128]{2,1,0:T(8,128)}, f32[2,128,128]{2,1,0:T(8,128)S(1)}, u32[]{:S(2)}, u32[]{:S(2)}) collective-permute-start(f32[2,128,128]{2,1,0:T(8,128)} %get-tuple-element.59), channel_id=1, source_target_pairs={{0,4},{12,8},{1,5},{13,9},{2,6},{14,10},{3,7},{15,11},{16,20},{28,... | collective-permute-start | bytes 393224 | tf_op jit(solution)/shard_map/ppermute | solution.py:510
  14.0 9.5 %collective-permute-start = (f32[2,128,128]{2,1,0:T(8,128)}, f32[2,128,128]{2,1,0:T(8,128)S(1)}, u32[]{:S(2)}, u32[]{:S(2)}) collective-permute-start(f32[2,128,128]{2,1,0:T(8,128)} %get-tuple-element.53), channel_id=1, source_target_pairs={{0,4},{12,8},{1,5},{13,9},{2,6},{14,10},{3,7},{15,11},{16,20},{28,... | collective-permute-start | bytes 393224 | tf_op jit(solution)/shard_map/ppermute | solution.py:510
  15.3 0.7 %copy-start.7 = (f32[4,128]{1,0:T(4,128)S(1)}, f32[4,128]{1,0:T(4,128)}, u32[]{:S(2)}) copy-start(f32[4,128]{1,0:T(4,128)} %refs_5_.5) | copy-start | bytes 6148
  16.0 1.2 %copy-start.1 = (bf16[1,1024,512]{2,1,0:T(8,128)(2,1)S(1)}, bf16[1,1024,512]{2,1,0:T(8,128)(2,1)}, u32[]{:S(2)}) copy-start(bf16[1,1024,512]{2,1,0:T(8,128)(2,1)} %copy-done) | copy-start | bytes 3145732
  22.8 7.2 %collective-permute-start.4 = (f32[2,128,128]{2,1,0:T(8,128)S(1)}, f32[2,128,128]{2,1,0:T(8,128)S(1)}, u32[]{:S(2)}, u32[]{:S(2)}) collective-permute-start(f32[2,128,128]{2,1,0:T(8,128)S(1)} %multiply_add_fusion.1), channel_id=1, source_target_pairs={{4,8},{8,4},{5,9},{9,5},{6,10},{10,6},{7,11},{11,7},{20,24},{24,20... | collective-permute-start | bytes 393224 | tf_op jit(solution)/shard_map/ppermute | solution.py:510
  24.4 5.6 %copy-start.6 = (f32[2,128,128]{2,1,0:T(8,128)S(1)}, f32[2,128,128]{2,1,0:T(8,128)}, u32[]{:S(2)}) copy-start(f32[2,128,128]{2,1,0:T(8,128)} %copy-done.5) | copy-start | bytes 393220
  24.4 5.8 %collective-permute-start.1 = (f32[2,128,128]{2,1,0:T(8,128)S(1)}, f32[2,128,128]{2,1,0:T(8,128)S(1)}, u32[]{:S(2)}, u32[]{:S(2)}) collective-permute-start(f32[2,128,128]{2,1,0:T(8,128)S(1)} %multiply_add_fusion.3), channel_id=1, source_target_pairs={{4,8},{8,4},{5,9},{9,5},{6,10},{10,6},{7,11},{11,7},{20,24},{24,20... | collective-permute-start | bytes 393224 | tf_op jit(solution)/shard_map/ppermute | solution.py:510
  25.3 5.0 %copy-start.4 = (f32[2,128,128]{2,1,0:T(8,128)S(1)}, f32[2,128,128]{2,1,0:T(8,128)}, u32[]{:S(2)}) copy-start(f32[2,128,128]{2,1,0:T(8,128)} %copy-done.3) | copy-start | bytes 393220
  30.0 10.0 %copy-start.2 = (bf16[1,1024,512]{2,1,0:T(8,128)(2,1)S(1)}, bf16[1,1024,512]{2,1,0:T(8,128)(2,1)}, u32[]{:S(2)}) copy-start(bf16[1,1024,512]{2,1,0:T(8,128)(2,1)} %copy-done) | copy-start | bytes 3145732
  30.5 2.6 %collective-permute-start.6 = (f32[4,64]{1,0:T(4,128)S(1)}, f32[4,64]{1,0:T(4,128)S(1)}, u32[]{:S(2)}, u32[]{:S(2)}) collective-permute-start(f32[4,64]{1,0:T(4,128)S(1)} %slice_select_fusion), channel_id=1, source_target_pairs={{0,16},{16,0},{1,17},{17,1},{2,18},{18,2},{3,19},{19,3},{4,20},{20... | collective-permute-start | bytes 3080 | tf_op jit(solution)/shard_map/ppermute | solution.py:543
  30.5 9.5 %collective-permute-start.5 = (f32[2,128,128]{2,1,0:T(8,128)S(1)}, f32[2,128,128]{2,1,0:T(8,128)S(1)}, u32[]{:S(2)}, u32[]{:S(2)}) collective-permute-start(f32[2,128,128]{2,1,0:T(8,128)S(1)} %get-tuple-element.91), channel_id=1, source_target_pairs={{8,12},{4,0},{9,13},{5,1},{10,14},{6,2},{11,15},{7,3},{24,28},{20,... | collective-permute-start | bytes 393224 | tf_op jit(solution)/shard_map/ppermute | solution.py:510
  31.8 12.6 %collective-permute-start.2 = (f32[2,128,128]{2,1,0:T(8,128)S(1)}, f32[2,128,128]{2,1,0:T(8,128)S(1)}, u32[]{:S(2)}, u32[]{:S(2)}) collective-permute-start(f32[2,128,128]{2,1,0:T(8,128)S(1)} %get-tuple-element.94), channel_id=1, source_target_pairs={{8,12},{4,0},{9,13},{5,1},{10,14},{6,2},{11,15},{7,3},{24,28},{20,... | collective-permute-start | bytes 393224 | tf_op jit(solution)/shard_map/ppermute | solution.py:510
  33.2 10.6 %collective-permute-start.7 = (f32[4,64]{1,0:T(4,128)S(1)}, f32[4,64]{1,0:T(4,128)S(1)}, u32[]{:S(2)}, u32[]{:S(2)}) collective-permute-start(f32[4,64]{1,0:T(4,128)S(1)} %select_add_fusion), channel_id=1, source_target_pairs={{0,4},{4,0},{8,12},{12,8},{1,5},{5,1},{9,13},{13,9},{2,6},{6,2},{1... | collective-permute-start | bytes 3080 | tf_op jit(solution)/shard_map/ppermute | solution.py:549
  43.8 4.9 %collective-permute-start.8 = (f32[4,64]{1,0:T(4,128)S(1)}, f32[4,64]{1,0:T(4,128)S(1)}, u32[]{:S(2)}, u32[]{:S(2)}) collective-permute-start(f32[4,64]{1,0:T(4,128)S(1)} %add.42), channel_id=1, source_target_pairs={{0,8},{4,12},{8,0},{12,4},{1,9},{5,13},{9,1},{13,5},{2,10},{6,14},... | collective-permute-start | bytes 3080 | tf_op jit(solution)/shard_map/ppermute | solution.py:549

commit v6 on v5

--- a/solution.py
+++ b/solution.py
@@ -11,6 +11,8 @@
 CHUNK = 128
 PARTS = 2
 UNROLL = 4
+ENDS_GRANT = 53 << 20
+GRANT = 53 << 20
 PRECISE = lax.Precision.HIGHEST
 F32 = jnp.float32
 BF16 = jnp.bfloat16
@@ -44,12 +46,12 @@
     return jnp.sum(jnp.where(kept, column, 0.0), axis=0, keepdims=True)
 
 
-def decay_tables(lengths_ref, ctx_ref, gates_ref, spread, cum_ref, chunk_fac_ref, shard_fac_ref):
+def decay_tables(docs, ctx_ref, small_ref, spread, cum_ref, chunk_fac_ref, shard_fac_ref):
     rows = cum_ref.shape[0]
     num_chunks = rows // 8
     tokens = num_chunks * CHUNK
     for chunk in range(num_chunks):
-        part = gates_ref[0, :, chunk * CHUNK : (chunk + 1) * CHUNK]
+        part = small_ref[:, chunk * CHUNK : (chunk + 1) * CHUNK]
         spread[chunk * 8 : chunk * 8 + 4, :] = part
         spread[chunk * 8 + 4 : chunk * 8 + 8, :] = part
     gates = spread[...] * LOG2E
@@ -66,54 +68,55 @@
 
     first = ctx_ref[0] * tokens
     chunk_first = first + (iota((rows, CHUNK), 0) // 8) * CHUNK
-    positions = chunk_first + iota((rows, CHUNK), 1)
     from_start = iota((rows, CHUNK), 0) % 8 < 4
-    chunk_anchor = jnp.where(from_start, chunk_first - 1, chunk_first + (CHUNK - 1))
+    chunk_anchor = jnp.where(from_start, chunk_first - 1, chunk_first + (CHUNK - 1)).astype(F32)
+    shard_anchor = jnp.where(from_start, first - 1, first + (tokens - 1)).astype(F32)
+    positions = (chunk_first + iota((rows, CHUNK), 1)).astype(F32)
     segment = jnp.zeros((rows, CHUNK), F32)
     chunk_segment = jnp.zeros((rows, CHUNK), F32)
-    shard_before = jnp.float32(0)
-    shard_last = jnp.float32(0)
-    start = jnp.int32(0)
-    for doc in range(lengths_ref.shape[1]):
+    shard_segment = jnp.zeros((rows, CHUNK), F32)
+    begin = small_ref.shape[1] - CHUNK
+    for doc in range(docs):
+        start = small_ref[0:1, begin + doc : begin + doc + 1]
         segment += jnp.where(positions >= start, 1.0, 0.0)
         chunk_segment += jnp.where(chunk_anchor >= start, 1.0, 0.0)
-        shard_before += jnp.where(first > start, 1.0, 0.0)
-        shard_last += jnp.where(first + (tokens - 1) >= start, 1.0, 0.0)
-        start += lengths_ref[0, doc]
+        shard_segment += jnp.where(shard_anchor >= start, 1.0, 0.0)
     cum_ref[...] = jnp.where(from_start, prefix, segment)
     exponent = jnp.where(from_start, prefix, suffix)
     chunk_fac_ref[...] = jnp.where(
         segment == chunk_segment, jnp.exp2(jnp.minimum(exponent, 0.0)), 0.0
     )
-    keep = segment == jnp.where(from_start, shard_before, shard_last)
+    keep = segment == shard_segment
     shard_fac_ref[...] = jnp.where(keep, jnp.exp2(jnp.minimum(exponent + others, 0.0)), 0.0)
 
 
-def ends_kernel(head_width, half_ctx, *refs):
-    lengths_ref, ctx_ref, gates_ref = refs[:3]
-    sources, targets = refs[3:7], refs[7:11]
+def ends_kernel(head_width, docs, half_ctx, *refs):
+    ctx_ref, small_ref = refs[:2]
+    sources = refs[2:6]
     near_refs, far_refs, decay_refs = (
-        refs[11 + i * PARTS : 11 + (i + 1) * PARTS] for i in range(3)
+        refs[6 + i * PARTS : 6 + (i + 1) * PARTS] for i in range(3)
     )
-    cum_ref, chunk_fac_ref, shard_fac_ref, spread, sems = refs[11 + 3 * PARTS :]
-    q_ref, k_ref, v_ref, cot_ref = targets
+    cum_ref, chunk_fac_ref, shard_fac_ref, gain_ref, held, spread, sems = refs[6 + 3 * PARTS :]
+    q_ref, k_ref, v_ref, cot_ref = (held.at[pl.ds(i, 1)] for i in range(4))
     heads = near_refs[0].shape[0]
     rows = shard_fac_ref.shape[0]
     steps = sems.shape[0]
-    block = q_ref.shape[1] // steps
+    block = held.shape[1] // steps
     chunks = block // CHUNK
 
     def copies(step):
         at = pl.ds(step * block, block)
         return [
-            pltpu.make_async_copy(source.at[:, at, :], target.at[:, at, :], sems.at[step, i])
-            for i, (source, target) in enumerate(zip(sources, targets))
+            pltpu.make_async_copy(source.at[0, at, :], held.at[i, at, :], sems.at[step, i])
+            for i, source in enumerate(sources)
         ]
 
     for step in range(steps):
         for i, copy in enumerate(copies(step)):
             copy.start(priority=i % 2)
-    decay_tables(lengths_ref, ctx_ref, gates_ref, spread, cum_ref, chunk_fac_ref, shard_fac_ref)
+    decay_tables(docs, ctx_ref, small_ref, spread, cum_ref, chunk_fac_ref, shard_fac_ref)
+    tokens = held.shape[1]
+    gain_ref[...] = small_ref[:, tokens : tokens + head_width]
     for part in range(PARTS):
         for head in range(heads):
             row = rows - 8 + part * heads + head
@@ -156,18 +159,41 @@
 
 
 def local_kernel(
-    head_width, part, q_ref, k_ref, v_ref, cot_ref, gain_ref, cum_ref, fac_ref,
-    out_ref, dq_ref, dk_ref, dv_ref, dgate_ref, dgain_ref, leaving, state,
+    head_width, part, q_src, k_src, v_src, cot_src, gain_ref, cum_ref, fac_ref,
+    target, dgate_ref, dgain_ref, held_in, staged, leaving, state, in_sems, out_sems,
 ):
+    q_ref, k_ref, v_ref, cot_ref = (held_in.at[pl.ds(i, 1)] for i in range(4))
+    out_ref, dq_ref, dk_ref, dv_ref = (staged.at[pl.ds(i, 1)] for i in range(4))
     heads = state.shape[0]
     num_chunks = leaving.shape[0]
     scale = head_width ** (-0.5)
     unroll = math.gcd(num_chunks, UNROLL)
 
+    groups = num_chunks // unroll
+    size = unroll * CHUNK
+    wide = slice(part * heads * head_width, (part + 1) * heads * head_width)
+
+    def copy_in(i, group):
+        at = pl.ds(pl.multiple_of(group * size, size), size)
+        source = (q_src, k_src, v_src, cot_src)[i]
+        return pltpu.make_async_copy(
+            source.at[0, at, wide], held_in.at[i, at, :], in_sems.at[i, group]
+        )
+
+    def copy_out(group):
+        at = pl.ds(pl.multiple_of(group * size, size), size)
+        return pltpu.make_async_copy(
+            staged.at[:, at, :], target.at[:, at, :], out_sems.at[group]
+        )
+
+    for group in range(groups - 1, -1, -1):
+        copy_in(0, group).start(priority=0)
+        copy_in(3, group).start(priority=1)
+    for group in range(groups):
+        copy_in(1, group).start(priority=0)
+        copy_in(2, group).start(priority=1)
+
     def lanes_of(head):
-        return slice((part * heads + head) * head_width, (part * heads + head + 1) * head_width)
-
-    def own_lanes(head):
         return slice(head * head_width, (head + 1) * head_width)
 
     def rows_of(chunk):
@@ -271,7 +297,7 @@
         for key in pairs:
             at, head = key
             row = part * heads + head
-            rows, own = rows_of(chunks[at]), own_lanes(head)
+            rows, own = rows_of(chunks[at]), lanes_of(head)
             out_ref[0, rows, own] = out[key].astype(BF16)
             dq_ref[0, rows, own] = dq[key].astype(BF16)
             dv_ref[0, rows, own] = dv[key].astype(BF16)
@@ -283,27 +309,34 @@
     state[...] = jnp.zeros_like(state)
 
     def backward_group(index, carry):
+        copy_in(0, groups - 1 - index).wait()
+        copy_in(3, groups - 1 - index).wait()
         backward([num_chunks - 1 - (index * unroll + at) for at in range(unroll)])
         return carry
 
-    lax.fori_loop(0, num_chunks // unroll, backward_group, 0)
+    lax.fori_loop(0, groups, backward_group, 0)
     state[...] = jnp.zeros_like(state)
     dgain_ref[...] = jnp.zeros_like(dgain_ref)
 
     def forward_group(index, carry):
+        copy_in(1, index).wait()
+        copy_in(2, index).wait()
         forward([index * unroll + at for at in range(unroll)])
+        copy_out(index).start()
         return carry
 
-    lax.fori_loop(0, num_chunks // unroll, forward_group, 0)
+    lax.fori_loop(0, groups, forward_group, 0)
+    for group in range(groups):
+        copy_out(group).wait()
 
 
 def merge_kernel(head_width, part, half_ctx, *refs):
-    (ctx_ref, q_ref, k_ref, v_ref, cot_ref, gain_ref, fac_ref, first_ref, second_ref, last_ref,
-     out_in, dq_in, dk_in, dv_in, dgate_in) = refs[:15]
-    refs = refs[15:]
+    sources = refs[:5]
+    ctx_ref, gain_ref, fac_ref, first_ref, second_ref, last_ref, dgate_in = refs[5:12]
+    refs = refs[12:]
     if part > 0:
         before_ref, refs = refs[0], refs[5:]
-    targets, dgate_ref, staged, entering, leaving, sems = refs[:4], *refs[4:]
+    targets, dgate_ref, held, staged, entering, leaving, in_sems, sems = refs[:4], *refs[4:]
     heads = first_ref.shape[0]
     steps = sems.shape[0]
     num_chunks = fac_ref.shape[0] // 8
@@ -311,7 +344,19 @@
     block = chunks * CHUNK
     scale = head_width ** (-0.5)
     group = slice(part * heads * head_width, (part + 1) * heads * head_width)
-    partials = (out_in, dq_in, dk_in, dv_in)
+
+    def copies_in(step):
+        at = pl.ds(step * block, block)
+        return [
+            pltpu.make_async_copy(
+                source.at[0, at, group], held.at[i, at, :], in_sems.at[step, i]
+            )
+            for i, source in enumerate(sources[:4])
+        ] + [
+            pltpu.make_async_copy(
+                sources[4].at[:, at, :], staged.at[:, at, :], in_sems.at[step, 4]
+            )
+        ]
 
     def copies(step):
         at = pl.ds(step * block, block)
@@ -327,6 +372,9 @@
         first, second = first_ref[head], second_ref[head] + last_ref[head]
         return jnp.where(low, first, second), jnp.where(low, second, first)
 
+    for step in range(steps):
+        for i, copy in enumerate(copies_in(step)):
+            copy.start(priority=i % 2)
     gain_columns = jnp.transpose(jnp.concatenate([gain_ref[...], gain_ref[...]], axis=0))
     entering[...] = jnp.zeros_like(entering)
     leaving[...] = jnp.zeros_like(leaving)
@@ -346,13 +394,15 @@
     for step in range(steps):
         numbers = range(step * chunks, (step + 1) * chunks)
         products, results = {}, {}
+        for copy in copies_in(step):
+            copy.wait()
         for number in numbers:
             rows = slice(number * CHUNK, (number + 1) * CHUNK)
             products[number] = (
-                dot_nn(q_ref[0, rows, group], entering[...]),
-                dot_nt(cot_ref[0, rows, group], entering[...]),
-                dot_nt(v_ref[0, rows, group], leaving[...]),
-                dot_nn(k_ref[0, rows, group], leaving[...]),
+                dot_nn(held[0, rows, :], entering[...]),
+                dot_nt(held[3, rows, :], entering[...]),
+                dot_nt(held[2, rows, :], leaving[...]),
+                dot_nn(held[1, rows, :], leaving[...]),
             )
         for number in numbers:
             columns = jnp.transpose(fac_ref[number * 8 : number * 8 + 8, :])
@@ -360,7 +410,6 @@
             for head in range(heads):
                 row = part * heads + head
                 lanes = slice(head * head_width, (head + 1) * head_width)
-                wide = slice(row * head_width, (row + 1) * head_width)
                 from_start, to_end = columns[:, row : row + 1], columns[:, 4 + row : 5 + row]
                 across, dq, dk, written = (
                     product[:, lanes] * factor
@@ -369,12 +418,12 @@
                     )
                 )
                 results[number, head] = [
-                    (partial[0, rows, lanes].astype(F32) + added).astype(BF16)
-                    for partial, added in zip(partials, (across, dq, dk, written))
+                    (staged[i, rows, lanes].astype(F32) + added).astype(BF16)
+                    for i, added in enumerate((across, dq, dk, written))
                 ]
-                kept = written * v_ref[0, rows, wide].astype(F32)
+                kept = written * held[2, rows, lanes].astype(F32)
                 balance = jnp.sum(
-                    across * cot_ref[0, rows, wide].astype(F32) - kept, axis=1, keepdims=True
+                    across * held[3, rows, lanes].astype(F32) - kept, axis=1, keepdims=True
                 )
                 gate_sums[number, head] = later_sums(balance)
                 kept_sums[number, head] = jnp.sum(kept, axis=0, keepdims=True)
@@ -417,86 +466,103 @@
     ctx = lax.axis_index("ctx")
     count = lax.axis_size("ctx")
     middle = count // 2 - 1
+    docs = lengths.shape[1]
+    earlier = jnp.arange(docs)[:, None] < jnp.arange(CHUNK)[None, :]
+    starts = jnp.sum(jnp.where(earlier, lengths[0][:, None], 0), axis=0).astype(F32)
+    small = jnp.concatenate(
+        [gates[0], key_gain, jnp.broadcast_to(starts[None], (all_heads, CHUNK))], axis=1
+    )
     ctx_scalar = jnp.reshape(ctx, (1,)).astype(jnp.int32)
 
     def shape_of(*shape, dtype=F32):
         return jax.ShapeDtypeStruct(shape, dtype)
 
+    hbm = pl.BlockSpec(memory_space=pltpu.HBM)
     smem = pl.BlockSpec(memory_space=pltpu.SMEM)
     vmem = pl.BlockSpec(memory_space=pltpu.VMEM)
     table = shape_of(rows, CHUNK)
     states = shape_of(heads, head_width, head_width)
     decays = shape_of(heads, 1, head_width)
     part_gates = shape_of(1, heads, tokens)
+    partials = shape_of(4, tokens, part_width, dtype=BF16)
+    streams = (queries, keys_raw, values, cotangent)
     product = 2 * tokens * part_width * head_width
 
     def ends():
-        held = shape_of(1, tokens, width, dtype=BF16)
-        outs = [held] * 4 + [states] * (2 * PARTS) + [decays] * PARTS + [table] * 3
+        outs = [states] * (2 * PARTS) + [decays] * PARTS + [table] * 3
+        outs.append(shape_of(all_heads, head_width))
         return pl.pallas_call(
-            functools.partial(ends_kernel, head_width, count // 2),
-            in_specs=[smem, smem, vmem] + [pl.BlockSpec(memory_space=pltpu.HBM)] * 4,
+            functools.partial(ends_kernel, head_width, lengths.shape[1], count // 2),
+            in_specs=[smem, vmem] + [hbm] * 4,
             out_specs=[vmem] * len(outs),
             out_shape=outs,
             scratch_shapes=[
+                pltpu.VMEM((4, tokens, width), BF16),
                 pltpu.VMEM((rows, CHUNK), F32),
                 pltpu.SemaphoreType.DMA((steps, 4)),
             ],
-            compiler_params=pltpu.CompilerParams(vmem_limit_bytes=49 << 20),
+            compiler_params=pltpu.CompilerParams(vmem_limit_bytes=ENDS_GRANT),
             cost_estimate=pl.CostEstimate(
                 flops=2 * product * PARTS, bytes_accessed=8 * tokens * width, transcendentals=0
             ),
             name="shard_ends",
-        )(lengths, ctx_scalar, gates, queries, keys_raw, values, cotangent)
-
-    def local(part, arrays, gain, cum, fac):
-        wide = shape_of(1, tokens, part_width, dtype=BF16)
+        )(ctx_scalar, small, *streams)
+
+    def local(part, gain, cum, fac):
+        groups = num_chunks // math.gcd(num_chunks, UNROLL)
         return pl.pallas_call(
             functools.partial(local_kernel, head_width, part),
-            in_specs=[vmem] * 7,
-            out_specs=[vmem] * 6,
-            out_shape=[wide] * 4 + [part_gates, shape_of(heads, head_width)],
+            in_specs=[hbm] * 4 + [vmem] * 3,
+            out_specs=[hbm] + [vmem] * 2,
+            out_shape=[partials, part_gates, shape_of(heads, head_width)],
             scratch_shapes=[
+                pltpu.VMEM((4, tokens, part_width), BF16),
+                pltpu.VMEM((4, tokens, part_width), BF16),
                 pltpu.VMEM((num_chunks, heads, head_width, head_width), BF16),
                 pltpu.VMEM((heads, head_width, head_width), F32),
+                pltpu.SemaphoreType.DMA((4, groups)),
+                pltpu.SemaphoreType.DMA((groups,)),
             ],
-            compiler_params=pltpu.CompilerParams(vmem_limit_bytes=24 << 20),
+            compiler_params=pltpu.CompilerParams(vmem_limit_bytes=GRANT),
             cost_estimate=pl.CostEstimate(
                 flops=12 * product, bytes_accessed=16 * tokens * part_width, transcendentals=0
             ),
             name=f"local_{part}",
-        )(*arrays, gain, cum, fac)
-
-    def merge(part, arrivals, locals_, done):
+        )(*streams, gain, cum, fac)
+
+    def merge(part, arrivals, local_part, done):
         full_gates = shape_of(1, (part + 1) * heads, tokens)
         extra, extra_specs, aliases = [], [], {}
         if part > 0:
             extra = [done[4]] + list(done[:4])
-            extra_specs = [vmem] + [pl.BlockSpec(memory_space=pl.ANY)] * 4
-            aliases = {16 + i: i for i in range(4)}
+            extra_specs = [vmem] + [hbm] * 4
+            aliases = {13 + i: i for i in range(4)}
         return pl.pallas_call(
             functools.partial(merge_kernel, head_width, part, count // 2),
-            in_specs=[smem] + [vmem] * 14 + extra_specs,
-            out_specs=[pl.BlockSpec(memory_space=pl.ANY)] * 4 + [vmem],
+            in_specs=[hbm] * 5 + [smem] + [vmem] * 6 + extra_specs,
+            out_specs=[hbm] * 4 + [vmem],
             out_shape=[shape_of(1, tokens, width, dtype=BF16)] * 4 + [full_gates],
             scratch_shapes=[
                 pltpu.VMEM((4, tokens, part_width), BF16),
+                pltpu.VMEM((4, tokens, part_width), BF16),
                 pltpu.VMEM((part_width, part_width), BF16),
                 pltpu.VMEM((part_width, part_width), BF16),
+                pltpu.SemaphoreType.DMA((steps, 5)),
                 pltpu.SemaphoreType.DMA((steps, 4)),
             ],
             input_output_aliases=aliases,
-            compiler_params=pltpu.CompilerParams(vmem_limit_bytes=24 << 20),
+            compiler_params=pltpu.CompilerParams(vmem_limit_bytes=GRANT),
             cost_estimate=pl.CostEstimate(
                 flops=4 * product, bytes_accessed=24 * tokens * part_width, transcendentals=0
             ),
             name=f"merge_{part}",
-        )(ctx_scalar, *streams, key_gain, shard_fac, *arrivals, *locals_, *extra)
+        )(
+            *streams, local_part[0], ctx_scalar, gain, shard_fac, *arrivals, local_part[1], *extra
+        )
 
     results = ends()
-    streams, results = results[:4], results[4:]
     near, far, decay = (results[i * PARTS : (i + 1) * PARTS] for i in range(3))
-    cum, chunk_fac, shard_fac = results[3 * PARTS :]
+    cum, chunk_fac, shard_fac, gain = results[3 * PARTS :]
     sent = [[] for _ in range(PARTS)]
     arrived = [[] for _ in range(PARTS)]
     local_parts = [None] * PARTS
@@ -519,10 +585,10 @@
             local_cum = cum
             if hop > 0:
                 local_cum, _ = lax.optimization_barrier((cum, arrived[0][hop - 1]))
-            local_parts[hop] = list(local(hop, streams, key_gain, local_cum, chunk_fac))
+            local_parts[hop] = list(local(hop, gain, local_cum, chunk_fac))
             if hop + 1 < count - 1:
-                local_parts[hop][5], arrived[0][-1] = lax.optimization_barrier(
-                    (local_parts[hop][5], arrived[0][-1])
+                local_parts[hop][2], arrived[0][-1] = lax.optimization_barrier(
+                    (local_parts[hop][2], arrived[0][-1])
                 )
         if hop + 1 < count - 1:
             for part in range(PARTS):
@@ -531,7 +597,7 @@
     terms = []
     for part in range(PARTS):
         crossed = jnp.sum(sent[part][middle] * arrived[part][middle], axis=2)
-        term = local_parts[part][5] + jnp.where(ctx == middle, crossed, 0.0)
+        term = local_parts[part][2] + jnp.where(ctx == middle, crossed, 0.0)
         if middle > 0:
             term = term + jnp.sum(sum(arrived[part][:middle]) * far[part], axis=2)
         terms.append(term)
@@ -551,7 +617,7 @@
         zeros = jnp.zeros(states.shape, F32)
         first = sum(arrived[part][:middle], zeros) if middle != 1 else arrived[part][0]
         second = sum(arrived[part][middle:-1], zeros) if middle != 1 else arrived[part][1]
-        done = list(merge(part, (first, second, arrived[part][-1]), local_parts[part][:5], done))
+        done = list(merge(part, (first, second, arrived[part][-1]), local_parts[part], done))
         if part < PARTS - 1:
             done[4], others = lax.optimization_barrier((done[4], others))
         grad_gain = grad_gain + others

time: 49.7 us -> 50.3 us (1.012)
  Pallas kernels: 22.2 us -> 28.8 us
  local copies, waits for them, and re-layouts: 5.55 us -> 0.01 us
    unnamed x20 -> x0, local copies, waits for them, and re-layouts: 5.55 us -> none
    pallas_call x2, Pallas kernels: 9.44 us -> 13.9 us  [local(): pl.pallas_call(functools.partial(local_kernel, head_width, part), in_spec...]
    pallas_call x2, Pallas kernels: 8.03 us -> 11.3 us  [merge(): pl.pallas_call(functools.partial(merge_kernel, head_width, part, count //...]
    add x2, other arithmetic: 1.85 us -> 0.04 us  [send(): payload = payload + decay[part] * arrived[part][-1]]
    pallas_call x1, Pallas kernels: 4.74 us -> 3.61 us  [ends(): pl.pallas_call(functools.partial(ends_kernel, head_width, lengths.shape[1...]
    reduce_sum x0 -> x1, other arithmetic: none -> 0.74 us  [shards(): jnp.sum(jnp.where(earlier, lengths[0][:, None], 0), axis=0).astype(F32)]
    concatenate x0 -> x1, other arithmetic: none -> 0.74 us  [shards(): jnp.concatenate([gates[0], key_gain, jnp.broadcast_to(starts[None], (all_...]
  transfers between devices with their start and end apart: 9 -> 9, of which waited for: 1 -> 1; matrix products, arithmetic and copies ran while one was open for 4% -> 1% of each run, Pallas kernels for 35% -> 51%
where the time goes in v6:
time: 50.3 us; the launch traced here: 49.9 us
  Pallas kernels  28.8 us (57%)
  starting transfers between devices  14.7 us (29%)
  waiting for transfers between devices  2.94 us (6%)
  other arithmetic  2.6 us (5%)
  between operations  0.85 us (2%)
    pallas_call x2, Pallas kernels, local(): pl.pallas_call(functools.partial(local_kernel, head_width, part), in_spec...  13.9 us
    pallas_call x2, Pallas kernels, merge(): pl.pallas_call(functools.partial(merge_kernel, head_width, part, count //...  11.3 us
    ppermute x6, starting transfers between devices, send(): lax.ppermute(payload, 'ctx', [(hop, hop + 1), (count - 1 - hop, count - 2...  10.2 us
    ppermute x2, starting transfers between devices, shards(): lax.ppermute(grad_gain, 'ctx', [(i, i ^ reach) for i in range(count)])  4.51 us
    pallas_call x1, Pallas kernels, ends(): pl.pallas_call(functools.partial(ends_kernel, head_width, lengths.shape[1...  3.61 us
    ppermute x6, waiting for transfers between devices, send(): lax.ppermute(payload, 'ctx', [(hop, hop + 1), (count - 1 - hop, count - 2...  2.94 us
  transfers between devices with their start and end apart: 9, of which 1 were waited for; matrix products, arithmetic and copies ran while one was open for 1% of the time, Pallas kernels for 51%

profile of v6, /device:TPU:0, one launch (start us, length us, event | category | flops | bytes accessed | tf_op | source)
XLA Modules:
  0.0 49.9 jit_solution(11141245809882754943)
XLA Ops:
  0.6 0.7 %select_reduce_fusion = s32[128]{0:T(128)S(1)} fusion(s32[16]{0:T(128)} %bitcast.10), kind=kLoop, calls=%fused_computation.9 | loop fusion | flops 6016 | bytes 576 | tf_op jit(solution)/shard_map/reduce_sum | solution.py:471
  1.4 0.7 %maximum_maximum_fusion.refs_1_ = f32[4,1280]{1,0:T(4,128)S(1)} fusion(f32[4,128]{1,0:T(4,128)} %param.12, f32[4,1024]{1,0:T(4,128)} %bitcast.9, f32[1280]{0:T(1024)S(1)} %pad.4.clone), kind=kLoop, calls=%fused_computation.8 | loop fusion | flops 10240 | bytes 44032 | tf_op jit(solution)/shard_map/concatenate | solution.py:472
  2.1 3.6 %shard_ends.1 = (f32[2,128,128]{2,1,0:T(8,128)S(1)}, f32[2,128,128]{2,1,0:T(8,128)S(1)}, f32[2,128,128]{2,1,0:T(8,128)S(1)}, f32[2,128,128]{2,1,0:T(8,128)S(1)},...) custom-call(s32[1]{0:T(128)} %bitcast.refs_0_.refs_5_, ...), custom_call_target="tpu_custom_call" | custom-call | flops 268435456 | bytes 4194304 | tf_op jit(solution)/shard_map/shard_ends/pallas_call | solution.py:494
  5.8 4.9 %collective-permute-start = (f32[2,128,128]{2,1,0:T(8,128)S(1)}, f32[2,128,128]{2,1,0:T(8,128)S(1)}, u32[]{:S(2)}, u32[]{:S(2)}) collective-permute-start(f32[2,128,128]{2,1,0:T(8,128)S(1)} %get-tuple-element.43), channel_id=1, source_target_pairs={{0,4},{12,8},{1,5},{13,9},{2,6},{14,10},{3,7},{15,11},{16,20},{28,... | collective-permute-start | bytes 393224 | tf_op jit(solution)/shard_map/ppermute | solution.py:576
  10.7 1.3 %collective-permute-start.1 = (f32[2,128,128]{2,1,0:T(8,128)S(1)}, f32[2,128,128]{2,1,0:T(8,128)S(1)}, u32[]{:S(2)}, u32[]{:S(2)}) collective-permute-start(f32[2,128,128]{2,1,0:T(8,128)S(1)} %get-tuple-element.48), channel_id=1, source_target_pairs={{0,4},{12,8},{1,5},{13,9},{2,6},{14,10},{3,7},{15,11},{16,20},{28,... | collective-permute-start | bytes 393224 | tf_op jit(solution)/shard_map/ppermute | solution.py:576
  12.0 7.0 %local_0.1 = (bf16[4,1024,256]{2,1,0:T(8,128)(2,1)}, f32[1,2,1024]{2,1,0:T(2,128)S(1)}, f32[2,128]{1,0:T(2,128)S(1)}) custom-call(bf16[1,1024,512]{2,1,0:T(8,128)(2,1)} %refs_0_.3, bf16[1,1024,512]{2,1,0:T(8,128)(2,1)} %refs_1_.3, bf16[1,1024,512]{2,1,0:T(8,128)(2,1)} %refs_2_.5, bf16[1,1024,512]{2,1,0:T(8,128)(2,1)} %refs_3_.5, ...), custom_call_target="tpu_custom_call" | custom-call | flops 805306368 | bytes 4194304 | tf_op jit(solution)/shard_map/local_0/pallas_call | solution.py:513
  19.0 0.0 collective-permute-done.refs_8_
  19.0 0.7 %collective-permute-start.4 = (f32[2,128,128]{2,1,0:T(8,128)S(1)}, f32[2,128,128]{2,1,0:T(8,128)S(1)}, u32[]{:S(2)}, u32[]{:S(2)}) collective-permute-start(f32[2,128,128]{2,1,0:T(8,128)S(1)} %multiply_add_fusion.1), channel_id=1, source_target_pairs={{4,8},{8,4},{5,9},{9,5},{6,10},{10,6},{7,11},{11,7},{20,24},{24,20... | collective-permute-start | bytes 393224 | tf_op jit(solution)/shard_map/ppermute | solution.py:576
  19.7 0.7 %collective-permute-start.2 = (f32[2,128,128]{2,1,0:T(8,128)S(1)}, f32[2,128,128]{2,1,0:T(8,128)S(1)}, u32[]{:S(2)}, u32[]{:S(2)}) collective-permute-start(f32[2,128,128]{2,1,0:T(8,128)S(1)} %multiply_add_fusion.3), channel_id=1, source_target_pairs={{4,8},{8,4},{5,9},{9,5},{6,10},{10,6},{7,11},{11,7},{20,24},{24,20... | collective-permute-start | bytes 393224 | tf_op jit(solution)/shard_map/ppermute | solution.py:576
  20.4 7.0 %local_1.1 = (bf16[4,1024,256]{2,1,0:T(8,128)(2,1)}, f32[1,2,1024]{2,1,0:T(2,128)S(1)}, f32[2,128]{1,0:T(2,128)S(1)}) custom-call(bf16[1,1024,512]{2,1,0:T(8,128)(2,1)} %refs_0_.3, bf16[1,1024,512]{2,1,0:T(8,128)(2,1)} %refs_1_.3, bf16[1,1024,512]{2,1,0:T(8,128)(2,1)} %refs_2_.5, bf16[1,1024,512]{2,1,0:T(8,128)(2,1)} %refs_3_.5, ...), custom_call_target="tpu_custom_call" | custom-call | flops 805306368 | bytes 4194304 | tf_op jit(solution)/shard_map/local_1/pallas_call | solution.py:513
  27.4 0.2 multiply_reduce_fusion.3
  27.6 0.2 multiply_reduce_fusion.1
  27.8 0.1 slice_select_fusion
  27.8 0.0 collective-permute-start.6
  27.9 1.3 %collective-permute-start.5 = (f32[2,128,128]{2,1,0:T(8,128)S(1)}, f32[2,128,128]{2,1,0:T(8,128)S(1)}, u32[]{:S(2)}, u32[]{:S(2)}) collective-permute-start(f32[2,128,128]{2,1,0:T(8,128)S(1)} %get-tuple-element.73), channel_id=1, source_target_pairs={{8,12},{4,0},{9,13},{5,1},{10,14},{6,2},{11,15},{7,3},{24,28},{20,... | collective-permute-start | bytes 393224 | tf_op jit(solution)/shard_map/ppermute | solution.py:576
  29.2 1.3 %collective-permute-start.3 = (f32[2,128,128]{2,1,0:T(8,128)S(1)}, f32[2,128,128]{2,1,0:T(8,128)S(1)}, u32[]{:S(2)}, u32[]{:S(2)}) collective-permute-start(f32[2,128,128]{2,1,0:T(8,128)S(1)} %get-tuple-element.76), channel_id=1, source_target_pairs={{8,12},{4,0},{9,13},{5,1},{10,14},{6,2},{11,15},{7,3},{24,28},{20,... | collective-permute-start | bytes 393224 | tf_op jit(solution)/shard_map/ppermute | solution.py:576
  30.5 0.0 collective-permute-done.6
  30.5 0.1 select_add_fusion
  30.6 3.9 %collective-permute-start.7 = (f32[4,64]{1,0:T(4,128)S(1)}, f32[4,64]{1,0:T(4,128)S(1)}, u32[]{:S(2)}, u32[]{:S(2)}) collective-permute-start(f32[4,64]{1,0:T(4,128)S(1)} %select_add_fusion), channel_id=1, source_target_pairs={{0,4},{4,0},{8,12},{12,8},{1,5},{5,1},{9,13},{13,9},{2,6},{6,2},{1... | collective-permute-start | bytes 3080 | tf_op jit(solution)/shard_map/ppermute | solution.py:615
  34.5 2.9 %collective-permute-done.5.refs_10_ = f32[2,128,128]{2,1,0:T(8,128)S(1)} collective-permute-done((f32[2,128,128]{2,1,0:T(8,128)S(1)}, f32[2,128,128]{2,1,0:T(8,128)S(1)}, u32[]{:S(2)}, u32[]{:S(2)}) %collective-permute-start.5) | collective-permute-done | bytes 131104 | tf_op jit(solution)/shard_map/ppermute | solution.py:576
  37.4 5.3 %merge_0.1 = (bf16[1,1024,512]{2,1,0:T(8,128)(2,1)}, bf16[1,1024,512]{2,1,0:T(8,128)(2,1)}, bf16[1,1024,512]{2,1,0:T(8,128)(2,1)}, bf16[1,1024,512]{2,1,0:T(8,128)(2,1)}, f32[1,2,1024]{2,1,0:T(2,128)S(1)}) custom-call(bf16[1,1024,512]{2,1,0:T(8,128)(2,1)} %refs_0_.3, bf16[1,1024,512]{2,1,0:T(8,128)(2,1)} %refs_1_.3, bf16[1,1024,512]{2,1,0:T(8,128)(2,1)} %refs_2_.5, ...), custom_call_target="tpu_custom_call" | custom-call | flops 268435456 | bytes 6291456 | tf_op jit(solution)/shard_map/merge_0/pallas_call | solution.py:540
  42.7 0.6 %collective-permute-start.8 = (f32[4,64]{1,0:T(4,128)S(1)}, f32[4,64]{1,0:T(4,128)S(1)}, u32[]{:S(2)}, u32[]{:S(2)}) collective-permute-start(f32[4,64]{1,0:T(4,128)S(1)} %add.42), channel_id=1, source_target_pairs={{0,8},{4,12},{8,0},{12,4},{1,9},{5,13},{9,1},{13,5},{2,10},{6,14},... | collective-permute-start | bytes 3080 | tf_op jit(solution)/shard_map/ppermute | solution.py:615
  43.4 5.9 %merge_1.1 = (bf16[1,1024,512]{2,1,0:T(8,128)(2,1)}, bf16[1,1024,512]{2,1,0:T(8,128)(2,1)}, bf16[1,1024,512]{2,1,0:T(8,128)(2,1)}, bf16[1,1024,512]{2,1,0:T(8,128)(2,1)}, f32[1,4,1024]{2,1,0:T(4,128)}) custom-call(bf16[1,1024,512]{2,1,0:T(8,128)(2,1)} %refs_0_.3, ...), custom_call_target="tpu_custom_call", output_to_operand_aliasing={{0}: (13, {}), {1}: (14, {}), {2}: (15, {}), {3}: (16, {})} | custom-call | flops 268435456 | bytes 6291456 | tf_op jit(solution)/shard_map/merge_1/pallas_call | solution.py:540
  49.3 0.6 %add.43 = f32[4,64]{1,0:T(4,128)} add(f32[4,64]{1,0:T(4,128)S(1)} %add.42, f32[4,64]{1,0:T(4,128)S(1)} %collective-permute-done.8) | non-fusion elementwise | flops 256 | bytes 3072 | tf_op jit(solution)/shard_map/add | solution.py:623
  (14 shorter events, 0.1 us)
Async XLA Ops:
  5.8 13.2 %collective-permute-start = (f32[2,128,128]{2,1,0:T(8,128)S(1)}, f32[2,128,128]{2,1,0:T(8,128)S(1)}, u32[]{:S(2)}, u32[]{:S(2)}) collective-permute-start(f32[2,128,128]{2,1,0:T(8,128)S(1)} %get-tuple-element.43), channel_id=1, source_target_pairs={{0,4},{12,8},{1,5},{13,9},{2,6},{14,10},{3,7},{15,11},{16,20},{28,... | collective-permute-start | bytes 393224 | tf_op jit(solution)/shard_map/ppermute | solution.py:576
  10.7 9.0 %collective-permute-start.1 = (f32[2,128,128]{2,1,0:T(8,128)S(1)}, f32[2,128,128]{2,1,0:T(8,128)S(1)}, u32[]{:S(2)}, u32[]{:S(2)}) collective-permute-start(f32[2,128,128]{2,1,0:T(8,128)S(1)} %get-tuple-element.48), channel_id=1, source_target_pairs={{0,4},{12,8},{1,5},{13,9},{2,6},{14,10},{3,7},{15,11},{16,20},{28,... | collective-permute-start | bytes 393224 | tf_op jit(solution)/shard_map/ppermute | solution.py:576
  19.0 8.4 %collective-permute-start.4 = (f32[2,128,128]{2,1,0:T(8,128)S(1)}, f32[2,128,128]{2,1,0:T(8,128)S(1)}, u32[]{:S(2)}, u32[]{:S(2)}) collective-permute-start(f32[2,128,128]{2,1,0:T(8,128)S(1)} %multiply_add_fusion.1), channel_id=1, source_target_pairs={{4,8},{8,4},{5,9},{9,5},{6,10},{10,6},{7,11},{11,7},{20,24},{24,20... | collective-permute-start | bytes 393224 | tf_op jit(solution)/shard_map/ppermute | solution.py:576
  19.7 7.8 %collective-permute-start.2 = (f32[2,128,128]{2,1,0:T(8,128)S(1)}, f32[2,128,128]{2,1,0:T(8,128)S(1)}, u32[]{:S(2)}, u32[]{:S(2)}) collective-permute-start(f32[2,128,128]{2,1,0:T(8,128)S(1)} %multiply_add_fusion.3), channel_id=1, source_target_pairs={{4,8},{8,4},{5,9},{9,5},{6,10},{10,6},{7,11},{11,7},{20,24},{24,20... | collective-permute-start | bytes 393224 | tf_op jit(solution)/shard_map/ppermute | solution.py:576
  27.8 2.6 %collective-permute-start.6 = (f32[4,64]{1,0:T(4,128)S(1)}, f32[4,64]{1,0:T(4,128)S(1)}, u32[]{:S(2)}, u32[]{:S(2)}) collective-permute-start(f32[4,64]{1,0:T(4,128)S(1)} %slice_select_fusion), channel_id=1, source_target_pairs={{0,16},{16,0},{1,17},{17,1},{2,18},{18,2},{3,19},{19,3},{4,20},{20... | collective-permute-start | bytes 3080 | tf_op jit(solution)/shard_map/ppermute | solution.py:609
  27.9 9.5 %collective-permute-start.5 = (f32[2,128,128]{2,1,0:T(8,128)S(1)}, f32[2,128,128]{2,1,0:T(8,128)S(1)}, u32[]{:S(2)}, u32[]{:S(2)}) collective-permute-start(f32[2,128,128]{2,1,0:T(8,128)S(1)} %get-tuple-element.73), channel_id=1, source_target_pairs={{8,12},{4,0},{9,13},{5,1},{10,14},{6,2},{11,15},{7,3},{24,28},{20,... | collective-permute-start | bytes 393224 | tf_op jit(solution)/shard_map/ppermute | solution.py:576
  29.2 14.2 %collective-permute-start.3 = (f32[2,128,128]{2,1,0:T(8,128)S(1)}, f32[2,128,128]{2,1,0:T(8,128)S(1)}, u32[]{:S(2)}, u32[]{:S(2)}) collective-permute-start(f32[2,128,128]{2,1,0:T(8,128)S(1)} %get-tuple-element.76), channel_id=1, source_target_pairs={{8,12},{4,0},{9,13},{5,1},{10,14},{6,2},{11,15},{7,3},{24,28},{20,... | collective-permute-start | bytes 393224 | tf_op jit(solution)/shard_map/ppermute | solution.py:576
  30.6 12.2 %collective-permute-start.7 = (f32[4,64]{1,0:T(4,128)S(1)}, f32[4,64]{1,0:T(4,128)S(1)}, u32[]{:S(2)}, u32[]{:S(2)}) collective-permute-start(f32[4,64]{1,0:T(4,128)S(1)} %select_add_fusion), channel_id=1, source_target_pairs={{0,4},{4,0},{8,12},{12,8},{1,5},{5,1},{9,13},{13,9},{2,6},{6,2},{1... | collective-permute-start | bytes 3080 | tf_op jit(solution)/shard_map/ppermute | solution.py:615
  42.7 6.6 %collective-permute-start.8 = (f32[4,64]{1,0:T(4,128)S(1)}, f32[4,64]{1,0:T(4,128)S(1)}, u32[]{:S(2)}, u32[]{:S(2)}) collective-permute-start(f32[4,64]{1,0:T(4,128)S(1)} %add.42), channel_id=1, source_target_pairs={{0,8},{4,12},{8,0},{12,4},{1,9},{5,13},{9,1},{13,5},{2,10},{6,14},... | collective-permute-start | bytes 3080 | tf_op jit(solution)/shard_map/ppermute | solution.py:615

commit v7 on v5

--- a/solution.py
+++ b/solution.py
@@ -44,12 +44,12 @@
     return jnp.sum(jnp.where(kept, column, 0.0), axis=0, keepdims=True)
 
 
-def decay_tables(lengths_ref, ctx_ref, gates_ref, spread, cum_ref, chunk_fac_ref, shard_fac_ref):
+def decay_tables(docs, place_ref, small_ref, spread, cum_ref, chunk_fac_ref, shard_fac_ref):
     rows = cum_ref.shape[0]
     num_chunks = rows // 8
     tokens = num_chunks * CHUNK
     for chunk in range(num_chunks):
-        part = gates_ref[0, :, chunk * CHUNK : (chunk + 1) * CHUNK]
+        part = small_ref[:, chunk * CHUNK : (chunk + 1) * CHUNK]
         spread[chunk * 8 : chunk * 8 + 4, :] = part
         spread[chunk * 8 + 4 : chunk * 8 + 8, :] = part
     gates = spread[...] * LOG2E
@@ -64,56 +64,58 @@
     )
     others = dot_nn((same & outside).astype(F32), totals, PRECISE)
 
-    first = ctx_ref[0] * tokens
+    first = place_ref[0] * tokens
     chunk_first = first + (iota((rows, CHUNK), 0) // 8) * CHUNK
-    positions = chunk_first + iota((rows, CHUNK), 1)
     from_start = iota((rows, CHUNK), 0) % 8 < 4
-    chunk_anchor = jnp.where(from_start, chunk_first - 1, chunk_first + (CHUNK - 1))
+    chunk_anchor = jnp.where(from_start, chunk_first - 1, chunk_first + (CHUNK - 1)).astype(F32)
+    shard_anchor = jnp.where(from_start, first - 1, first + (tokens - 1)).astype(F32)
+    positions = (chunk_first + iota((rows, CHUNK), 1)).astype(F32)
     segment = jnp.zeros((rows, CHUNK), F32)
     chunk_segment = jnp.zeros((rows, CHUNK), F32)
-    shard_before = jnp.float32(0)
-    shard_last = jnp.float32(0)
-    start = jnp.int32(0)
-    for doc in range(lengths_ref.shape[1]):
+    shard_segment = jnp.zeros((rows, CHUNK), F32)
+    begin = small_ref.shape[1] - CHUNK
+    start = jnp.zeros((1, 1), F32)
+    for doc in range(docs):
         segment += jnp.where(positions >= start, 1.0, 0.0)
         chunk_segment += jnp.where(chunk_anchor >= start, 1.0, 0.0)
-        shard_before += jnp.where(first > start, 1.0, 0.0)
-        shard_last += jnp.where(first + (tokens - 1) >= start, 1.0, 0.0)
-        start += lengths_ref[0, doc]
+        shard_segment += jnp.where(shard_anchor >= start, 1.0, 0.0)
+        start = start + small_ref[0:1, begin + doc : begin + doc + 1]
     cum_ref[...] = jnp.where(from_start, prefix, segment)
     exponent = jnp.where(from_start, prefix, suffix)
     chunk_fac_ref[...] = jnp.where(
         segment == chunk_segment, jnp.exp2(jnp.minimum(exponent, 0.0)), 0.0
     )
-    keep = segment == jnp.where(from_start, shard_before, shard_last)
+    keep = segment == shard_segment
     shard_fac_ref[...] = jnp.where(keep, jnp.exp2(jnp.minimum(exponent + others, 0.0)), 0.0)
 
 
-def ends_kernel(head_width, half_ctx, *refs):
-    lengths_ref, ctx_ref, gates_ref = refs[:3]
-    sources, targets = refs[3:7], refs[7:11]
+def ends_kernel(head_width, docs, half_ctx, *refs):
+    place_ref, small_ref = refs[:2]
+    sources = refs[2:6]
     near_refs, far_refs, decay_refs = (
-        refs[11 + i * PARTS : 11 + (i + 1) * PARTS] for i in range(3)
+        refs[6 + i * PARTS : 6 + (i + 1) * PARTS] for i in range(3)
     )
-    cum_ref, chunk_fac_ref, shard_fac_ref, spread, sems = refs[11 + 3 * PARTS :]
-    q_ref, k_ref, v_ref, cot_ref = targets
+    (cum_ref, chunk_fac_ref, shard_fac_ref, gain_ref, flag_ref, q_ref, k_ref, v_ref, cot_ref,
+     spread, sems) = refs[6 + 3 * PARTS :]
     heads = near_refs[0].shape[0]
     rows = shard_fac_ref.shape[0]
     steps = sems.shape[0]
-    block = q_ref.shape[1] // steps
+    tokens = q_ref.shape[1]
+    block = tokens // steps
     chunks = block // CHUNK
 
     def copies(step):
         at = pl.ds(step * block, block)
         return [
             pltpu.make_async_copy(source.at[:, at, :], target.at[:, at, :], sems.at[step, i])
-            for i, (source, target) in enumerate(zip(sources, targets))
+            for i, (source, target) in enumerate(zip(sources, (q_ref, k_ref, v_ref, cot_ref)))
         ]
 
     for step in range(steps):
         for i, copy in enumerate(copies(step)):
             copy.start(priority=i % 2)
-    decay_tables(lengths_ref, ctx_ref, gates_ref, spread, cum_ref, chunk_fac_ref, shard_fac_ref)
+    decay_tables(docs, place_ref, small_ref, spread, cum_ref, chunk_fac_ref, shard_fac_ref)
+    gain_ref[...] = small_ref[:, tokens : tokens + head_width]
     for part in range(PARTS):
         for head in range(heads):
             row = rows - 8 + part * heads + head
@@ -147,7 +149,11 @@
             grad = dot_nn(turned(q_ref, step, row, head_width ** (-0.5)), cot_ref[0, at, lanes])
             ends[row] = ends[row] + end if step else end
             grads[row] = grads[row] + grad if step else grad
-    low = ctx_ref[0] < half_ctx
+    middle = jnp.where(place_ref[0] == half_ctx - 1, 1.0, 0.0)
+    flag_ref[...] = jnp.where(
+        iota(flag_ref.shape, 0) == 0, middle, place_ref[1].astype(F32)
+    )
+    low = place_ref[0] < half_ctx
     for part in range(PARTS):
         for head in range(heads):
             row = part * heads + head
@@ -157,17 +163,20 @@
 
 def local_kernel(
     head_width, part, q_ref, k_ref, v_ref, cot_ref, gain_ref, cum_ref, fac_ref,
-    out_ref, dq_ref, dk_ref, dv_ref, dgate_ref, dgain_ref, leaving, state,
+    target, dgate_ref, dgain_ref, leaving, state,
 ):
+    out_ref, dq_ref, dk_ref, dv_ref = (target.at[pl.ds(i, 1)] for i in range(4))
     heads = state.shape[0]
     num_chunks = leaving.shape[0]
     scale = head_width ** (-0.5)
     unroll = math.gcd(num_chunks, UNROLL)
 
+    groups = num_chunks // unroll
+    def wide_lanes(head):
+        row = part * heads + head
+        return slice(row * head_width, (row + 1) * head_width)
+
     def lanes_of(head):
-        return slice((part * heads + head) * head_width, (part * heads + head + 1) * head_width)
-
-    def own_lanes(head):
         return slice(head * head_width, (head + 1) * head_width)
 
     def rows_of(chunk):
@@ -183,7 +192,7 @@
         added = {}
         for at, head in pairs:
             row = part * heads + head
-            rows, lanes = rows_of(chunks[at]), lanes_of(head)
+            rows, lanes = rows_of(chunks[at]), wide_lanes(head)
             turned = jnp.transpose(q_ref[0, rows, lanes]).astype(F32)
             turned = (turned * (facs[at][row : row + 1, :] * scale)).astype(BF16)
             added[at, head] = dot_nn(turned, cot_ref[0, rows, lanes])
@@ -212,9 +221,10 @@
             at, head = key
             row = part * heads + head
             rows, lanes = rows_of(chunks[at]), lanes_of(head)
-            q[key], v[key], cot[key] = q_ref[0, rows, lanes], v_ref[0, rows, lanes], cot_ref[0, rows, lanes]
+            q[key], cot[key] = q_ref[0, rows, wide_lanes(head)], cot_ref[0, rows, wide_lanes(head)]
+            v[key] = v_ref[0, rows, wide_lanes(head)]
             later[key] = leaving[chunks[at], head]
-            k_raw[key] = k_ref[0, rows, lanes].astype(F32)
+            k_raw[key] = k_ref[0, rows, wide_lanes(head)].astype(F32)
             k_wide = k_raw[key] * gain_ref[row : row + 1, :]
             k[key] = k_wide.astype(BF16)
             from_start[key] = fac_columns[at][:, row : row + 1] * scale
@@ -271,7 +281,7 @@
         for key in pairs:
             at, head = key
             row = part * heads + head
-            rows, own = rows_of(chunks[at]), own_lanes(head)
+            rows, own = rows_of(chunks[at]), lanes_of(head)
             out_ref[0, rows, own] = out[key].astype(BF16)
             dq_ref[0, rows, own] = dq[key].astype(BF16)
             dv_ref[0, rows, own] = dv[key].astype(BF16)
@@ -286,7 +296,7 @@
         backward([num_chunks - 1 - (index * unroll + at) for at in range(unroll)])
         return carry
 
-    lax.fori_loop(0, num_chunks // unroll, backward_group, 0)
+    lax.fori_loop(0, groups, backward_group, 0)
     state[...] = jnp.zeros_like(state)
     dgain_ref[...] = jnp.zeros_like(dgain_ref)
 
@@ -294,13 +304,13 @@
         forward([index * unroll + at for at in range(unroll)])
         return carry
 
-    lax.fori_loop(0, num_chunks // unroll, forward_group, 0)
+    lax.fori_loop(0, groups, forward_group, 0)
 
 
 def merge_kernel(head_width, part, half_ctx, *refs):
-    (ctx_ref, q_ref, k_ref, v_ref, cot_ref, gain_ref, fac_ref, first_ref, second_ref, last_ref,
-     out_in, dq_in, dk_in, dv_in, dgate_in) = refs[:15]
-    refs = refs[15:]
+    q_ref, k_ref, v_ref, cot_ref, partial_ref = refs[:5]
+    place_ref, gain_ref, fac_ref, first_ref, second_ref, last_ref, dgate_in = refs[5:12]
+    refs = refs[12:]
     if part > 0:
         before_ref, refs = refs[0], refs[5:]
     targets, dgate_ref, staged, entering, leaving, sems = refs[:4], *refs[4:]
@@ -311,7 +321,6 @@
     block = chunks * CHUNK
     scale = head_width ** (-0.5)
     group = slice(part * heads * head_width, (part + 1) * heads * head_width)
-    partials = (out_in, dq_in, dk_in, dv_in)
 
     def copies(step):
         at = pl.ds(step * block, block)
@@ -323,7 +332,7 @@
         ]
 
     def arrived(head):
-        low = ctx_ref[0] < half_ctx
+        low = place_ref[0] < half_ctx
         first, second = first_ref[head], second_ref[head] + last_ref[head]
         return jnp.where(low, first, second), jnp.where(low, second, first)
 
@@ -369,8 +378,8 @@
                     )
                 )
                 results[number, head] = [
-                    (partial[0, rows, lanes].astype(F32) + added).astype(BF16)
-                    for partial, added in zip(partials, (across, dq, dk, written))
+                    (partial_ref[i, rows, lanes].astype(F32) + added).astype(BF16)
+                    for i, added in enumerate((across, dq, dk, written))
                 ]
                 kept = written * v_ref[0, rows, wide].astype(F32)
                 balance = jnp.sum(
@@ -417,25 +426,32 @@
     ctx = lax.axis_index("ctx")
     count = lax.axis_size("ctx")
     middle = count // 2 - 1
-    ctx_scalar = jnp.reshape(ctx, (1,)).astype(jnp.int32)
+    docs = lengths.shape[1]
+    sizes = jnp.pad(lengths.astype(F32), ((0, all_heads - 1), (0, CHUNK - docs)))
+    small = jnp.concatenate([gates[0], key_gain, sizes], axis=1)
+    place = jnp.stack([ctx, lax.axis_index("dp")]).astype(jnp.int32)
 
     def shape_of(*shape, dtype=F32):
         return jax.ShapeDtypeStruct(shape, dtype)
 
+    hbm = pl.BlockSpec(memory_space=pltpu.HBM)
     smem = pl.BlockSpec(memory_space=pltpu.SMEM)
     vmem = pl.BlockSpec(memory_space=pltpu.VMEM)
     table = shape_of(rows, CHUNK)
     states = shape_of(heads, head_width, head_width)
     decays = shape_of(heads, 1, head_width)
     part_gates = shape_of(1, heads, tokens)
+    partials = shape_of(4, tokens, part_width, dtype=BF16)
+    streams = (queries, keys_raw, values, cotangent)
     product = 2 * tokens * part_width * head_width
 
     def ends():
-        held = shape_of(1, tokens, width, dtype=BF16)
-        outs = [held] * 4 + [states] * (2 * PARTS) + [decays] * PARTS + [table] * 3
+        outs = [states] * (2 * PARTS) + [decays] * PARTS + [table] * 3
+        outs += [shape_of(all_heads, head_width), shape_of(2, head_width)]
+        outs += [shape_of(1, tokens, width, dtype=BF16)] * 4
         return pl.pallas_call(
-            functools.partial(ends_kernel, head_width, count // 2),
-            in_specs=[smem, smem, vmem] + [pl.BlockSpec(memory_space=pltpu.HBM)] * 4,
+            functools.partial(ends_kernel, head_width, lengths.shape[1], count // 2),
+            in_specs=[smem, vmem] + [hbm] * 4,
             out_specs=[vmem] * len(outs),
             out_shape=outs,
             scratch_shapes=[
@@ -447,15 +463,14 @@
                 flops=2 * product * PARTS, bytes_accessed=8 * tokens * width, transcendentals=0
             ),
             name="shard_ends",
-        )(lengths, ctx_scalar, gates, queries, keys_raw, values, cotangent)
-
-    def local(part, arrays, gain, cum, fac):
-        wide = shape_of(1, tokens, part_width, dtype=BF16)
+        )(place, small, *streams)
+
+    def local(part, gain, cum, fac):
         return pl.pallas_call(
             functools.partial(local_kernel, head_width, part),
             in_specs=[vmem] * 7,
-            out_specs=[vmem] * 6,
-            out_shape=[wide] * 4 + [part_gates, shape_of(heads, head_width)],
+            out_specs=[vmem] * 3,
+            out_shape=[partials, part_gates, shape_of(heads, head_width)],
             scratch_shapes=[
                 pltpu.VMEM((num_chunks, heads, head_width, head_width), BF16),
                 pltpu.VMEM((heads, head_width, head_width), F32),
@@ -465,19 +480,19 @@
                 flops=12 * product, bytes_accessed=16 * tokens * part_width, transcendentals=0
             ),
             name=f"local_{part}",
-        )(*arrays, gain, cum, fac)
-
-    def merge(part, arrivals, locals_, done):
+        )(*held, gain, cum, fac)
+
+    def merge(part, arrivals, local_part, done):
         full_gates = shape_of(1, (part + 1) * heads, tokens)
         extra, extra_specs, aliases = [], [], {}
         if part > 0:
             extra = [done[4]] + list(done[:4])
-            extra_specs = [vmem] + [pl.BlockSpec(memory_space=pl.ANY)] * 4
-            aliases = {16 + i: i for i in range(4)}
+            extra_specs = [vmem] + [hbm] * 4
+            aliases = {13 + i: i for i in range(4)}
         return pl.pallas_call(
             functools.partial(merge_kernel, head_width, part, count // 2),
-            in_specs=[smem] + [vmem] * 14 + extra_specs,
-            out_specs=[pl.BlockSpec(memory_space=pl.ANY)] * 4 + [vmem],
+            in_specs=[vmem] * 5 + [smem] + [vmem] * 6 + extra_specs,
+            out_specs=[hbm] * 4 + [vmem],
             out_shape=[shape_of(1, tokens, width, dtype=BF16)] * 4 + [full_gates],
             scratch_shapes=[
                 pltpu.VMEM((4, tokens, part_width), BF16),
@@ -491,12 +506,14 @@
                 flops=4 * product, bytes_accessed=24 * tokens * part_width, transcendentals=0
             ),
             name=f"merge_{part}",
-        )(ctx_scalar, *streams, key_gain, shard_fac, *arrivals, *locals_, *extra)
+        )(
+            *held, local_part[0], place, gain, shard_fac, *arrivals, local_part[1], *extra
+        )
 
     results = ends()
-    streams, results = results[:4], results[4:]
     near, far, decay = (results[i * PARTS : (i + 1) * PARTS] for i in range(3))
-    cum, chunk_fac, shard_fac = results[3 * PARTS :]
+    cum, chunk_fac, shard_fac, gain, flags = results[3 * PARTS : 3 * PARTS + 5]
+    held = results[3 * PARTS + 5 :]
     sent = [[] for _ in range(PARTS)]
     arrived = [[] for _ in range(PARTS)]
     local_parts = [None] * PARTS
@@ -519,10 +536,10 @@
             local_cum = cum
             if hop > 0:
                 local_cum, _ = lax.optimization_barrier((cum, arrived[0][hop - 1]))
-            local_parts[hop] = list(local(hop, streams, key_gain, local_cum, chunk_fac))
+            local_parts[hop] = list(local(hop, gain, local_cum, chunk_fac))
             if hop + 1 < count - 1:
-                local_parts[hop][5], arrived[0][-1] = lax.optimization_barrier(
-                    (local_parts[hop][5], arrived[0][-1])
+                local_parts[hop][2], arrived[0][-1] = lax.optimization_barrier(
+                    (local_parts[hop][2], arrived[0][-1])
                 )
         if hop + 1 < count - 1:
             for part in range(PARTS):
@@ -531,35 +548,24 @@
     terms = []
     for part in range(PARTS):
         crossed = jnp.sum(sent[part][middle] * arrived[part][middle], axis=2)
-        term = local_parts[part][5] + jnp.where(ctx == middle, crossed, 0.0)
+        term = local_parts[part][2] + flags[0:1] * crossed
         if middle > 0:
             term = term + jnp.sum(sum(arrived[part][:middle]) * far[part], axis=2)
         terms.append(term)
     gain_term = jnp.concatenate(terms, axis=0)
-    half = head_width // lax.axis_size("dp")
-    dp = lax.axis_index("dp")
-    away = jnp.where(dp == 0, gain_term[:, half:], gain_term[:, :half])
-    kept = jnp.where(dp == 0, gain_term[:, :half], gain_term[:, half:])
-    grad_gain = kept + lax.ppermute(away, "dp", [(0, 1), (1, 0)])
-
-    done, reach = None, 1
+    gathered = lax.all_gather(gain_term, ("dp", "ctx"))
+
+    done = None
     for part in range(PARTS):
-        others = jnp.zeros_like(grad_gain)
-        if reach < count:
-            others = lax.ppermute(grad_gain, "ctx", [(i, i ^ reach) for i in range(count)])
-            reach *= 2
         zeros = jnp.zeros(states.shape, F32)
         first = sum(arrived[part][:middle], zeros) if middle != 1 else arrived[part][0]
         second = sum(arrived[part][middle:-1], zeros) if middle != 1 else arrived[part][1]
-        done = list(merge(part, (first, second, arrived[part][-1]), local_parts[part][:5], done))
-        if part < PARTS - 1:
-            done[4], others = lax.optimization_barrier((done[4], others))
-        grad_gain = grad_gain + others
-    while reach < count:
-        grad_gain = grad_gain + lax.ppermute(
-            grad_gain, "ctx", [(i, i ^ reach) for i in range(count)]
-        )
-        reach *= 2
+        done = list(merge(part, (first, second, arrived[part][-1]), local_parts[part], done))
+    gathered, done[4] = lax.optimization_barrier((gathered, done[4]))
+    total = jnp.sum(gathered, axis=0)
+    half = head_width // lax.axis_size("dp")
+    second_half = flags[1:2, :half]
+    grad_gain = (1.0 - second_half) * total[:, :half] + second_half * total[:, half:]
     return (*done, grad_gain)
 
 

time: 49.7 us -> 62.3 us (1.25)
  blocking collectives: 0 us -> 25.4 us
  local copies, waits for them, and re-layouts: 5.55 us -> 0.01 us
  starting transfers between devices: 14.8 us -> 10.2 us
  waiting for transfers between devices: 2.94 us -> 0.02 us
  Pallas kernels: 22.2 us -> 22.9 us
    all_gather x0 -> x1, blocking collectives: none -> 25.4 us  [shards(): gathered = lax.all_gather(gain_term, ('dp', 'ctx'))]
    unnamed x20 -> x0, local copies, waits for them, and re-layouts: 5.55 us -> none
    ppermute x3 -> x0, starting transfers between devices: 4.53 us -> none  [the longest x2 4.51 us: shards(): lax.ppermute(grad_gain, 'ctx', [(i, i ^ reach) for i in range(count)])]
    ppermute x6, waiting for transfers between devices: 2.94 us -> 0.02 us  [send(): lax.ppermute(payload, 'ctx', [(hop, hop + 1), (count - 1 - hop, count - 2...]
    add x2, other arithmetic: 1.85 us -> 0.05 us  [send(): payload = payload + decay[part] * arrived[part][-1]]
    pallas_call x2, Pallas kernels: 8.03 us -> 9.03 us  [merge(): pl.pallas_call(functools.partial(merge_kernel, head_width, part, count //...]
    concatenate x1, other arithmetic: 0.01 us -> 0.74 us  [shards(): small = jnp.concatenate([gates[0], key_gain, sizes], axis=1)]
    convert_element_type x0 -> x1, other arithmetic: none -> 0.66 us  [shards(): lengths.astype(F32)]
  transfers between devices with their start and end apart: 9 -> 6, of which waited for: 1 -> 0; matrix products, arithmetic and copies ran while one was open for 4% -> 1% of each run, Pallas kernels for 35% -> 23%
where the time goes in v7:
time: 62.3 us; the launch traced here: 61.8 us
  blocking collectives  25.4 us (41%)
  Pallas kernels  22.9 us (37%)
  starting transfers between devices  10.2 us (16%)
  other arithmetic  2.54 us (4%)
  between operations  0.8 us (1%)
    all_gather x1, blocking collectives, shards(): gathered = lax.all_gather(gain_term, ('dp', 'ctx'))  25.4 us
    ppermute x6, starting transfers between devices, send(): lax.ppermute(payload, 'ctx', [(hop, hop + 1), (count - 1 - hop, count - 2...  10.2 us
    pallas_call x2, Pallas kernels, local(): pl.pallas_call(functools.partial(local_kernel, head_width, part), in_spec...  9.7 us
    pallas_call x2, Pallas kernels, merge(): pl.pallas_call(functools.partial(merge_kernel, head_width, part, count //...  9.03 us
    pallas_call x1, Pallas kernels, ends(): pl.pallas_call(functools.partial(ends_kernel, head_width, lengths.shape[1...  4.16 us
  transfers between devices with their start and end apart: 6, of which 0 were waited for; matrix products, arithmetic and copies ran while one was open for 1% of the time, Pallas kernels for 23%

profile of v7, /device:TPU:0, one launch (start us, length us, event | category | flops | bytes accessed | tf_op | source)
XLA Modules:
  0.0 61.8 jit_solution(15728547901655587672)
XLA Ops:
  0.6 0.7 %convert_element_type.5 = f32[1,16]{1,0:T(1,128)S(1)} convert(s32[1,16]{1,0:T(1,128)} %param.11) | non-fusion elementwise | flops 16 | bytes 128 | tf_op jit(solution)/shard_map/convert_element_type | solution.py:430
  1.3 0.1 pad_add_fusion.refs_0_.refs_5_
  1.4 0.7 %select_maximum_fusion.refs_1_ = f32[4,1280]{1,0:T(4,128)S(1)} fusion(f32[1,16]{1,0:T(1,128)S(1)} %convert_element_type.5, f32[4,128]{1,0:T(4,128)} %param.12, f32[4,1024]{1,0:T(4,128)} %bitcast.17), kind=kLoop, calls=%fused_computation.8 | loop fusion | flops 20480 | bytes 38976 | tf_op jit(solution)/shard_map/concatenate | solution.py:431
  2.1 4.2 %shard_ends.1 = (f32[2,128,128]{2,1,0:T(8,128)S(1)}, f32[2,128,128]{2,1,0:T(8,128)S(1)}, f32[2,128,128]{2,1,0:T(8,128)S(1)}, f32[2,128,128]{2,1,0:T(8,128)S(1)},...) custom-call(s32[2]{0:T(128)S(1)} %pad_add_fusion.refs_0_.refs_5_, ...), custom_call_target="tpu_custom_call" | custom-call | flops 268435456 | bytes 4194304 | tf_op jit(solution)/shard_map/shard_ends/pallas_call | solution.py:452
  6.3 4.9 %collective-permute-start = (f32[2,128,128]{2,1,0:T(8,128)S(1)}, f32[2,128,128]{2,1,0:T(8,128)S(1)}, u32[]{:S(2)}, u32[]{:S(2)}) collective-permute-start(f32[2,128,128]{2,1,0:T(8,128)S(1)} %get-tuple-element.52), channel_id=1, source_target_pairs={{0,4},{12,8},{1,5},{13,9},{2,6},{14,10},{3,7},{15,11},{16,20},{28,... | collective-permute-start | bytes 393224 | tf_op jit(solution)/shard_map/ppermute | solution.py:527
  11.2 1.3 %collective-permute-start.1 = (f32[2,128,128]{2,1,0:T(8,128)S(1)}, f32[2,128,128]{2,1,0:T(8,128)S(1)}, u32[]{:S(2)}, u32[]{:S(2)}) collective-permute-start(f32[2,128,128]{2,1,0:T(8,128)S(1)} %get-tuple-element.57), channel_id=1, source_target_pairs={{0,4},{12,8},{1,5},{13,9},{2,6},{14,10},{3,7},{15,11},{16,20},{28,... | collective-permute-start | bytes 393224 | tf_op jit(solution)/shard_map/ppermute | solution.py:527
  12.6 4.8 %local_0.1 = (bf16[4,1024,256]{2,1,0:T(8,128)(2,1)S(1)}, f32[1,2,1024]{2,1,0:T(2,128)S(1)}, f32[2,128]{1,0:T(2,128)S(1)}) custom-call(bf16[1,1024,512]{2,1,0:T(8,128)(2,1)S(1)} %get-tuple-element.44.q_ref.refs_0_, bf16[1,1024,512]{2,1,0:T(8,128)(2,1)S(1)} %get-tuple-element.45.k_ref.refs_1_, bf16[1,1024,512]{2,1,0:T(8,128)(2,1)S(1)} %get-tuple-element.46.v_ref.refs_2_, ...), custom_call_target="tpu_custom_call" | custom-call | flops 805306368 | bytes 4194304 | tf_op jit(solution)/shard_map/local_0/pallas_call | solution.py:469
  17.4 0.0 collective-permute-done.refs_8_
  17.4 0.0 collective-permute-done.1.refs_8_
  17.4 0.7 %collective-permute-start.2 = (f32[2,128,128]{2,1,0:T(8,128)S(1)}, f32[2,128,128]{2,1,0:T(8,128)S(1)}, u32[]{:S(2)}, u32[]{:S(2)}) collective-permute-start(f32[2,128,128]{2,1,0:T(8,128)S(1)} %multiply_add_fusion.3), channel_id=1, source_target_pairs={{4,8},{8,4},{5,9},{9,5},{6,10},{10,6},{7,11},{11,7},{20,24},{24,20... | collective-permute-start | bytes 393224 | tf_op jit(solution)/shard_map/ppermute | solution.py:527
  18.1 0.7 %collective-permute-start.4 = (f32[2,128,128]{2,1,0:T(8,128)S(1)}, f32[2,128,128]{2,1,0:T(8,128)S(1)}, u32[]{:S(2)}, u32[]{:S(2)}) collective-permute-start(f32[2,128,128]{2,1,0:T(8,128)S(1)} %multiply_add_fusion.1), channel_id=1, source_target_pairs={{4,8},{8,4},{5,9},{9,5},{6,10},{10,6},{7,11},{11,7},{20,24},{24,20... | collective-permute-start | bytes 393224 | tf_op jit(solution)/shard_map/ppermute | solution.py:527
  18.8 4.9 %local_1.1 = (bf16[4,1024,256]{2,1,0:T(8,128)(2,1)S(1)}, f32[1,2,1024]{2,1,0:T(2,128)S(1)}, f32[2,128]{1,0:T(2,128)S(1)}) custom-call(bf16[1,1024,512]{2,1,0:T(8,128)(2,1)S(1)} %get-tuple-element.44.q_ref.refs_0_, bf16[1,1024,512]{2,1,0:T(8,128)(2,1)S(1)} %get-tuple-element.45.k_ref.refs_1_, bf16[1,1024,512]{2,1,0:T(8,128)(2,1)S(1)} %get-tuple-element.46.v_ref.refs_2_, ...), custom_call_target="tpu_custom_call" | custom-call | flops 805306368 | bytes 4194304 | tf_op jit(solution)/shard_map/local_1/pallas_call | solution.py:469
  23.7 0.0 collective-permute-done.2.refs_9_
  23.7 0.2 multiply_reduce_fusion.1
  23.9 1.3 %collective-permute-start.3 = (f32[2,128,128]{2,1,0:T(8,128)S(1)}, f32[2,128,128]{2,1,0:T(8,128)S(1)}, u32[]{:S(2)}, u32[]{:S(2)}) collective-permute-start(f32[2,128,128]{2,1,0:T(8,128)S(1)} %get-tuple-element.86), channel_id=1, source_target_pairs={{8,12},{4,0},{9,13},{5,1},{10,14},{6,2},{11,15},{7,3},{24,28},{20,... | collective-permute-start | bytes 393224 | tf_op jit(solution)/shard_map/ppermute | solution.py:527
  25.2 0.0 collective-permute-done.4.refs_9_
  25.2 0.2 multiply_reduce_fusion.3
  25.3 1.3 %collective-permute-start.5 = (f32[2,128,128]{2,1,0:T(8,128)S(1)}, f32[2,128,128]{2,1,0:T(8,128)S(1)}, u32[]{:S(2)}, u32[]{:S(2)}) collective-permute-start(f32[2,128,128]{2,1,0:T(8,128)S(1)} %get-tuple-element.83), channel_id=1, source_target_pairs={{8,12},{4,0},{9,13},{5,1},{10,14},{6,2},{11,15},{7,3},{24,28},{20,... | collective-permute-start | bytes 393224 | tf_op jit(solution)/shard_map/ppermute | solution.py:527
  26.7 25.4 %all-gather.1 = f32[8,4,128]{2,1,0:T(4,128)S(1)} all-gather(f32[1,4,128]{2,1,0:T(4,128)S(1)} %maximum_bitcast_fusion), channel_id=2, replica_groups=mesh['dp'=2,'ctx'=4,'head'=4] {'dp','ctx'}, dimensions={0}, use_global_device_ids=true | all-gather | bytes 18432 | tf_op jit(solution)/shard_map/all_gather | solution.py:556
  52.1 0.0 collective-permute-done.5.refs_10_
  52.1 4.2 %merge_0.1 = (bf16[1,1024,512]{2,1,0:T(8,128)(2,1)}, bf16[1,1024,512]{2,1,0:T(8,128)(2,1)}, bf16[1,1024,512]{2,1,0:T(8,128)(2,1)}, bf16[1,1024,512]{2,1,0:T(8,128)(2,1)}, f32[1,2,1024]{2,1,0:T(2,128)S(1)}) custom-call(bf16[1,1024,512]{2,1,0:T(8,128)(2,1)S(1)} %get-tuple-element.44.q_ref.refs_0_, bf16[1,1024,512]{2,1,0:T(8,128)(2,1)S(1)} %get-tuple-element.45.k_ref.refs_1_, ...), custom_call_target="tpu_custom_call" | custom-call | flops 268435456 | bytes 6291456 | tf_op jit(solution)/shard_map/merge_0/pallas_call | solution.py:492
  56.3 0.0 collective-permute-done.3.refs_10_
  56.3 4.8 %merge_1.1 = (bf16[1,1024,512]{2,1,0:T(8,128)(2,1)}, bf16[1,1024,512]{2,1,0:T(8,128)(2,1)}, bf16[1,1024,512]{2,1,0:T(8,128)(2,1)}, bf16[1,1024,512]{2,1,0:T(8,128)(2,1)}, f32[1,4,1024]{2,1,0:T(4,128)}) custom-call(bf16[1,1024,512]{2,1,0:T(8,128)(2,1)S(1)} %get-tuple-element.44.q_ref.refs_, ...), custom_call_target="tpu_custom_call", output_to_operand_aliasing={{0}: (13, {}), {1}: (14, {}), {2}: (15, {}), {3}: (16, {})} | custom-call | flops 268435456 | bytes 6291456 | tf_op jit(solution)/shard_map/merge_1/pallas_call | solution.py:492
  61.1 0.7 %multiply_add_fusion.4 = f32[4,64]{1,0:T(4,128)} fusion(f32[4,128]{1,0:T(4,128)S(1)} %reduce_sum.49, f32[64]{0:T(128)S(1)} %get-tuple-element.89, f32[64]{0:T(128)S(1)} %get-tuple-element.88), kind=kLoop, calls=%fused_computation.11 | loop fusion | flops 768 | bytes 3584 | tf_op jit(solution)/shard_map/add | solution.py:568
  (7 shorter events, 0.1 us)
Async XLA Ops:
  6.3 11.1 %collective-permute-start = (f32[2,128,128]{2,1,0:T(8,128)S(1)}, f32[2,128,128]{2,1,0:T(8,128)S(1)}, u32[]{:S(2)}, u32[]{:S(2)}) collective-permute-start(f32[2,128,128]{2,1,0:T(8,128)S(1)} %get-tuple-element.52), channel_id=1, source_target_pairs={{0,4},{12,8},{1,5},{13,9},{2,6},{14,10},{3,7},{15,11},{16,20},{28,... | collective-permute-start | bytes 393224 | tf_op jit(solution)/shard_map/ppermute | solution.py:527
  11.2 6.2 %collective-permute-start.1 = (f32[2,128,128]{2,1,0:T(8,128)S(1)}, f32[2,128,128]{2,1,0:T(8,128)S(1)}, u32[]{:S(2)}, u32[]{:S(2)}) collective-permute-start(f32[2,128,128]{2,1,0:T(8,128)S(1)} %get-tuple-element.57), channel_id=1, source_target_pairs={{0,4},{12,8},{1,5},{13,9},{2,6},{14,10},{3,7},{15,11},{16,20},{28,... | collective-permute-start | bytes 393224 | tf_op jit(solution)/shard_map/ppermute | solution.py:527
  17.4 6.3 %collective-permute-start.2 = (f32[2,128,128]{2,1,0:T(8,128)S(1)}, f32[2,128,128]{2,1,0:T(8,128)S(1)}, u32[]{:S(2)}, u32[]{:S(2)}) collective-permute-start(f32[2,128,128]{2,1,0:T(8,128)S(1)} %multiply_add_fusion.3), channel_id=1, source_target_pairs={{4,8},{8,4},{5,9},{9,5},{6,10},{10,6},{7,11},{11,7},{20,24},{24,20... | collective-permute-start | bytes 393224 | tf_op jit(solution)/shard_map/ppermute | solution.py:527
  18.1 7.0 %collective-permute-start.4 = (f32[2,128,128]{2,1,0:T(8,128)S(1)}, f32[2,128,128]{2,1,0:T(8,128)S(1)}, u32[]{:S(2)}, u32[]{:S(2)}) collective-permute-start(f32[2,128,128]{2,1,0:T(8,128)S(1)} %multiply_add_fusion.1), channel_id=1, source_target_pairs={{4,8},{8,4},{5,9},{9,5},{6,10},{10,6},{7,11},{11,7},{20,24},{24,20... | collective-permute-start | bytes 393224 | tf_op jit(solution)/shard_map/ppermute | solution.py:527
  23.9 32.4 %collective-permute-start.3 = (f32[2,128,128]{2,1,0:T(8,128)S(1)}, f32[2,128,128]{2,1,0:T(8,128)S(1)}, u32[]{:S(2)}, u32[]{:S(2)}) collective-permute-start(f32[2,128,128]{2,1,0:T(8,128)S(1)} %get-tuple-element.86), channel_id=1, source_target_pairs={{8,12},{4,0},{9,13},{5,1},{10,14},{6,2},{11,15},{7,3},{24,28},{20,... | collective-permute-start | bytes 393224 | tf_op jit(solution)/shard_map/ppermute | solution.py:527
  25.3 26.7 %collective-permute-start.5 = (f32[2,128,128]{2,1,0:T(8,128)S(1)}, f32[2,128,128]{2,1,0:T(8,128)S(1)}, u32[]{:S(2)}, u32[]{:S(2)}) collective-permute-start(f32[2,128,128]{2,1,0:T(8,128)S(1)} %get-tuple-element.83), channel_id=1, source_target_pairs={{8,12},{4,0},{9,13},{5,1},{10,14},{6,2},{11,15},{7,3},{24,28},{20,... | collective-permute-start | bytes 393224 | tf_op jit(solution)/shard_map/ppermute | solution.py:527

commit v8 on v7

--- a/solution.py
+++ b/solution.py
@@ -44,7 +44,7 @@
     return jnp.sum(jnp.where(kept, column, 0.0), axis=0, keepdims=True)
 
 
-def decay_tables(docs, place_ref, small_ref, spread, cum_ref, chunk_fac_ref, shard_fac_ref):
+def decay_tables(docs, ctx, small_ref, spread, cum_ref, chunk_fac_ref, shard_fac_ref):
     rows = cum_ref.shape[0]
     num_chunks = rows // 8
     tokens = num_chunks * CHUNK
@@ -64,7 +64,7 @@
     )
     others = dot_nn((same & outside).astype(F32), totals, PRECISE)
 
-    first = place_ref[0] * tokens
+    first = ctx * tokens
     chunk_first = first + (iota((rows, CHUNK), 0) // 8) * CHUNK
     from_start = iota((rows, CHUNK), 0) % 8 < 4
     chunk_anchor = jnp.where(from_start, chunk_first - 1, chunk_first + (CHUNK - 1)).astype(F32)
@@ -90,13 +90,13 @@
 
 
 def ends_kernel(head_width, docs, half_ctx, *refs):
-    place_ref, small_ref = refs[:2]
-    sources = refs[2:6]
+    small_ref, sources = refs[0], refs[1:5]
+    ctx, dp = lax.axis_index("ctx"), lax.axis_index("dp")
     near_refs, far_refs, decay_refs = (
-        refs[6 + i * PARTS : 6 + (i + 1) * PARTS] for i in range(3)
+        refs[5 + i * PARTS : 5 + (i + 1) * PARTS] for i in range(3)
     )
     (cum_ref, chunk_fac_ref, shard_fac_ref, gain_ref, flag_ref, q_ref, k_ref, v_ref, cot_ref,
-     spread, sems) = refs[6 + 3 * PARTS :]
+     spread, sems) = refs[5 + 3 * PARTS :]
     heads = near_refs[0].shape[0]
     rows = shard_fac_ref.shape[0]
     steps = sems.shape[0]
@@ -114,7 +114,7 @@
     for step in range(steps):
         for i, copy in enumerate(copies(step)):
             copy.start(priority=i % 2)
-    decay_tables(docs, place_ref, small_ref, spread, cum_ref, chunk_fac_ref, shard_fac_ref)
+    decay_tables(docs, ctx, small_ref, spread, cum_ref, chunk_fac_ref, shard_fac_ref)
     gain_ref[...] = small_ref[:, tokens : tokens + head_width]
     for part in range(PARTS):
         for head in range(heads):
@@ -149,11 +149,12 @@
             grad = dot_nn(turned(q_ref, step, row, head_width ** (-0.5)), cot_ref[0, at, lanes])
             ends[row] = ends[row] + end if step else end
             grads[row] = grads[row] + grad if step else grad
-    middle = jnp.where(place_ref[0] == half_ctx - 1, 1.0, 0.0)
+    middle = jnp.where(ctx == half_ctx - 1, 1.0, 0.0)
+    low = ctx < half_ctx
+    row = iota(flag_ref.shape, 0)
     flag_ref[...] = jnp.where(
-        iota(flag_ref.shape, 0) == 0, middle, place_ref[1].astype(F32)
-    )
-    low = place_ref[0] < half_ctx
+        row == 0, middle, jnp.where(row == 1, dp.astype(F32), jnp.where(low, 1.0, 0.0))
+    )
     for part in range(PARTS):
         for head in range(heads):
             row = part * heads + head
@@ -307,49 +308,46 @@
     lax.fori_loop(0, groups, forward_group, 0)
 
 
-def merge_kernel(head_width, part, half_ctx, *refs):
-    q_ref, k_ref, v_ref, cot_ref, partial_ref = refs[:5]
-    place_ref, gain_ref, fac_ref, first_ref, second_ref, last_ref, dgate_in = refs[5:12]
-    refs = refs[12:]
-    if part > 0:
-        before_ref, refs = refs[0], refs[5:]
+def merge_kernel(head_width, *refs):
+    q_ref, k_ref, v_ref, cot_ref, gain_ref, flag_ref, fac_ref = refs[:7]
+    partial_refs, gate_refs, first_refs, second_refs, last_refs = (
+        refs[7 + i * PARTS : 7 + (i + 1) * PARTS] for i in range(5)
+    )
+    refs = refs[7 + 5 * PARTS :]
     targets, dgate_ref, staged, entering, leaving, sems = refs[:4], *refs[4:]
-    heads = first_ref.shape[0]
+    heads = first_refs[0].shape[0]
     steps = sems.shape[0]
     num_chunks = fac_ref.shape[0] // 8
     chunks = num_chunks // steps
     block = chunks * CHUNK
+    group_width = heads * head_width
     scale = head_width ** (-0.5)
-    group = slice(part * heads * head_width, (part + 1) * heads * head_width)
 
     def copies(step):
         at = pl.ds(step * block, block)
         return [
-            pltpu.make_async_copy(
-                staged.at[i, at, :], target.at[0, at, group], sems.at[step, i]
-            )
+            pltpu.make_async_copy(staged.at[i, at, :], target.at[0, at, :], sems.at[step, i])
             for i, target in enumerate(targets)
         ]
-
-    def arrived(head):
-        low = place_ref[0] < half_ctx
-        first, second = first_ref[head], second_ref[head] + last_ref[head]
-        return jnp.where(low, first, second), jnp.where(low, second, first)
 
     gain_columns = jnp.transpose(jnp.concatenate([gain_ref[...], gain_ref[...]], axis=0))
     entering[...] = jnp.zeros_like(entering)
     leaving[...] = jnp.zeros_like(leaving)
-    last = fac_ref[(num_chunks - 1) * 8 : num_chunks * 8, CHUNK - 1 : CHUNK]
+    last_factors = fac_ref[(num_chunks - 1) * 8 : num_chunks * 8, CHUNK - 1 : CHUNK]
+    low = jnp.broadcast_to(flag_ref[2:3, :], (head_width, head_width)) > 0.5
     constants = []
-    for head in range(heads):
-        row = part * heads + head
-        own = slice(head * head_width, (head + 1) * head_width)
-        gain = gain_columns[:, row : row + 1]
-        state, later = arrived(head)
-        state = state * gain
-        entering[own, own] = (state * scale).astype(BF16)
-        leaving[own, own] = (later * gain).astype(BF16)
-        constants.append(total_of(state * later) * last[row : row + 1])
+    for part in range(PARTS):
+        for head in range(heads):
+            row = part * heads + head
+            own = slice(head * head_width, (head + 1) * head_width)
+            gain = gain_columns[:, row : row + 1]
+            first = first_refs[part][head]
+            second = second_refs[part][head] + last_refs[part][head]
+            state = jnp.where(low, first, second) * gain
+            later = jnp.where(low, second, first)
+            entering[part, own, own] = (state * scale).astype(BF16)
+            leaving[part, own, own] = (later * gain).astype(BF16)
+            constants.append(total_of(state * later) * last_factors[row : row + 1])
 
     gate_sums, kept_sums = {}, {}
     for step in range(steps):
@@ -357,61 +355,67 @@
         products, results = {}, {}
         for number in numbers:
             rows = slice(number * CHUNK, (number + 1) * CHUNK)
-            products[number] = (
-                dot_nn(q_ref[0, rows, group], entering[...]),
-                dot_nt(cot_ref[0, rows, group], entering[...]),
-                dot_nt(v_ref[0, rows, group], leaving[...]),
-                dot_nn(k_ref[0, rows, group], leaving[...]),
-            )
+            for part in range(PARTS):
+                group = slice(part * group_width, (part + 1) * group_width)
+                products[number, part] = (
+                    dot_nn(q_ref[0, rows, group], entering[part]),
+                    dot_nt(cot_ref[0, rows, group], entering[part]),
+                    dot_nt(v_ref[0, rows, group], leaving[part]),
+                    dot_nn(k_ref[0, rows, group], leaving[part]),
+                )
         for number in numbers:
             columns = jnp.transpose(fac_ref[number * 8 : number * 8 + 8, :])
             rows = slice(number * CHUNK, (number + 1) * CHUNK)
-            for head in range(heads):
-                row = part * heads + head
+            for row in range(PARTS * heads):
+                part, head = divmod(row, heads)
                 lanes = slice(head * head_width, (head + 1) * head_width)
                 wide = slice(row * head_width, (row + 1) * head_width)
                 from_start, to_end = columns[:, row : row + 1], columns[:, 4 + row : 5 + row]
                 across, dq, dk, written = (
                     product[:, lanes] * factor
                     for product, factor in zip(
-                        products[number], (from_start, from_start, to_end, to_end)
+                        products[number, part], (from_start, from_start, to_end, to_end)
                     )
                 )
-                results[number, head] = [
-                    (partial_ref[i, rows, lanes].astype(F32) + added).astype(BF16)
+                results[number, row] = [
+                    (partial_refs[part][i, rows, lanes].astype(F32) + added).astype(BF16)
                     for i, added in enumerate((across, dq, dk, written))
                 ]
                 kept = written * v_ref[0, rows, wide].astype(F32)
                 balance = jnp.sum(
                     across * cot_ref[0, rows, wide].astype(F32) - kept, axis=1, keepdims=True
                 )
-                gate_sums[number, head] = later_sums(balance)
-                kept_sums[number, head] = jnp.sum(kept, axis=0, keepdims=True)
+                gate_sums[number, row] = later_sums(balance)
+                kept_sums[number, row] = jnp.sum(kept, axis=0, keepdims=True)
         for number in numbers:
             rows = slice(number * CHUNK, (number + 1) * CHUNK)
-            for head in range(heads):
-                lanes = slice(head * head_width, (head + 1) * head_width)
+            for row in range(PARTS * heads):
+                wide = slice(row * head_width, (row + 1) * head_width)
                 for i in range(4):
-                    staged[i, rows, lanes] = results[number, head][i]
+                    staged[i, rows, wide] = results[number, row][i]
         for i, copy in enumerate(copies(step)):
             copy.start(priority=i % 2)
 
-    if part > 0:
-        dgate_ref[0, : part * heads, :] = before_ref[0]
-    for head in range(heads):
-        row = part * heads + head
-        kept = sum(kept_sums[number, head] for number in range(num_chunks))
-        base = jnp.sum(kept, axis=1, keepdims=True) + constants[head]
+    for row in range(PARTS * heads):
+        part, head = divmod(row, heads)
+        kept = sum(kept_sums[number, row] for number in range(num_chunks))
+        base = jnp.sum(kept, axis=1, keepdims=True) + constants[row]
         for number in range(num_chunks - 1, -1, -1):
             lanes = slice(number * CHUNK, (number + 1) * CHUNK)
-            sums = gate_sums[number, head]
+            sums = gate_sums[number, row]
             dgate_ref[0, row : row + 1, lanes] = (
-                dgate_in[0, head : head + 1, lanes] + sums + base
+                gate_refs[part][0, head : head + 1, lanes] + sums + base
             )
             base = base + sums[:, 0:1]
     for step in range(steps):
         for copy in copies(step):
             copy.wait()
+
+
+def summed(own, others):
+    if len(others) == 1:
+        return own + others[0]
+    return (own + others[0]) + (others[1] + others[2])
 
 
 def shards(queries, keys_raw, values, gates, lengths, key_gain, cotangent):
@@ -423,19 +427,16 @@
     rows = num_chunks * 8
     block = min(256, tokens)
     steps = tokens // block
-    ctx = lax.axis_index("ctx")
     count = lax.axis_size("ctx")
     middle = count // 2 - 1
     docs = lengths.shape[1]
-    sizes = jnp.pad(lengths.astype(F32), ((0, all_heads - 1), (0, CHUNK - docs)))
+    sizes = jnp.pad(lengths, ((0, all_heads - 1), (0, CHUNK - docs))).astype(F32)
     small = jnp.concatenate([gates[0], key_gain, sizes], axis=1)
-    place = jnp.stack([ctx, lax.axis_index("dp")]).astype(jnp.int32)
 
     def shape_of(*shape, dtype=F32):
         return jax.ShapeDtypeStruct(shape, dtype)
 
     hbm = pl.BlockSpec(memory_space=pltpu.HBM)
-    smem = pl.BlockSpec(memory_space=pltpu.SMEM)
     vmem = pl.BlockSpec(memory_space=pltpu.VMEM)
     table = shape_of(rows, CHUNK)
     states = shape_of(heads, head_width, head_width)
@@ -447,11 +448,11 @@
 
     def ends():
         outs = [states] * (2 * PARTS) + [decays] * PARTS + [table] * 3
-        outs += [shape_of(all_heads, head_width), shape_of(2, head_width)]
+        outs += [shape_of(all_heads, head_width), shape_of(4, head_width)]
         outs += [shape_of(1, tokens, width, dtype=BF16)] * 4
         return pl.pallas_call(
             functools.partial(ends_kernel, head_width, lengths.shape[1], count // 2),
-            in_specs=[smem, vmem] + [hbm] * 4,
+            in_specs=[vmem] + [hbm] * 4,
             out_specs=[vmem] * len(outs),
             out_shape=outs,
             scratch_shapes=[
@@ -463,7 +464,7 @@
                 flops=2 * product * PARTS, bytes_accessed=8 * tokens * width, transcendentals=0
             ),
             name="shard_ends",
-        )(place, small, *streams)
+        )(small, *streams)
 
     def local(part, gain, cum, fac):
         return pl.pallas_call(
@@ -482,33 +483,24 @@
             name=f"local_{part}",
         )(*held, gain, cum, fac)
 
-    def merge(part, arrivals, local_part, done):
-        full_gates = shape_of(1, (part + 1) * heads, tokens)
-        extra, extra_specs, aliases = [], [], {}
-        if part > 0:
-            extra = [done[4]] + list(done[:4])
-            extra_specs = [vmem] + [hbm] * 4
-            aliases = {13 + i: i for i in range(4)}
+    def merge(*arrays):
         return pl.pallas_call(
-            functools.partial(merge_kernel, head_width, part, count // 2),
-            in_specs=[vmem] * 5 + [smem] + [vmem] * 6 + extra_specs,
+            functools.partial(merge_kernel, head_width),
+            in_specs=[vmem] * len(arrays),
             out_specs=[hbm] * 4 + [vmem],
-            out_shape=[shape_of(1, tokens, width, dtype=BF16)] * 4 + [full_gates],
+            out_shape=[shape_of(1, tokens, width, dtype=BF16)] * 4 + [shape_of(*gates.shape)],
             scratch_shapes=[
-                pltpu.VMEM((4, tokens, part_width), BF16),
-                pltpu.VMEM((part_width, part_width), BF16),
-                pltpu.VMEM((part_width, part_width), BF16),
+                pltpu.VMEM((4, tokens, width), BF16),
+                pltpu.VMEM((PARTS, part_width, part_width), BF16),
+                pltpu.VMEM((PARTS, part_width, part_width), BF16),
                 pltpu.SemaphoreType.DMA((steps, 4)),
             ],
-            input_output_aliases=aliases,
             compiler_params=pltpu.CompilerParams(vmem_limit_bytes=24 << 20),
             cost_estimate=pl.CostEstimate(
-                flops=4 * product, bytes_accessed=24 * tokens * part_width, transcendentals=0
+                flops=4 * product * PARTS, bytes_accessed=24 * tokens * width, transcendentals=0
             ),
-            name=f"merge_{part}",
-        )(
-            *held, local_part[0], place, gain, shard_fac, *arrivals, local_part[1], *extra
-        )
+            name="merge",
+        )(*arrays)
 
     results = ends()
     near, far, decay = (results[i * PARTS : (i + 1) * PARTS] for i in range(3))
@@ -553,20 +545,41 @@
             term = term + jnp.sum(sum(arrived[part][:middle]) * far[part], axis=2)
         terms.append(term)
     gain_term = jnp.concatenate(terms, axis=0)
-    gathered = lax.all_gather(gain_term, ("dp", "ctx"))
-
-    done = None
-    for part in range(PARTS):
-        zeros = jnp.zeros(states.shape, F32)
-        first = sum(arrived[part][:middle], zeros) if middle != 1 else arrived[part][0]
-        second = sum(arrived[part][middle:-1], zeros) if middle != 1 else arrived[part][1]
-        done = list(merge(part, (first, second, arrived[part][-1]), local_parts[part], done))
-    gathered, done[4] = lax.optimization_barrier((gathered, done[4]))
-    total = jnp.sum(gathered, axis=0)
     half = head_width // lax.axis_size("dp")
     second_half = flags[1:2, :half]
-    grad_gain = (1.0 - second_half) * total[:, :half] + second_half * total[:, half:]
-    return (*done, grad_gain)
+    lower_half, upper_half = gain_term[:, :half], gain_term[:, half:]
+    away = (1.0 - second_half) * upper_half + second_half * lower_half
+    kept = (1.0 - second_half) * lower_half + second_half * upper_half
+    grad_gain = kept + lax.ppermute(away, "dp", [(0, 1), (1, 0)])
+
+    def exchanged(array, reach):
+        return lax.ppermute(array, "ctx", [(i, i ^ reach) for i in range(count)])
+
+    pending, reach = [], 1
+    while reach < count:
+        if pending:
+            grad_gain = summed(grad_gain, pending)
+        pending = [exchanged(grad_gain, reach)]
+        if reach * 2 < count:
+            pending += [exchanged(grad_gain, reach * 2), exchanged(grad_gain, reach * 3)]
+        reach *= 2 * min(len(pending), 2)
+
+    zeros = jnp.zeros(states.shape, F32)
+    if middle == 1:
+        firsts, seconds = ([own[i] for own in arrived] for i in range(2))
+    else:
+        firsts = [sum(own[:middle], zeros) for own in arrived]
+        seconds = [sum(own[middle:-1], zeros) for own in arrived]
+    done = list(
+        merge(
+            *held, gain, flags, shard_fac,
+            *[local_part[0] for local_part in local_parts],
+            *[local_part[1] for local_part in local_parts],
+            *firsts, *seconds, *[own[-1] for own in arrived],
+        )
+    )
+    pending, done[4] = lax.optimization_barrier((pending, done[4]))
+    return (*done, summed(grad_gain, pending))
 
 
 def solution(mesh):

time: 62.3 us -> 44.3 us (0.71)
  blocking collectives: 25.4 us -> 0 us
  starting transfers between devices: 10.2 us -> 17.4 us
  waiting for transfers between devices: 0.02 us -> 3.13 us
  Pallas kernels: 22.9 us -> 20 us
    all_gather x1 -> x0, blocking collectives: 25.4 us -> none  [shards(): gathered = lax.all_gather(gain_term, ('dp', 'ctx'))]
    ppermute x0 -> x4, starting transfers between devices: none -> 7.21 us  [the longest x3 7.2 us: exchanged(): return lax.ppermute(array, 'ctx', [(i, i ^ reach) for i in range(count)])]
    ppermute x6, waiting for transfers between devices: 0.02 us -> 3.12 us  [send(): lax.ppermute(payload, 'ctx', [(hop, hop + 1), (count - 1 - hop, count - 2...]
    pallas_call x2 -> x1, Pallas kernels: 9.03 us -> 6.7 us  [merge(): pl.pallas_call(functools.partial(merge_kernel, head_width), in_specs=[vme...]
  transfers between devices with their start and end apart: 6 -> 10, of which waited for: 0 -> 2; matrix products, arithmetic and copies ran while one was open for 1% -> 1% of each run, Pallas kernels for 23% -> 37%
where the time goes in v8:
time: 44.3 us; the launch traced here: 43.9 us
  Pallas kernels  20 us (45%)
  starting transfers between devices  17.4 us (39%)
  waiting for transfers between devices  3.13 us (7%)
  other arithmetic  2.53 us (6%)
  between operations  0.82 us (2%)
    ppermute x6, starting transfers between devices, send(): lax.ppermute(payload, 'ctx', [(hop, hop + 1), (count - 1 - hop, count - 2...  10.2 us
    pallas_call x2, Pallas kernels, local(): pl.pallas_call(functools.partial(local_kernel, head_width, part), in_spec...  9.69 us
    ppermute x3, starting transfers between devices, exchanged(): return lax.ppermute(array, 'ctx', [(i, i ^ reach) for i in range(count)])  7.2 us
    pallas_call x1, Pallas kernels, merge(): pl.pallas_call(functools.partial(merge_kernel, head_width), in_specs=[vme...  6.7 us
    pallas_call x1, Pallas kernels, ends(): pl.pallas_call(functools.partial(ends_kernel, head_width, lengths.shape[1...  3.64 us
    ppermute x6, waiting for transfers between devices, send(): lax.ppermute(payload, 'ctx', [(hop, hop + 1), (count - 1 - hop, count - 2...  3.12 us
  transfers between devices with their start and end apart: 10, of which 2 were waited for; matrix products, arithmetic and copies ran while one was open for 1% of the time, Pallas kernels for 37%

profile of v8, /device:TPU:0, one launch (start us, length us, event | category | flops | bytes accessed | tf_op | source)
XLA Modules:
  0.0 43.9 jit_solution(11111995384646952530)
XLA Ops:
  0.6 0.7 %pad_convert_fusion = f32[4,128]{1,0:T(4,128)S(1)} fusion(s32[1,16]{1,0:T(1,128)} %param.11), kind=kLoop, calls=%fused_computation.13 | loop fusion | flops 512 | bytes 2112 | tf_op jit(solution)/shard_map/convert_element_type | solution.py:433
  1.3 0.7 %pad_maximum_fusion.refs_0_ = f32[4,1280]{1,0:T(4,128)S(1)} fusion(f32[4,128]{1,0:T(4,128)S(1)} %pad_convert_fusion, f32[4,128]{1,0:T(4,128)} %param.12, f32[4,1024]{1,0:T(4,128)} %bitcast.13), kind=kLoop, calls=%fused_computation.8 | loop fusion | flops 10240 | bytes 40960 | tf_op jit(solution)/shard_map/concatenate | solution.py:434
  2.0 3.6 %shard_ends.1 = (f32[2,128,128]{2,1,0:T(8,128)S(1)}, f32[2,128,128]{2,1,0:T(8,128)S(1)}, f32[2,128,128]{2,1,0:T(8,128)S(1)}, f32[2,128,128]{2,1,0:T(8,128)S(1)},...) custom-call(f32[4,1280]{1,0:T(4,128)S(1)} %pad_maximum_fusion.refs_0, ...), custom_call_target="tpu_custom_call" | custom-call | flops 268435456 | bytes 4194304 | tf_op jit(solution)/shard_map/shard_ends/pallas_call | solution.py:453
  5.7 4.9 %collective-permute-start = (f32[2,128,128]{2,1,0:T(8,128)S(1)}, f32[2,128,128]{2,1,0:T(8,128)S(1)}, u32[]{:S(2)}, u32[]{:S(2)}) collective-permute-start(f32[2,128,128]{2,1,0:T(8,128)S(1)} %get-tuple-element.52), channel_id=1, source_target_pairs={{0,4},{12,8},{1,5},{13,9},{2,6},{14,10},{3,7},{15,11},{16,20},{28,... | collective-permute-start | bytes 393224 | tf_op jit(solution)/shard_map/ppermute | solution.py:519
  10.6 1.3 %collective-permute-start.1 = (f32[2,128,128]{2,1,0:T(8,128)S(1)}, f32[2,128,128]{2,1,0:T(8,128)S(1)}, u32[]{:S(2)}, u32[]{:S(2)}) collective-permute-start(f32[2,128,128]{2,1,0:T(8,128)S(1)} %get-tuple-element.58), channel_id=1, source_target_pairs={{0,4},{12,8},{1,5},{13,9},{2,6},{14,10},{3,7},{15,11},{16,20},{28,... | collective-permute-start | bytes 393224 | tf_op jit(solution)/shard_map/ppermute | solution.py:519
  12.0 4.8 %local_0.1 = (bf16[4,1024,256]{2,1,0:T(8,128)(2,1)S(1)}, f32[1,2,1024]{2,1,0:T(2,128)S(1)}, f32[2,128]{1,0:T(2,128)S(1)}) custom-call(bf16[1,1024,512]{2,1,0:T(8,128)(2,1)S(1)} %get-tuple-element.41.q_ref.refs_0_, bf16[1,1024,512]{2,1,0:T(8,128)(2,1)S(1)} %get-tuple-element.42.k_ref.refs_1_, bf16[1,1024,512]{2,1,0:T(8,128)(2,1)S(1)} %get-tuple-element.43.v_ref.refs_2_, ...), custom_call_target="tpu_custom_call" | custom-call | flops 805306368 | bytes 4194304 | tf_op jit(solution)/shard_map/local_0/pallas_call | solution.py:470
  16.8 0.7 %collective-permute-start.2 = (f32[2,128,128]{2,1,0:T(8,128)S(1)}, f32[2,128,128]{2,1,0:T(8,128)S(1)}, u32[]{:S(2)}, u32[]{:S(2)}) collective-permute-start(f32[2,128,128]{2,1,0:T(8,128)S(1)} %multiply_add_fusion.3), channel_id=1, source_target_pairs={{4,8},{8,4},{5,9},{9,5},{6,10},{10,6},{7,11},{11,7},{20,24},{24,20... | collective-permute-start | bytes 393224 | tf_op jit(solution)/shard_map/ppermute | solution.py:519
  17.5 0.0 collective-permute-done.1.refs_12_
  17.5 0.7 %collective-permute-start.3 = (f32[2,128,128]{2,1,0:T(8,128)S(1)}, f32[2,128,128]{2,1,0:T(8,128)S(1)}, u32[]{:S(2)}, u32[]{:S(2)}) collective-permute-start(f32[2,128,128]{2,1,0:T(8,128)S(1)} %multiply_add_fusion.2), channel_id=1, source_target_pairs={{4,8},{8,4},{5,9},{9,5},{6,10},{10,6},{7,11},{11,7},{20,24},{24,20... | collective-permute-start | bytes 393224 | tf_op jit(solution)/shard_map/ppermute | solution.py:519
  18.2 4.9 %local_1.1 = (bf16[4,1024,256]{2,1,0:T(8,128)(2,1)S(1)}, f32[1,2,1024]{2,1,0:T(2,128)S(1)}, f32[2,128]{1,0:T(2,128)S(1)}) custom-call(bf16[1,1024,512]{2,1,0:T(8,128)(2,1)S(1)} %get-tuple-element.41.q_ref.refs_0_, bf16[1,1024,512]{2,1,0:T(8,128)(2,1)S(1)} %get-tuple-element.42.k_ref.refs_1_, bf16[1,1024,512]{2,1,0:T(8,128)(2,1)S(1)} %get-tuple-element.43.v_ref.refs_2_, ...), custom_call_target="tpu_custom_call" | custom-call | flops 805306368 | bytes 4194304 | tf_op jit(solution)/shard_map/local_1/pallas_call | solution.py:470
  23.1 0.2 multiply_reduce_fusion.3
  23.3 0.2 multiply_reduce_fusion.1
  23.5 0.1 multiply_add_fusion.4
  23.5 0.0 collective-permute-start.6
  23.6 1.3 %collective-permute-start.4 = (f32[2,128,128]{2,1,0:T(8,128)S(1)}, f32[2,128,128]{2,1,0:T(8,128)S(1)}, u32[]{:S(2)}, u32[]{:S(2)}) collective-permute-start(f32[2,128,128]{2,1,0:T(8,128)S(1)} %get-tuple-element.77), channel_id=1, source_target_pairs={{8,12},{4,0},{9,13},{5,1},{10,14},{6,2},{11,15},{7,3},{24,28},{20,... | collective-permute-start | bytes 393224 | tf_op jit(solution)/shard_map/ppermute | solution.py:519
  24.9 1.3 %collective-permute-start.5 = (f32[2,128,128]{2,1,0:T(8,128)S(1)}, f32[2,128,128]{2,1,0:T(8,128)S(1)}, u32[]{:S(2)}, u32[]{:S(2)}) collective-permute-start(f32[2,128,128]{2,1,0:T(8,128)S(1)} %get-tuple-element.80), channel_id=1, source_target_pairs={{8,12},{4,0},{9,13},{5,1},{10,14},{6,2},{11,15},{7,3},{24,28},{20,... | collective-permute-start | bytes 393224 | tf_op jit(solution)/shard_map/ppermute | solution.py:519
  26.2 0.1 add_add_fusion.1
  26.2 4.7 %collective-permute-start.7 = (f32[4,64]{1,0:T(4,128)S(1)}, f32[4,64]{1,0:T(4,128)S(1)}, u32[]{:S(2)}, u32[]{:S(2)}) collective-permute-start(f32[4,64]{1,0:T(4,128)S(1)} %add_add_fusion.1), channel_id=1, source_target_pairs={{0,4},{4,0},{8,12},{12,8},{1,5},{5,1},{9,13},{13,9},{2,6},{6,2},{1... | collective-permute-start | bytes 3080 | tf_op jit(solution)/shard_map/ppermute | solution.py:556
  31.0 1.1 %collective-permute-start.8 = (f32[4,64]{1,0:T(4,128)S(1)}, f32[4,64]{1,0:T(4,128)S(1)}, u32[]{:S(2)}, u32[]{:S(2)}) collective-permute-start(f32[4,64]{1,0:T(4,128)S(1)} %add_add_fusion.1), channel_id=1, source_target_pairs={{0,8},{4,12},{8,0},{12,4},{1,9},{5,13},{9,1},{13,5},{2,10},{6,14},... | collective-permute-start | bytes 3080 | tf_op jit(solution)/shard_map/ppermute | solution.py:556
  32.1 1.4 %collective-permute-start.9 = (f32[4,64]{1,0:T(4,128)S(1)}, f32[4,64]{1,0:T(4,128)S(1)}, u32[]{:S(2)}, u32[]{:S(2)}) collective-permute-start(f32[4,64]{1,0:T(4,128)S(1)} %add_add_fusion.1), channel_id=1, source_target_pairs={{0,12},{4,8},{8,4},{12,0},{1,13},{5,9},{9,5},{13,1},{2,14},{6,10},... | collective-permute-start | bytes 3080 | tf_op jit(solution)/shard_map/ppermute | solution.py:556
  33.4 0.4 %collective-permute-done.4.refs_15_ = f32[2,128,128]{2,1,0:T(8,128)S(1)} collective-permute-done((f32[2,128,128]{2,1,0:T(8,128)S(1)}, f32[2,128,128]{2,1,0:T(8,128)S(1)}, u32[]{:S(2)}, u32[]{:S(2)}) %collective-permute-start.4) | collective-permute-done | bytes 131104 | tf_op jit(solution)/shard_map/ppermute | solution.py:519
  33.9 2.7 %collective-permute-done.5.refs_16_ = f32[2,128,128]{2,1,0:T(8,128)S(1)} collective-permute-done((f32[2,128,128]{2,1,0:T(8,128)S(1)}, f32[2,128,128]{2,1,0:T(8,128)S(1)}, u32[]{:S(2)}, u32[]{:S(2)}) %collective-permute-start.5) | collective-permute-done | bytes 131104 | tf_op jit(solution)/shard_map/ppermute | solution.py:519
  36.6 6.7 %merge.1 = (bf16[1,1024,512]{2,1,0:T(8,128)(2,1)}, bf16[1,1024,512]{2,1,0:T(8,128)(2,1)}, bf16[1,1024,512]{2,1,0:T(8,128)(2,1)}, bf16[1,1024,512]{2,1,0:T(8,128)(2,1)}, f32[1,4,1024]{2,1,0:T(4,128)}) custom-call(bf16[1,1024,512]{2,1,0:T(8,128)(2,1)S(1)} %get-tuple-element.41.q_ref.refs_0_, bf16[1,1024,512]{2,1,0:T(8,128)(2,1)S(1)} %get-tuple-element.42.k_ref.refs_1_, ...), custom_call_target="tpu_custom_call" | custom-call | flops 536870912 | bytes 12582912 | tf_op jit(solution)/shard_map/merge/pallas_call | solution.py:487
  43.3 0.6 %add_add_fusion = f32[4,64]{1,0:T(4,128)} fusion(f32[4,64]{1,0:T(4,128)S(1)} %collective-permute-done.8, f32[4,64]{1,0:T(4,128)S(1)} %collective-permute-done.9, f32[4,64]{1,0:T(4,128)S(1)} %add_add_fusion.1, f32[4,64]{1,0:T(4,128)S(1)} %collective-permute-done.7), kind=kLoop, calls=%fused_computation.10 | loop fusion | flops 768 | bytes 5120 | tf_op jit(solution)/shard_map/add | solution.py:418
  (13 shorter events, 0.1 us)
Async XLA Ops:
  5.7 11.1 %collective-permute-start = (f32[2,128,128]{2,1,0:T(8,128)S(1)}, f32[2,128,128]{2,1,0:T(8,128)S(1)}, u32[]{:S(2)}, u32[]{:S(2)}) collective-permute-start(f32[2,128,128]{2,1,0:T(8,128)S(1)} %get-tuple-element.52), channel_id=1, source_target_pairs={{0,4},{12,8},{1,5},{13,9},{2,6},{14,10},{3,7},{15,11},{16,20},{28,... | collective-permute-start | bytes 393224 | tf_op jit(solution)/shard_map/ppermute | solution.py:519
  10.6 6.9 %collective-permute-start.1 = (f32[2,128,128]{2,1,0:T(8,128)S(1)}, f32[2,128,128]{2,1,0:T(8,128)S(1)}, u32[]{:S(2)}, u32[]{:S(2)}) collective-permute-start(f32[2,128,128]{2,1,0:T(8,128)S(1)} %get-tuple-element.58), channel_id=1, source_target_pairs={{0,4},{12,8},{1,5},{13,9},{2,6},{14,10},{3,7},{15,11},{16,20},{28,... | collective-permute-start | bytes 393224 | tf_op jit(solution)/shard_map/ppermute | solution.py:519
  16.8 6.3 %collective-permute-start.2 = (f32[2,128,128]{2,1,0:T(8,128)S(1)}, f32[2,128,128]{2,1,0:T(8,128)S(1)}, u32[]{:S(2)}, u32[]{:S(2)}) collective-permute-start(f32[2,128,128]{2,1,0:T(8,128)S(1)} %multiply_add_fusion.3), channel_id=1, source_target_pairs={{4,8},{8,4},{5,9},{9,5},{6,10},{10,6},{7,11},{11,7},{20,24},{24,20... | collective-permute-start | bytes 393224 | tf_op jit(solution)/shard_map/ppermute | solution.py:519
  17.5 5.7 %collective-permute-start.3 = (f32[2,128,128]{2,1,0:T(8,128)S(1)}, f32[2,128,128]{2,1,0:T(8,128)S(1)}, u32[]{:S(2)}, u32[]{:S(2)}) collective-permute-start(f32[2,128,128]{2,1,0:T(8,128)S(1)} %multiply_add_fusion.2), channel_id=1, source_target_pairs={{4,8},{8,4},{5,9},{9,5},{6,10},{10,6},{7,11},{11,7},{20,24},{24,20... | collective-permute-start | bytes 393224 | tf_op jit(solution)/shard_map/ppermute | solution.py:519
  23.5 2.6 %collective-permute-start.6 = (f32[4,64]{1,0:T(4,128)S(1)}, f32[4,64]{1,0:T(4,128)S(1)}, u32[]{:S(2)}, u32[]{:S(2)}) collective-permute-start(f32[4,64]{1,0:T(4,128)S(1)} %multiply_add_fusion.4), channel_id=1, source_target_pairs={{0,16},{16,0},{1,17},{17,1},{2,18},{18,2},{3,19},{19,3},{4,20},{20... | collective-permute-start | bytes 3080 | tf_op jit(solution)/shard_map/ppermute | solution.py:553
  23.6 10.3 %collective-permute-start.4 = (f32[2,128,128]{2,1,0:T(8,128)S(1)}, f32[2,128,128]{2,1,0:T(8,128)S(1)}, u32[]{:S(2)}, u32[]{:S(2)}) collective-permute-start(f32[2,128,128]{2,1,0:T(8,128)S(1)} %get-tuple-element.77), channel_id=1, source_target_pairs={{8,12},{4,0},{9,13},{5,1},{10,14},{6,2},{11,15},{7,3},{24,28},{20,... | collective-permute-start | bytes 393224 | tf_op jit(solution)/shard_map/ppermute | solution.py:519
  24.9 11.7 %collective-permute-start.5 = (f32[2,128,128]{2,1,0:T(8,128)S(1)}, f32[2,128,128]{2,1,0:T(8,128)S(1)}, u32[]{:S(2)}, u32[]{:S(2)}) collective-permute-start(f32[2,128,128]{2,1,0:T(8,128)S(1)} %get-tuple-element.80), channel_id=1, source_target_pairs={{8,12},{4,0},{9,13},{5,1},{10,14},{6,2},{11,15},{7,3},{24,28},{20,... | collective-permute-start | bytes 393224 | tf_op jit(solution)/shard_map/ppermute | solution.py:519
  26.2 17.0 %collective-permute-start.7 = (f32[4,64]{1,0:T(4,128)S(1)}, f32[4,64]{1,0:T(4,128)S(1)}, u32[]{:S(2)}, u32[]{:S(2)}) collective-permute-start(f32[4,64]{1,0:T(4,128)S(1)} %add_add_fusion.1), channel_id=1, source_target_pairs={{0,4},{4,0},{8,12},{12,8},{1,5},{5,1},{9,13},{13,9},{2,6},{6,2},{1... | collective-permute-start | bytes 3080 | tf_op jit(solution)/shard_map/ppermute | solution.py:556
  31.0 12.3 %collective-permute-start.8 = (f32[4,64]{1,0:T(4,128)S(1)}, f32[4,64]{1,0:T(4,128)S(1)}, u32[]{:S(2)}, u32[]{:S(2)}) collective-permute-start(f32[4,64]{1,0:T(4,128)S(1)} %add_add_fusion.1), channel_id=1, source_target_pairs={{0,8},{4,12},{8,0},{12,4},{1,9},{5,13},{9,1},{13,5},{2,10},{6,14},... | collective-permute-start | bytes 3080 | tf_op jit(solution)/shard_map/ppermute | solution.py:556
  32.1 11.2 %collective-permute-start.9 = (f32[4,64]{1,0:T(4,128)S(1)}, f32[4,64]{1,0:T(4,128)S(1)}, u32[]{:S(2)}, u32[]{:S(2)}) collective-permute-start(f32[4,64]{1,0:T(4,128)S(1)} %add_add_fusion.1), channel_id=1, source_target_pairs={{0,12},{4,8},{8,4},{12,0},{1,13},{5,9},{9,5},{13,1},{2,14},{6,10},... | collective-permute-start | bytes 3080 | tf_op jit(solution)/shard_map/ppermute | solution.py:556

commit v9 on v8

--- a/solution.py
+++ b/solution.py
@@ -10,7 +10,7 @@
 
 CHUNK = 128
 PARTS = 2
-UNROLL = 4
+UNROLL = 8
 PRECISE = lax.Precision.HIGHEST
 F32 = jnp.float32
 BF16 = jnp.bfloat16
@@ -41,6 +41,11 @@
 
 def later_sums(column):
     kept = iota((CHUNK, CHUNK), 0) >= iota((CHUNK, CHUNK), 1)
+    return jnp.sum(jnp.where(kept, column, 0.0), axis=0, keepdims=True)
+
+
+def earlier_sums(column):
+    kept = iota((CHUNK, CHUNK), 0) < iota((CHUNK, CHUNK), 1)
     return jnp.sum(jnp.where(kept, column, 0.0), axis=0, keepdims=True)
 
 
@@ -308,108 +313,117 @@
     lax.fori_loop(0, groups, forward_group, 0)
 
 
-def merge_kernel(head_width, *refs):
-    q_ref, k_ref, v_ref, cot_ref, gain_ref, flag_ref, fac_ref = refs[:7]
-    partial_refs, gate_refs, first_refs, second_refs, last_refs = (
-        refs[7 + i * PARTS : 7 + (i + 1) * PARTS] for i in range(5)
-    )
-    refs = refs[7 + 5 * PARTS :]
-    targets, dgate_ref, staged, entering, leaving, sems = refs[:4], *refs[4:]
-    heads = first_refs[0].shape[0]
+def merge_kernel(head_width, stage, half_ctx, *refs):
+    streams = refs[:4]
+    gain_ref, fac_ref, gate_src = refs[4:7]
+    rows_all = fac_ref.shape[0]
+    all_heads = gain_ref.shape[0]
+    partial_refs, refs = refs[7 : 7 + all_heads], refs[7 + all_heads :]
+    first_refs, refs = refs[:PARTS], refs[PARTS:]
+    if stage == 1:
+        second_refs, last_refs, refs = refs[:PARTS], refs[PARTS : 2 * PARTS], refs[2 * PARTS + 4 :]
+    targets, dgate_ref, staged, matrix, sems = refs[:4], *refs[4:]
+    heads = all_heads // PARTS
     steps = sems.shape[0]
-    num_chunks = fac_ref.shape[0] // 8
+    num_chunks = rows_all // 8
     chunks = num_chunks // steps
     block = chunks * CHUNK
     group_width = heads * head_width
     scale = head_width ** (-0.5)
 
-    def copies(step):
-        at = pl.ds(step * block, block)
-        return [
-            pltpu.make_async_copy(staged.at[i, at, :], target.at[0, at, :], sems.at[step, i])
-            for i, target in enumerate(targets)
-        ]
-
-    gain_columns = jnp.transpose(jnp.concatenate([gain_ref[...], gain_ref[...]], axis=0))
-    entering[...] = jnp.zeros_like(entering)
-    leaving[...] = jnp.zeros_like(leaving)
-    last_factors = fac_ref[(num_chunks - 1) * 8 : num_chunks * 8, CHUNK - 1 : CHUNK]
-    low = jnp.broadcast_to(flag_ref[2:3, :], (head_width, head_width)) > 0.5
-    constants = []
-    for part in range(PARTS):
-        for head in range(heads):
-            row = part * heads + head
+    def run(query_side):
+        a_ref, b_ref = (streams[0], streams[3]) if query_side else (streams[1], streams[2])
+        outputs = (0, 1) if query_side else (3, 2)
+
+        def copies(step):
+            at = pl.ds(step * block, block)
+            return [
+                pltpu.make_async_copy(
+                    staged.at[i, at, :], targets[output].at[0, at, :], sems.at[step, i]
+                )
+                for i, output in enumerate(outputs)
+            ]
+
+        gain_columns = jnp.transpose(jnp.concatenate([gain_ref[...], gain_ref[...]], axis=0))
+        matrix[...] = jnp.zeros_like(matrix)
+        constants = [jnp.zeros((1, 1), F32)] * all_heads
+        for row in range(all_heads):
+            part, head = divmod(row, heads)
             own = slice(head * head_width, (head + 1) * head_width)
             gain = gain_columns[:, row : row + 1]
-            first = first_refs[part][head]
-            second = second_refs[part][head] + last_refs[part][head]
-            state = jnp.where(low, first, second) * gain
-            later = jnp.where(low, second, first)
-            entering[part, own, own] = (state * scale).astype(BF16)
-            leaving[part, own, own] = (later * gain).astype(BF16)
-            constants.append(total_of(state * later) * last_factors[row : row + 1])
-
-    gate_sums, kept_sums = {}, {}
-    for step in range(steps):
-        numbers = range(step * chunks, (step + 1) * chunks)
-        products, results = {}, {}
-        for number in numbers:
-            rows = slice(number * CHUNK, (number + 1) * CHUNK)
-            for part in range(PARTS):
-                group = slice(part * group_width, (part + 1) * group_width)
-                products[number, part] = (
-                    dot_nn(q_ref[0, rows, group], entering[part]),
-                    dot_nt(cot_ref[0, rows, group], entering[part]),
-                    dot_nt(v_ref[0, rows, group], leaving[part]),
-                    dot_nn(k_ref[0, rows, group], leaving[part]),
+            state = first_refs[part][head]
+            if stage == 1:
+                second = second_refs[part][head] + last_refs[part][head]
+                decay = fac_ref[rows_all - 8 + row : rows_all - 7 + row, CHUNK - 1 : CHUNK]
+                constants[row] = total_of(state * second * gain) * decay
+                state = second
+            gain = gain * scale if query_side else gain
+            matrix[part, own, own] = (state * gain).astype(BF16)
+
+        gate_sums, totals = {}, {}
+        for step in range(steps):
+            numbers = range(step * chunks, (step + 1) * chunks)
+            products, results = {}, {}
+            for number in numbers:
+                rows = slice(number * CHUNK, (number + 1) * CHUNK)
+                for part in range(PARTS):
+                    group = slice(part * group_width, (part + 1) * group_width)
+                    products[number, part] = (
+                        dot_nn(a_ref[0, rows, group], matrix[part]),
+                        dot_nt(b_ref[0, rows, group], matrix[part]),
+                    )
+            for number in numbers:
+                columns = jnp.transpose(fac_ref[number * 8 : number * 8 + 8, :])
+                rows = slice(number * CHUNK, (number + 1) * CHUNK)
+                for row in range(all_heads):
+                    part, head = divmod(row, heads)
+                    lanes = slice(head * head_width, (head + 1) * head_width)
+                    wide = slice(row * head_width, (row + 1) * head_width)
+                    column = row if query_side else 4 + row
+                    factor = columns[:, column : column + 1]
+                    added = [product[:, lanes] * factor for product in products[number, part]]
+                    results[number, row] = [
+                        (partial_refs[row][output, rows, :].astype(F32) + term).astype(BF16)
+                        for output, term in zip(outputs, added)
+                    ]
+                    share = jnp.sum(
+                        added[0] * b_ref[0, rows, wide].astype(F32), axis=1, keepdims=True
+                    )
+                    if query_side:
+                        gate_sums[number, row] = later_sums(share)
+                    else:
+                        gate_sums[number, row] = earlier_sums(share)
+                    totals[number, row] = jnp.sum(share, axis=0, keepdims=True)
+            for number in numbers:
+                rows = slice(number * CHUNK, (number + 1) * CHUNK)
+                for row in range(all_heads):
+                    wide = slice(row * head_width, (row + 1) * head_width)
+                    for i in range(2):
+                        staged[i, rows, wide] = results[number, row][i]
+            for i, copy in enumerate(copies(step)):
+                copy.start(priority=i % 2)
+        order = range(num_chunks - 1, -1, -1) if query_side else range(num_chunks)
+        for row in range(all_heads):
+            base = constants[row]
+            for number in order:
+                lanes = slice(number * CHUNK, (number + 1) * CHUNK)
+                dgate_ref[0, row : row + 1, lanes] = (
+                    gate_src[0, row : row + 1, lanes] + gate_sums[number, row] + base
                 )
-        for number in numbers:
-            columns = jnp.transpose(fac_ref[number * 8 : number * 8 + 8, :])
-            rows = slice(number * CHUNK, (number + 1) * CHUNK)
-            for row in range(PARTS * heads):
-                part, head = divmod(row, heads)
-                lanes = slice(head * head_width, (head + 1) * head_width)
-                wide = slice(row * head_width, (row + 1) * head_width)
-                from_start, to_end = columns[:, row : row + 1], columns[:, 4 + row : 5 + row]
-                across, dq, dk, written = (
-                    product[:, lanes] * factor
-                    for product, factor in zip(
-                        products[number, part], (from_start, from_start, to_end, to_end)
-                    )
-                )
-                results[number, row] = [
-                    (partial_refs[part][i, rows, lanes].astype(F32) + added).astype(BF16)
-                    for i, added in enumerate((across, dq, dk, written))
-                ]
-                kept = written * v_ref[0, rows, wide].astype(F32)
-                balance = jnp.sum(
-                    across * cot_ref[0, rows, wide].astype(F32) - kept, axis=1, keepdims=True
-                )
-                gate_sums[number, row] = later_sums(balance)
-                kept_sums[number, row] = jnp.sum(kept, axis=0, keepdims=True)
-        for number in numbers:
-            rows = slice(number * CHUNK, (number + 1) * CHUNK)
-            for row in range(PARTS * heads):
-                wide = slice(row * head_width, (row + 1) * head_width)
-                for i in range(4):
-                    staged[i, rows, wide] = results[number, row][i]
-        for i, copy in enumerate(copies(step)):
-            copy.start(priority=i % 2)
-
-    for row in range(PARTS * heads):
-        part, head = divmod(row, heads)
-        kept = sum(kept_sums[number, row] for number in range(num_chunks))
-        base = jnp.sum(kept, axis=1, keepdims=True) + constants[row]
-        for number in range(num_chunks - 1, -1, -1):
-            lanes = slice(number * CHUNK, (number + 1) * CHUNK)
-            sums = gate_sums[number, row]
-            dgate_ref[0, row : row + 1, lanes] = (
-                gate_refs[part][0, head : head + 1, lanes] + sums + base
-            )
-            base = base + sums[:, 0:1]
-    for step in range(steps):
-        for copy in copies(step):
-            copy.wait()
+                base = base + totals[number, row]
+        for step in range(steps):
+            for copy in copies(step):
+                copy.wait()
+
+    low = lax.axis_index("ctx") < half_ctx
+
+    @pl.when(low)
+    def _():
+        run(stage == 0)
+
+    @pl.when(jnp.logical_not(low))
+    def _():
+        run(stage == 1)
 
 
 def summed(own, others):
@@ -441,8 +455,7 @@
     table = shape_of(rows, CHUNK)
     states = shape_of(heads, head_width, head_width)
     decays = shape_of(heads, 1, head_width)
-    part_gates = shape_of(1, heads, tokens)
-    partials = shape_of(4, tokens, part_width, dtype=BF16)
+    partials = shape_of(4, tokens, head_width, dtype=BF16)
     streams = (queries, keys_raw, values, cotangent)
     product = 2 * tokens * part_width * head_width
 
@@ -466,41 +479,44 @@
             name="shard_ends",
         )(small, *streams)
 
-    def local(part, gain, cum, fac):
+    def local(row, cum):
         return pl.pallas_call(
-            functools.partial(local_kernel, head_width, part),
+            functools.partial(local_kernel, head_width, row),
             in_specs=[vmem] * 7,
             out_specs=[vmem] * 3,
-            out_shape=[partials, part_gates, shape_of(heads, head_width)],
+            out_shape=[partials, shape_of(1, 1, tokens), shape_of(1, head_width)],
             scratch_shapes=[
-                pltpu.VMEM((num_chunks, heads, head_width, head_width), BF16),
-                pltpu.VMEM((heads, head_width, head_width), F32),
+                pltpu.VMEM((num_chunks, 1, head_width, head_width), BF16),
+                pltpu.VMEM((1, head_width, head_width), F32),
             ],
             compiler_params=pltpu.CompilerParams(vmem_limit_bytes=24 << 20),
             cost_estimate=pl.CostEstimate(
-                flops=12 * product, bytes_accessed=16 * tokens * part_width, transcendentals=0
+                flops=12 * product // heads, bytes_accessed=16 * tokens * head_width, transcendentals=0
             ),
-            name=f"local_{part}",
-        )(*held, gain, cum, fac)
-
-    def merge(*arrays):
+            name=f"local_{row}",
+        )(*held, gain, cum, chunk_fac)
+
+    def merge(stage, gate_grads, states_in, done):
+        inputs = [*held, gain, shard_fac, gate_grads]
+        inputs += [local_part[0] for local_part in locals_] + states_in
+        aliases = {len(inputs) + i: i for i in range(len(done))}
         return pl.pallas_call(
-            functools.partial(merge_kernel, head_width),
-            in_specs=[vmem] * len(arrays),
+            functools.partial(merge_kernel, head_width, stage, count // 2),
+            in_specs=[vmem] * len(inputs) + [hbm] * len(done),
             out_specs=[hbm] * 4 + [vmem],
             out_shape=[shape_of(1, tokens, width, dtype=BF16)] * 4 + [shape_of(*gates.shape)],
             scratch_shapes=[
-                pltpu.VMEM((4, tokens, width), BF16),
+                pltpu.VMEM((2, tokens, width), BF16),
                 pltpu.VMEM((PARTS, part_width, part_width), BF16),
-                pltpu.VMEM((PARTS, part_width, part_width), BF16),
-                pltpu.SemaphoreType.DMA((steps, 4)),
+                pltpu.SemaphoreType.DMA((steps, 2)),
             ],
+            input_output_aliases=aliases,
             compiler_params=pltpu.CompilerParams(vmem_limit_bytes=24 << 20),
             cost_estimate=pl.CostEstimate(
-                flops=4 * product * PARTS, bytes_accessed=24 * tokens * width, transcendentals=0
+                flops=2 * product * PARTS, bytes_accessed=12 * tokens * width, transcendentals=0
             ),
-            name="merge",
-        )(*arrays)
+            name=f"merge_{stage}",
+        )(*inputs, *done)
 
     results = ends()
     near, far, decay = (results[i * PARTS : (i + 1) * PARTS] for i in range(3))
@@ -508,7 +524,6 @@
     held = results[3 * PARTS + 5 :]
     sent = [[] for _ in range(PARTS)]
     arrived = [[] for _ in range(PARTS)]
-    local_parts = [None] * PARTS
 
     def send(part, hop):
         payload = near[part] if hop <= middle else far[part]
@@ -521,30 +536,40 @@
             )
         )
 
-    for part in range(PARTS):
-        send(part, 0)
+    locals_, per_hop = [], [2, 1, 1]
     for hop in range(count - 1):
-        if hop < PARTS:
+        for part in range(PARTS):
+            send(part, hop)
+        for _ in range(per_hop[hop] if hop < 3 else 0):
             local_cum = cum
             if hop > 0:
-                local_cum, _ = lax.optimization_barrier((cum, arrived[0][hop - 1]))
-            local_parts[hop] = list(local(hop, gain, local_cum, chunk_fac))
+                local_cum, *_ = lax.optimization_barrier((cum, *[own[hop] for own in sent]))
+            locals_.append(list(local(len(locals_), local_cum)))
             if hop + 1 < count - 1:
-                local_parts[hop][2], arrived[0][-1] = lax.optimization_barrier(
-                    (local_parts[hop][2], arrived[0][-1])
+                locals_[-1][2], arrived[0][-1] = lax.optimization_barrier(
+                    (locals_[-1][2], arrived[0][-1])
                 )
-        if hop + 1 < count - 1:
-            for part in range(PARTS):
-                send(part, hop + 1)
 
     terms = []
     for part in range(PARTS):
         crossed = jnp.sum(sent[part][middle] * arrived[part][middle], axis=2)
-        term = local_parts[part][2] + flags[0:1] * crossed
+        term = flags[0:1] * crossed
         if middle > 0:
             term = term + jnp.sum(sum(arrived[part][:middle]) * far[part], axis=2)
         terms.append(term)
-    gain_term = jnp.concatenate(terms, axis=0)
+    gain_term = jnp.concatenate(terms, axis=0) + jnp.concatenate(
+        [local_part[2] for local_part in locals_], axis=0
+    )
+    local_gates = jnp.concatenate([local_part[1] for local_part in locals_], axis=1)
+
+    zeros = jnp.zeros(states.shape, F32)
+    if middle == 1:
+        firsts, seconds = ([own[i] for own in arrived] for i in range(2))
+    else:
+        firsts = [sum(own[:middle], zeros) for own in arrived]
+        seconds = [sum(own[middle:-1], zeros) for own in arrived]
+    lasts = [own[-1] for own in arrived]
+    half_done = merge(0, local_gates, firsts, [])
     half = head_width // lax.axis_size("dp")
     second_half = flags[1:2, :half]
     lower_half, upper_half = gain_term[:, :half], gain_term[:, half:]
@@ -564,20 +589,7 @@
             pending += [exchanged(grad_gain, reach * 2), exchanged(grad_gain, reach * 3)]
         reach *= 2 * min(len(pending), 2)
 
-    zeros = jnp.zeros(states.shape, F32)
-    if middle == 1:
-        firsts, seconds = ([own[i] for own in arrived] for i in range(2))
-    else:
-        firsts = [sum(own[:middle], zeros) for own in arrived]
-        seconds = [sum(own[middle:-1], zeros) for own in arrived]
-    done = list(
-        merge(
-            *held, gain, flags, shard_fac,
-            *[local_part[0] for local_part in local_parts],
-            *[local_part[1] for local_part in local_parts],
-            *firsts, *seconds, *[own[-1] for own in arrived],
-        )
-    )
+    done = list(merge(1, half_done[4], firsts + seconds + lasts, half_done[:4]))
     pending, done[4] = lax.optimization_barrier((pending, done[4]))
     return (*done, summed(grad_gain, pending))
 

time: 44.3 us -> 45.9 us (1.036)
  Pallas kernels: 20 us -> 23.6 us
  waiting for transfers between devices: 3.13 us -> 0.03 us
  starting transfers between devices: 17.4 us -> 18.5 us
    pallas_call x3 -> x6, Pallas kernels: 16.4 us -> 19.9 us  [the longest x2 10.2 us: merge(): pl.pallas_call(functools.partial(merge_kernel, head_width, stage, count /...]
    ppermute x6, waiting for transfers between devices: 3.12 us -> 0.02 us  [send(): lax.ppermute(payload, 'ctx', [(hop, hop + 1), (count - 1 - hop, count - 2...]
    ppermute x3, starting transfers between devices: 7.2 us -> 8.35 us  [exchanged(): return lax.ppermute(array, 'ctx', [(i, i ^ reach) for i in range(count)])]
  transfers between devices with their start and end apart: 10 -> 10, of which waited for: 2 -> 0; matrix products, arithmetic and copies ran while one was open for 1% -> 1% of each run, Pallas kernels for 37% -> 44%
where the time goes in v9:
time: 45.9 us; the launch traced here: 45.5 us
  Pallas kernels  23.6 us (51%)
  starting transfers between devices  18.5 us (40%)
  other arithmetic  2.52 us (5%)
  between operations  0.87 us (2%)
    pallas_call x2, Pallas kernels, merge(): pl.pallas_call(functools.partial(merge_kernel, head_width, stage, count /...  10.2 us
    ppermute x6, starting transfers between devices, send(): lax.ppermute(payload, 'ctx', [(hop, hop + 1), (count - 1 - hop, count - 2...  10.2 us
    pallas_call x4, Pallas kernels, local(): pl.pallas_call(functools.partial(local_kernel, head_width, row), in_specs...  9.76 us
    ppermute x3, starting transfers between devices, exchanged(): return lax.ppermute(array, 'ctx', [(i, i ^ reach) for i in range(count)])  8.35 us
    pallas_call x1, Pallas kernels, ends(): pl.pallas_call(functools.partial(ends_kernel, head_width, lengths.shape[1...  3.64 us
  transfers between devices with their start and end apart: 10, of which 0 were waited for; matrix products, arithmetic and copies ran while one was open for 1% of the time, Pallas kernels for 44%

profile of v9, /device:TPU:0, one launch (start us, length us, event | category | flops | bytes accessed | tf_op | source)
XLA Modules:
  0.0 45.5 jit_solution(15404044578551966481)
XLA Ops:
  0.6 0.7 %pad_convert_fusion = f32[4,128]{1,0:T(4,128)S(1)} fusion(s32[1,16]{1,0:T(1,128)} %param.11), kind=kLoop, calls=%fused_computation.14 | loop fusion | flops 512 | bytes 2112 | tf_op jit(solution)/shard_map/convert_element_type | solution.py:447
  1.3 0.0 copy-done
  1.3 0.7 %pad_maximum_fusion.refs_0_ = f32[4,1280]{1,0:T(4,128)S(1)} fusion(f32[4,128]{1,0:T(4,128)S(1)} %pad_convert_fusion, f32[4,128]{1,0:T(4,128)S(1)} %copy-done, f32[4,1024]{1,0:T(4,128)} %bitcast.13), kind=kLoop, calls=%fused_computation.8 | loop fusion | flops 10240 | bytes 40960 | tf_op jit(solution)/shard_map/concatenate | solution.py:448
  2.0 3.6 %shard_ends.1 = (f32[2,128,128]{2,1,0:T(8,128)S(1)}, f32[2,128,128]{2,1,0:T(8,128)S(1)}, f32[2,128,128]{2,1,0:T(8,128)S(1)}, f32[2,128,128]{2,1,0:T(8,128)S(1)},...) custom-call(f32[4,1280]{1,0:T(4,128)S(1)} %pad_maximum_fusion.refs_0, ...), custom_call_target="tpu_custom_call" | custom-call | flops 268435456 | bytes 4194304 | tf_op jit(solution)/shard_map/shard_ends/pallas_call | solution.py:466
  5.7 4.9 %collective-permute-start = (f32[2,128,128]{2,1,0:T(8,128)S(1)}, f32[2,128,128]{2,1,0:T(8,128)S(1)}, u32[]{:S(2)}, u32[]{:S(2)}) collective-permute-start(f32[2,128,128]{2,1,0:T(8,128)S(1)} %get-tuple-element.65), channel_id=1, source_target_pairs={{0,4},{12,8},{1,5},{13,9},{2,6},{14,10},{3,7},{15,11},{16,20},{28,... | collective-permute-start | bytes 393224 | tf_op jit(solution)/shard_map/ppermute | solution.py:534
  10.6 1.3 %collective-permute-start.1 = (f32[2,128,128]{2,1,0:T(8,128)S(1)}, f32[2,128,128]{2,1,0:T(8,128)S(1)}, u32[]{:S(2)}, u32[]{:S(2)}) collective-permute-start(f32[2,128,128]{2,1,0:T(8,128)S(1)} %get-tuple-element.71), channel_id=1, source_target_pairs={{0,4},{12,8},{1,5},{13,9},{2,6},{14,10},{3,7},{15,11},{16,20},{28,... | collective-permute-start | bytes 393224 | tf_op jit(solution)/shard_map/ppermute | solution.py:534
  11.9 2.5 %local_1.1 = (bf16[4,1024,128]{2,1,0:T(8,128)(2,1)S(1)}, f32[1,1,1024]{2,1,0:T(1,128)S(1)}, f32[1,128]{1,0:T(1,128)S(1)}) custom-call(bf16[1,1024,512]{2,1,0:T(8,128)(2,1)S(1)} %get-tuple-element.55.q_ref.refs_0_, bf16[1,1024,512]{2,1,0:T(8,128)(2,1)S(1)} %get-tuple-element.56.k_ref.refs_1_, bf16[1,1024,512]{2,1,0:T(8,128)(2,1)S(1)} %get-tuple-element.57.v_ref.refs_2_, ...), custom_call_target="tpu_custom_call" | custom-call | flops 402653184 | bytes 2097152 | tf_op jit(solution)/shard_map/local_1/pallas_call | solution.py:483
  14.4 2.4 %local_0.1 = (bf16[4,1024,128]{2,1,0:T(8,128)(2,1)S(1)}, f32[1,1,1024]{2,1,0:T(1,128)S(1)}, f32[1,128]{1,0:T(1,128)S(1)}) custom-call(bf16[1,1024,512]{2,1,0:T(8,128)(2,1)S(1)} %get-tuple-element.55.q_ref.refs_0_, bf16[1,1024,512]{2,1,0:T(8,128)(2,1)S(1)} %get-tuple-element.56.k_ref.refs_1_, bf16[1,1024,512]{2,1,0:T(8,128)(2,1)S(1)} %get-tuple-element.57.v_ref.refs_2_, ...), custom_call_target="tpu_custom_call" | custom-call | flops 402653184 | bytes 2097152 | tf_op jit(solution)/shard_map/local_0/pallas_call | solution.py:483
  16.8 0.7 %collective-permute-start.3 = (f32[2,128,128]{2,1,0:T(8,128)S(1)}, f32[2,128,128]{2,1,0:T(8,128)S(1)}, u32[]{:S(2)}, u32[]{:S(2)}) collective-permute-start(f32[2,128,128]{2,1,0:T(8,128)S(1)} %multiply_add_fusion.2), channel_id=1, source_target_pairs={{4,8},{8,4},{5,9},{9,5},{6,10},{10,6},{7,11},{11,7},{20,24},{24,20... | collective-permute-start | bytes 393224 | tf_op jit(solution)/shard_map/ppermute | solution.py:534
  17.6 0.7 %collective-permute-start.2 = (f32[2,128,128]{2,1,0:T(8,128)S(1)}, f32[2,128,128]{2,1,0:T(8,128)S(1)}, u32[]{:S(2)}, u32[]{:S(2)}) collective-permute-start(f32[2,128,128]{2,1,0:T(8,128)S(1)} %multiply_add_fusion.3), channel_id=1, source_target_pairs={{4,8},{8,4},{5,9},{9,5},{6,10},{10,6},{7,11},{11,7},{20,24},{24,20... | collective-permute-start | bytes 393224 | tf_op jit(solution)/shard_map/ppermute | solution.py:534
  18.2 2.5 %local_2.1 = (bf16[4,1024,128]{2,1,0:T(8,128)(2,1)S(1)}, f32[1,1,1024]{2,1,0:T(1,128)S(1)}, f32[1,128]{1,0:T(1,128)S(1)}) custom-call(bf16[1,1024,512]{2,1,0:T(8,128)(2,1)S(1)} %get-tuple-element.55.q_ref.refs_0_, bf16[1,1024,512]{2,1,0:T(8,128)(2,1)S(1)} %get-tuple-element.56.k_ref.refs_1_, bf16[1,1024,512]{2,1,0:T(8,128)(2,1)S(1)} %get-tuple-element.57.v_ref.refs_2_, ...), custom_call_target="tpu_custom_call" | custom-call | flops 402653184 | bytes 2097152 | tf_op jit(solution)/shard_map/local_2/pallas_call | solution.py:483
  20.7 0.2 multiply_reduce_fusion.1
  20.9 1.3 %collective-permute-start.5 = (f32[2,128,128]{2,1,0:T(8,128)S(1)}, f32[2,128,128]{2,1,0:T(8,128)S(1)}, u32[]{:S(2)}, u32[]{:S(2)}) collective-permute-start(f32[2,128,128]{2,1,0:T(8,128)S(1)} %get-tuple-element.108), channel_id=1, source_target_pairs={{8,12},{4,0},{9,13},{5,1},{10,14},{6,2},{11,15},{7,3},{24,28},{20,... | collective-permute-start | bytes 393224 | tf_op jit(solution)/shard_map/ppermute | solution.py:534
  22.2 0.2 multiply_reduce_fusion.3
  22.3 1.3 %collective-permute-start.4 = (f32[2,128,128]{2,1,0:T(8,128)S(1)}, f32[2,128,128]{2,1,0:T(8,128)S(1)}, u32[]{:S(2)}, u32[]{:S(2)}) collective-permute-start(f32[2,128,128]{2,1,0:T(8,128)S(1)} %get-tuple-element.105), channel_id=1, source_target_pairs={{8,12},{4,0},{9,13},{5,1},{10,14},{6,2},{11,15},{7,3},{24,28},{20,... | collective-permute-start | bytes 393224 | tf_op jit(solution)/shard_map/ppermute | solution.py:534
  23.6 2.5 %local_3.1 = (bf16[4,1024,128]{2,1,0:T(8,128)(2,1)S(1)}, f32[1,1,1024]{2,1,0:T(1,128)S(1)}, f32[1,128]{1,0:T(1,128)S(1)}) custom-call(bf16[1,1024,512]{2,1,0:T(8,128)(2,1)S(1)} %get-tuple-element.55.q_ref.refs_0_, bf16[1,1024,512]{2,1,0:T(8,128)(2,1)S(1)} %get-tuple-element.56.k_ref.refs_1_, bf16[1,1024,512]{2,1,0:T(8,128)(2,1)S(1)} %get-tuple-element.57.v_ref.refs_2_, ...), custom_call_target="tpu_custom_call" | custom-call | flops 402653184 | bytes 2097152 | tf_op jit(solution)/shard_map/local_3/pallas_call | solution.py:483
  26.1 0.1 multiply_add_fusion.4
  26.2 0.0 collective-permute-start.6
  26.3 4.7 %merge_0.1 = (bf16[1,1024,512]{2,1,0:T(8,128)(2,1)}, bf16[1,1024,512]{2,1,0:T(8,128)(2,1)}, bf16[1,1024,512]{2,1,0:T(8,128)(2,1)}, bf16[1,1024,512]{2,1,0:T(8,128)(2,1)}, f32[1,4,1024]{2,1,0:T(4,128)S(1)}) custom-call(bf16[1,1024,512]{2,1,0:T(8,128)(2,1)S(1)} %get-tuple-element.55.q_ref.refs_0_, bf16[1,1024,512]{2,1,0:T(8,128)(2,1)S(1)} %get-tuple-element.56.k_ref.refs_1_, ...), custom_call_target="tpu_custom_call" | custom-call | flops 268435456 | bytes 6291456 | tf_op jit(solution)/shard_map/merge_0/pallas_call | solution.py:503
  31.0 0.1 add_add_fusion.1
  31.1 2.5 %collective-permute-start.9 = (f32[4,64]{1,0:T(4,128)S(1)}, f32[4,64]{1,0:T(4,128)S(1)}, u32[]{:S(2)}, u32[]{:S(2)}) collective-permute-start(f32[4,64]{1,0:T(4,128)S(1)} %add_add_fusion.1), channel_id=1, source_target_pairs={{0,12},{4,8},{8,4},{12,0},{1,13},{5,9},{9,5},{13,1},{2,14},{6,10},... | collective-permute-start | bytes 3080 | tf_op jit(solution)/shard_map/ppermute | solution.py:581
  33.6 5.8 %collective-permute-start.8 = (f32[4,64]{1,0:T(4,128)S(1)}, f32[4,64]{1,0:T(4,128)S(1)}, u32[]{:S(2)}, u32[]{:S(2)}) collective-permute-start(f32[4,64]{1,0:T(4,128)S(1)} %add_add_fusion.1), channel_id=1, source_target_pairs={{0,8},{4,12},{8,0},{12,4},{1,9},{5,13},{9,1},{13,5},{2,10},{6,14},... | collective-permute-start | bytes 3080 | tf_op jit(solution)/shard_map/ppermute | solution.py:581
  39.5 5.4 %merge_1.1 = (bf16[1,1024,512]{2,1,0:T(8,128)(2,1)}, bf16[1,1024,512]{2,1,0:T(8,128)(2,1)}, bf16[1,1024,512]{2,1,0:T(8,128)(2,1)}, bf16[1,1024,512]{2,1,0:T(8,128)(2,1)}, f32[1,4,1024]{2,1,0:T(4,128)}) custom-call(bf16[1,1024,512]{2,1,0:T(8,128)(2,1)S(1)} %get-tuple-element.55.q_ref.refs_, ...), custom_call_target="tpu_custom_call", output_to_operand_aliasing={{0}: (17, {}), {1}: (18, {}), {2}: (19, {}), {3}: (20, {})} | custom-call | flops 268435456 | bytes 6291456 | tf_op jit(solution)/shard_map/merge_1/pallas_call | solution.py:503
  44.9 0.6 %add_add_fusion = f32[4,64]{1,0:T(4,128)} fusion(f32[4,64]{1,0:T(4,128)S(1)} %collective-permute-done.8, f32[4,64]{1,0:T(4,128)S(1)} %collective-permute-done.9, f32[4,64]{1,0:T(4,128)S(1)} %add_add_fusion.1, f32[4,64]{1,0:T(4,128)S(1)} %collective-permute-done.7), kind=kLoop, calls=%fused_computation.11 | loop fusion | flops 768 | bytes 5120 | tf_op jit(solution)/shard_map/add | solution.py:432
  (19 shorter events, 0.1 us)
Async XLA Ops:
  0.6 0.7 %copy-start = (f32[4,128]{1,0:T(4,128)S(1)}, f32[4,128]{1,0:T(4,128)}, u32[]{:S(2)}) copy-start(f32[4,128]{1,0:T(4,128)} %param.12) | copy-start | bytes 6148
  5.7 11.8 %collective-permute-start = (f32[2,128,128]{2,1,0:T(8,128)S(1)}, f32[2,128,128]{2,1,0:T(8,128)S(1)}, u32[]{:S(2)}, u32[]{:S(2)}) collective-permute-start(f32[2,128,128]{2,1,0:T(8,128)S(1)} %get-tuple-element.65), channel_id=1, source_target_pairs={{0,4},{12,8},{1,5},{13,9},{2,6},{14,10},{3,7},{15,11},{16,20},{28,... | collective-permute-start | bytes 393224 | tf_op jit(solution)/shard_map/ppermute | solution.py:534
  10.6 6.2 %collective-permute-start.1 = (f32[2,128,128]{2,1,0:T(8,128)S(1)}, f32[2,128,128]{2,1,0:T(8,128)S(1)}, u32[]{:S(2)}, u32[]{:S(2)}) collective-permute-start(f32[2,128,128]{2,1,0:T(8,128)S(1)} %get-tuple-element.71), channel_id=1, source_target_pairs={{0,4},{12,8},{1,5},{13,9},{2,6},{14,10},{3,7},{15,11},{16,20},{28,... | collective-permute-start | bytes 393224 | tf_op jit(solution)/shard_map/ppermute | solution.py:534
  16.8 3.9 %collective-permute-start.3 = (f32[2,128,128]{2,1,0:T(8,128)S(1)}, f32[2,128,128]{2,1,0:T(8,128)S(1)}, u32[]{:S(2)}, u32[]{:S(2)}) collective-permute-start(f32[2,128,128]{2,1,0:T(8,128)S(1)} %multiply_add_fusion.2), channel_id=1, source_target_pairs={{4,8},{8,4},{5,9},{9,5},{6,10},{10,6},{7,11},{11,7},{20,24},{24,20... | collective-permute-start | bytes 393224 | tf_op jit(solution)/shard_map/ppermute | solution.py:534
  17.6 4.6 %collective-permute-start.2 = (f32[2,128,128]{2,1,0:T(8,128)S(1)}, f32[2,128,128]{2,1,0:T(8,128)S(1)}, u32[]{:S(2)}, u32[]{:S(2)}) collective-permute-start(f32[2,128,128]{2,1,0:T(8,128)S(1)} %multiply_add_fusion.3), channel_id=1, source_target_pairs={{4,8},{8,4},{5,9},{9,5},{6,10},{10,6},{7,11},{11,7},{20,24},{24,20... | collective-permute-start | bytes 393224 | tf_op jit(solution)/shard_map/ppermute | solution.py:534
  20.9 18.6 %collective-permute-start.5 = (f32[2,128,128]{2,1,0:T(8,128)S(1)}, f32[2,128,128]{2,1,0:T(8,128)S(1)}, u32[]{:S(2)}, u32[]{:S(2)}) collective-permute-start(f32[2,128,128]{2,1,0:T(8,128)S(1)} %get-tuple-element.108), channel_id=1, source_target_pairs={{8,12},{4,0},{9,13},{5,1},{10,14},{6,2},{11,15},{7,3},{24,28},{20,... | collective-permute-start | bytes 393224 | tf_op jit(solution)/shard_map/ppermute | solution.py:534
  22.3 17.1 %collective-permute-start.4 = (f32[2,128,128]{2,1,0:T(8,128)S(1)}, f32[2,128,128]{2,1,0:T(8,128)S(1)}, u32[]{:S(2)}, u32[]{:S(2)}) collective-permute-start(f32[2,128,128]{2,1,0:T(8,128)S(1)} %get-tuple-element.105), channel_id=1, source_target_pairs={{8,12},{4,0},{9,13},{5,1},{10,14},{6,2},{11,15},{7,3},{24,28},{20,... | collective-permute-start | bytes 393224 | tf_op jit(solution)/shard_map/ppermute | solution.py:534
  26.2 4.8 %collective-permute-start.6 = (f32[4,64]{1,0:T(4,128)S(1)}, f32[4,64]{1,0:T(4,128)S(1)}, u32[]{:S(2)}, u32[]{:S(2)}) collective-permute-start(f32[4,64]{1,0:T(4,128)S(1)} %multiply_add_fusion.4), channel_id=1, source_target_pairs={{0,16},{16,0},{1,17},{17,1},{2,18},{18,2},{3,19},{19,3},{4,20},{20... | collective-permute-start | bytes 3080 | tf_op jit(solution)/shard_map/ppermute | solution.py:578
  31.1 13.8 %collective-permute-start.9 = (f32[4,64]{1,0:T(4,128)S(1)}, f32[4,64]{1,0:T(4,128)S(1)}, u32[]{:S(2)}, u32[]{:S(2)}) collective-permute-start(f32[4,64]{1,0:T(4,128)S(1)} %add_add_fusion.1), channel_id=1, source_target_pairs={{0,12},{4,8},{8,4},{12,0},{1,13},{5,9},{9,5},{13,1},{2,14},{6,10},... | collective-permute-start | bytes 3080 | tf_op jit(solution)/shard_map/ppermute | solution.py:581
  33.6 11.3 %collective-permute-start.8 = (f32[4,64]{1,0:T(4,128)S(1)}, f32[4,64]{1,0:T(4,128)S(1)}, u32[]{:S(2)}, u32[]{:S(2)}) collective-permute-start(f32[4,64]{1,0:T(4,128)S(1)} %add_add_fusion.1), channel_id=1, source_target_pairs={{0,8},{4,12},{8,0},{12,4},{1,9},{5,13},{9,1},{13,5},{2,10},{6,14},... | collective-permute-start | bytes 3080 | tf_op jit(solution)/shard_map/ppermute | solution.py:581
  39.4 5.5 %collective-permute-start.7 = (f32[4,64]{1,0:T(4,128)S(1)}, f32[4,64]{1,0:T(4,128)S(1)}, u32[]{:S(2)}, u32[]{:S(2)}) collective-permute-start(f32[4,64]{1,0:T(4,128)S(1)} %add_add_fusion.1), channel_id=1, source_target_pairs={{0,4},{4,0},{8,12},{12,8},{1,5},{5,1},{9,13},{13,9},{2,6},{6,2},{1... | collective-permute-start | bytes 3080 | tf_op jit(solution)/shard_map/ppermute | solution.py:581

commit v10 on v8

--- a/solution.py
+++ b/solution.py
@@ -10,7 +10,7 @@
 
 CHUNK = 128
 PARTS = 2
-UNROLL = 4
+UNROLL = 8
 PRECISE = lax.Precision.HIGHEST
 F32 = jnp.float32
 BF16 = jnp.bfloat16
@@ -310,11 +310,14 @@
 
 def merge_kernel(head_width, *refs):
     q_ref, k_ref, v_ref, cot_ref, gain_ref, flag_ref, fac_ref = refs[:7]
-    partial_refs, gate_refs, first_refs, second_refs, last_refs = (
-        refs[7 + i * PARTS : 7 + (i + 1) * PARTS] for i in range(5)
-    )
-    refs = refs[7 + 5 * PARTS :]
-    targets, dgate_ref, staged, entering, leaving, sems = refs[:4], *refs[4:]
+    all_heads = gain_ref.shape[0]
+    partial_refs, gate_refs = (
+        refs[7 + i * all_heads : 7 + (i + 1) * all_heads] for i in range(2)
+    )
+    refs = refs[7 + 2 * all_heads :]
+    first_refs, second_refs, last_refs = (refs[i * PARTS : (i + 1) * PARTS] for i in range(3))
+    refs = refs[3 * PARTS :]
+    targets, dgate_ref, staged, matrices, sems = refs[:4], *refs[4:]
     heads = first_refs[0].shape[0]
     steps = sems.shape[0]
     num_chunks = fac_ref.shape[0] // 8
@@ -331,8 +334,7 @@
         ]
 
     gain_columns = jnp.transpose(jnp.concatenate([gain_ref[...], gain_ref[...]], axis=0))
-    entering[...] = jnp.zeros_like(entering)
-    leaving[...] = jnp.zeros_like(leaving)
+    matrices[...] = jnp.zeros_like(matrices)
     last_factors = fac_ref[(num_chunks - 1) * 8 : num_chunks * 8, CHUNK - 1 : CHUNK]
     low = jnp.broadcast_to(flag_ref[2:3, :], (head_width, head_width)) > 0.5
     constants = []
@@ -345,24 +347,30 @@
             second = second_refs[part][head] + last_refs[part][head]
             state = jnp.where(low, first, second) * gain
             later = jnp.where(low, second, first)
-            entering[part, own, own] = (state * scale).astype(BF16)
-            leaving[part, own, own] = (later * gain).astype(BF16)
+            entering = (state * scale).astype(BF16)
+            leaving = (later * gain).astype(BF16)
+            for i, matrix in enumerate(
+                (entering, jnp.transpose(entering), leaving, jnp.transpose(leaving))
+            ):
+                matrices[part, i, own, own] = matrix
             constants.append(total_of(state * later) * last_factors[row : row + 1])
 
-    gate_sums, kept_sums = {}, {}
+    gate_sums, kept_sums, totals = {}, {}, {}
     for step in range(steps):
         numbers = range(step * chunks, (step + 1) * chunks)
         products, results = {}, {}
-        for number in numbers:
-            rows = slice(number * CHUNK, (number + 1) * CHUNK)
-            for part in range(PARTS):
-                group = slice(part * group_width, (part + 1) * group_width)
-                products[number, part] = (
-                    dot_nn(q_ref[0, rows, group], entering[part]),
-                    dot_nt(cot_ref[0, rows, group], entering[part]),
-                    dot_nt(v_ref[0, rows, group], leaving[part]),
-                    dot_nn(k_ref[0, rows, group], leaving[part]),
-                )
+        at = slice(step * block, (step + 1) * block)
+        for part in range(PARTS):
+            group = slice(part * group_width, (part + 1) * group_width)
+            q_out, cot_out, k_out, v_out = (
+                dot_nn(ref[0, at, group], matrices[part, i])
+                for i, ref in enumerate((q_ref, cot_ref, k_ref, v_ref))
+            )
+            for i, number in enumerate(numbers):
+                rows = slice(i * CHUNK, (i + 1) * CHUNK)
+                products[number, part] = [
+                    product[rows] for product in (q_out, cot_out, v_out, k_out)
+                ]
         for number in numbers:
             columns = jnp.transpose(fac_ref[number * 8 : number * 8 + 8, :])
             rows = slice(number * CHUNK, (number + 1) * CHUNK)
@@ -378,7 +386,7 @@
                     )
                 )
                 results[number, row] = [
-                    (partial_refs[part][i, rows, lanes].astype(F32) + added).astype(BF16)
+                    (partial_refs[row][i, rows, :].astype(F32) + added).astype(BF16)
                     for i, added in enumerate((across, dq, dk, written))
                 ]
                 kept = written * v_ref[0, rows, wide].astype(F32)
@@ -386,6 +394,7 @@
                     across * cot_ref[0, rows, wide].astype(F32) - kept, axis=1, keepdims=True
                 )
                 gate_sums[number, row] = later_sums(balance)
+                totals[number, row] = jnp.sum(balance, axis=0, keepdims=True)
                 kept_sums[number, row] = jnp.sum(kept, axis=0, keepdims=True)
         for number in numbers:
             rows = slice(number * CHUNK, (number + 1) * CHUNK)
@@ -397,16 +406,14 @@
             copy.start(priority=i % 2)
 
     for row in range(PARTS * heads):
-        part, head = divmod(row, heads)
         kept = sum(kept_sums[number, row] for number in range(num_chunks))
         base = jnp.sum(kept, axis=1, keepdims=True) + constants[row]
         for number in range(num_chunks - 1, -1, -1):
             lanes = slice(number * CHUNK, (number + 1) * CHUNK)
-            sums = gate_sums[number, row]
             dgate_ref[0, row : row + 1, lanes] = (
-                gate_refs[part][0, head : head + 1, lanes] + sums + base
-            )
-            base = base + sums[:, 0:1]
+                gate_refs[row][0, :, lanes] + gate_sums[number, row] + base
+            )
+            base = base + totals[number, row]
     for step in range(steps):
         for copy in copies(step):
             copy.wait()
@@ -441,8 +448,7 @@
     table = shape_of(rows, CHUNK)
     states = shape_of(heads, head_width, head_width)
     decays = shape_of(heads, 1, head_width)
-    part_gates = shape_of(1, heads, tokens)
-    partials = shape_of(4, tokens, part_width, dtype=BF16)
+    partials = shape_of(4, tokens, head_width, dtype=BF16)
     streams = (queries, keys_raw, values, cotangent)
     product = 2 * tokens * part_width * head_width
 
@@ -466,22 +472,22 @@
             name="shard_ends",
         )(small, *streams)
 
-    def local(part, gain, cum, fac):
+    def local(row, cum):
         return pl.pallas_call(
-            functools.partial(local_kernel, head_width, part),
+            functools.partial(local_kernel, head_width, row),
             in_specs=[vmem] * 7,
             out_specs=[vmem] * 3,
-            out_shape=[partials, part_gates, shape_of(heads, head_width)],
+            out_shape=[partials, shape_of(1, 1, tokens), shape_of(1, head_width)],
             scratch_shapes=[
-                pltpu.VMEM((num_chunks, heads, head_width, head_width), BF16),
-                pltpu.VMEM((heads, head_width, head_width), F32),
+                pltpu.VMEM((num_chunks, 1, head_width, head_width), BF16),
+                pltpu.VMEM((1, head_width, head_width), F32),
             ],
             compiler_params=pltpu.CompilerParams(vmem_limit_bytes=24 << 20),
             cost_estimate=pl.CostEstimate(
-                flops=12 * product, bytes_accessed=16 * tokens * part_width, transcendentals=0
+                flops=12 * product // heads, bytes_accessed=16 * tokens * head_width, transcendentals=0
             ),
-            name=f"local_{part}",
-        )(*held, gain, cum, fac)
+            name=f"local_{row}",
+        )(*held, gain, cum, chunk_fac)
 
     def merge(*arrays):
         return pl.pallas_call(
@@ -491,8 +497,7 @@
             out_shape=[shape_of(1, tokens, width, dtype=BF16)] * 4 + [shape_of(*gates.shape)],
             scratch_shapes=[
                 pltpu.VMEM((4, tokens, width), BF16),
-                pltpu.VMEM((PARTS, part_width, part_width), BF16),
-                pltpu.VMEM((PARTS, part_width, part_width), BF16),
+                pltpu.VMEM((PARTS, 4, part_width, part_width), BF16),
                 pltpu.SemaphoreType.DMA((steps, 4)),
             ],
             compiler_params=pltpu.CompilerParams(vmem_limit_bytes=24 << 20),
@@ -508,11 +513,14 @@
     held = results[3 * PARTS + 5 :]
     sent = [[] for _ in range(PARTS)]
     arrived = [[] for _ in range(PARTS)]
-    local_parts = [None] * PARTS
 
     def send(part, hop):
         payload = near[part] if hop <= middle else far[part]
         if hop > 0:
+            if part > 0:
+                arrived[part][-1], _ = lax.optimization_barrier(
+                    (arrived[part][-1], sent[part - 1][hop])
+                )
             payload = payload + decay[part] * arrived[part][-1]
         sent[part].append(payload)
         arrived[part].append(
@@ -521,30 +529,38 @@
             )
         )
 
-    for part in range(PARTS):
-        send(part, 0)
+    locals_, per_hop = [], [3, 1, 0]
     for hop in range(count - 1):
-        if hop < PARTS:
+        for part in range(PARTS):
+            send(part, hop)
+        for _ in range(per_hop[hop] if hop < 3 else 0):
             local_cum = cum
             if hop > 0:
-                local_cum, _ = lax.optimization_barrier((cum, arrived[0][hop - 1]))
-            local_parts[hop] = list(local(hop, gain, local_cum, chunk_fac))
+                local_cum, *_ = lax.optimization_barrier((cum, *[own[hop] for own in sent]))
+            locals_.append(list(local(len(locals_), local_cum)))
             if hop + 1 < count - 1:
-                local_parts[hop][2], arrived[0][-1] = lax.optimization_barrier(
-                    (local_parts[hop][2], arrived[0][-1])
+                locals_[-1][2], arrived[0][-1] = lax.optimization_barrier(
+                    (locals_[-1][2], arrived[0][-1])
                 )
-        if hop + 1 < count - 1:
-            for part in range(PARTS):
-                send(part, hop + 1)
 
     terms = []
     for part in range(PARTS):
         crossed = jnp.sum(sent[part][middle] * arrived[part][middle], axis=2)
-        term = local_parts[part][2] + flags[0:1] * crossed
+        term = flags[0:1] * crossed
         if middle > 0:
             term = term + jnp.sum(sum(arrived[part][:middle]) * far[part], axis=2)
         terms.append(term)
-    gain_term = jnp.concatenate(terms, axis=0)
+    gain_term = jnp.concatenate(terms, axis=0) + jnp.concatenate(
+        [local_part[2] for local_part in locals_], axis=0
+    )
+
+    zeros = jnp.zeros(states.shape, F32)
+    if middle == 1:
+        firsts, seconds = ([own[i] for own in arrived] for i in range(2))
+    else:
+        firsts = [sum(own[:middle], zeros) for own in arrived]
+        seconds = [sum(own[middle:-1], zeros) for own in arrived]
+    lasts = [own[-1] for own in arrived]
     half = head_width // lax.axis_size("dp")
     second_half = flags[1:2, :half]
     lower_half, upper_half = gain_term[:, :half], gain_term[:, half:]
@@ -564,18 +580,12 @@
             pending += [exchanged(grad_gain, reach * 2), exchanged(grad_gain, reach * 3)]
         reach *= 2 * min(len(pending), 2)
 
-    zeros = jnp.zeros(states.shape, F32)
-    if middle == 1:
-        firsts, seconds = ([own[i] for own in arrived] for i in range(2))
-    else:
-        firsts = [sum(own[:middle], zeros) for own in arrived]
-        seconds = [sum(own[middle:-1], zeros) for own in arrived]
     done = list(
         merge(
             *held, gain, flags, shard_fac,
-            *[local_part[0] for local_part in local_parts],
-            *[local_part[1] for local_part in local_parts],
-            *firsts, *seconds, *[own[-1] for own in arrived],
+            *[local_part[0] for local_part in locals_],
+            *[local_part[1] for local_part in locals_],
+            *firsts, *seconds, *lasts,
         )
     )
     pending, done[4] = lax.optimization_barrier((pending, done[4]))

time: 44.3 us -> 45.7 us (1.032)
  starting transfers between devices: 17.4 us -> 18.5 us
  Pallas kernels: 20 us -> 20.5 us
    ppermute x3, starting transfers between devices: 7.2 us -> 8.17 us  [exchanged(): return lax.ppermute(array, 'ctx', [(i, i ^ reach) for i in range(count)])]
    pallas_call x2 -> x4, Pallas kernels: 9.69 us -> 9.75 us  [local(): pl.pallas_call(functools.partial(local_kernel, head_width, row), in_specs...]
where the time goes in v10:
time: 45.7 us; the launch traced here: 45.4 us
  Pallas kernels  20.5 us (45%)
  starting transfers between devices  18.5 us (40%)
  waiting for transfers between devices  3.01 us (7%)
  other arithmetic  2.51 us (5%)
  between operations  0.85 us (2%)
    ppermute x6, starting transfers between devices, send(): lax.ppermute(payload, 'ctx', [(hop, hop + 1), (count - 1 - hop, count - 2...  10.3 us
    pallas_call x4, Pallas kernels, local(): pl.pallas_call(functools.partial(local_kernel, head_width, row), in_specs...  9.75 us
    ppermute x3, starting transfers between devices, exchanged(): return lax.ppermute(array, 'ctx', [(i, i ^ reach) for i in range(count)])  8.17 us
    pallas_call x1, Pallas kernels, merge(): pl.pallas_call(functools.partial(merge_kernel, head_width), in_specs=[vme...  7.08 us
    pallas_call x1, Pallas kernels, ends(): pl.pallas_call(functools.partial(ends_kernel, head_width, lengths.shape[1...  3.64 us
    ppermute x6, waiting for transfers between devices, send(): lax.ppermute(payload, 'ctx', [(hop, hop + 1), (count - 1 - hop, count - 2...  3 us
  transfers between devices with their start and end apart: 10, of which 2 were waited for; matrix products, arithmetic and copies ran while one was open for 1% of the time, Pallas kernels for 37%

profile of v10, /device:TPU:0, one launch (start us, length us, event | category | flops | bytes accessed | tf_op | source)
XLA Modules:
  0.0 45.4 jit_solution(8868166681535641731)
XLA Ops:
  0.6 0.7 %pad_convert_fusion = f32[4,128]{1,0:T(4,128)S(1)} fusion(s32[1,16]{1,0:T(1,128)} %param.11), kind=kLoop, calls=%fused_computation.13 | loop fusion | flops 512 | bytes 2112 | tf_op jit(solution)/shard_map/convert_element_type | solution.py:440
  1.3 0.7 %pad_maximum_fusion.refs_0_ = f32[4,1280]{1,0:T(4,128)S(1)} fusion(f32[4,128]{1,0:T(4,128)S(1)} %pad_convert_fusion, f32[4,128]{1,0:T(4,128)S(1)} %copy-done, f32[4,1024]{1,0:T(4,128)} %bitcast.13), kind=kLoop, calls=%fused_computation.8 | loop fusion | flops 10240 | bytes 40960 | tf_op jit(solution)/shard_map/concatenate | solution.py:441
  2.0 3.6 %shard_ends.1 = (f32[2,128,128]{2,1,0:T(8,128)S(1)}, f32[2,128,128]{2,1,0:T(8,128)S(1)}, f32[2,128,128]{2,1,0:T(8,128)S(1)}, f32[2,128,128]{2,1,0:T(8,128)S(1)},...) custom-call(f32[4,1280]{1,0:T(4,128)S(1)} %pad_maximum_fusion.refs_0, ...), custom_call_target="tpu_custom_call" | custom-call | flops 268435456 | bytes 4194304 | tf_op jit(solution)/shard_map/shard_ends/pallas_call | solution.py:459
  5.7 4.9 %collective-permute-start = (f32[2,128,128]{2,1,0:T(8,128)S(1)}, f32[2,128,128]{2,1,0:T(8,128)S(1)}, u32[]{:S(2)}, u32[]{:S(2)}) collective-permute-start(f32[2,128,128]{2,1,0:T(8,128)S(1)} %get-tuple-element.65), channel_id=1, source_target_pairs={{0,4},{12,8},{1,5},{13,9},{2,6},{14,10},{3,7},{15,11},{16,20},{28,... | collective-permute-start | bytes 393224 | tf_op jit(solution)/shard_map/ppermute | solution.py:527
  10.6 1.3 %collective-permute-start.1 = (f32[2,128,128]{2,1,0:T(8,128)S(1)}, f32[2,128,128]{2,1,0:T(8,128)S(1)}, u32[]{:S(2)}, u32[]{:S(2)}) collective-permute-start(f32[2,128,128]{2,1,0:T(8,128)S(1)} %get-tuple-element.73), channel_id=1, source_target_pairs={{0,4},{12,8},{1,5},{13,9},{2,6},{14,10},{3,7},{15,11},{16,20},{28,... | collective-permute-start | bytes 393224 | tf_op jit(solution)/shard_map/ppermute | solution.py:527
  11.9 2.4 %local_0.1 = (bf16[4,1024,128]{2,1,0:T(8,128)(2,1)S(1)}, f32[1,1,1024]{2,1,0:T(1,128)S(1)}, f32[1,128]{1,0:T(1,128)S(1)}) custom-call(bf16[1,1024,512]{2,1,0:T(8,128)(2,1)S(1)} %get-tuple-element.53.q_ref.refs_0_, bf16[1,1024,512]{2,1,0:T(8,128)(2,1)S(1)} %get-tuple-element.54.k_ref.refs_1_, bf16[1,1024,512]{2,1,0:T(8,128)(2,1)S(1)} %get-tuple-element.55.v_ref.refs_2_, ...), custom_call_target="tpu_custom_call" | custom-call | flops 402653184 | bytes 2097152 | tf_op jit(solution)/shard_map/local_0/pallas_call | solution.py:476
  14.3 2.5 %local_1.1 = (bf16[4,1024,128]{2,1,0:T(8,128)(2,1)S(1)}, f32[1,1,1024]{2,1,0:T(1,128)S(1)}, f32[1,128]{1,0:T(1,128)S(1)}) custom-call(bf16[1,1024,512]{2,1,0:T(8,128)(2,1)S(1)} %get-tuple-element.53.q_ref.refs_0_, bf16[1,1024,512]{2,1,0:T(8,128)(2,1)S(1)} %get-tuple-element.54.k_ref.refs_1_, bf16[1,1024,512]{2,1,0:T(8,128)(2,1)S(1)} %get-tuple-element.55.v_ref.refs_2_, ...), custom_call_target="tpu_custom_call" | custom-call | flops 402653184 | bytes 2097152 | tf_op jit(solution)/shard_map/local_1/pallas_call | solution.py:476
  16.8 2.5 %local_2.1 = (bf16[4,1024,128]{2,1,0:T(8,128)(2,1)S(1)}, f32[1,1,1024]{2,1,0:T(1,128)S(1)}, f32[1,128]{1,0:T(1,128)S(1)}) custom-call(bf16[1,1024,512]{2,1,0:T(8,128)(2,1)S(1)} %get-tuple-element.53.q_ref.refs_0_, bf16[1,1024,512]{2,1,0:T(8,128)(2,1)S(1)} %get-tuple-element.54.k_ref.refs_1_, bf16[1,1024,512]{2,1,0:T(8,128)(2,1)S(1)} %get-tuple-element.55.v_ref.refs_2_, ...), custom_call_target="tpu_custom_call" | custom-call | flops 402653184 | bytes 2097152 | tf_op jit(solution)/shard_map/local_2/pallas_call | solution.py:476
  19.3 0.7 %collective-permute-start.2 = (f32[2,128,128]{2,1,0:T(8,128)S(1)}, f32[2,128,128]{2,1,0:T(8,128)S(1)}, u32[]{:S(2)}, u32[]{:S(2)}) collective-permute-start(f32[2,128,128]{2,1,0:T(8,128)S(1)} %multiply_add_fusion.3), channel_id=1, source_target_pairs={{4,8},{8,4},{5,9},{9,5},{6,10},{10,6},{7,11},{11,7},{20,24},{24,20... | collective-permute-start | bytes 393224 | tf_op jit(solution)/shard_map/ppermute | solution.py:527
  20.0 0.7 %collective-permute-start.3 = (f32[2,128,128]{2,1,0:T(8,128)S(1)}, f32[2,128,128]{2,1,0:T(8,128)S(1)}, u32[]{:S(2)}, u32[]{:S(2)}) collective-permute-start(f32[2,128,128]{2,1,0:T(8,128)S(1)} %multiply_add_fusion.2), channel_id=1, source_target_pairs={{4,8},{8,4},{5,9},{9,5},{6,10},{10,6},{7,11},{11,7},{20,24},{24,20... | collective-permute-start | bytes 393224 | tf_op jit(solution)/shard_map/ppermute | solution.py:527
  20.7 2.5 %local_3.1 = (bf16[4,1024,128]{2,1,0:T(8,128)(2,1)S(1)}, f32[1,1,1024]{2,1,0:T(1,128)S(1)}, f32[1,128]{1,0:T(1,128)S(1)}) custom-call(bf16[1,1024,512]{2,1,0:T(8,128)(2,1)S(1)} %get-tuple-element.53.q_ref.refs_0_, bf16[1,1024,512]{2,1,0:T(8,128)(2,1)S(1)} %get-tuple-element.54.k_ref.refs_1_, bf16[1,1024,512]{2,1,0:T(8,128)(2,1)S(1)} %get-tuple-element.55.v_ref.refs_2_, ...), custom_call_target="tpu_custom_call" | custom-call | flops 402653184 | bytes 2097152 | tf_op jit(solution)/shard_map/local_3/pallas_call | solution.py:476
  23.2 0.2 multiply_reduce_fusion.3
  23.3 0.2 multiply_reduce_fusion.1
  23.5 0.1 multiply_add_fusion.4
  23.6 1.3 %collective-permute-start.4 = (f32[2,128,128]{2,1,0:T(8,128)S(1)}, f32[2,128,128]{2,1,0:T(8,128)S(1)}, u32[]{:S(2)}, u32[]{:S(2)}) collective-permute-start(f32[2,128,128]{2,1,0:T(8,128)S(1)} %get-tuple-element.101), channel_id=1, source_target_pairs={{8,12},{4,0},{9,13},{5,1},{10,14},{6,2},{11,15},{7,3},{24,28},{20,... | collective-permute-start | bytes 393224 | tf_op jit(solution)/shard_map/ppermute | solution.py:527
  24.9 1.5 %collective-permute-start.5 = (f32[2,128,128]{2,1,0:T(8,128)S(1)}, f32[2,128,128]{2,1,0:T(8,128)S(1)}, u32[]{:S(2)}, u32[]{:S(2)}) collective-permute-start(f32[2,128,128]{2,1,0:T(8,128)S(1)} %get-tuple-element.104), channel_id=1, source_target_pairs={{8,12},{4,0},{9,13},{5,1},{10,14},{6,2},{11,15},{7,3},{24,28},{20,... | collective-permute-start | bytes 393224 | tf_op jit(solution)/shard_map/ppermute | solution.py:527
  26.4 0.1 add_add_fusion.1
  26.5 5.7 %collective-permute-start.7 = (f32[4,64]{1,0:T(4,128)S(1)}, f32[4,64]{1,0:T(4,128)S(1)}, u32[]{:S(2)}, u32[]{:S(2)}) collective-permute-start(f32[4,64]{1,0:T(4,128)S(1)} %add_add_fusion.1), channel_id=1, source_target_pairs={{0,4},{4,0},{8,12},{12,8},{1,5},{5,1},{9,13},{13,9},{2,6},{6,2},{1... | collective-permute-start | bytes 3080 | tf_op jit(solution)/shard_map/ppermute | solution.py:572
  32.2 0.6 %collective-permute-start.8 = (f32[4,64]{1,0:T(4,128)S(1)}, f32[4,64]{1,0:T(4,128)S(1)}, u32[]{:S(2)}, u32[]{:S(2)}) collective-permute-start(f32[4,64]{1,0:T(4,128)S(1)} %add_add_fusion.1), channel_id=1, source_target_pairs={{0,8},{4,12},{8,0},{12,4},{1,9},{5,13},{9,1},{13,5},{2,10},{6,14},... | collective-permute-start | bytes 3080 | tf_op jit(solution)/shard_map/ppermute | solution.py:572
  32.9 1.8 %collective-permute-start.9 = (f32[4,64]{1,0:T(4,128)S(1)}, f32[4,64]{1,0:T(4,128)S(1)}, u32[]{:S(2)}, u32[]{:S(2)}) collective-permute-start(f32[4,64]{1,0:T(4,128)S(1)} %add_add_fusion.1), channel_id=1, source_target_pairs={{0,12},{4,8},{8,4},{12,0},{1,13},{5,9},{9,5},{13,1},{2,14},{6,10},... | collective-permute-start | bytes 3080 | tf_op jit(solution)/shard_map/ppermute | solution.py:572
  34.7 0.3 collective-permute-done.4.refs_19_
  35.0 2.7 %collective-permute-done.5.refs_20_ = f32[2,128,128]{2,1,0:T(8,128)S(1)} collective-permute-done((f32[2,128,128]{2,1,0:T(8,128)S(1)}, f32[2,128,128]{2,1,0:T(8,128)S(1)}, u32[]{:S(2)}, u32[]{:S(2)}) %collective-permute-start.5) | collective-permute-done | bytes 131104 | tf_op jit(solution)/shard_map/ppermute | solution.py:527
  37.7 7.1 %merge.1 = (bf16[1,1024,512]{2,1,0:T(8,128)(2,1)}, bf16[1,1024,512]{2,1,0:T(8,128)(2,1)}, bf16[1,1024,512]{2,1,0:T(8,128)(2,1)}, bf16[1,1024,512]{2,1,0:T(8,128)(2,1)}, f32[1,4,1024]{2,1,0:T(4,128)}) custom-call(bf16[1,1024,512]{2,1,0:T(8,128)(2,1)S(1)} %get-tuple-element.53.q_ref.refs_0_, bf16[1,1024,512]{2,1,0:T(8,128)(2,1)S(1)} %get-tuple-element.54.k_ref.refs_1_, ...), custom_call_target="tpu_custom_call" | custom-call | flops 536870912 | bytes 12582912 | tf_op jit(solution)/shard_map/merge/pallas_call | solution.py:493
  44.8 0.6 %add_add_fusion = f32[4,64]{1,0:T(4,128)} fusion(f32[4,64]{1,0:T(4,128)S(1)} %collective-permute-done.8, f32[4,64]{1,0:T(4,128)S(1)} %collective-permute-done.9, f32[4,64]{1,0:T(4,128)S(1)} %add_add_fusion.1, f32[4,64]{1,0:T(4,128)S(1)} %collective-permute-done.7), kind=kLoop, calls=%fused_computation.10 | loop fusion | flops 768 | bytes 5120 | tf_op jit(solution)/shard_map/add | solution.py:425
  (17 shorter events, 0.1 us)
Async XLA Ops:
  0.6 0.7 %copy-start = (f32[4,128]{1,0:T(4,128)S(1)}, f32[4,128]{1,0:T(4,128)}, u32[]{:S(2)}) copy-start(f32[4,128]{1,0:T(4,128)} %param.12) | copy-start | bytes 6148
  5.7 13.6 %collective-permute-start = (f32[2,128,128]{2,1,0:T(8,128)S(1)}, f32[2,128,128]{2,1,0:T(8,128)S(1)}, u32[]{:S(2)}, u32[]{:S(2)}) collective-permute-start(f32[2,128,128]{2,1,0:T(8,128)S(1)} %get-tuple-element.65), channel_id=1, source_target_pairs={{0,4},{12,8},{1,5},{13,9},{2,6},{14,10},{3,7},{15,11},{16,20},{28,... | collective-permute-start | bytes 393224 | tf_op jit(solution)/shard_map/ppermute | solution.py:527
  10.6 9.4 %collective-permute-start.1 = (f32[2,128,128]{2,1,0:T(8,128)S(1)}, f32[2,128,128]{2,1,0:T(8,128)S(1)}, u32[]{:S(2)}, u32[]{:S(2)}) collective-permute-start(f32[2,128,128]{2,1,0:T(8,128)S(1)} %get-tuple-element.73), channel_id=1, source_target_pairs={{0,4},{12,8},{1,5},{13,9},{2,6},{14,10},{3,7},{15,11},{16,20},{28,... | collective-permute-start | bytes 393224 | tf_op jit(solution)/shard_map/ppermute | solution.py:527
  19.3 3.9 %collective-permute-start.2 = (f32[2,128,128]{2,1,0:T(8,128)S(1)}, f32[2,128,128]{2,1,0:T(8,128)S(1)}, u32[]{:S(2)}, u32[]{:S(2)}) collective-permute-start(f32[2,128,128]{2,1,0:T(8,128)S(1)} %multiply_add_fusion.3), channel_id=1, source_target_pairs={{4,8},{8,4},{5,9},{9,5},{6,10},{10,6},{7,11},{11,7},{20,24},{24,20... | collective-permute-start | bytes 393224 | tf_op jit(solution)/shard_map/ppermute | solution.py:527
  20.0 3.3 %collective-permute-start.3 = (f32[2,128,128]{2,1,0:T(8,128)S(1)}, f32[2,128,128]{2,1,0:T(8,128)S(1)}, u32[]{:S(2)}, u32[]{:S(2)}) collective-permute-start(f32[2,128,128]{2,1,0:T(8,128)S(1)} %multiply_add_fusion.2), channel_id=1, source_target_pairs={{4,8},{8,4},{5,9},{9,5},{6,10},{10,6},{7,11},{11,7},{20,24},{24,20... | collective-permute-start | bytes 393224 | tf_op jit(solution)/shard_map/ppermute | solution.py:527
  23.6 2.8 %collective-permute-start.6 = (f32[4,64]{1,0:T(4,128)S(1)}, f32[4,64]{1,0:T(4,128)S(1)}, u32[]{:S(2)}, u32[]{:S(2)}) collective-permute-start(f32[4,64]{1,0:T(4,128)S(1)} %multiply_add_fusion.4), channel_id=1, source_target_pairs={{0,16},{16,0},{1,17},{17,1},{2,18},{18,2},{3,19},{19,3},{4,20},{20... | collective-permute-start | bytes 3080 | tf_op jit(solution)/shard_map/ppermute | solution.py:569
  23.6 11.3 %collective-permute-start.4 = (f32[2,128,128]{2,1,0:T(8,128)S(1)}, f32[2,128,128]{2,1,0:T(8,128)S(1)}, u32[]{:S(2)}, u32[]{:S(2)}) collective-permute-start(f32[2,128,128]{2,1,0:T(8,128)S(1)} %get-tuple-element.101), channel_id=1, source_target_pairs={{8,12},{4,0},{9,13},{5,1},{10,14},{6,2},{11,15},{7,3},{24,28},{20,... | collective-permute-start | bytes 393224 | tf_op jit(solution)/shard_map/ppermute | solution.py:527
  24.9 12.7 %collective-permute-start.5 = (f32[2,128,128]{2,1,0:T(8,128)S(1)}, f32[2,128,128]{2,1,0:T(8,128)S(1)}, u32[]{:S(2)}, u32[]{:S(2)}) collective-permute-start(f32[2,128,128]{2,1,0:T(8,128)S(1)} %get-tuple-element.104), channel_id=1, source_target_pairs={{8,12},{4,0},{9,13},{5,1},{10,14},{6,2},{11,15},{7,3},{24,28},{20,... | collective-permute-start | bytes 393224 | tf_op jit(solution)/shard_map/ppermute | solution.py:527
  26.5 18.3 %collective-permute-start.7 = (f32[4,64]{1,0:T(4,128)S(1)}, f32[4,64]{1,0:T(4,128)S(1)}, u32[]{:S(2)}, u32[]{:S(2)}) collective-permute-start(f32[4,64]{1,0:T(4,128)S(1)} %add_add_fusion.1), channel_id=1, source_target_pairs={{0,4},{4,0},{8,12},{12,8},{1,5},{5,1},{9,13},{13,9},{2,6},{6,2},{1... | collective-permute-start | bytes 3080 | tf_op jit(solution)/shard_map/ppermute | solution.py:572
  32.2 12.5 %collective-permute-start.8 = (f32[4,64]{1,0:T(4,128)S(1)}, f32[4,64]{1,0:T(4,128)S(1)}, u32[]{:S(2)}, u32[]{:S(2)}) collective-permute-start(f32[4,64]{1,0:T(4,128)S(1)} %add_add_fusion.1), channel_id=1, source_target_pairs={{0,8},{4,12},{8,0},{12,4},{1,9},{5,13},{9,1},{13,5},{2,10},{6,14},... | collective-permute-start | bytes 3080 | tf_op jit(solution)/shard_map/ppermute | solution.py:572
  32.9 11.9 %collective-permute-start.9 = (f32[4,64]{1,0:T(4,128)S(1)}, f32[4,64]{1,0:T(4,128)S(1)}, u32[]{:S(2)}, u32[]{:S(2)}) collective-permute-start(f32[4,64]{1,0:T(4,128)S(1)} %add_add_fusion.1), channel_id=1, source_target_pairs={{0,12},{4,8},{8,4},{12,0},{1,13},{5,9},{9,5},{13,1},{2,14},{6,10},... | collective-permute-start | bytes 3080 | tf_op jit(solution)/shard_map/ppermute | solution.py:572

commit v11 on v7

--- a/solution.py
+++ b/solution.py
@@ -10,7 +10,7 @@
 
 CHUNK = 128
 PARTS = 2
-UNROLL = 4
+UNROLL = 8
 PRECISE = lax.Precision.HIGHEST
 F32 = jnp.float32
 BF16 = jnp.bfloat16
@@ -44,7 +44,7 @@
     return jnp.sum(jnp.where(kept, column, 0.0), axis=0, keepdims=True)
 
 
-def decay_tables(docs, place_ref, small_ref, spread, cum_ref, chunk_fac_ref, shard_fac_ref):
+def decay_tables(docs, ctx, small_ref, spread, cum_ref, chunk_fac_ref, shard_fac_ref):
     rows = cum_ref.shape[0]
     num_chunks = rows // 8
     tokens = num_chunks * CHUNK
@@ -64,7 +64,7 @@
     )
     others = dot_nn((same & outside).astype(F32), totals, PRECISE)
 
-    first = place_ref[0] * tokens
+    first = ctx * tokens
     chunk_first = first + (iota((rows, CHUNK), 0) // 8) * CHUNK
     from_start = iota((rows, CHUNK), 0) % 8 < 4
     chunk_anchor = jnp.where(from_start, chunk_first - 1, chunk_first + (CHUNK - 1)).astype(F32)
@@ -90,13 +90,13 @@
 
 
 def ends_kernel(head_width, docs, half_ctx, *refs):
-    place_ref, small_ref = refs[:2]
-    sources = refs[2:6]
+    small_ref, sources = refs[0], refs[1:5]
+    ctx, dp = lax.axis_index("ctx"), lax.axis_index("dp")
     near_refs, far_refs, decay_refs = (
-        refs[6 + i * PARTS : 6 + (i + 1) * PARTS] for i in range(3)
+        refs[5 + i * PARTS : 5 + (i + 1) * PARTS] for i in range(3)
     )
     (cum_ref, chunk_fac_ref, shard_fac_ref, gain_ref, flag_ref, q_ref, k_ref, v_ref, cot_ref,
-     spread, sems) = refs[6 + 3 * PARTS :]
+     spread, sems) = refs[5 + 3 * PARTS :]
     heads = near_refs[0].shape[0]
     rows = shard_fac_ref.shape[0]
     steps = sems.shape[0]
@@ -114,7 +114,7 @@
     for step in range(steps):
         for i, copy in enumerate(copies(step)):
             copy.start(priority=i % 2)
-    decay_tables(docs, place_ref, small_ref, spread, cum_ref, chunk_fac_ref, shard_fac_ref)
+    decay_tables(docs, ctx, small_ref, spread, cum_ref, chunk_fac_ref, shard_fac_ref)
     gain_ref[...] = small_ref[:, tokens : tokens + head_width]
     for part in range(PARTS):
         for head in range(heads):
@@ -149,11 +149,12 @@
             grad = dot_nn(turned(q_ref, step, row, head_width ** (-0.5)), cot_ref[0, at, lanes])
             ends[row] = ends[row] + end if step else end
             grads[row] = grads[row] + grad if step else grad
-    middle = jnp.where(place_ref[0] == half_ctx - 1, 1.0, 0.0)
+    middle = jnp.where(ctx == half_ctx - 1, 1.0, 0.0)
+    low = ctx < half_ctx
+    row = iota(flag_ref.shape, 0)
     flag_ref[...] = jnp.where(
-        iota(flag_ref.shape, 0) == 0, middle, place_ref[1].astype(F32)
+        row == 0, middle, jnp.where(row == 1, dp.astype(F32), jnp.where(low, 1.0, 0.0))
     )
-    low = place_ref[0] < half_ctx
     for part in range(PARTS):
         for head in range(heads):
             row = part * heads + head
@@ -307,14 +308,15 @@
     lax.fori_loop(0, groups, forward_group, 0)
 
 
-def merge_kernel(head_width, part, half_ctx, *refs):
-    q_ref, k_ref, v_ref, cot_ref, partial_ref = refs[:5]
-    place_ref, gain_ref, fac_ref, first_ref, second_ref, last_ref, dgate_in = refs[5:12]
-    refs = refs[12:]
+def merge_kernel(head_width, part, *refs):
+    q_ref, k_ref, v_ref, cot_ref, gain_ref, flag_ref, fac_ref = refs[:7]
+    first_ref, second_ref, last_ref = refs[7:10]
+    heads = first_ref.shape[0]
+    partial_refs, gate_refs = refs[10 : 10 + heads], refs[10 + heads : 10 + 2 * heads]
+    refs = refs[10 + 2 * heads :]
     if part > 0:
         before_ref, refs = refs[0], refs[5:]
     targets, dgate_ref, staged, entering, leaving, sems = refs[:4], *refs[4:]
-    heads = first_ref.shape[0]
     steps = sems.shape[0]
     num_chunks = fac_ref.shape[0] // 8
     chunks = num_chunks // steps
@@ -332,7 +334,7 @@
         ]
 
     def arrived(head):
-        low = place_ref[0] < half_ctx
+        low = jnp.broadcast_to(flag_ref[2:3, :], (head_width, head_width)) > 0.5
         first, second = first_ref[head], second_ref[head] + last_ref[head]
         return jnp.where(low, first, second), jnp.where(low, second, first)
 
@@ -351,7 +353,7 @@
         leaving[own, own] = (later * gain).astype(BF16)
         constants.append(total_of(state * later) * last[row : row + 1])
 
-    gate_sums, kept_sums = {}, {}
+    gate_sums, kept_sums, totals = {}, {}, {}
     for step in range(steps):
         numbers = range(step * chunks, (step + 1) * chunks)
         products, results = {}, {}
@@ -378,7 +380,7 @@
                     )
                 )
                 results[number, head] = [
-                    (partial_ref[i, rows, lanes].astype(F32) + added).astype(BF16)
+                    (partial_refs[head][i, rows, :].astype(F32) + added).astype(BF16)
                     for i, added in enumerate((across, dq, dk, written))
                 ]
                 kept = written * v_ref[0, rows, wide].astype(F32)
@@ -386,6 +388,7 @@
                     across * cot_ref[0, rows, wide].astype(F32) - kept, axis=1, keepdims=True
                 )
                 gate_sums[number, head] = later_sums(balance)
+                totals[number, head] = jnp.sum(balance, axis=0, keepdims=True)
                 kept_sums[number, head] = jnp.sum(kept, axis=0, keepdims=True)
         for number in numbers:
             rows = slice(number * CHUNK, (number + 1) * CHUNK)
@@ -404,14 +407,19 @@
         base = jnp.sum(kept, axis=1, keepdims=True) + constants[head]
         for number in range(num_chunks - 1, -1, -1):
             lanes = slice(number * CHUNK, (number + 1) * CHUNK)
-            sums = gate_sums[number, head]
             dgate_ref[0, row : row + 1, lanes] = (
-                dgate_in[0, head : head + 1, lanes] + sums + base
-            )
-            base = base + sums[:, 0:1]
+                gate_refs[head][0, :, lanes] + gate_sums[number, head] + base
+            )
+            base = base + totals[number, head]
     for step in range(steps):
         for copy in copies(step):
             copy.wait()
+
+
+def summed(own, others):
+    if len(others) == 1:
+        return own + others[0]
+    return (own + others[0]) + (others[1] + others[2])
 
 
 def shards(queries, keys_raw, values, gates, lengths, key_gain, cotangent):
@@ -423,35 +431,31 @@
     rows = num_chunks * 8
     block = min(256, tokens)
     steps = tokens // block
-    ctx = lax.axis_index("ctx")
     count = lax.axis_size("ctx")
     middle = count // 2 - 1
     docs = lengths.shape[1]
-    sizes = jnp.pad(lengths.astype(F32), ((0, all_heads - 1), (0, CHUNK - docs)))
+    sizes = jnp.pad(lengths, ((0, all_heads - 1), (0, CHUNK - docs))).astype(F32)
     small = jnp.concatenate([gates[0], key_gain, sizes], axis=1)
-    place = jnp.stack([ctx, lax.axis_index("dp")]).astype(jnp.int32)
 
     def shape_of(*shape, dtype=F32):
         return jax.ShapeDtypeStruct(shape, dtype)
 
     hbm = pl.BlockSpec(memory_space=pltpu.HBM)
-    smem = pl.BlockSpec(memory_space=pltpu.SMEM)
     vmem = pl.BlockSpec(memory_space=pltpu.VMEM)
     table = shape_of(rows, CHUNK)
     states = shape_of(heads, head_width, head_width)
     decays = shape_of(heads, 1, head_width)
-    part_gates = shape_of(1, heads, tokens)
-    partials = shape_of(4, tokens, part_width, dtype=BF16)
+    partials = shape_of(4, tokens, head_width, dtype=BF16)
     streams = (queries, keys_raw, values, cotangent)
     product = 2 * tokens * part_width * head_width
 
     def ends():
         outs = [states] * (2 * PARTS) + [decays] * PARTS + [table] * 3
-        outs += [shape_of(all_heads, head_width), shape_of(2, head_width)]
+        outs += [shape_of(all_heads, head_width), shape_of(4, head_width)]
         outs += [shape_of(1, tokens, width, dtype=BF16)] * 4
         return pl.pallas_call(
             functools.partial(ends_kernel, head_width, lengths.shape[1], count // 2),
-            in_specs=[smem, vmem] + [hbm] * 4,
+            in_specs=[vmem] + [hbm] * 4,
             out_specs=[vmem] * len(outs),
             out_shape=outs,
             scratch_shapes=[
@@ -463,35 +467,35 @@
                 flops=2 * product * PARTS, bytes_accessed=8 * tokens * width, transcendentals=0
             ),
             name="shard_ends",
-        )(place, small, *streams)
-
-    def local(part, gain, cum, fac):
+        )(small, *streams)
+
+    def local(row, cum):
         return pl.pallas_call(
-            functools.partial(local_kernel, head_width, part),
+            functools.partial(local_kernel, head_width, row),
             in_specs=[vmem] * 7,
             out_specs=[vmem] * 3,
-            out_shape=[partials, part_gates, shape_of(heads, head_width)],
+            out_shape=[partials, shape_of(1, 1, tokens), shape_of(1, head_width)],
             scratch_shapes=[
-                pltpu.VMEM((num_chunks, heads, head_width, head_width), BF16),
-                pltpu.VMEM((heads, head_width, head_width), F32),
+                pltpu.VMEM((num_chunks, 1, head_width, head_width), BF16),
+                pltpu.VMEM((1, head_width, head_width), F32),
             ],
             compiler_params=pltpu.CompilerParams(vmem_limit_bytes=24 << 20),
             cost_estimate=pl.CostEstimate(
-                flops=12 * product, bytes_accessed=16 * tokens * part_width, transcendentals=0
+                flops=12 * product // heads, bytes_accessed=16 * tokens * head_width, transcendentals=0
             ),
-            name=f"local_{part}",
-        )(*held, gain, cum, fac)
-
-    def merge(part, arrivals, local_part, done):
+            name=f"local_{row}",
+        )(*held, gain, cum, chunk_fac)
+
+    def merge(part, flag_rows, arrivals, done):
+        own = locals_[part * heads : (part + 1) * heads]
+        inputs = [*held, gain, flag_rows, shard_fac, *arrivals]
+        inputs += [local_part[0] for local_part in own] + [local_part[1] for local_part in own]
+        extra = [done[4], *done[:4]] if part > 0 else []
+        aliases = {len(inputs) + 1 + i: i for i in range(4)} if part > 0 else {}
         full_gates = shape_of(1, (part + 1) * heads, tokens)
-        extra, extra_specs, aliases = [], [], {}
-        if part > 0:
-            extra = [done[4]] + list(done[:4])
-            extra_specs = [vmem] + [hbm] * 4
-            aliases = {13 + i: i for i in range(4)}
         return pl.pallas_call(
-            functools.partial(merge_kernel, head_width, part, count // 2),
-            in_specs=[vmem] * 5 + [smem] + [vmem] * 6 + extra_specs,
+            functools.partial(merge_kernel, head_width, part),
+            in_specs=[vmem] * len(inputs) + ([vmem] + [hbm] * 4 if part > 0 else []),
             out_specs=[hbm] * 4 + [vmem],
             out_shape=[shape_of(1, tokens, width, dtype=BF16)] * 4 + [full_gates],
             scratch_shapes=[
@@ -506,9 +510,7 @@
                 flops=4 * product, bytes_accessed=24 * tokens * part_width, transcendentals=0
             ),
             name=f"merge_{part}",
-        )(
-            *held, local_part[0], place, gain, shard_fac, *arrivals, local_part[1], *extra
-        )
+        )(*inputs, *extra)
 
     results = ends()
     near, far, decay = (results[i * PARTS : (i + 1) * PARTS] for i in range(3))
@@ -516,12 +518,13 @@
     held = results[3 * PARTS + 5 :]
     sent = [[] for _ in range(PARTS)]
     arrived = [[] for _ in range(PARTS)]
-    local_parts = [None] * PARTS
-
-    def send(part, hop):
+
+    def send(part, hop, started):
         payload = near[part] if hop <= middle else far[part]
         if hop > 0:
             payload = payload + decay[part] * arrived[part][-1]
+        if started:
+            payload, *_ = lax.optimization_barrier((payload, *started))
         sent[part].append(payload)
         arrived[part].append(
             lax.ppermute(
@@ -529,44 +532,68 @@
             )
         )
 
-    for part in range(PARTS):
-        send(part, 0)
-    for hop in range(count - 1):
-        if hop < PARTS:
+    locals_, per_stage = [], [2, 1, 1]
+    for stage in range(count - 2 + PARTS):
+        started = []
+        for part in range(PARTS):
+            if 0 <= stage - part < count - 1:
+                send(part, stage - part, started)
+                started.append(sent[part][-1])
+        for _ in range(per_stage[stage] if stage < 3 else 0):
             local_cum = cum
-            if hop > 0:
-                local_cum, _ = lax.optimization_barrier((cum, arrived[0][hop - 1]))
-            local_parts[hop] = list(local(hop, gain, local_cum, chunk_fac))
-            if hop + 1 < count - 1:
-                local_parts[hop][2], arrived[0][-1] = lax.optimization_barrier(
-                    (local_parts[hop][2], arrived[0][-1])
-                )
-        if hop + 1 < count - 1:
-            for part in range(PARTS):
-                send(part, hop + 1)
+            if stage > 0:
+                local_cum, *_ = lax.optimization_barrier((cum, *started))
+            locals_.append(list(local(len(locals_), local_cum)))
+            behind = 0 if stage + 1 < count - 1 else PARTS - 1
+            locals_[-1][2], arrived[behind][-1] = lax.optimization_barrier(
+                (locals_[-1][2], arrived[behind][-1])
+            )
 
     terms = []
     for part in range(PARTS):
         crossed = jnp.sum(sent[part][middle] * arrived[part][middle], axis=2)
-        term = local_parts[part][2] + flags[0:1] * crossed
+        term = flags[0:1] * crossed
         if middle > 0:
             term = term + jnp.sum(sum(arrived[part][:middle]) * far[part], axis=2)
         terms.append(term)
-    gain_term = jnp.concatenate(terms, axis=0)
-    gathered = lax.all_gather(gain_term, ("dp", "ctx"))
-
-    done = None
-    for part in range(PARTS):
-        zeros = jnp.zeros(states.shape, F32)
-        first = sum(arrived[part][:middle], zeros) if middle != 1 else arrived[part][0]
-        second = sum(arrived[part][middle:-1], zeros) if middle != 1 else arrived[part][1]
-        done = list(merge(part, (first, second, arrived[part][-1]), local_parts[part], done))
-    gathered, done[4] = lax.optimization_barrier((gathered, done[4]))
-    total = jnp.sum(gathered, axis=0)
+    gain_term = jnp.concatenate(terms, axis=0) + jnp.concatenate(
+        [local_part[2] for local_part in locals_], axis=0
+    )
+
+    zeros = jnp.zeros(states.shape, F32)
+    if middle == 1:
+        firsts, seconds = ([own[i] for own in arrived] for i in range(2))
+    else:
+        firsts = [sum(own[:middle], zeros) for own in arrived]
+        seconds = [sum(own[middle:-1], zeros) for own in arrived]
+    lasts = [own[-1] for own in arrived]
     half = head_width // lax.axis_size("dp")
     second_half = flags[1:2, :half]
-    grad_gain = (1.0 - second_half) * total[:, :half] + second_half * total[:, half:]
-    return (*done, grad_gain)
+    lower_half, upper_half = gain_term[:, :half], gain_term[:, half:]
+    away = (1.0 - second_half) * upper_half + second_half * lower_half
+    kept = (1.0 - second_half) * lower_half + second_half * upper_half
+    grad_gain = kept + lax.ppermute(away, "dp", [(0, 1), (1, 0)])
+
+    def exchanged(array, reach):
+        return lax.ppermute(array, "ctx", [(i, i ^ reach) for i in range(count)])
+
+    pending, reach = [], 1
+    while reach < count:
+        if pending:
+            grad_gain = summed(grad_gain, pending)
+        pending = [exchanged(grad_gain, reach)]
+        if reach * 2 < count:
+            pending += [exchanged(grad_gain, reach * 2), exchanged(grad_gain, reach * 3)]
+        reach *= 2 * min(len(pending), 2)
+
+    done = []
+    for part in range(PARTS):
+        flag_rows = flags
+        if part < PARTS - 1:
+            flag_rows, _ = lax.optimization_barrier((flags, sent[part + 1][-1]))
+        done = list(merge(part, flag_rows, (firsts[part], seconds[part], lasts[part]), done))
+    pending, done[4] = lax.optimization_barrier((pending, done[4]))
+    return (*done, summed(grad_gain, pending))
 
 
 def solution(mesh):

time: 62.3 us -> 47.1 us (0.76)
  blocking collectives: 25.4 us -> 0 us
  starting transfers between devices: 10.2 us -> 18.5 us
  waiting for transfers between devices: 0.02 us -> 3.41 us
  Pallas kernels: 22.9 us -> 21.5 us
    all_gather x1 -> x0, blocking collectives: 25.4 us -> none  [shards(): gathered = lax.all_gather(gain_term, ('dp', 'ctx'))]
    ppermute x0 -> x4, starting transfers between devices: none -> 4.4 us  [the longest x3 4.39 us: exchanged(): return lax.ppermute(array, 'ctx', [(i, i ^ reach) for i in range(count)])]
    ppermute x6, starting transfers between devices: 10.2 us -> 14.1 us  [send(): lax.ppermute(payload, 'ctx', [(hop, hop + 1), (count - 1 - hop, count - 2...]
    ppermute x6, waiting for transfers between devices: 0.02 us -> 3.4 us  [send(): lax.ppermute(payload, 'ctx', [(hop, hop + 1), (count - 1 - hop, count - 2...]
    pallas_call x4 -> x6, Pallas kernels: 18.7 us -> 17.8 us  [the longest x4 9.75 us: local(): pl.pallas_call(functools.partial(local_kernel, head_width, row), in_specs...]
  transfers between devices with their start and end apart: 6 -> 10, of which waited for: 0 -> 1; matrix products, arithmetic and copies ran while one was open for 1% -> 1% of each run, Pallas kernels for 23% -> 38%
where the time goes in v11:
time: 47.1 us; the launch traced here: 46.8 us
  Pallas kernels  21.5 us (46%)
  starting transfers between devices  18.5 us (39%)
  waiting for transfers between devices  3.41 us (7%)
  other arithmetic  2.49 us (5%)
  between operations  0.86 us (2%)
    ppermute x6, starting transfers between devices, send(): lax.ppermute(payload, 'ctx', [(hop, hop + 1), (count - 1 - hop, count - 2...  14.1 us
    pallas_call x4, Pallas kernels, local(): pl.pallas_call(functools.partial(local_kernel, head_width, row), in_specs...  9.75 us
    pallas_call x2, Pallas kernels, merge(): pl.pallas_call(functools.partial(merge_kernel, head_width, part), in_spec...  8.07 us
    ppermute x3, starting transfers between devices, exchanged(): return lax.ppermute(array, 'ctx', [(i, i ^ reach) for i in range(count)])  4.39 us
    pallas_call x1, Pallas kernels, ends(): pl.pallas_call(functools.partial(ends_kernel, head_width, lengths.shape[1...  3.64 us
    ppermute x6, waiting for transfers between devices, send(): lax.ppermute(payload, 'ctx', [(hop, hop + 1), (count - 1 - hop, count - 2...  3.4 us
  transfers between devices with their start and end apart: 10, of which 1 were waited for; matrix products, arithmetic and copies ran while one was open for 1% of the time, Pallas kernels for 38%

profile of v11, /device:TPU:0, one launch (start us, length us, event | category | flops | bytes accessed | tf_op | source)
XLA Modules:
  0.0 46.8 jit_solution(12889244971211498074)
XLA Ops:
  0.6 0.7 %pad_convert_fusion = f32[4,128]{1,0:T(4,128)S(1)} fusion(s32[1,16]{1,0:T(1,128)} %param.11), kind=kLoop, calls=%fused_computation.13 | loop fusion | flops 512 | bytes 2112 | tf_op jit(solution)/shard_map/convert_element_type | solution.py:437
  1.3 0.7 %pad_maximum_fusion.refs_0_ = f32[4,1280]{1,0:T(4,128)S(1)} fusion(f32[4,128]{1,0:T(4,128)S(1)} %pad_convert_fusion, f32[4,128]{1,0:T(4,128)S(1)} %copy-done, f32[4,1024]{1,0:T(4,128)} %bitcast.13), kind=kLoop, calls=%fused_computation.8 | loop fusion | flops 10240 | bytes 40960 | tf_op jit(solution)/shard_map/concatenate | solution.py:438
  2.0 3.6 %shard_ends.1 = (f32[2,128,128]{2,1,0:T(8,128)S(1)}, f32[2,128,128]{2,1,0:T(8,128)S(1)}, f32[2,128,128]{2,1,0:T(8,128)S(1)}, f32[2,128,128]{2,1,0:T(8,128)S(1)},...) custom-call(f32[4,1280]{1,0:T(4,128)S(1)} %pad_maximum_fusion.refs_0, ...), custom_call_target="tpu_custom_call" | custom-call | flops 268435456 | bytes 4194304 | tf_op jit(solution)/shard_map/shard_ends/pallas_call | solution.py:456
  5.7 4.9 %collective-permute-start = (f32[2,128,128]{2,1,0:T(8,128)S(1)}, f32[2,128,128]{2,1,0:T(8,128)S(1)}, u32[]{:S(2)}, u32[]{:S(2)}) collective-permute-start(f32[2,128,128]{2,1,0:T(8,128)S(1)} %get-tuple-element.68), channel_id=1, source_target_pairs={{0,4},{12,8},{1,5},{13,9},{2,6},{14,10},{3,7},{15,11},{16,20},{28,... | collective-permute-start | bytes 393224 | tf_op jit(solution)/shard_map/ppermute | solution.py:530
  10.6 2.5 %local_1.1 = (bf16[4,1024,128]{2,1,0:T(8,128)(2,1)S(1)}, f32[1,1,1024]{2,1,0:T(1,128)S(1)}, f32[1,128]{1,0:T(1,128)S(1)}) custom-call(bf16[1,1024,512]{2,1,0:T(8,128)(2,1)S(1)} %get-tuple-element.60.q_ref.refs_0_, bf16[1,1024,512]{2,1,0:T(8,128)(2,1)S(1)} %get-tuple-element.61.k_ref.refs_1_, bf16[1,1024,512]{2,1,0:T(8,128)(2,1)S(1)} %get-tuple-element.62.v_ref.refs_2_, ...), custom_call_target="tpu_custom_call" | custom-call | flops 402653184 | bytes 2097152 | tf_op jit(solution)/shard_map/local_1/pallas_call | solution.py:473
  13.1 2.4 %local_0.1 = (bf16[4,1024,128]{2,1,0:T(8,128)(2,1)S(1)}, f32[1,1,1024]{2,1,0:T(1,128)S(1)}, f32[1,128]{1,0:T(1,128)S(1)}) custom-call(bf16[1,1024,512]{2,1,0:T(8,128)(2,1)S(1)} %get-tuple-element.60.q_ref.refs_0_, bf16[1,1024,512]{2,1,0:T(8,128)(2,1)S(1)} %get-tuple-element.61.k_ref.refs_1_, bf16[1,1024,512]{2,1,0:T(8,128)(2,1)S(1)} %get-tuple-element.62.v_ref.refs_2_, ...), custom_call_target="tpu_custom_call" | custom-call | flops 402653184 | bytes 2097152 | tf_op jit(solution)/shard_map/local_0/pallas_call | solution.py:473
  15.5 0.7 %collective-permute-start.2 = (f32[2,128,128]{2,1,0:T(8,128)S(1)}, f32[2,128,128]{2,1,0:T(8,128)S(1)}, u32[]{:S(2)}, u32[]{:S(2)}) collective-permute-start(f32[2,128,128]{2,1,0:T(8,128)S(1)} %multiply_add_fusion.3), channel_id=1, source_target_pairs={{4,8},{8,4},{5,9},{9,5},{6,10},{10,6},{7,11},{11,7},{20,24},{24,20... | collective-permute-start | bytes 393224 | tf_op jit(solution)/shard_map/ppermute | solution.py:530
  16.2 5.1 %collective-permute-start.1 = (f32[2,128,128]{2,1,0:T(8,128)S(1)}, f32[2,128,128]{2,1,0:T(8,128)S(1)}, u32[]{:S(2)}, u32[]{:S(2)}) collective-permute-start(f32[2,128,128]{2,1,0:T(8,128)S(1)} %get-tuple-element.76), channel_id=1, source_target_pairs={{0,4},{12,8},{1,5},{13,9},{2,6},{14,10},{3,7},{15,11},{16,20},{28,... | collective-permute-start | bytes 393224 | tf_op jit(solution)/shard_map/ppermute | solution.py:530
  21.3 2.5 %local_2.1 = (bf16[4,1024,128]{2,1,0:T(8,128)(2,1)S(1)}, f32[1,1,1024]{2,1,0:T(1,128)S(1)}, f32[1,128]{1,0:T(1,128)S(1)}) custom-call(bf16[1,1024,512]{2,1,0:T(8,128)(2,1)S(1)} %get-tuple-element.60.q_ref.refs_0_, bf16[1,1024,512]{2,1,0:T(8,128)(2,1)S(1)} %get-tuple-element.61.k_ref.refs_1_, bf16[1,1024,512]{2,1,0:T(8,128)(2,1)S(1)} %get-tuple-element.62.v_ref.refs_2_, ...), custom_call_target="tpu_custom_call" | custom-call | flops 402653184 | bytes 2097152 | tf_op jit(solution)/shard_map/local_2/pallas_call | solution.py:473
  23.8 0.2 multiply_reduce_fusion.3
  24.0 0.7 %collective-permute-start.3 = (f32[2,128,128]{2,1,0:T(8,128)S(1)}, f32[2,128,128]{2,1,0:T(8,128)S(1)}, u32[]{:S(2)}, u32[]{:S(2)}) collective-permute-start(f32[2,128,128]{2,1,0:T(8,128)S(1)} %multiply_add_fusion.1), channel_id=1, source_target_pairs={{4,8},{8,4},{5,9},{9,5},{6,10},{10,6},{7,11},{11,7},{20,24},{24,20... | collective-permute-start | bytes 393224 | tf_op jit(solution)/shard_map/ppermute | solution.py:530
  24.6 1.3 %collective-permute-start.5 = (f32[2,128,128]{2,1,0:T(8,128)S(1)}, f32[2,128,128]{2,1,0:T(8,128)S(1)}, u32[]{:S(2)}, u32[]{:S(2)}) collective-permute-start(f32[2,128,128]{2,1,0:T(8,128)S(1)} %get-tuple-element.115), channel_id=1, source_target_pairs={{8,12},{4,0},{9,13},{5,1},{10,14},{6,2},{11,15},{7,3},{24,28},{20,... | collective-permute-start | bytes 393224 | tf_op jit(solution)/shard_map/ppermute | solution.py:530
  25.9 2.5 %local_3.1 = (bf16[4,1024,128]{2,1,0:T(8,128)(2,1)S(1)}, f32[1,1,1024]{2,1,0:T(1,128)S(1)}, f32[1,128]{1,0:T(1,128)S(1)}) custom-call(bf16[1,1024,512]{2,1,0:T(8,128)(2,1)S(1)} %get-tuple-element.60.q_ref.refs_0_, bf16[1,1024,512]{2,1,0:T(8,128)(2,1)S(1)} %get-tuple-element.61.k_ref.refs_1_, bf16[1,1024,512]{2,1,0:T(8,128)(2,1)S(1)} %get-tuple-element.62.v_ref.refs_2_, ...), custom_call_target="tpu_custom_call" | custom-call | flops 402653184 | bytes 2097152 | tf_op jit(solution)/shard_map/local_3/pallas_call | solution.py:473
  28.4 0.1 multiply_reduce_fusion.1
  28.6 1.5 %collective-permute-start.4 = (f32[2,128,128]{2,1,0:T(8,128)S(1)}, f32[2,128,128]{2,1,0:T(8,128)S(1)}, u32[]{:S(2)}, u32[]{:S(2)}) collective-permute-start(f32[2,128,128]{2,1,0:T(8,128)S(1)} %get-tuple-element.118), channel_id=1, source_target_pairs={{8,12},{4,0},{9,13},{5,1},{10,14},{6,2},{11,15},{7,3},{24,28},{20,... | collective-permute-start | bytes 393224 | tf_op jit(solution)/shard_map/ppermute | solution.py:530
  30.1 0.1 multiply_add_fusion.4
  30.2 3.4 %collective-permute-done.5.refs_9_ = f32[2,128,128]{2,1,0:T(8,128)S(1)} collective-permute-done((f32[2,128,128]{2,1,0:T(8,128)S(1)}, f32[2,128,128]{2,1,0:T(8,128)S(1)}, u32[]{:S(2)}, u32[]{:S(2)}) %collective-permute-start.5) | collective-permute-done | bytes 131104 | tf_op jit(solution)/shard_map/ppermute | solution.py:530
  33.6 3.7 %merge_0.1 = (bf16[1,1024,512]{2,1,0:T(8,128)(2,1)}, bf16[1,1024,512]{2,1,0:T(8,128)(2,1)}, bf16[1,1024,512]{2,1,0:T(8,128)(2,1)}, bf16[1,1024,512]{2,1,0:T(8,128)(2,1)}, f32[1,2,1024]{2,1,0:T(2,128)S(1)}) custom-call(bf16[1,1024,512]{2,1,0:T(8,128)(2,1)S(1)} %get-tuple-element.60.q_ref.refs_0_, bf16[1,1024,512]{2,1,0:T(8,128)(2,1)S(1)} %get-tuple-element.61.k_ref.refs_1_, ...), custom_call_target="tpu_custom_call" | custom-call | flops 268435456 | bytes 6291456 | tf_op jit(solution)/shard_map/merge_0/pallas_call | solution.py:496
  37.3 0.1 add_add_fusion.1
  37.4 1.3 %collective-permute-start.7 = (f32[4,64]{1,0:T(4,128)S(1)}, f32[4,64]{1,0:T(4,128)S(1)}, u32[]{:S(2)}, u32[]{:S(2)}) collective-permute-start(f32[4,64]{1,0:T(4,128)S(1)} %add_add_fusion.1), channel_id=1, source_target_pairs={{0,4},{4,0},{8,12},{12,8},{1,5},{5,1},{9,13},{13,9},{2,6},{6,2},{1... | collective-permute-start | bytes 3080 | tf_op jit(solution)/shard_map/ppermute | solution.py:578
  38.7 2.0 %collective-permute-start.8 = (f32[4,64]{1,0:T(4,128)S(1)}, f32[4,64]{1,0:T(4,128)S(1)}, u32[]{:S(2)}, u32[]{:S(2)}) collective-permute-start(f32[4,64]{1,0:T(4,128)S(1)} %add_add_fusion.1), channel_id=1, source_target_pairs={{0,8},{4,12},{8,0},{12,4},{1,9},{5,13},{9,1},{13,5},{2,10},{6,14},... | collective-permute-start | bytes 3080 | tf_op jit(solution)/shard_map/ppermute | solution.py:578
  40.7 1.1 %collective-permute-start.9 = (f32[4,64]{1,0:T(4,128)S(1)}, f32[4,64]{1,0:T(4,128)S(1)}, u32[]{:S(2)}, u32[]{:S(2)}) collective-permute-start(f32[4,64]{1,0:T(4,128)S(1)} %add_add_fusion.1), channel_id=1, source_target_pairs={{0,12},{4,8},{8,4},{12,0},{1,13},{5,9},{9,5},{13,1},{2,14},{6,10},... | collective-permute-start | bytes 3080 | tf_op jit(solution)/shard_map/ppermute | solution.py:578
  41.8 4.3 %merge_1.1 = (bf16[1,1024,512]{2,1,0:T(8,128)(2,1)}, bf16[1,1024,512]{2,1,0:T(8,128)(2,1)}, bf16[1,1024,512]{2,1,0:T(8,128)(2,1)}, bf16[1,1024,512]{2,1,0:T(8,128)(2,1)}, f32[1,4,1024]{2,1,0:T(4,128)}) custom-call(bf16[1,1024,512]{2,1,0:T(8,128)(2,1)S(1)} %get-tuple-element.60.q_ref.refs_, ...), custom_call_target="tpu_custom_call", output_to_operand_aliasing={{0}: (15, {}), {1}: (16, {}), {2}: (17, {}), {3}: (18, {})} | custom-call | flops 268435456 | bytes 6291456 | tf_op jit(solution)/shard_map/merge_1/pallas_call | solution.py:496
  46.2 0.6 %add_add_fusion = f32[4,64]{1,0:T(4,128)} fusion(f32[4,64]{1,0:T(4,128)S(1)} %collective-permute-done.8, f32[4,64]{1,0:T(4,128)S(1)} %collective-permute-done.9, f32[4,64]{1,0:T(4,128)S(1)} %add_add_fusion.1, f32[4,64]{1,0:T(4,128)S(1)} %collective-permute-done.7), kind=kLoop, calls=%fused_computation.10 | loop fusion | flops 768 | bytes 5120 | tf_op jit(solution)/shard_map/add | solution.py:422
  (18 shorter events, 0.1 us)
Async XLA Ops:
  0.6 0.7 %copy-start = (f32[4,128]{1,0:T(4,128)S(1)}, f32[4,128]{1,0:T(4,128)}, u32[]{:S(2)}) copy-start(f32[4,128]{1,0:T(4,128)} %param.12) | copy-start | bytes 6148
  5.7 9.8 %collective-permute-start = (f32[2,128,128]{2,1,0:T(8,128)S(1)}, f32[2,128,128]{2,1,0:T(8,128)S(1)}, u32[]{:S(2)}, u32[]{:S(2)}) collective-permute-start(f32[2,128,128]{2,1,0:T(8,128)S(1)} %get-tuple-element.68), channel_id=1, source_target_pairs={{0,4},{12,8},{1,5},{13,9},{2,6},{14,10},{3,7},{15,11},{16,20},{28,... | collective-permute-start | bytes 393224 | tf_op jit(solution)/shard_map/ppermute | solution.py:530
  15.5 8.2 %collective-permute-start.2 = (f32[2,128,128]{2,1,0:T(8,128)S(1)}, f32[2,128,128]{2,1,0:T(8,128)S(1)}, u32[]{:S(2)}, u32[]{:S(2)}) collective-permute-start(f32[2,128,128]{2,1,0:T(8,128)S(1)} %multiply_add_fusion.3), channel_id=1, source_target_pairs={{4,8},{8,4},{5,9},{9,5},{6,10},{10,6},{7,11},{11,7},{20,24},{24,20... | collective-permute-start | bytes 393224 | tf_op jit(solution)/shard_map/ppermute | solution.py:530
  16.2 7.7 %collective-permute-start.1 = (f32[2,128,128]{2,1,0:T(8,128)S(1)}, f32[2,128,128]{2,1,0:T(8,128)S(1)}, u32[]{:S(2)}, u32[]{:S(2)}) collective-permute-start(f32[2,128,128]{2,1,0:T(8,128)S(1)} %get-tuple-element.76), channel_id=1, source_target_pairs={{0,4},{12,8},{1,5},{13,9},{2,6},{14,10},{3,7},{15,11},{16,20},{28,... | collective-permute-start | bytes 393224 | tf_op jit(solution)/shard_map/ppermute | solution.py:530
  24.0 4.5 %collective-permute-start.3 = (f32[2,128,128]{2,1,0:T(8,128)S(1)}, f32[2,128,128]{2,1,0:T(8,128)S(1)}, u32[]{:S(2)}, u32[]{:S(2)}) collective-permute-start(f32[2,128,128]{2,1,0:T(8,128)S(1)} %multiply_add_fusion.1), channel_id=1, source_target_pairs={{4,8},{8,4},{5,9},{9,5},{6,10},{10,6},{7,11},{11,7},{20,24},{24,20... | collective-permute-start | bytes 393224 | tf_op jit(solution)/shard_map/ppermute | solution.py:530
  24.6 8.9 %collective-permute-start.5 = (f32[2,128,128]{2,1,0:T(8,128)S(1)}, f32[2,128,128]{2,1,0:T(8,128)S(1)}, u32[]{:S(2)}, u32[]{:S(2)}) collective-permute-start(f32[2,128,128]{2,1,0:T(8,128)S(1)} %get-tuple-element.115), channel_id=1, source_target_pairs={{8,12},{4,0},{9,13},{5,1},{10,14},{6,2},{11,15},{7,3},{24,28},{20,... | collective-permute-start | bytes 393224 | tf_op jit(solution)/shard_map/ppermute | solution.py:530
  28.6 13.2 %collective-permute-start.4 = (f32[2,128,128]{2,1,0:T(8,128)S(1)}, f32[2,128,128]{2,1,0:T(8,128)S(1)}, u32[]{:S(2)}, u32[]{:S(2)}) collective-permute-start(f32[2,128,128]{2,1,0:T(8,128)S(1)} %get-tuple-element.118), channel_id=1, source_target_pairs={{8,12},{4,0},{9,13},{5,1},{10,14},{6,2},{11,15},{7,3},{24,28},{20,... | collective-permute-start | bytes 393224 | tf_op jit(solution)/shard_map/ppermute | solution.py:530
  30.2 7.2 %collective-permute-start.6 = (f32[4,64]{1,0:T(4,128)S(1)}, f32[4,64]{1,0:T(4,128)S(1)}, u32[]{:S(2)}, u32[]{:S(2)}) collective-permute-start(f32[4,64]{1,0:T(4,128)S(1)} %multiply_add_fusion.4), channel_id=1, source_target_pairs={{0,16},{16,0},{1,17},{17,1},{2,18},{18,2},{3,19},{19,3},{4,20},{20... | collective-permute-start | bytes 3080 | tf_op jit(solution)/shard_map/ppermute | solution.py:575
  37.4 8.7 %collective-permute-start.7 = (f32[4,64]{1,0:T(4,128)S(1)}, f32[4,64]{1,0:T(4,128)S(1)}, u32[]{:S(2)}, u32[]{:S(2)}) collective-permute-start(f32[4,64]{1,0:T(4,128)S(1)} %add_add_fusion.1), channel_id=1, source_target_pairs={{0,4},{4,0},{8,12},{12,8},{1,5},{5,1},{9,13},{13,9},{2,6},{6,2},{1... | collective-permute-start | bytes 3080 | tf_op jit(solution)/shard_map/ppermute | solution.py:578
  38.7 7.4 %collective-permute-start.8 = (f32[4,64]{1,0:T(4,128)S(1)}, f32[4,64]{1,0:T(4,128)S(1)}, u32[]{:S(2)}, u32[]{:S(2)}) collective-permute-start(f32[4,64]{1,0:T(4,128)S(1)} %add_add_fusion.1), channel_id=1, source_target_pairs={{0,8},{4,12},{8,0},{12,4},{1,9},{5,13},{9,1},{13,5},{2,10},{6,14},... | collective-permute-start | bytes 3080 | tf_op jit(solution)/shard_map/ppermute | solution.py:578
  40.7 5.5 %collective-permute-start.9 = (f32[4,64]{1,0:T(4,128)S(1)}, f32[4,64]{1,0:T(4,128)S(1)}, u32[]{:S(2)}, u32[]{:S(2)}) collective-permute-start(f32[4,64]{1,0:T(4,128)S(1)} %add_add_fusion.1), channel_id=1, source_target_pairs={{0,12},{4,8},{8,4},{12,0},{1,13},{5,9},{9,5},{13,1},{2,14},{6,10},... | collective-permute-start | bytes 3080 | tf_op jit(solution)/shard_map/ppermute | solution.py:578

commit v12 on v8

--- a/solution.py
+++ b/solution.py
@@ -314,7 +314,7 @@
         refs[7 + i * PARTS : 7 + (i + 1) * PARTS] for i in range(5)
     )
     refs = refs[7 + 5 * PARTS :]
-    targets, dgate_ref, staged, entering, leaving, sems = refs[:4], *refs[4:]
+    targets, dgate_ref, staged, entering, leaving, spread_ref, gate_scr, sems = refs[:4], *refs[4:]
     heads = first_refs[0].shape[0]
     steps = sems.shape[0]
     num_chunks = fac_ref.shape[0] // 8
@@ -349,12 +349,18 @@
             leaving[part, own, own] = (later * gain).astype(BF16)
             constants.append(total_of(state * later) * last_factors[row : row + 1])
 
-    gate_sums, kept_sums = {}, {}
+    spread = (iota(spread_ref.shape, 1) // head_width == iota(spread_ref.shape, 0) % 8).astype(F32)
+    spread_ref[...] = spread.astype(BF16)
+    ones = jnp.ones((8, head_width), BF16)
     for step in range(steps):
         numbers = range(step * chunks, (step + 1) * chunks)
-        products, results = {}, {}
+        products, results, factors = {}, {}, {}
         for number in numbers:
             rows = slice(number * CHUNK, (number + 1) * CHUNK)
+            fac = fac_ref[number * 8 : number * 8 + 8, :]
+            high = fac.astype(BF16).astype(F32)
+            both = jnp.concatenate([high, fac - high], axis=0).astype(BF16)
+            factors[number] = dot_tn(both, spread_ref[...])
             for part in range(PARTS):
                 group = slice(part * group_width, (part + 1) * group_width)
                 products[number, part] = (
@@ -364,13 +370,13 @@
                     dot_nn(k_ref[0, rows, group], leaving[part]),
                 )
         for number in numbers:
-            columns = jnp.transpose(fac_ref[number * 8 : number * 8 + 8, :])
             rows = slice(number * CHUNK, (number + 1) * CHUNK)
             for row in range(PARTS * heads):
                 part, head = divmod(row, heads)
                 lanes = slice(head * head_width, (head + 1) * head_width)
                 wide = slice(row * head_width, (row + 1) * head_width)
-                from_start, to_end = columns[:, row : row + 1], columns[:, 4 + row : 5 + row]
+                from_start = factors[number][:, wide]
+                to_end = factors[number][:, (4 + row) * head_width : (5 + row) * head_width]
                 across, dq, dk, written = (
                     product[:, lanes] * factor
                     for product, factor in zip(
@@ -381,12 +387,12 @@
                     (partial_refs[part][i, rows, lanes].astype(F32) + added).astype(BF16)
                     for i, added in enumerate((across, dq, dk, written))
                 ]
-                kept = written * v_ref[0, rows, wide].astype(F32)
-                balance = jnp.sum(
-                    across * cot_ref[0, rows, wide].astype(F32) - kept, axis=1, keepdims=True
-                )
-                gate_sums[number, row] = later_sums(balance)
-                kept_sums[number, row] = jnp.sum(kept, axis=0, keepdims=True)
+                queried = (across * cot_ref[0, rows, wide].astype(F32)).astype(BF16)
+                kept = (written * v_ref[0, rows, wide].astype(F32)).astype(BF16)
+                shares = dot_nt(ones, jnp.concatenate([queried, kept], axis=0))
+                at = number * 8 + row
+                gate_scr[at : at + 1, :] = shares[0:1, :CHUNK]
+                gate_scr[at + 4 : at + 5, :] = shares[0:1, CHUNK:]
         for number in numbers:
             rows = slice(number * CHUNK, (number + 1) * CHUNK)
             for row in range(PARTS * heads):
@@ -396,17 +402,31 @@
         for i, copy in enumerate(copies(step)):
             copy.start(priority=i % 2)
 
-    for row in range(PARTS * heads):
-        part, head = divmod(row, heads)
-        kept = sum(kept_sums[number, row] for number in range(num_chunks))
-        base = jnp.sum(kept, axis=1, keepdims=True) + constants[row]
-        for number in range(num_chunks - 1, -1, -1):
-            lanes = slice(number * CHUNK, (number + 1) * CHUNK)
-            sums = gate_sums[number, row]
+    shares = gate_scr[...]
+    lane_a, lane_b = iota((CHUNK, CHUNK), 0), iota((CHUNK, CHUNK), 1)
+    from_here = dot_nn(shares, (lane_a >= lane_b).astype(F32), PRECISE)
+    up_to_here = dot_nn(shares, (lane_a < lane_b).astype(F32), PRECISE)
+    all_rows = shares.shape[0]
+    totals = jnp.broadcast_to(from_here[:, 0:1], shares.shape)
+    row_a, row_b = iota((all_rows, all_rows), 0), iota((all_rows, all_rows), 1)
+    outside = ((row_a % 8 < 4) & (row_b // 8 > row_a // 8)) | (
+        (row_a % 8 >= 4) & (row_b // 8 < row_a // 8)
+    )
+    outside = (outside & (row_a % 8 == row_b % 8)).astype(F32)
+    sums = dot_nn(outside, totals, PRECISE) + jnp.where(
+        iota(shares.shape, 0) % 8 < 4, from_here, up_to_here
+    )
+    for number in range(num_chunks):
+        lanes = slice(number * CHUNK, (number + 1) * CHUNK)
+        for row in range(PARTS * heads):
+            part, head = divmod(row, heads)
+            at = number * 8 + row
             dgate_ref[0, row : row + 1, lanes] = (
-                gate_refs[part][0, head : head + 1, lanes] + sums + base
-            )
-            base = base + sums[:, 0:1]
+                gate_refs[part][0, head : head + 1, lanes]
+                + sums[at : at + 1, :]
+                + sums[at + 4 : at + 5, :]
+                + constants[row]
+            )
     for step in range(steps):
         for copy in copies(step):
             copy.wait()
@@ -430,8 +450,12 @@
     count = lax.axis_size("ctx")
     middle = count // 2 - 1
     docs = lengths.shape[1]
-    sizes = jnp.pad(lengths, ((0, all_heads - 1), (0, CHUNK - docs))).astype(F32)
-    small = jnp.concatenate([gates[0], key_gain, sizes], axis=1)
+    after = head_width + CHUNK
+    small = (
+        jnp.pad(gates[0], ((0, 0), (0, after)))
+        + jnp.pad(key_gain, ((0, 0), (tokens, CHUNK)))
+        + jnp.pad(lengths, ((0, all_heads - 1), (tokens + head_width, CHUNK - docs))).astype(F32)
+    )
 
     def shape_of(*shape, dtype=F32):
         return jax.ShapeDtypeStruct(shape, dtype)
@@ -493,6 +517,8 @@
                 pltpu.VMEM((4, tokens, width), BF16),
                 pltpu.VMEM((PARTS, part_width, part_width), BF16),
                 pltpu.VMEM((PARTS, part_width, part_width), BF16),
+                pltpu.VMEM((16, 8 * head_width), BF16),
+                pltpu.VMEM((rows, CHUNK), F32),
                 pltpu.SemaphoreType.DMA((steps, 4)),
             ],
             compiler_params=pltpu.CompilerParams(vmem_limit_bytes=24 << 20),

time: 44.3 us -> 42 us (0.948)
  Pallas kernels: 20 us -> 18.4 us
  other arithmetic: 2.53 us -> 1.88 us
    pallas_call x1, Pallas kernels: 6.7 us -> 5.08 us  [merge(): pl.pallas_call(functools.partial(merge_kernel, head_width), in_specs=[vme...]
    add x0 -> x1, other arithmetic: none -> 0.76 us  [shards(): jnp.pad(gates[0], ((0, 0), (0, after)))]
    concatenate x1 -> x0, other arithmetic: 0.74 us -> none  [shards(): small = jnp.concatenate([gates[0], key_gain, sizes], axis=1)]
    convert_element_type x1 -> x0, other arithmetic: 0.66 us -> none  [shards(): jnp.pad(lengths, ((0, all_heads - 1), (0, CHUNK - docs))).astype(F32)]
  transfers between devices with their start and end apart: 10 -> 10, of which waited for: 2 -> 2; matrix products, arithmetic and copies ran while one was open for 1% -> 1% of each run, Pallas kernels for 37% -> 35%
where the time goes in v12:
time: 42 us; the launch traced here: 41.6 us
  Pallas kernels  18.4 us (44%)
  starting transfers between devices  17.4 us (41%)
  waiting for transfers between devices  3.14 us (7%)
  other arithmetic  1.88 us (4%)
  between operations  0.82 us (2%)
    ppermute x6, starting transfers between devices, send(): lax.ppermute(payload, 'ctx', [(hop, hop + 1), (count - 1 - hop, count - 2...  10.2 us
    pallas_call x2, Pallas kernels, local(): pl.pallas_call(functools.partial(local_kernel, head_width, part), in_spec...  9.69 us
    ppermute x3, starting transfers between devices, exchanged(): return lax.ppermute(array, 'ctx', [(i, i ^ reach) for i in range(count)])  7.2 us
    pallas_call x1, Pallas kernels, merge(): pl.pallas_call(functools.partial(merge_kernel, head_width), in_specs=[vme...  5.08 us
    pallas_call x1, Pallas kernels, ends(): pl.pallas_call(functools.partial(ends_kernel, head_width, lengths.shape[1...  3.64 us
    ppermute x6, waiting for transfers between devices, send(): lax.ppermute(payload, 'ctx', [(hop, hop + 1), (count - 1 - hop, count - 2...  3.13 us
  transfers between devices with their start and end apart: 10, of which 2 were waited for; matrix products, arithmetic and copies ran while one was open for 1% of the time, Pallas kernels for 35%

profile of v12, /device:TPU:0, one launch (start us, length us, event | category | flops | bytes accessed | tf_op | source)
XLA Modules:
  0.0 41.6 jit_solution(14185567610188833369)
XLA Ops:
  0.6 0.8 %convert_add_fusion.refs_0_ = f32[4,1280]{1,0:T(4,128)S(1)} fusion(s32[1,16]{1,0:T(1,128)} %param.11, f32[4,128]{1,0:T(4,128)} %param.12, f32[4,1024]{1,0:T(4,128)} %bitcast.13), kind=kLoop, calls=%fused_computation.8 | loop fusion | flops 15360 | bytes 38976 | tf_op jit(solution)/shard_map/add | solution.py:455
  1.4 3.6 %shard_ends.1 = (f32[2,128,128]{2,1,0:T(8,128)S(1)}, f32[2,128,128]{2,1,0:T(8,128)S(1)}, f32[2,128,128]{2,1,0:T(8,128)S(1)}, f32[2,128,128]{2,1,0:T(8,128)S(1)},...) custom-call(f32[4,1280]{1,0:T(4,128)S(1)} %convert_add_fusion.refs_0, ...), custom_call_target="tpu_custom_call" | custom-call | flops 268435456 | bytes 4194304 | tf_op jit(solution)/shard_map/shard_ends/pallas_call | solution.py:477
  5.0 4.9 %collective-permute-start = (f32[2,128,128]{2,1,0:T(8,128)S(1)}, f32[2,128,128]{2,1,0:T(8,128)S(1)}, u32[]{:S(2)}, u32[]{:S(2)}) collective-permute-start(f32[2,128,128]{2,1,0:T(8,128)S(1)} %get-tuple-element.52), channel_id=1, source_target_pairs={{0,4},{12,8},{1,5},{13,9},{2,6},{14,10},{3,7},{15,11},{16,20},{28,... | collective-permute-start | bytes 393224 | tf_op jit(solution)/shard_map/ppermute | solution.py:545
  10.0 1.3 %collective-permute-start.1 = (f32[2,128,128]{2,1,0:T(8,128)S(1)}, f32[2,128,128]{2,1,0:T(8,128)S(1)}, u32[]{:S(2)}, u32[]{:S(2)}) collective-permute-start(f32[2,128,128]{2,1,0:T(8,128)S(1)} %get-tuple-element.58), channel_id=1, source_target_pairs={{0,4},{12,8},{1,5},{13,9},{2,6},{14,10},{3,7},{15,11},{16,20},{28,... | collective-permute-start | bytes 393224 | tf_op jit(solution)/shard_map/ppermute | solution.py:545
  11.3 4.8 %local_0.1 = (bf16[4,1024,256]{2,1,0:T(8,128)(2,1)S(1)}, f32[1,2,1024]{2,1,0:T(2,128)S(1)}, f32[2,128]{1,0:T(2,128)S(1)}) custom-call(bf16[1,1024,512]{2,1,0:T(8,128)(2,1)S(1)} %get-tuple-element.41.q_ref.refs_0_, bf16[1,1024,512]{2,1,0:T(8,128)(2,1)S(1)} %get-tuple-element.42.k_ref.refs_1_, bf16[1,1024,512]{2,1,0:T(8,128)(2,1)S(1)} %get-tuple-element.43.v_ref.refs_2_, ...), custom_call_target="tpu_custom_call" | custom-call | flops 805306368 | bytes 4194304 | tf_op jit(solution)/shard_map/local_0/pallas_call | solution.py:494
  16.2 0.7 %collective-permute-start.2 = (f32[2,128,128]{2,1,0:T(8,128)S(1)}, f32[2,128,128]{2,1,0:T(8,128)S(1)}, u32[]{:S(2)}, u32[]{:S(2)}) collective-permute-start(f32[2,128,128]{2,1,0:T(8,128)S(1)} %multiply_add_fusion.3), channel_id=1, source_target_pairs={{4,8},{8,4},{5,9},{9,5},{6,10},{10,6},{7,11},{11,7},{20,24},{24,20... | collective-permute-start | bytes 393224 | tf_op jit(solution)/shard_map/ppermute | solution.py:545
  16.8 0.0 collective-permute-done.1.refs_12_
  16.9 0.7 %collective-permute-start.3 = (f32[2,128,128]{2,1,0:T(8,128)S(1)}, f32[2,128,128]{2,1,0:T(8,128)S(1)}, u32[]{:S(2)}, u32[]{:S(2)}) collective-permute-start(f32[2,128,128]{2,1,0:T(8,128)S(1)} %multiply_add_fusion.2), channel_id=1, source_target_pairs={{4,8},{8,4},{5,9},{9,5},{6,10},{10,6},{7,11},{11,7},{20,24},{24,20... | collective-permute-start | bytes 393224 | tf_op jit(solution)/shard_map/ppermute | solution.py:545
  17.6 4.9 %local_1.1 = (bf16[4,1024,256]{2,1,0:T(8,128)(2,1)S(1)}, f32[1,2,1024]{2,1,0:T(2,128)S(1)}, f32[2,128]{1,0:T(2,128)S(1)}) custom-call(bf16[1,1024,512]{2,1,0:T(8,128)(2,1)S(1)} %get-tuple-element.41.q_ref.refs_0_, bf16[1,1024,512]{2,1,0:T(8,128)(2,1)S(1)} %get-tuple-element.42.k_ref.refs_1_, bf16[1,1024,512]{2,1,0:T(8,128)(2,1)S(1)} %get-tuple-element.43.v_ref.refs_2_, ...), custom_call_target="tpu_custom_call" | custom-call | flops 805306368 | bytes 4194304 | tf_op jit(solution)/shard_map/local_1/pallas_call | solution.py:494
  22.4 0.2 multiply_reduce_fusion.3
  22.6 0.0 collective-permute-done.3.refs_14_
  22.6 0.2 multiply_reduce_fusion.1
  22.8 0.1 multiply_add_fusion.4
  22.9 0.0 collective-permute-start.6
  22.9 1.3 %collective-permute-start.4 = (f32[2,128,128]{2,1,0:T(8,128)S(1)}, f32[2,128,128]{2,1,0:T(8,128)S(1)}, u32[]{:S(2)}, u32[]{:S(2)}) collective-permute-start(f32[2,128,128]{2,1,0:T(8,128)S(1)} %get-tuple-element.77), channel_id=1, source_target_pairs={{8,12},{4,0},{9,13},{5,1},{10,14},{6,2},{11,15},{7,3},{24,28},{20,... | collective-permute-start | bytes 393224 | tf_op jit(solution)/shard_map/ppermute | solution.py:545
  24.2 1.3 %collective-permute-start.5 = (f32[2,128,128]{2,1,0:T(8,128)S(1)}, f32[2,128,128]{2,1,0:T(8,128)S(1)}, u32[]{:S(2)}, u32[]{:S(2)}) collective-permute-start(f32[2,128,128]{2,1,0:T(8,128)S(1)} %get-tuple-element.80), channel_id=1, source_target_pairs={{8,12},{4,0},{9,13},{5,1},{10,14},{6,2},{11,15},{7,3},{24,28},{20,... | collective-permute-start | bytes 393224 | tf_op jit(solution)/shard_map/ppermute | solution.py:545
  25.5 0.1 add_add_fusion.1
  25.6 4.7 %collective-permute-start.7 = (f32[4,64]{1,0:T(4,128)S(1)}, f32[4,64]{1,0:T(4,128)S(1)}, u32[]{:S(2)}, u32[]{:S(2)}) collective-permute-start(f32[4,64]{1,0:T(4,128)S(1)} %add_add_fusion.1), channel_id=1, source_target_pairs={{0,4},{4,0},{8,12},{12,8},{1,5},{5,1},{9,13},{13,9},{2,6},{6,2},{1... | collective-permute-start | bytes 3080 | tf_op jit(solution)/shard_map/ppermute | solution.py:582
  30.3 1.1 %collective-permute-start.8 = (f32[4,64]{1,0:T(4,128)S(1)}, f32[4,64]{1,0:T(4,128)S(1)}, u32[]{:S(2)}, u32[]{:S(2)}) collective-permute-start(f32[4,64]{1,0:T(4,128)S(1)} %add_add_fusion.1), channel_id=1, source_target_pairs={{0,8},{4,12},{8,0},{12,4},{1,9},{5,13},{9,1},{13,5},{2,10},{6,14},... | collective-permute-start | bytes 3080 | tf_op jit(solution)/shard_map/ppermute | solution.py:582
  31.4 1.4 %collective-permute-start.9 = (f32[4,64]{1,0:T(4,128)S(1)}, f32[4,64]{1,0:T(4,128)S(1)}, u32[]{:S(2)}, u32[]{:S(2)}) collective-permute-start(f32[4,64]{1,0:T(4,128)S(1)} %add_add_fusion.1), channel_id=1, source_target_pairs={{0,12},{4,8},{8,4},{12,0},{1,13},{5,9},{9,5},{13,1},{2,14},{6,10},... | collective-permute-start | bytes 3080 | tf_op jit(solution)/shard_map/ppermute | solution.py:582
  32.8 0.4 %collective-permute-done.4.refs_15_ = f32[2,128,128]{2,1,0:T(8,128)S(1)} collective-permute-done((f32[2,128,128]{2,1,0:T(8,128)S(1)}, f32[2,128,128]{2,1,0:T(8,128)S(1)}, u32[]{:S(2)}, u32[]{:S(2)}) %collective-permute-start.4) | collective-permute-done | bytes 131104 | tf_op jit(solution)/shard_map/ppermute | solution.py:545
  33.2 2.7 %collective-permute-done.5.refs_16_ = f32[2,128,128]{2,1,0:T(8,128)S(1)} collective-permute-done((f32[2,128,128]{2,1,0:T(8,128)S(1)}, f32[2,128,128]{2,1,0:T(8,128)S(1)}, u32[]{:S(2)}, u32[]{:S(2)}) %collective-permute-start.5) | collective-permute-done | bytes 131104 | tf_op jit(solution)/shard_map/ppermute | solution.py:545
  35.9 5.1 %merge.1 = (bf16[1,1024,512]{2,1,0:T(8,128)(2,1)}, bf16[1,1024,512]{2,1,0:T(8,128)(2,1)}, bf16[1,1024,512]{2,1,0:T(8,128)(2,1)}, bf16[1,1024,512]{2,1,0:T(8,128)(2,1)}, f32[1,4,1024]{2,1,0:T(4,128)}) custom-call(bf16[1,1024,512]{2,1,0:T(8,128)(2,1)S(1)} %get-tuple-element.41.q_ref.refs_0_, bf16[1,1024,512]{2,1,0:T(8,128)(2,1)S(1)} %get-tuple-element.42.k_ref.refs_1_, ...), custom_call_target="tpu_custom_call" | custom-call | flops 536870912 | bytes 12582912 | tf_op jit(solution)/shard_map/merge/pallas_call | solution.py:511
  41.0 0.6 %add_add_fusion = f32[4,64]{1,0:T(4,128)} fusion(f32[4,64]{1,0:T(4,128)S(1)} %collective-permute-done.8, f32[4,64]{1,0:T(4,128)S(1)} %collective-permute-done.9, f32[4,64]{1,0:T(4,128)S(1)} %add_add_fusion.1, f32[4,64]{1,0:T(4,128)S(1)} %collective-permute-done.7), kind=kLoop, calls=%fused_computation.10 | loop fusion | flops 768 | bytes 5120 | tf_op jit(solution)/shard_map/add | solution.py:438
  (12 shorter events, 0.1 us)
Async XLA Ops:
  5.0 11.1 %collective-permute-start = (f32[2,128,128]{2,1,0:T(8,128)S(1)}, f32[2,128,128]{2,1,0:T(8,128)S(1)}, u32[]{:S(2)}, u32[]{:S(2)}) collective-permute-start(f32[2,128,128]{2,1,0:T(8,128)S(1)} %get-tuple-element.52), channel_id=1, source_target_pairs={{0,4},{12,8},{1,5},{13,9},{2,6},{14,10},{3,7},{15,11},{16,20},{28,... | collective-permute-start | bytes 393224 | tf_op jit(solution)/shard_map/ppermute | solution.py:545
  10.0 6.9 %collective-permute-start.1 = (f32[2,128,128]{2,1,0:T(8,128)S(1)}, f32[2,128,128]{2,1,0:T(8,128)S(1)}, u32[]{:S(2)}, u32[]{:S(2)}) collective-permute-start(f32[2,128,128]{2,1,0:T(8,128)S(1)} %get-tuple-element.58), channel_id=1, source_target_pairs={{0,4},{12,8},{1,5},{13,9},{2,6},{14,10},{3,7},{15,11},{16,20},{28,... | collective-permute-start | bytes 393224 | tf_op jit(solution)/shard_map/ppermute | solution.py:545
  16.2 6.3 %collective-permute-start.2 = (f32[2,128,128]{2,1,0:T(8,128)S(1)}, f32[2,128,128]{2,1,0:T(8,128)S(1)}, u32[]{:S(2)}, u32[]{:S(2)}) collective-permute-start(f32[2,128,128]{2,1,0:T(8,128)S(1)} %multiply_add_fusion.3), channel_id=1, source_target_pairs={{4,8},{8,4},{5,9},{9,5},{6,10},{10,6},{7,11},{11,7},{20,24},{24,20... | collective-permute-start | bytes 393224 | tf_op jit(solution)/shard_map/ppermute | solution.py:545
  16.9 5.7 %collective-permute-start.3 = (f32[2,128,128]{2,1,0:T(8,128)S(1)}, f32[2,128,128]{2,1,0:T(8,128)S(1)}, u32[]{:S(2)}, u32[]{:S(2)}) collective-permute-start(f32[2,128,128]{2,1,0:T(8,128)S(1)} %multiply_add_fusion.2), channel_id=1, source_target_pairs={{4,8},{8,4},{5,9},{9,5},{6,10},{10,6},{7,11},{11,7},{20,24},{24,20... | collective-permute-start | bytes 393224 | tf_op jit(solution)/shard_map/ppermute | solution.py:545
  22.9 2.6 %collective-permute-start.6 = (f32[4,64]{1,0:T(4,128)S(1)}, f32[4,64]{1,0:T(4,128)S(1)}, u32[]{:S(2)}, u32[]{:S(2)}) collective-permute-start(f32[4,64]{1,0:T(4,128)S(1)} %multiply_add_fusion.4), channel_id=1, source_target_pairs={{0,16},{16,0},{1,17},{17,1},{2,18},{18,2},{3,19},{19,3},{4,20},{20... | collective-permute-start | bytes 3080 | tf_op jit(solution)/shard_map/ppermute | solution.py:579
  22.9 10.3 %collective-permute-start.4 = (f32[2,128,128]{2,1,0:T(8,128)S(1)}, f32[2,128,128]{2,1,0:T(8,128)S(1)}, u32[]{:S(2)}, u32[]{:S(2)}) collective-permute-start(f32[2,128,128]{2,1,0:T(8,128)S(1)} %get-tuple-element.77), channel_id=1, source_target_pairs={{8,12},{4,0},{9,13},{5,1},{10,14},{6,2},{11,15},{7,3},{24,28},{20,... | collective-permute-start | bytes 393224 | tf_op jit(solution)/shard_map/ppermute | solution.py:545
  24.2 11.7 %collective-permute-start.5 = (f32[2,128,128]{2,1,0:T(8,128)S(1)}, f32[2,128,128]{2,1,0:T(8,128)S(1)}, u32[]{:S(2)}, u32[]{:S(2)}) collective-permute-start(f32[2,128,128]{2,1,0:T(8,128)S(1)} %get-tuple-element.80), channel_id=1, source_target_pairs={{8,12},{4,0},{9,13},{5,1},{10,14},{6,2},{11,15},{7,3},{24,28},{20,... | collective-permute-start | bytes 393224 | tf_op jit(solution)/shard_map/ppermute | solution.py:545
  25.6 15.4 %collective-permute-start.7 = (f32[4,64]{1,0:T(4,128)S(1)}, f32[4,64]{1,0:T(4,128)S(1)}, u32[]{:S(2)}, u32[]{:S(2)}) collective-permute-start(f32[4,64]{1,0:T(4,128)S(1)} %add_add_fusion.1), channel_id=1, source_target_pairs={{0,4},{4,0},{8,12},{12,8},{1,5},{5,1},{9,13},{13,9},{2,6},{6,2},{1... | collective-permute-start | bytes 3080 | tf_op jit(solution)/shard_map/ppermute | solution.py:582
  30.3 10.7 %collective-permute-start.8 = (f32[4,64]{1,0:T(4,128)S(1)}, f32[4,64]{1,0:T(4,128)S(1)}, u32[]{:S(2)}, u32[]{:S(2)}) collective-permute-start(f32[4,64]{1,0:T(4,128)S(1)} %add_add_fusion.1), channel_id=1, source_target_pairs={{0,8},{4,12},{8,0},{12,4},{1,9},{5,13},{9,1},{13,5},{2,10},{6,14},... | collective-permute-start | bytes 3080 | tf_op jit(solution)/shard_map/ppermute | solution.py:582
  31.4 9.6 %collective-permute-start.9 = (f32[4,64]{1,0:T(4,128)S(1)}, f32[4,64]{1,0:T(4,128)S(1)}, u32[]{:S(2)}, u32[]{:S(2)}) collective-permute-start(f32[4,64]{1,0:T(4,128)S(1)} %add_add_fusion.1), channel_id=1, source_target_pairs={{0,12},{4,8},{8,4},{12,0},{1,13},{5,9},{9,5},{13,1},{2,14},{6,10},... | collective-permute-start | bytes 3080 | tf_op jit(solution)/shard_map/ppermute | solution.py:582

commit v13 on v12

--- a/solution.py
+++ b/solution.py
@@ -314,7 +314,12 @@
         refs[7 + i * PARTS : 7 + (i + 1) * PARTS] for i in range(5)
     )
     refs = refs[7 + 5 * PARTS :]
-    targets, dgate_ref, staged, entering, leaving, spread_ref, gate_scr, sems = refs[:4], *refs[4:]
+    extra = len(refs) - 12
+    gain_refs, refs = refs[:extra], refs[extra:]
+    targets, dgate_ref, dgain_ref, staged, entering, leaving, spread_ref, gate_scr, sems = (
+        refs[:4], *refs[4:]
+    )
+    dgain_ref[...] = summed(gain_refs[0][...], [ref[...] for ref in gain_refs[1:]])
     heads = first_refs[0].shape[0]
     steps = sems.shape[0]
     num_chunks = fac_ref.shape[0] // 8
@@ -433,6 +438,8 @@
 
 
 def summed(own, others):
+    if not others:
+        return own
     if len(others) == 1:
         return own + others[0]
     return (own + others[0]) + (others[1] + others[2])
@@ -445,7 +452,7 @@
     part_width = width // PARTS
     num_chunks = tokens // CHUNK
     rows = num_chunks * 8
-    block = min(256, tokens)
+    block = min(128, tokens)
     steps = tokens // block
     count = lax.axis_size("ctx")
     middle = count // 2 - 1
@@ -511,8 +518,9 @@
         return pl.pallas_call(
             functools.partial(merge_kernel, head_width),
             in_specs=[vmem] * len(arrays),
-            out_specs=[hbm] * 4 + [vmem],
-            out_shape=[shape_of(1, tokens, width, dtype=BF16)] * 4 + [shape_of(*gates.shape)],
+            out_specs=[hbm] * 4 + [vmem] * 2,
+            out_shape=[shape_of(1, tokens, width, dtype=BF16)] * 4
+            + [shape_of(*gates.shape), shape_of(*arrays[-1].shape)],
             scratch_shapes=[
                 pltpu.VMEM((4, tokens, width), BF16),
                 pltpu.VMEM((PARTS, part_width, part_width), BF16),
@@ -602,10 +610,10 @@
             *[local_part[0] for local_part in local_parts],
             *[local_part[1] for local_part in local_parts],
             *firsts, *seconds, *[own[-1] for own in arrived],
+            grad_gain, *pending,
         )
     )
-    pending, done[4] = lax.optimization_barrier((pending, done[4]))
-    return (*done, summed(grad_gain, pending))
+    return tuple(done)
 
 
 def solution(mesh):

time: 42 us -> 41.8 us (level)
  waiting for transfers between devices: 3.14 us -> 4.1 us
  starting transfers between devices: 17.4 us -> 16.5 us
  other arithmetic: 1.88 us -> 1.3 us
    ppermute x3, waiting for transfers between devices: 0.01 us -> 4.08 us  [exchanged(): return lax.ppermute(array, 'ctx', [(i, i ^ reach) for i in range(count)])]
    ppermute x6, waiting for transfers between devices: 3.13 us -> 0.02 us  [send(): lax.ppermute(payload, 'ctx', [(hop, hop + 1), (count - 1 - hop, count - 2...]
    ppermute x3, starting transfers between devices: 7.2 us -> 6.3 us  [exchanged(): return lax.ppermute(array, 'ctx', [(i, i ^ reach) for i in range(count)])]
    add x1 -> x0, other arithmetic: 0.58 us -> none  [summed(): return own + others[0] + (others[1] + others[2])]
  transfers between devices with their start and end apart: 10 -> 10, of which waited for: 2 -> 2; matrix products, arithmetic and copies ran while one was open for 1% -> 1% of each run, Pallas kernels for 35% -> 23%
where the time goes in v13:
time: 41.8 us; the launch traced here: 41.5 us
  Pallas kernels  18.8 us (45%)
  starting transfers between devices  16.5 us (39%)
  waiting for transfers between devices  4.1 us (10%)
  other arithmetic  1.3 us (3%)
  between operations  0.79 us (2%)
    ppermute x6, starting transfers between devices, send(): lax.ppermute(payload, 'ctx', [(hop, hop + 1), (count - 1 - hop, count - 2...  10.2 us
    pallas_call x2, Pallas kernels, local(): pl.pallas_call(functools.partial(local_kernel, head_width, part), in_spec...  9.68 us
    ppermute x3, starting transfers between devices, exchanged(): return lax.ppermute(array, 'ctx', [(i, i ^ reach) for i in range(count)])  6.3 us
    pallas_call x1, Pallas kernels, merge(): pl.pallas_call(functools.partial(merge_kernel, head_width), in_specs=[vme...  5.4 us
    ppermute x3, waiting for transfers between devices, exchanged(): return lax.ppermute(array, 'ctx', [(i, i ^ reach) for i in range(count)])  4.08 us
    pallas_call x1, Pallas kernels, ends(): pl.pallas_call(functools.partial(ends_kernel, head_width, lengths.shape[1...  3.74 us
  transfers between devices with their start and end apart: 10, of which 2 were waited for; matrix products, arithmetic and copies ran while one was open for 1% of the time, Pallas kernels for 23%

profile of v13, /device:TPU:0, one launch (start us, length us, event | category | flops | bytes accessed | tf_op | source)
XLA Modules:
  0.0 41.5 jit_solution(18206522326653730100)
XLA Ops:
  0.6 0.8 %convert_add_fusion.refs_0_ = f32[4,1280]{1,0:T(4,128)S(1)} fusion(s32[1,16]{1,0:T(1,128)} %param.11, f32[4,128]{1,0:T(4,128)} %param.12, f32[4,1024]{1,0:T(4,128)} %bitcast.13), kind=kLoop, calls=%fused_computation.8 | loop fusion | flops 15360 | bytes 38976 | tf_op jit(solution)/shard_map/add | solution.py:462
  1.4 3.7 %shard_ends.1 = (f32[2,128,128]{2,1,0:T(8,128)S(1)}, f32[2,128,128]{2,1,0:T(8,128)S(1)}, f32[2,128,128]{2,1,0:T(8,128)S(1)}, f32[2,128,128]{2,1,0:T(8,128)S(1)},...) custom-call(f32[4,1280]{1,0:T(4,128)S(1)} %convert_add_fusion.refs_0, ...), custom_call_target="tpu_custom_call" | custom-call | flops 268435456 | bytes 4194304 | tf_op jit(solution)/shard_map/shard_ends/pallas_call | solution.py:484
  5.1 4.9 %collective-permute-start = (f32[2,128,128]{2,1,0:T(8,128)S(1)}, f32[2,128,128]{2,1,0:T(8,128)S(1)}, u32[]{:S(2)}, u32[]{:S(2)}) collective-permute-start(f32[2,128,128]{2,1,0:T(8,128)S(1)} %get-tuple-element.43), channel_id=1, source_target_pairs={{0,4},{12,8},{1,5},{13,9},{2,6},{14,10},{3,7},{15,11},{16,20},{28,... | collective-permute-start | bytes 393224 | tf_op jit(solution)/shard_map/ppermute | solution.py:553
  10.1 1.3 %collective-permute-start.1 = (f32[2,128,128]{2,1,0:T(8,128)S(1)}, f32[2,128,128]{2,1,0:T(8,128)S(1)}, u32[]{:S(2)}, u32[]{:S(2)}) collective-permute-start(f32[2,128,128]{2,1,0:T(8,128)S(1)} %get-tuple-element.49), channel_id=1, source_target_pairs={{0,4},{12,8},{1,5},{13,9},{2,6},{14,10},{3,7},{15,11},{16,20},{28,... | collective-permute-start | bytes 393224 | tf_op jit(solution)/shard_map/ppermute | solution.py:553
  11.4 4.8 %local_0.1 = (bf16[4,1024,256]{2,1,0:T(8,128)(2,1)S(1)}, f32[1,2,1024]{2,1,0:T(2,128)S(1)}, f32[2,128]{1,0:T(2,128)S(1)}) custom-call(bf16[1,1024,512]{2,1,0:T(8,128)(2,1)S(1)} %get-tuple-element.32.q_ref.refs_0_, bf16[1,1024,512]{2,1,0:T(8,128)(2,1)S(1)} %get-tuple-element.33.k_ref.refs_1_, bf16[1,1024,512]{2,1,0:T(8,128)(2,1)S(1)} %get-tuple-element.34.v_ref.refs_2_, ...), custom_call_target="tpu_custom_call" | custom-call | flops 805306368 | bytes 4194304 | tf_op jit(solution)/shard_map/local_0/pallas_call | solution.py:501
  16.2 0.0 collective-permute-done.refs_11_
  16.3 0.7 %collective-permute-start.2 = (f32[2,128,128]{2,1,0:T(8,128)S(1)}, f32[2,128,128]{2,1,0:T(8,128)S(1)}, u32[]{:S(2)}, u32[]{:S(2)}) collective-permute-start(f32[2,128,128]{2,1,0:T(8,128)S(1)} %multiply_add_fusion.3), channel_id=1, source_target_pairs={{4,8},{8,4},{5,9},{9,5},{6,10},{10,6},{7,11},{11,7},{20,24},{24,20... | collective-permute-start | bytes 393224 | tf_op jit(solution)/shard_map/ppermute | solution.py:553
  16.9 0.0 collective-permute-done.1.refs_12_
  17.0 0.7 %collective-permute-start.3 = (f32[2,128,128]{2,1,0:T(8,128)S(1)}, f32[2,128,128]{2,1,0:T(8,128)S(1)}, u32[]{:S(2)}, u32[]{:S(2)}) collective-permute-start(f32[2,128,128]{2,1,0:T(8,128)S(1)} %multiply_add_fusion.2), channel_id=1, source_target_pairs={{4,8},{8,4},{5,9},{9,5},{6,10},{10,6},{7,11},{11,7},{20,24},{24,20... | collective-permute-start | bytes 393224 | tf_op jit(solution)/shard_map/ppermute | solution.py:553
  17.6 4.9 %local_1.1 = (bf16[4,1024,256]{2,1,0:T(8,128)(2,1)S(1)}, f32[1,2,1024]{2,1,0:T(2,128)S(1)}, f32[2,128]{1,0:T(2,128)S(1)}) custom-call(bf16[1,1024,512]{2,1,0:T(8,128)(2,1)S(1)} %get-tuple-element.32.q_ref.refs_0_, bf16[1,1024,512]{2,1,0:T(8,128)(2,1)S(1)} %get-tuple-element.33.k_ref.refs_1_, bf16[1,1024,512]{2,1,0:T(8,128)(2,1)S(1)} %get-tuple-element.34.v_ref.refs_2_, ...), custom_call_target="tpu_custom_call" | custom-call | flops 805306368 | bytes 4194304 | tf_op jit(solution)/shard_map/local_1/pallas_call | solution.py:501
  22.5 0.2 multiply_reduce_fusion.3
  22.7 0.0 collective-permute-done.3.refs_14_
  22.7 0.2 multiply_reduce_fusion.1
  22.9 0.1 multiply_add_fusion.4
  23.0 0.0 collective-permute-start.6
  23.0 1.3 %collective-permute-start.5 = (f32[2,128,128]{2,1,0:T(8,128)S(1)}, f32[2,128,128]{2,1,0:T(8,128)S(1)}, u32[]{:S(2)}, u32[]{:S(2)}) collective-permute-start(f32[2,128,128]{2,1,0:T(8,128)S(1)} %get-tuple-element.62), channel_id=1, source_target_pairs={{8,12},{4,0},{9,13},{5,1},{10,14},{6,2},{11,15},{7,3},{24,28},{20,... | collective-permute-start | bytes 393224 | tf_op jit(solution)/shard_map/ppermute | solution.py:553
  24.3 1.3 %collective-permute-start.4 = (f32[2,128,128]{2,1,0:T(8,128)S(1)}, f32[2,128,128]{2,1,0:T(8,128)S(1)}, u32[]{:S(2)}, u32[]{:S(2)}) collective-permute-start(f32[2,128,128]{2,1,0:T(8,128)S(1)} %get-tuple-element.59), channel_id=1, source_target_pairs={{8,12},{4,0},{9,13},{5,1},{10,14},{6,2},{11,15},{7,3},{24,28},{20,... | collective-permute-start | bytes 393224 | tf_op jit(solution)/shard_map/ppermute | solution.py:553
  25.6 0.1 add_add_fusion.refs_17_
  25.7 2.5 %collective-permute-start.9 = (f32[4,64]{1,0:T(4,128)S(1)}, f32[4,64]{1,0:T(4,128)S(1)}, u32[]{:S(2)}, u32[]{:S(2)}) collective-permute-start(f32[4,64]{1,0:T(4,128)S(1)} %add_add_fusion.refs_17_), channel_id=1, source_target_pairs={{0,12},{4,8},{8,4},{12,0},{1,13},{5,9},{9,5},{13,1},{2,14},{6,10},... | collective-permute-start | bytes 3080 | tf_op jit(solution)/shard_map/ppermute | solution.py:590
  28.2 3.7 %collective-permute-start.8 = (f32[4,64]{1,0:T(4,128)S(1)}, f32[4,64]{1,0:T(4,128)S(1)}, u32[]{:S(2)}, u32[]{:S(2)}) collective-permute-start(f32[4,64]{1,0:T(4,128)S(1)} %add_add_fusion.refs_17_), channel_id=1, source_target_pairs={{0,8},{4,12},{8,0},{12,4},{1,9},{5,13},{9,1},{13,5},{2,10},{6,14},... | collective-permute-start | bytes 3080 | tf_op jit(solution)/shard_map/ppermute | solution.py:590
  31.9 0.1 collective-permute-start.7
  32.0 1.5 %collective-permute-done.8.refs_19_ = f32[4,64]{1,0:T(4,128)S(1)} collective-permute-done((f32[4,64]{1,0:T(4,128)S(1)}, f32[4,64]{1,0:T(4,128)S(1)}, u32[]{:S(2)}, u32[]{:S(2)}) %collective-permute-start.8) | collective-permute-done | bytes 1056 | tf_op jit(solution)/shard_map/ppermute | solution.py:590
  33.5 2.6 %collective-permute-done.7.refs_18_ = f32[4,64]{1,0:T(4,128)S(1)} collective-permute-done((f32[4,64]{1,0:T(4,128)S(1)}, f32[4,64]{1,0:T(4,128)S(1)}, u32[]{:S(2)}, u32[]{:S(2)}) %collective-permute-start.7) | collective-permute-done | bytes 1056 | tf_op jit(solution)/shard_map/ppermute | solution.py:590
  36.1 5.4 %merge.1 = (bf16[1,1024,512]{2,1,0:T(8,128)(2,1)}, bf16[1,1024,512]{2,1,0:T(8,128)(2,1)}, bf16[1,1024,512]{2,1,0:T(8,128)(2,1)}, bf16[1,1024,512]{2,1,0:T(8,128)...) custom-call(bf16[1,1024,512]{2,1,0:T(8,128)(2,1)S(1)} %get-tuple-element.32.q_ref.refs_0_, ...), custom_call_target="tpu_custom_call" | custom-call | flops 536870912 | bytes 12582912 | tf_op jit(solution)/shard_map/merge/pallas_call | solution.py:518
  (11 shorter events, 0.1 us)
Async XLA Ops:
  5.1 11.1 %collective-permute-start = (f32[2,128,128]{2,1,0:T(8,128)S(1)}, f32[2,128,128]{2,1,0:T(8,128)S(1)}, u32[]{:S(2)}, u32[]{:S(2)}) collective-permute-start(f32[2,128,128]{2,1,0:T(8,128)S(1)} %get-tuple-element.43), channel_id=1, source_target_pairs={{0,4},{12,8},{1,5},{13,9},{2,6},{14,10},{3,7},{15,11},{16,20},{28,... | collective-permute-start | bytes 393224 | tf_op jit(solution)/shard_map/ppermute | solution.py:553
  10.1 6.9 %collective-permute-start.1 = (f32[2,128,128]{2,1,0:T(8,128)S(1)}, f32[2,128,128]{2,1,0:T(8,128)S(1)}, u32[]{:S(2)}, u32[]{:S(2)}) collective-permute-start(f32[2,128,128]{2,1,0:T(8,128)S(1)} %get-tuple-element.49), channel_id=1, source_target_pairs={{0,4},{12,8},{1,5},{13,9},{2,6},{14,10},{3,7},{15,11},{16,20},{28,... | collective-permute-start | bytes 393224 | tf_op jit(solution)/shard_map/ppermute | solution.py:553
  16.3 6.3 %collective-permute-start.2 = (f32[2,128,128]{2,1,0:T(8,128)S(1)}, f32[2,128,128]{2,1,0:T(8,128)S(1)}, u32[]{:S(2)}, u32[]{:S(2)}) collective-permute-start(f32[2,128,128]{2,1,0:T(8,128)S(1)} %multiply_add_fusion.3), channel_id=1, source_target_pairs={{4,8},{8,4},{5,9},{9,5},{6,10},{10,6},{7,11},{11,7},{20,24},{24,20... | collective-permute-start | bytes 393224 | tf_op jit(solution)/shard_map/ppermute | solution.py:553
  17.0 5.7 %collective-permute-start.3 = (f32[2,128,128]{2,1,0:T(8,128)S(1)}, f32[2,128,128]{2,1,0:T(8,128)S(1)}, u32[]{:S(2)}, u32[]{:S(2)}) collective-permute-start(f32[2,128,128]{2,1,0:T(8,128)S(1)} %multiply_add_fusion.2), channel_id=1, source_target_pairs={{4,8},{8,4},{5,9},{9,5},{6,10},{10,6},{7,11},{11,7},{20,24},{24,20... | collective-permute-start | bytes 393224 | tf_op jit(solution)/shard_map/ppermute | solution.py:553
  23.0 2.6 %collective-permute-start.6 = (f32[4,64]{1,0:T(4,128)S(1)}, f32[4,64]{1,0:T(4,128)S(1)}, u32[]{:S(2)}, u32[]{:S(2)}) collective-permute-start(f32[4,64]{1,0:T(4,128)S(1)} %multiply_add_fusion.4), channel_id=1, source_target_pairs={{0,16},{16,0},{1,17},{17,1},{2,18},{18,2},{3,19},{19,3},{4,20},{20... | collective-permute-start | bytes 3080 | tf_op jit(solution)/shard_map/ppermute | solution.py:587
  23.0 13.1 %collective-permute-start.5 = (f32[2,128,128]{2,1,0:T(8,128)S(1)}, f32[2,128,128]{2,1,0:T(8,128)S(1)}, u32[]{:S(2)}, u32[]{:S(2)}) collective-permute-start(f32[2,128,128]{2,1,0:T(8,128)S(1)} %get-tuple-element.62), channel_id=1, source_target_pairs={{8,12},{4,0},{9,13},{5,1},{10,14},{6,2},{11,15},{7,3},{24,28},{20,... | collective-permute-start | bytes 393224 | tf_op jit(solution)/shard_map/ppermute | solution.py:553
  24.3 11.8 %collective-permute-start.4 = (f32[2,128,128]{2,1,0:T(8,128)S(1)}, f32[2,128,128]{2,1,0:T(8,128)S(1)}, u32[]{:S(2)}, u32[]{:S(2)}) collective-permute-start(f32[2,128,128]{2,1,0:T(8,128)S(1)} %get-tuple-element.59), channel_id=1, source_target_pairs={{8,12},{4,0},{9,13},{5,1},{10,14},{6,2},{11,15},{7,3},{24,28},{20,... | collective-permute-start | bytes 393224 | tf_op jit(solution)/shard_map/ppermute | solution.py:553
  25.7 6.3 %collective-permute-start.9 = (f32[4,64]{1,0:T(4,128)S(1)}, f32[4,64]{1,0:T(4,128)S(1)}, u32[]{:S(2)}, u32[]{:S(2)}) collective-permute-start(f32[4,64]{1,0:T(4,128)S(1)} %add_add_fusion.refs_17_), channel_id=1, source_target_pairs={{0,12},{4,8},{8,4},{12,0},{1,13},{5,9},{9,5},{13,1},{2,14},{6,10},... | collective-permute-start | bytes 3080 | tf_op jit(solution)/shard_map/ppermute | solution.py:590
  28.2 5.3 %collective-permute-start.8 = (f32[4,64]{1,0:T(4,128)S(1)}, f32[4,64]{1,0:T(4,128)S(1)}, u32[]{:S(2)}, u32[]{:S(2)}) collective-permute-start(f32[4,64]{1,0:T(4,128)S(1)} %add_add_fusion.refs_17_), channel_id=1, source_target_pairs={{0,8},{4,12},{8,0},{12,4},{1,9},{5,13},{9,1},{13,5},{2,10},{6,14},... | collective-permute-start | bytes 3080 | tf_op jit(solution)/shard_map/ppermute | solution.py:590
  31.9 4.2 %collective-permute-start.7 = (f32[4,64]{1,0:T(4,128)S(1)}, f32[4,64]{1,0:T(4,128)S(1)}, u32[]{:S(2)}, u32[]{:S(2)}) collective-permute-start(f32[4,64]{1,0:T(4,128)S(1)} %add_add_fusion.refs_17_), channel_id=1, source_target_pairs={{0,4},{4,0},{8,12},{12,8},{1,5},{5,1},{9,13},{13,9},{2,6},{6,2},{1... | collective-permute-start | bytes 3080 | tf_op jit(solution)/shard_map/ppermute | solution.py:590

commit v14 on v13

--- a/solution.py
+++ b/solution.py
@@ -314,9 +314,9 @@
         refs[7 + i * PARTS : 7 + (i + 1) * PARTS] for i in range(5)
     )
     refs = refs[7 + 5 * PARTS :]
-    extra = len(refs) - 12
+    extra = len(refs) - 11
     gain_refs, refs = refs[:extra], refs[extra:]
-    targets, dgate_ref, dgain_ref, staged, entering, leaving, spread_ref, gate_scr, sems = (
+    targets, dgate_ref, dgain_ref, staged, matrices, spread_ref, gate_scr, sems = (
         refs[:4], *refs[4:]
     )
     dgain_ref[...] = summed(gain_refs[0][...], [ref[...] for ref in gain_refs[1:]])
@@ -336,8 +336,7 @@
         ]
 
     gain_columns = jnp.transpose(jnp.concatenate([gain_ref[...], gain_ref[...]], axis=0))
-    entering[...] = jnp.zeros_like(entering)
-    leaving[...] = jnp.zeros_like(leaving)
+    matrices[...] = jnp.zeros_like(matrices)
     last_factors = fac_ref[(num_chunks - 1) * 8 : num_chunks * 8, CHUNK - 1 : CHUNK]
     low = jnp.broadcast_to(flag_ref[2:3, :], (head_width, head_width)) > 0.5
     constants = []
@@ -350,8 +349,11 @@
             second = second_refs[part][head] + last_refs[part][head]
             state = jnp.where(low, first, second) * gain
             later = jnp.where(low, second, first)
-            entering[part, own, own] = (state * scale).astype(BF16)
-            leaving[part, own, own] = (later * gain).astype(BF16)
+            entering, leaving = state * scale, later * gain
+            for i, matrix in enumerate(
+                (entering, jnp.transpose(entering), jnp.transpose(leaving), leaving)
+            ):
+                matrices[part, i, own, own] = matrix.astype(BF16)
             constants.append(total_of(state * later) * last_factors[row : row + 1])
 
     spread = (iota(spread_ref.shape, 1) // head_width == iota(spread_ref.shape, 0) % 8).astype(F32)
@@ -360,20 +362,22 @@
     for step in range(steps):
         numbers = range(step * chunks, (step + 1) * chunks)
         products, results, factors = {}, {}, {}
+        block_rows = slice(step * block, (step + 1) * block)
+        for part in range(PARTS):
+            group = slice(part * group_width, (part + 1) * group_width)
+            block_products = [
+                dot_nn(ref[0, block_rows, group], matrices[part, i])
+                for i, ref in enumerate((q_ref, cot_ref, v_ref, k_ref))
+            ]
+            for i, number in enumerate(numbers):
+                products[number, part] = [
+                    product[i * CHUNK : (i + 1) * CHUNK] for product in block_products
+                ]
         for number in numbers:
-            rows = slice(number * CHUNK, (number + 1) * CHUNK)
             fac = fac_ref[number * 8 : number * 8 + 8, :]
             high = fac.astype(BF16).astype(F32)
             both = jnp.concatenate([high, fac - high], axis=0).astype(BF16)
             factors[number] = dot_tn(both, spread_ref[...])
-            for part in range(PARTS):
-                group = slice(part * group_width, (part + 1) * group_width)
-                products[number, part] = (
-                    dot_nn(q_ref[0, rows, group], entering[part]),
-                    dot_nt(cot_ref[0, rows, group], entering[part]),
-                    dot_nt(v_ref[0, rows, group], leaving[part]),
-                    dot_nn(k_ref[0, rows, group], leaving[part]),
-                )
         for number in numbers:
             rows = slice(number * CHUNK, (number + 1) * CHUNK)
             for row in range(PARTS * heads):
@@ -452,7 +456,7 @@
     part_width = width // PARTS
     num_chunks = tokens // CHUNK
     rows = num_chunks * 8
-    block = min(128, tokens)
+    block = min(256, tokens)
     steps = tokens // block
     count = lax.axis_size("ctx")
     middle = count // 2 - 1
@@ -523,8 +527,7 @@
             + [shape_of(*gates.shape), shape_of(*arrays[-1].shape)],
             scratch_shapes=[
                 pltpu.VMEM((4, tokens, width), BF16),
-                pltpu.VMEM((PARTS, part_width, part_width), BF16),
-                pltpu.VMEM((PARTS, part_width, part_width), BF16),
+                pltpu.VMEM((PARTS, 4, part_width, part_width), BF16),
                 pltpu.VMEM((16, 8 * head_width), BF16),
                 pltpu.VMEM((rows, CHUNK), F32),
                 pltpu.SemaphoreType.DMA((steps, 4)),

time: 41.8 us -> 41.9 us (level)
  no operation moved by 1% of the time
where the time goes in v14:
time: 41.9 us; the launch traced here: 41.6 us
  Pallas kernels  18.9 us (45%)
  starting transfers between devices  16.5 us (39%)
  waiting for transfers between devices  4.1 us (10%)
  other arithmetic  1.3 us (3%)
  between operations  0.79 us (2%)
    ppermute x6, starting transfers between devices, send(): lax.ppermute(payload, 'ctx', [(hop, hop + 1), (count - 1 - hop, count - 2...  10.2 us
    pallas_call x2, Pallas kernels, local(): pl.pallas_call(functools.partial(local_kernel, head_width, part), in_spec...  9.68 us
    ppermute x3, starting transfers between devices, exchanged(): return lax.ppermute(array, 'ctx', [(i, i ^ reach) for i in range(count)])  6.3 us
    pallas_call x1, Pallas kernels, merge(): pl.pallas_call(functools.partial(merge_kernel, head_width), in_specs=[vme...  5.57 us
    ppermute x3, waiting for transfers between devices, exchanged(): return lax.ppermute(array, 'ctx', [(i, i ^ reach) for i in range(count)])  4.08 us
    pallas_call x1, Pallas kernels, ends(): pl.pallas_call(functools.partial(ends_kernel, head_width, lengths.shape[1...  3.64 us
  transfers between devices with their start and end apart: 10, of which 2 were waited for; matrix products, arithmetic and copies ran while one was open for 1% of the time, Pallas kernels for 23%

profile of v14, /device:TPU:0, one launch (start us, length us, event | category | flops | bytes accessed | tf_op | source)
XLA Modules:
  0.0 41.6 jit_solution(6143250475146365786)
XLA Ops:
  0.6 0.8 %convert_add_fusion.refs_0_ = f32[4,1280]{1,0:T(4,128)S(1)} fusion(s32[1,16]{1,0:T(1,128)} %param.11, f32[4,128]{1,0:T(4,128)} %param.12, f32[4,1024]{1,0:T(4,128)} %bitcast.13), kind=kLoop, calls=%fused_computation.8 | loop fusion | flops 15360 | bytes 38976 | tf_op jit(solution)/shard_map/add | solution.py:466
  1.4 3.6 %shard_ends.1 = (f32[2,128,128]{2,1,0:T(8,128)S(1)}, f32[2,128,128]{2,1,0:T(8,128)S(1)}, f32[2,128,128]{2,1,0:T(8,128)S(1)}, f32[2,128,128]{2,1,0:T(8,128)S(1)},...) custom-call(f32[4,1280]{1,0:T(4,128)S(1)} %convert_add_fusion.refs_0, ...), custom_call_target="tpu_custom_call" | custom-call | flops 268435456 | bytes 4194304 | tf_op jit(solution)/shard_map/shard_ends/pallas_call | solution.py:488
  5.0 4.9 %collective-permute-start = (f32[2,128,128]{2,1,0:T(8,128)S(1)}, f32[2,128,128]{2,1,0:T(8,128)S(1)}, u32[]{:S(2)}, u32[]{:S(2)}) collective-permute-start(f32[2,128,128]{2,1,0:T(8,128)S(1)} %get-tuple-element.43), channel_id=1, source_target_pairs={{0,4},{12,8},{1,5},{13,9},{2,6},{14,10},{3,7},{15,11},{16,20},{28,... | collective-permute-start | bytes 393224 | tf_op jit(solution)/shard_map/ppermute | solution.py:556
  10.0 1.3 %collective-permute-start.1 = (f32[2,128,128]{2,1,0:T(8,128)S(1)}, f32[2,128,128]{2,1,0:T(8,128)S(1)}, u32[]{:S(2)}, u32[]{:S(2)}) collective-permute-start(f32[2,128,128]{2,1,0:T(8,128)S(1)} %get-tuple-element.49), channel_id=1, source_target_pairs={{0,4},{12,8},{1,5},{13,9},{2,6},{14,10},{3,7},{15,11},{16,20},{28,... | collective-permute-start | bytes 393224 | tf_op jit(solution)/shard_map/ppermute | solution.py:556
  11.3 4.8 %local_0.1 = (bf16[4,1024,256]{2,1,0:T(8,128)(2,1)S(1)}, f32[1,2,1024]{2,1,0:T(2,128)S(1)}, f32[2,128]{1,0:T(2,128)S(1)}) custom-call(bf16[1,1024,512]{2,1,0:T(8,128)(2,1)S(1)} %get-tuple-element.32.q_ref.refs_0_, bf16[1,1024,512]{2,1,0:T(8,128)(2,1)S(1)} %get-tuple-element.33.k_ref.refs_1_, bf16[1,1024,512]{2,1,0:T(8,128)(2,1)S(1)} %get-tuple-element.34.v_ref.refs_2_, ...), custom_call_target="tpu_custom_call" | custom-call | flops 805306368 | bytes 4194304 | tf_op jit(solution)/shard_map/local_0/pallas_call | solution.py:505
  16.1 0.0 collective-permute-done.refs_11_
  16.2 0.7 %collective-permute-start.2 = (f32[2,128,128]{2,1,0:T(8,128)S(1)}, f32[2,128,128]{2,1,0:T(8,128)S(1)}, u32[]{:S(2)}, u32[]{:S(2)}) collective-permute-start(f32[2,128,128]{2,1,0:T(8,128)S(1)} %multiply_add_fusion.3), channel_id=1, source_target_pairs={{4,8},{8,4},{5,9},{9,5},{6,10},{10,6},{7,11},{11,7},{20,24},{24,20... | collective-permute-start | bytes 393224 | tf_op jit(solution)/shard_map/ppermute | solution.py:556
  16.9 0.7 %collective-permute-start.3 = (f32[2,128,128]{2,1,0:T(8,128)S(1)}, f32[2,128,128]{2,1,0:T(8,128)S(1)}, u32[]{:S(2)}, u32[]{:S(2)}) collective-permute-start(f32[2,128,128]{2,1,0:T(8,128)S(1)} %multiply_add_fusion.2), channel_id=1, source_target_pairs={{4,8},{8,4},{5,9},{9,5},{6,10},{10,6},{7,11},{11,7},{20,24},{24,20... | collective-permute-start | bytes 393224 | tf_op jit(solution)/shard_map/ppermute | solution.py:556
  17.6 4.9 %local_1.1 = (bf16[4,1024,256]{2,1,0:T(8,128)(2,1)S(1)}, f32[1,2,1024]{2,1,0:T(2,128)S(1)}, f32[2,128]{1,0:T(2,128)S(1)}) custom-call(bf16[1,1024,512]{2,1,0:T(8,128)(2,1)S(1)} %get-tuple-element.32.q_ref.refs_0_, bf16[1,1024,512]{2,1,0:T(8,128)(2,1)S(1)} %get-tuple-element.33.k_ref.refs_1_, bf16[1,1024,512]{2,1,0:T(8,128)(2,1)S(1)} %get-tuple-element.34.v_ref.refs_2_, ...), custom_call_target="tpu_custom_call" | custom-call | flops 805306368 | bytes 4194304 | tf_op jit(solution)/shard_map/local_1/pallas_call | solution.py:505
  22.4 0.2 multiply_reduce_fusion.3
  22.6 0.0 collective-permute-done.3.refs_14_
  22.6 0.2 multiply_reduce_fusion.1
  22.8 0.1 multiply_add_fusion.4
  22.9 0.0 collective-permute-start.6
  22.9 1.3 %collective-permute-start.5 = (f32[2,128,128]{2,1,0:T(8,128)S(1)}, f32[2,128,128]{2,1,0:T(8,128)S(1)}, u32[]{:S(2)}, u32[]{:S(2)}) collective-permute-start(f32[2,128,128]{2,1,0:T(8,128)S(1)} %get-tuple-element.62), channel_id=1, source_target_pairs={{8,12},{4,0},{9,13},{5,1},{10,14},{6,2},{11,15},{7,3},{24,28},{20,... | collective-permute-start | bytes 393224 | tf_op jit(solution)/shard_map/ppermute | solution.py:556
  24.2 1.3 %collective-permute-start.4 = (f32[2,128,128]{2,1,0:T(8,128)S(1)}, f32[2,128,128]{2,1,0:T(8,128)S(1)}, u32[]{:S(2)}, u32[]{:S(2)}) collective-permute-start(f32[2,128,128]{2,1,0:T(8,128)S(1)} %get-tuple-element.59), channel_id=1, source_target_pairs={{8,12},{4,0},{9,13},{5,1},{10,14},{6,2},{11,15},{7,3},{24,28},{20,... | collective-permute-start | bytes 393224 | tf_op jit(solution)/shard_map/ppermute | solution.py:556
  25.5 0.0 collective-permute-done.6
  25.5 0.1 add_add_fusion.refs_17_
  25.6 2.5 %collective-permute-start.9 = (f32[4,64]{1,0:T(4,128)S(1)}, f32[4,64]{1,0:T(4,128)S(1)}, u32[]{:S(2)}, u32[]{:S(2)}) collective-permute-start(f32[4,64]{1,0:T(4,128)S(1)} %add_add_fusion.refs_17_), channel_id=1, source_target_pairs={{0,12},{4,8},{8,4},{12,0},{1,13},{5,9},{9,5},{13,1},{2,14},{6,10},... | collective-permute-start | bytes 3080 | tf_op jit(solution)/shard_map/ppermute | solution.py:593
  28.1 3.7 %collective-permute-start.8 = (f32[4,64]{1,0:T(4,128)S(1)}, f32[4,64]{1,0:T(4,128)S(1)}, u32[]{:S(2)}, u32[]{:S(2)}) collective-permute-start(f32[4,64]{1,0:T(4,128)S(1)} %add_add_fusion.refs_17_), channel_id=1, source_target_pairs={{0,8},{4,12},{8,0},{12,4},{1,9},{5,13},{9,1},{13,5},{2,10},{6,14},... | collective-permute-start | bytes 3080 | tf_op jit(solution)/shard_map/ppermute | solution.py:593
  31.8 0.1 collective-permute-start.7
  31.9 1.5 %collective-permute-done.8.refs_19_ = f32[4,64]{1,0:T(4,128)S(1)} collective-permute-done((f32[4,64]{1,0:T(4,128)S(1)}, f32[4,64]{1,0:T(4,128)S(1)}, u32[]{:S(2)}, u32[]{:S(2)}) %collective-permute-start.8) | collective-permute-done | bytes 1056 | tf_op jit(solution)/shard_map/ppermute | solution.py:593
  33.4 2.6 %collective-permute-done.7.refs_18_ = f32[4,64]{1,0:T(4,128)S(1)} collective-permute-done((f32[4,64]{1,0:T(4,128)S(1)}, f32[4,64]{1,0:T(4,128)S(1)}, u32[]{:S(2)}, u32[]{:S(2)}) %collective-permute-start.7) | collective-permute-done | bytes 1056 | tf_op jit(solution)/shard_map/ppermute | solution.py:593
  36.0 5.6 %merge.1 = (bf16[1,1024,512]{2,1,0:T(8,128)(2,1)}, bf16[1,1024,512]{2,1,0:T(8,128)(2,1)}, bf16[1,1024,512]{2,1,0:T(8,128)(2,1)}, bf16[1,1024,512]{2,1,0:T(8,128)...) custom-call(bf16[1,1024,512]{2,1,0:T(8,128)(2,1)S(1)} %get-tuple-element.32.q_ref.refs_0_, ...), custom_call_target="tpu_custom_call" | custom-call | flops 536870912 | bytes 12582912 | tf_op jit(solution)/shard_map/merge/pallas_call | solution.py:522
  (11 shorter events, 0.1 us)
Async XLA Ops:
  5.0 11.1 %collective-permute-start = (f32[2,128,128]{2,1,0:T(8,128)S(1)}, f32[2,128,128]{2,1,0:T(8,128)S(1)}, u32[]{:S(2)}, u32[]{:S(2)}) collective-permute-start(f32[2,128,128]{2,1,0:T(8,128)S(1)} %get-tuple-element.43), channel_id=1, source_target_pairs={{0,4},{12,8},{1,5},{13,9},{2,6},{14,10},{3,7},{15,11},{16,20},{28,... | collective-permute-start | bytes 393224 | tf_op jit(solution)/shard_map/ppermute | solution.py:556
  10.0 6.9 %collective-permute-start.1 = (f32[2,128,128]{2,1,0:T(8,128)S(1)}, f32[2,128,128]{2,1,0:T(8,128)S(1)}, u32[]{:S(2)}, u32[]{:S(2)}) collective-permute-start(f32[2,128,128]{2,1,0:T(8,128)S(1)} %get-tuple-element.49), channel_id=1, source_target_pairs={{0,4},{12,8},{1,5},{13,9},{2,6},{14,10},{3,7},{15,11},{16,20},{28,... | collective-permute-start | bytes 393224 | tf_op jit(solution)/shard_map/ppermute | solution.py:556
  16.2 6.3 %collective-permute-start.2 = (f32[2,128,128]{2,1,0:T(8,128)S(1)}, f32[2,128,128]{2,1,0:T(8,128)S(1)}, u32[]{:S(2)}, u32[]{:S(2)}) collective-permute-start(f32[2,128,128]{2,1,0:T(8,128)S(1)} %multiply_add_fusion.3), channel_id=1, source_target_pairs={{4,8},{8,4},{5,9},{9,5},{6,10},{10,6},{7,11},{11,7},{20,24},{24,20... | collective-permute-start | bytes 393224 | tf_op jit(solution)/shard_map/ppermute | solution.py:556
  16.9 5.7 %collective-permute-start.3 = (f32[2,128,128]{2,1,0:T(8,128)S(1)}, f32[2,128,128]{2,1,0:T(8,128)S(1)}, u32[]{:S(2)}, u32[]{:S(2)}) collective-permute-start(f32[2,128,128]{2,1,0:T(8,128)S(1)} %multiply_add_fusion.2), channel_id=1, source_target_pairs={{4,8},{8,4},{5,9},{9,5},{6,10},{10,6},{7,11},{11,7},{20,24},{24,20... | collective-permute-start | bytes 393224 | tf_op jit(solution)/shard_map/ppermute | solution.py:556
  22.9 2.6 %collective-permute-start.6 = (f32[4,64]{1,0:T(4,128)S(1)}, f32[4,64]{1,0:T(4,128)S(1)}, u32[]{:S(2)}, u32[]{:S(2)}) collective-permute-start(f32[4,64]{1,0:T(4,128)S(1)} %multiply_add_fusion.4), channel_id=1, source_target_pairs={{0,16},{16,0},{1,17},{17,1},{2,18},{18,2},{3,19},{19,3},{4,20},{20... | collective-permute-start | bytes 3080 | tf_op jit(solution)/shard_map/ppermute | solution.py:590
  22.9 13.1 %collective-permute-start.5 = (f32[2,128,128]{2,1,0:T(8,128)S(1)}, f32[2,128,128]{2,1,0:T(8,128)S(1)}, u32[]{:S(2)}, u32[]{:S(2)}) collective-permute-start(f32[2,128,128]{2,1,0:T(8,128)S(1)} %get-tuple-element.62), channel_id=1, source_target_pairs={{8,12},{4,0},{9,13},{5,1},{10,14},{6,2},{11,15},{7,3},{24,28},{20,... | collective-permute-start | bytes 393224 | tf_op jit(solution)/shard_map/ppermute | solution.py:556
  24.2 11.8 %collective-permute-start.4 = (f32[2,128,128]{2,1,0:T(8,128)S(1)}, f32[2,128,128]{2,1,0:T(8,128)S(1)}, u32[]{:S(2)}, u32[]{:S(2)}) collective-permute-start(f32[2,128,128]{2,1,0:T(8,128)S(1)} %get-tuple-element.59), channel_id=1, source_target_pairs={{8,12},{4,0},{9,13},{5,1},{10,14},{6,2},{11,15},{7,3},{24,28},{20,... | collective-permute-start | bytes 393224 | tf_op jit(solution)/shard_map/ppermute | solution.py:556
  25.6 6.3 %collective-permute-start.9 = (f32[4,64]{1,0:T(4,128)S(1)}, f32[4,64]{1,0:T(4,128)S(1)}, u32[]{:S(2)}, u32[]{:S(2)}) collective-permute-start(f32[4,64]{1,0:T(4,128)S(1)} %add_add_fusion.refs_17_), channel_id=1, source_target_pairs={{0,12},{4,8},{8,4},{12,0},{1,13},{5,9},{9,5},{13,1},{2,14},{6,10},... | collective-permute-start | bytes 3080 | tf_op jit(solution)/shard_map/ppermute | solution.py:593
  28.1 5.3 %collective-permute-start.8 = (f32[4,64]{1,0:T(4,128)S(1)}, f32[4,64]{1,0:T(4,128)S(1)}, u32[]{:S(2)}, u32[]{:S(2)}) collective-permute-start(f32[4,64]{1,0:T(4,128)S(1)} %add_add_fusion.refs_17_), channel_id=1, source_target_pairs={{0,8},{4,12},{8,0},{12,4},{1,9},{5,13},{9,1},{13,5},{2,10},{6,14},... | collective-permute-start | bytes 3080 | tf_op jit(solution)/shard_map/ppermute | solution.py:593
  31.8 4.2 %collective-permute-start.7 = (f32[4,64]{1,0:T(4,128)S(1)}, f32[4,64]{1,0:T(4,128)S(1)}, u32[]{:S(2)}, u32[]{:S(2)}) collective-permute-start(f32[4,64]{1,0:T(4,128)S(1)} %add_add_fusion.refs_17_), channel_id=1, source_target_pairs={{0,4},{4,0},{8,12},{12,8},{1,5},{5,1},{9,13},{13,9},{2,6},{6,2},{1... | collective-permute-start | bytes 3080 | tf_op jit(solution)/shard_map/ppermute | solution.py:593

commit v15 on v13

--- a/solution.py
+++ b/solution.py
@@ -452,7 +452,7 @@
     part_width = width // PARTS
     num_chunks = tokens // CHUNK
     rows = num_chunks * 8
-    block = min(128, tokens)
+    block = min(256, tokens)
     steps = tokens // block
     count = lax.axis_size("ctx")
     middle = count // 2 - 1

time: 41.8 us -> 41.4 us (level)
  transfers between devices with their start and end apart: 10 -> 10, of which waited for: 2 -> 2; matrix products, arithmetic and copies ran while one was open for 1% -> 1% of each run, Pallas kernels for 23% -> 24%
where the time goes in v15:
time: 41.4 us; the launch traced here: 41.1 us
  Pallas kernels  18.4 us (44%)
  starting transfers between devices  16.5 us (40%)
  waiting for transfers between devices  4.1 us (10%)
  other arithmetic  1.3 us (3%)
  between operations  0.79 us (2%)
    ppermute x6, starting transfers between devices, send(): lax.ppermute(payload, 'ctx', [(hop, hop + 1), (count - 1 - hop, count - 2...  10.2 us
    pallas_call x2, Pallas kernels, local(): pl.pallas_call(functools.partial(local_kernel, head_width, part), in_spec...  9.68 us
    ppermute x3, starting transfers between devices, exchanged(): return lax.ppermute(array, 'ctx', [(i, i ^ reach) for i in range(count)])  6.3 us
    pallas_call x1, Pallas kernels, merge(): pl.pallas_call(functools.partial(merge_kernel, head_width), in_specs=[vme...  5.08 us
    ppermute x3, waiting for transfers between devices, exchanged(): return lax.ppermute(array, 'ctx', [(i, i ^ reach) for i in range(count)])  4.08 us
    pallas_call x1, Pallas kernels, ends(): pl.pallas_call(functools.partial(ends_kernel, head_width, lengths.shape[1...  3.64 us
  transfers between devices with their start and end apart: 10, of which 2 were waited for; matrix products, arithmetic and copies ran while one was open for 1% of the time, Pallas kernels for 24%

profile of v15, /device:TPU:0, one launch (start us, length us, event | category | flops | bytes accessed | tf_op | source)
XLA Modules:
  0.0 41.1 jit_solution(2011742054433344279)
XLA Ops:
  0.6 0.8 %convert_add_fusion.refs_0_ = f32[4,1280]{1,0:T(4,128)S(1)} fusion(s32[1,16]{1,0:T(1,128)} %param.11, f32[4,128]{1,0:T(4,128)} %param.12, f32[4,1024]{1,0:T(4,128)} %bitcast.13), kind=kLoop, calls=%fused_computation.8 | loop fusion | flops 15360 | bytes 38976 | tf_op jit(solution)/shard_map/add | solution.py:462
  1.4 3.6 %shard_ends.1 = (f32[2,128,128]{2,1,0:T(8,128)S(1)}, f32[2,128,128]{2,1,0:T(8,128)S(1)}, f32[2,128,128]{2,1,0:T(8,128)S(1)}, f32[2,128,128]{2,1,0:T(8,128)S(1)},...) custom-call(f32[4,1280]{1,0:T(4,128)S(1)} %convert_add_fusion.refs_0, ...), custom_call_target="tpu_custom_call" | custom-call | flops 268435456 | bytes 4194304 | tf_op jit(solution)/shard_map/shard_ends/pallas_call | solution.py:484
  5.0 4.9 %collective-permute-start = (f32[2,128,128]{2,1,0:T(8,128)S(1)}, f32[2,128,128]{2,1,0:T(8,128)S(1)}, u32[]{:S(2)}, u32[]{:S(2)}) collective-permute-start(f32[2,128,128]{2,1,0:T(8,128)S(1)} %get-tuple-element.43), channel_id=1, source_target_pairs={{0,4},{12,8},{1,5},{13,9},{2,6},{14,10},{3,7},{15,11},{16,20},{28,... | collective-permute-start | bytes 393224 | tf_op jit(solution)/shard_map/ppermute | solution.py:553
  10.0 1.3 %collective-permute-start.1 = (f32[2,128,128]{2,1,0:T(8,128)S(1)}, f32[2,128,128]{2,1,0:T(8,128)S(1)}, u32[]{:S(2)}, u32[]{:S(2)}) collective-permute-start(f32[2,128,128]{2,1,0:T(8,128)S(1)} %get-tuple-element.49), channel_id=1, source_target_pairs={{0,4},{12,8},{1,5},{13,9},{2,6},{14,10},{3,7},{15,11},{16,20},{28,... | collective-permute-start | bytes 393224 | tf_op jit(solution)/shard_map/ppermute | solution.py:553
  11.3 4.8 %local_0.1 = (bf16[4,1024,256]{2,1,0:T(8,128)(2,1)S(1)}, f32[1,2,1024]{2,1,0:T(2,128)S(1)}, f32[2,128]{1,0:T(2,128)S(1)}) custom-call(bf16[1,1024,512]{2,1,0:T(8,128)(2,1)S(1)} %get-tuple-element.32.q_ref.refs_0_, bf16[1,1024,512]{2,1,0:T(8,128)(2,1)S(1)} %get-tuple-element.33.k_ref.refs_1_, bf16[1,1024,512]{2,1,0:T(8,128)(2,1)S(1)} %get-tuple-element.34.v_ref.refs_2_, ...), custom_call_target="tpu_custom_call" | custom-call | flops 805306368 | bytes 4194304 | tf_op jit(solution)/shard_map/local_0/pallas_call | solution.py:501
  16.2 0.7 %collective-permute-start.2 = (f32[2,128,128]{2,1,0:T(8,128)S(1)}, f32[2,128,128]{2,1,0:T(8,128)S(1)}, u32[]{:S(2)}, u32[]{:S(2)}) collective-permute-start(f32[2,128,128]{2,1,0:T(8,128)S(1)} %multiply_add_fusion.3), channel_id=1, source_target_pairs={{4,8},{8,4},{5,9},{9,5},{6,10},{10,6},{7,11},{11,7},{20,24},{24,20... | collective-permute-start | bytes 393224 | tf_op jit(solution)/shard_map/ppermute | solution.py:553
  16.8 0.0 collective-permute-done.1.refs_12_
  16.9 0.7 %collective-permute-start.3 = (f32[2,128,128]{2,1,0:T(8,128)S(1)}, f32[2,128,128]{2,1,0:T(8,128)S(1)}, u32[]{:S(2)}, u32[]{:S(2)}) collective-permute-start(f32[2,128,128]{2,1,0:T(8,128)S(1)} %multiply_add_fusion.2), channel_id=1, source_target_pairs={{4,8},{8,4},{5,9},{9,5},{6,10},{10,6},{7,11},{11,7},{20,24},{24,20... | collective-permute-start | bytes 393224 | tf_op jit(solution)/shard_map/ppermute | solution.py:553
  17.6 4.9 %local_1.1 = (bf16[4,1024,256]{2,1,0:T(8,128)(2,1)S(1)}, f32[1,2,1024]{2,1,0:T(2,128)S(1)}, f32[2,128]{1,0:T(2,128)S(1)}) custom-call(bf16[1,1024,512]{2,1,0:T(8,128)(2,1)S(1)} %get-tuple-element.32.q_ref.refs_0_, bf16[1,1024,512]{2,1,0:T(8,128)(2,1)S(1)} %get-tuple-element.33.k_ref.refs_1_, bf16[1,1024,512]{2,1,0:T(8,128)(2,1)S(1)} %get-tuple-element.34.v_ref.refs_2_, ...), custom_call_target="tpu_custom_call" | custom-call | flops 805306368 | bytes 4194304 | tf_op jit(solution)/shard_map/local_1/pallas_call | solution.py:501
  22.4 0.0 collective-permute-done.2.refs_13_
  22.4 0.2 multiply_reduce_fusion.3
  22.6 0.2 multiply_reduce_fusion.1
  22.8 0.1 multiply_add_fusion.4
  22.9 0.0 collective-permute-start.6
  22.9 1.3 %collective-permute-start.5 = (f32[2,128,128]{2,1,0:T(8,128)S(1)}, f32[2,128,128]{2,1,0:T(8,128)S(1)}, u32[]{:S(2)}, u32[]{:S(2)}) collective-permute-start(f32[2,128,128]{2,1,0:T(8,128)S(1)} %get-tuple-element.62), channel_id=1, source_target_pairs={{8,12},{4,0},{9,13},{5,1},{10,14},{6,2},{11,15},{7,3},{24,28},{20,... | collective-permute-start | bytes 393224 | tf_op jit(solution)/shard_map/ppermute | solution.py:553
  24.2 1.3 %collective-permute-start.4 = (f32[2,128,128]{2,1,0:T(8,128)S(1)}, f32[2,128,128]{2,1,0:T(8,128)S(1)}, u32[]{:S(2)}, u32[]{:S(2)}) collective-permute-start(f32[2,128,128]{2,1,0:T(8,128)S(1)} %get-tuple-element.59), channel_id=1, source_target_pairs={{8,12},{4,0},{9,13},{5,1},{10,14},{6,2},{11,15},{7,3},{24,28},{20,... | collective-permute-start | bytes 393224 | tf_op jit(solution)/shard_map/ppermute | solution.py:553
  25.5 0.0 collective-permute-done.6
  25.5 0.1 add_add_fusion.refs_17_
  25.6 2.5 %collective-permute-start.9 = (f32[4,64]{1,0:T(4,128)S(1)}, f32[4,64]{1,0:T(4,128)S(1)}, u32[]{:S(2)}, u32[]{:S(2)}) collective-permute-start(f32[4,64]{1,0:T(4,128)S(1)} %add_add_fusion.refs_17_), channel_id=1, source_target_pairs={{0,12},{4,8},{8,4},{12,0},{1,13},{5,9},{9,5},{13,1},{2,14},{6,10},... | collective-permute-start | bytes 3080 | tf_op jit(solution)/shard_map/ppermute | solution.py:590
  28.1 3.7 %collective-permute-start.8 = (f32[4,64]{1,0:T(4,128)S(1)}, f32[4,64]{1,0:T(4,128)S(1)}, u32[]{:S(2)}, u32[]{:S(2)}) collective-permute-start(f32[4,64]{1,0:T(4,128)S(1)} %add_add_fusion.refs_17_), channel_id=1, source_target_pairs={{0,8},{4,12},{8,0},{12,4},{1,9},{5,13},{9,1},{13,5},{2,10},{6,14},... | collective-permute-start | bytes 3080 | tf_op jit(solution)/shard_map/ppermute | solution.py:590
  31.8 0.1 collective-permute-start.7
  31.9 1.5 %collective-permute-done.8.refs_19_ = f32[4,64]{1,0:T(4,128)S(1)} collective-permute-done((f32[4,64]{1,0:T(4,128)S(1)}, f32[4,64]{1,0:T(4,128)S(1)}, u32[]{:S(2)}, u32[]{:S(2)}) %collective-permute-start.8) | collective-permute-done | bytes 1056 | tf_op jit(solution)/shard_map/ppermute | solution.py:590
  33.4 2.6 %collective-permute-done.7.refs_18_ = f32[4,64]{1,0:T(4,128)S(1)} collective-permute-done((f32[4,64]{1,0:T(4,128)S(1)}, f32[4,64]{1,0:T(4,128)S(1)}, u32[]{:S(2)}, u32[]{:S(2)}) %collective-permute-start.7) | collective-permute-done | bytes 1056 | tf_op jit(solution)/shard_map/ppermute | solution.py:590
  36.0 5.1 %merge.1 = (bf16[1,1024,512]{2,1,0:T(8,128)(2,1)}, bf16[1,1024,512]{2,1,0:T(8,128)(2,1)}, bf16[1,1024,512]{2,1,0:T(8,128)(2,1)}, bf16[1,1024,512]{2,1,0:T(8,128)...) custom-call(bf16[1,1024,512]{2,1,0:T(8,128)(2,1)S(1)} %get-tuple-element.32.q_ref.refs_0_, ...), custom_call_target="tpu_custom_call" | custom-call | flops 536870912 | bytes 12582912 | tf_op jit(solution)/shard_map/merge/pallas_call | solution.py:518
  (11 shorter events, 0.1 us)
Async XLA Ops:
  5.0 11.1 %collective-permute-start = (f32[2,128,128]{2,1,0:T(8,128)S(1)}, f32[2,128,128]{2,1,0:T(8,128)S(1)}, u32[]{:S(2)}, u32[]{:S(2)}) collective-permute-start(f32[2,128,128]{2,1,0:T(8,128)S(1)} %get-tuple-element.43), channel_id=1, source_target_pairs={{0,4},{12,8},{1,5},{13,9},{2,6},{14,10},{3,7},{15,11},{16,20},{28,... | collective-permute-start | bytes 393224 | tf_op jit(solution)/shard_map/ppermute | solution.py:553
  10.0 6.9 %collective-permute-start.1 = (f32[2,128,128]{2,1,0:T(8,128)S(1)}, f32[2,128,128]{2,1,0:T(8,128)S(1)}, u32[]{:S(2)}, u32[]{:S(2)}) collective-permute-start(f32[2,128,128]{2,1,0:T(8,128)S(1)} %get-tuple-element.49), channel_id=1, source_target_pairs={{0,4},{12,8},{1,5},{13,9},{2,6},{14,10},{3,7},{15,11},{16,20},{28,... | collective-permute-start | bytes 393224 | tf_op jit(solution)/shard_map/ppermute | solution.py:553
  16.2 6.3 %collective-permute-start.2 = (f32[2,128,128]{2,1,0:T(8,128)S(1)}, f32[2,128,128]{2,1,0:T(8,128)S(1)}, u32[]{:S(2)}, u32[]{:S(2)}) collective-permute-start(f32[2,128,128]{2,1,0:T(8,128)S(1)} %multiply_add_fusion.3), channel_id=1, source_target_pairs={{4,8},{8,4},{5,9},{9,5},{6,10},{10,6},{7,11},{11,7},{20,24},{24,20... | collective-permute-start | bytes 393224 | tf_op jit(solution)/shard_map/ppermute | solution.py:553
  16.9 5.7 %collective-permute-start.3 = (f32[2,128,128]{2,1,0:T(8,128)S(1)}, f32[2,128,128]{2,1,0:T(8,128)S(1)}, u32[]{:S(2)}, u32[]{:S(2)}) collective-permute-start(f32[2,128,128]{2,1,0:T(8,128)S(1)} %multiply_add_fusion.2), channel_id=1, source_target_pairs={{4,8},{8,4},{5,9},{9,5},{6,10},{10,6},{7,11},{11,7},{20,24},{24,20... | collective-permute-start | bytes 393224 | tf_op jit(solution)/shard_map/ppermute | solution.py:553
  22.9 2.6 %collective-permute-start.6 = (f32[4,64]{1,0:T(4,128)S(1)}, f32[4,64]{1,0:T(4,128)S(1)}, u32[]{:S(2)}, u32[]{:S(2)}) collective-permute-start(f32[4,64]{1,0:T(4,128)S(1)} %multiply_add_fusion.4), channel_id=1, source_target_pairs={{0,16},{16,0},{1,17},{17,1},{2,18},{18,2},{3,19},{19,3},{4,20},{20... | collective-permute-start | bytes 3080 | tf_op jit(solution)/shard_map/ppermute | solution.py:587
  22.9 13.1 %collective-permute-start.5 = (f32[2,128,128]{2,1,0:T(8,128)S(1)}, f32[2,128,128]{2,1,0:T(8,128)S(1)}, u32[]{:S(2)}, u32[]{:S(2)}) collective-permute-start(f32[2,128,128]{2,1,0:T(8,128)S(1)} %get-tuple-element.62), channel_id=1, source_target_pairs={{8,12},{4,0},{9,13},{5,1},{10,14},{6,2},{11,15},{7,3},{24,28},{20,... | collective-permute-start | bytes 393224 | tf_op jit(solution)/shard_map/ppermute | solution.py:553
  24.2 11.8 %collective-permute-start.4 = (f32[2,128,128]{2,1,0:T(8,128)S(1)}, f32[2,128,128]{2,1,0:T(8,128)S(1)}, u32[]{:S(2)}, u32[]{:S(2)}) collective-permute-start(f32[2,128,128]{2,1,0:T(8,128)S(1)} %get-tuple-element.59), channel_id=1, source_target_pairs={{8,12},{4,0},{9,13},{5,1},{10,14},{6,2},{11,15},{7,3},{24,28},{20,... | collective-permute-start | bytes 393224 | tf_op jit(solution)/shard_map/ppermute | solution.py:553
  25.6 6.3 %collective-permute-start.9 = (f32[4,64]{1,0:T(4,128)S(1)}, f32[4,64]{1,0:T(4,128)S(1)}, u32[]{:S(2)}, u32[]{:S(2)}) collective-permute-start(f32[4,64]{1,0:T(4,128)S(1)} %add_add_fusion.refs_17_), channel_id=1, source_target_pairs={{0,12},{4,8},{8,4},{12,0},{1,13},{5,9},{9,5},{13,1},{2,14},{6,10},... | collective-permute-start | bytes 3080 | tf_op jit(solution)/shard_map/ppermute | solution.py:590
  28.1 5.3 %collective-permute-start.8 = (f32[4,64]{1,0:T(4,128)S(1)}, f32[4,64]{1,0:T(4,128)S(1)}, u32[]{:S(2)}, u32[]{:S(2)}) collective-permute-start(f32[4,64]{1,0:T(4,128)S(1)} %add_add_fusion.refs_17_), channel_id=1, source_target_pairs={{0,8},{4,12},{8,0},{12,4},{1,9},{5,13},{9,1},{13,5},{2,10},{6,14},... | collective-permute-start | bytes 3080 | tf_op jit(solution)/shard_map/ppermute | solution.py:590
  31.8 4.2 %collective-permute-start.7 = (f32[4,64]{1,0:T(4,128)S(1)}, f32[4,64]{1,0:T(4,128)S(1)}, u32[]{:S(2)}, u32[]{:S(2)}) collective-permute-start(f32[4,64]{1,0:T(4,128)S(1)} %add_add_fusion.refs_17_), channel_id=1, source_target_pairs={{0,4},{4,0},{8,12},{12,8},{1,5},{5,1},{9,13},{13,9},{2,6},{6,2},{1... | collective-permute-start | bytes 3080 | tf_op jit(solution)/shard_map/ppermute | solution.py:590

commit v16 on v15

--- a/solution.py
+++ b/solution.py
@@ -452,7 +452,7 @@
     part_width = width // PARTS
     num_chunks = tokens // CHUNK
     rows = num_chunks * 8
-    block = min(256, tokens)
+    block = min(512, tokens)
     steps = tokens // block
     count = lax.axis_size("ctx")
     middle = count // 2 - 1

time: 41.4 us -> 41.4 us (level)
  no operation moved by 1% of the time
where the time goes in v16:
time: 41.4 us; the launch traced here: 41.1 us
  Pallas kernels  18.4 us (44%)
  starting transfers between devices  16.5 us (40%)
  waiting for transfers between devices  4.09 us (10%)
  other arithmetic  1.3 us (3%)
  between operations  0.79 us (2%)
    ppermute x6, starting transfers between devices, send(): lax.ppermute(payload, 'ctx', [(hop, hop + 1), (count - 1 - hop, count - 2...  10.2 us
    pallas_call x2, Pallas kernels, local(): pl.pallas_call(functools.partial(local_kernel, head_width, part), in_spec...  9.69 us
    ppermute x3, starting transfers between devices, exchanged(): return lax.ppermute(array, 'ctx', [(i, i ^ reach) for i in range(count)])  6.3 us
    pallas_call x1, Pallas kernels, merge(): pl.pallas_call(functools.partial(merge_kernel, head_width), in_specs=[vme...  5.18 us
    ppermute x3, waiting for transfers between devices, exchanged(): return lax.ppermute(array, 'ctx', [(i, i ^ reach) for i in range(count)])  4.08 us
    pallas_call x1, Pallas kernels, ends(): pl.pallas_call(functools.partial(ends_kernel, head_width, lengths.shape[1...  3.56 us
  transfers between devices with their start and end apart: 10, of which 2 were waited for; matrix products, arithmetic and copies ran while one was open for 1% of the time, Pallas kernels for 24%

profile of v16, /device:TPU:0, one launch (start us, length us, event | category | flops | bytes accessed | tf_op | source)
XLA Modules:
  0.0 41.1 jit_solution(3025738313223591837)
XLA Ops:
  0.6 0.8 %convert_add_fusion.refs_0_ = f32[4,1280]{1,0:T(4,128)S(1)} fusion(s32[1,16]{1,0:T(1,128)} %param.11, f32[4,128]{1,0:T(4,128)} %param.12, f32[4,1024]{1,0:T(4,128)} %bitcast.13), kind=kLoop, calls=%fused_computation.8 | loop fusion | flops 15360 | bytes 38976 | tf_op jit(solution)/shard_map/add | solution.py:462
  1.4 3.6 %shard_ends.1 = (f32[2,128,128]{2,1,0:T(8,128)S(1)}, f32[2,128,128]{2,1,0:T(8,128)S(1)}, f32[2,128,128]{2,1,0:T(8,128)S(1)}, f32[2,128,128]{2,1,0:T(8,128)S(1)},...) custom-call(f32[4,1280]{1,0:T(4,128)S(1)} %convert_add_fusion.refs_0, ...), custom_call_target="tpu_custom_call" | custom-call | flops 268435456 | bytes 4194304 | tf_op jit(solution)/shard_map/shard_ends/pallas_call | solution.py:484
  5.0 4.9 %collective-permute-start = (f32[2,128,128]{2,1,0:T(8,128)S(1)}, f32[2,128,128]{2,1,0:T(8,128)S(1)}, u32[]{:S(2)}, u32[]{:S(2)}) collective-permute-start(f32[2,128,128]{2,1,0:T(8,128)S(1)} %get-tuple-element.43), channel_id=1, source_target_pairs={{0,4},{12,8},{1,5},{13,9},{2,6},{14,10},{3,7},{15,11},{16,20},{28,... | collective-permute-start | bytes 393224 | tf_op jit(solution)/shard_map/ppermute | solution.py:553
  9.9 1.3 %collective-permute-start.1 = (f32[2,128,128]{2,1,0:T(8,128)S(1)}, f32[2,128,128]{2,1,0:T(8,128)S(1)}, u32[]{:S(2)}, u32[]{:S(2)}) collective-permute-start(f32[2,128,128]{2,1,0:T(8,128)S(1)} %get-tuple-element.49), channel_id=1, source_target_pairs={{0,4},{12,8},{1,5},{13,9},{2,6},{14,10},{3,7},{15,11},{16,20},{28,... | collective-permute-start | bytes 393224 | tf_op jit(solution)/shard_map/ppermute | solution.py:553
  11.2 4.8 %local_0.1 = (bf16[4,1024,256]{2,1,0:T(8,128)(2,1)S(1)}, f32[1,2,1024]{2,1,0:T(2,128)S(1)}, f32[2,128]{1,0:T(2,128)S(1)}) custom-call(bf16[1,1024,512]{2,1,0:T(8,128)(2,1)S(1)} %get-tuple-element.32.q_ref.refs_0_, bf16[1,1024,512]{2,1,0:T(8,128)(2,1)S(1)} %get-tuple-element.33.k_ref.refs_1_, bf16[1,1024,512]{2,1,0:T(8,128)(2,1)S(1)} %get-tuple-element.34.v_ref.refs_2_, ...), custom_call_target="tpu_custom_call" | custom-call | flops 805306368 | bytes 4194304 | tf_op jit(solution)/shard_map/local_0/pallas_call | solution.py:501
  16.0 0.0 collective-permute-done.refs_11_
  16.1 0.7 %collective-permute-start.2 = (f32[2,128,128]{2,1,0:T(8,128)S(1)}, f32[2,128,128]{2,1,0:T(8,128)S(1)}, u32[]{:S(2)}, u32[]{:S(2)}) collective-permute-start(f32[2,128,128]{2,1,0:T(8,128)S(1)} %multiply_add_fusion.3), channel_id=1, source_target_pairs={{4,8},{8,4},{5,9},{9,5},{6,10},{10,6},{7,11},{11,7},{20,24},{24,20... | collective-permute-start | bytes 393224 | tf_op jit(solution)/shard_map/ppermute | solution.py:553
  16.8 0.0 collective-permute-done.1.refs_12_
  16.8 0.7 %collective-permute-start.3 = (f32[2,128,128]{2,1,0:T(8,128)S(1)}, f32[2,128,128]{2,1,0:T(8,128)S(1)}, u32[]{:S(2)}, u32[]{:S(2)}) collective-permute-start(f32[2,128,128]{2,1,0:T(8,128)S(1)} %multiply_add_fusion.2), channel_id=1, source_target_pairs={{4,8},{8,4},{5,9},{9,5},{6,10},{10,6},{7,11},{11,7},{20,24},{24,20... | collective-permute-start | bytes 393224 | tf_op jit(solution)/shard_map/ppermute | solution.py:553
  17.5 4.9 %local_1.1 = (bf16[4,1024,256]{2,1,0:T(8,128)(2,1)S(1)}, f32[1,2,1024]{2,1,0:T(2,128)S(1)}, f32[2,128]{1,0:T(2,128)S(1)}) custom-call(bf16[1,1024,512]{2,1,0:T(8,128)(2,1)S(1)} %get-tuple-element.32.q_ref.refs_0_, bf16[1,1024,512]{2,1,0:T(8,128)(2,1)S(1)} %get-tuple-element.33.k_ref.refs_1_, bf16[1,1024,512]{2,1,0:T(8,128)(2,1)S(1)} %get-tuple-element.34.v_ref.refs_2_, ...), custom_call_target="tpu_custom_call" | custom-call | flops 805306368 | bytes 4194304 | tf_op jit(solution)/shard_map/local_1/pallas_call | solution.py:501
  22.4 0.2 multiply_reduce_fusion.3
  22.5 0.0 collective-permute-done.3.refs_14_
  22.5 0.2 multiply_reduce_fusion.1
  22.7 0.1 multiply_add_fusion.4
  22.8 0.0 collective-permute-start.6
  22.8 1.3 %collective-permute-start.5 = (f32[2,128,128]{2,1,0:T(8,128)S(1)}, f32[2,128,128]{2,1,0:T(8,128)S(1)}, u32[]{:S(2)}, u32[]{:S(2)}) collective-permute-start(f32[2,128,128]{2,1,0:T(8,128)S(1)} %get-tuple-element.62), channel_id=1, source_target_pairs={{8,12},{4,0},{9,13},{5,1},{10,14},{6,2},{11,15},{7,3},{24,28},{20,... | collective-permute-start | bytes 393224 | tf_op jit(solution)/shard_map/ppermute | solution.py:553
  24.1 1.3 %collective-permute-start.4 = (f32[2,128,128]{2,1,0:T(8,128)S(1)}, f32[2,128,128]{2,1,0:T(8,128)S(1)}, u32[]{:S(2)}, u32[]{:S(2)}) collective-permute-start(f32[2,128,128]{2,1,0:T(8,128)S(1)} %get-tuple-element.59), channel_id=1, source_target_pairs={{8,12},{4,0},{9,13},{5,1},{10,14},{6,2},{11,15},{7,3},{24,28},{20,... | collective-permute-start | bytes 393224 | tf_op jit(solution)/shard_map/ppermute | solution.py:553
  25.4 0.1 add_add_fusion.refs_17_
  25.5 2.5 %collective-permute-start.9 = (f32[4,64]{1,0:T(4,128)S(1)}, f32[4,64]{1,0:T(4,128)S(1)}, u32[]{:S(2)}, u32[]{:S(2)}) collective-permute-start(f32[4,64]{1,0:T(4,128)S(1)} %add_add_fusion.refs_17_), channel_id=1, source_target_pairs={{0,12},{4,8},{8,4},{12,0},{1,13},{5,9},{9,5},{13,1},{2,14},{6,10},... | collective-permute-start | bytes 3080 | tf_op jit(solution)/shard_map/ppermute | solution.py:590
  28.0 3.7 %collective-permute-start.8 = (f32[4,64]{1,0:T(4,128)S(1)}, f32[4,64]{1,0:T(4,128)S(1)}, u32[]{:S(2)}, u32[]{:S(2)}) collective-permute-start(f32[4,64]{1,0:T(4,128)S(1)} %add_add_fusion.refs_17_), channel_id=1, source_target_pairs={{0,8},{4,12},{8,0},{12,4},{1,9},{5,13},{9,1},{13,5},{2,10},{6,14},... | collective-permute-start | bytes 3080 | tf_op jit(solution)/shard_map/ppermute | solution.py:590
  31.7 0.1 collective-permute-start.7
  31.8 1.5 %collective-permute-done.8.refs_19_ = f32[4,64]{1,0:T(4,128)S(1)} collective-permute-done((f32[4,64]{1,0:T(4,128)S(1)}, f32[4,64]{1,0:T(4,128)S(1)}, u32[]{:S(2)}, u32[]{:S(2)}) %collective-permute-start.8) | collective-permute-done | bytes 1056 | tf_op jit(solution)/shard_map/ppermute | solution.py:590
  33.3 2.6 %collective-permute-done.7.refs_18_ = f32[4,64]{1,0:T(4,128)S(1)} collective-permute-done((f32[4,64]{1,0:T(4,128)S(1)}, f32[4,64]{1,0:T(4,128)S(1)}, u32[]{:S(2)}, u32[]{:S(2)}) %collective-permute-start.7) | collective-permute-done | bytes 1056 | tf_op jit(solution)/shard_map/ppermute | solution.py:590
  35.9 5.2 %merge.1 = (bf16[1,1024,512]{2,1,0:T(8,128)(2,1)}, bf16[1,1024,512]{2,1,0:T(8,128)(2,1)}, bf16[1,1024,512]{2,1,0:T(8,128)(2,1)}, bf16[1,1024,512]{2,1,0:T(8,128)...) custom-call(bf16[1,1024,512]{2,1,0:T(8,128)(2,1)S(1)} %get-tuple-element.32.q_ref.refs_0_, ...), custom_call_target="tpu_custom_call" | custom-call | flops 536870912 | bytes 12582912 | tf_op jit(solution)/shard_map/merge/pallas_call | solution.py:518
  (11 shorter events, 0.1 us)
Async XLA Ops:
  5.0 11.1 %collective-permute-start = (f32[2,128,128]{2,1,0:T(8,128)S(1)}, f32[2,128,128]{2,1,0:T(8,128)S(1)}, u32[]{:S(2)}, u32[]{:S(2)}) collective-permute-start(f32[2,128,128]{2,1,0:T(8,128)S(1)} %get-tuple-element.43), channel_id=1, source_target_pairs={{0,4},{12,8},{1,5},{13,9},{2,6},{14,10},{3,7},{15,11},{16,20},{28,... | collective-permute-start | bytes 393224 | tf_op jit(solution)/shard_map/ppermute | solution.py:553
  9.9 6.9 %collective-permute-start.1 = (f32[2,128,128]{2,1,0:T(8,128)S(1)}, f32[2,128,128]{2,1,0:T(8,128)S(1)}, u32[]{:S(2)}, u32[]{:S(2)}) collective-permute-start(f32[2,128,128]{2,1,0:T(8,128)S(1)} %get-tuple-element.49), channel_id=1, source_target_pairs={{0,4},{12,8},{1,5},{13,9},{2,6},{14,10},{3,7},{15,11},{16,20},{28,... | collective-permute-start | bytes 393224 | tf_op jit(solution)/shard_map/ppermute | solution.py:553
  16.1 6.3 %collective-permute-start.2 = (f32[2,128,128]{2,1,0:T(8,128)S(1)}, f32[2,128,128]{2,1,0:T(8,128)S(1)}, u32[]{:S(2)}, u32[]{:S(2)}) collective-permute-start(f32[2,128,128]{2,1,0:T(8,128)S(1)} %multiply_add_fusion.3), channel_id=1, source_target_pairs={{4,8},{8,4},{5,9},{9,5},{6,10},{10,6},{7,11},{11,7},{20,24},{24,20... | collective-permute-start | bytes 393224 | tf_op jit(solution)/shard_map/ppermute | solution.py:553
  16.8 5.7 %collective-permute-start.3 = (f32[2,128,128]{2,1,0:T(8,128)S(1)}, f32[2,128,128]{2,1,0:T(8,128)S(1)}, u32[]{:S(2)}, u32[]{:S(2)}) collective-permute-start(f32[2,128,128]{2,1,0:T(8,128)S(1)} %multiply_add_fusion.2), channel_id=1, source_target_pairs={{4,8},{8,4},{5,9},{9,5},{6,10},{10,6},{7,11},{11,7},{20,24},{24,20... | collective-permute-start | bytes 393224 | tf_op jit(solution)/shard_map/ppermute | solution.py:553
  22.8 2.6 %collective-permute-start.6 = (f32[4,64]{1,0:T(4,128)S(1)}, f32[4,64]{1,0:T(4,128)S(1)}, u32[]{:S(2)}, u32[]{:S(2)}) collective-permute-start(f32[4,64]{1,0:T(4,128)S(1)} %multiply_add_fusion.4), channel_id=1, source_target_pairs={{0,16},{16,0},{1,17},{17,1},{2,18},{18,2},{3,19},{19,3},{4,20},{20... | collective-permute-start | bytes 3080 | tf_op jit(solution)/shard_map/ppermute | solution.py:587
  22.8 13.1 %collective-permute-start.5 = (f32[2,128,128]{2,1,0:T(8,128)S(1)}, f32[2,128,128]{2,1,0:T(8,128)S(1)}, u32[]{:S(2)}, u32[]{:S(2)}) collective-permute-start(f32[2,128,128]{2,1,0:T(8,128)S(1)} %get-tuple-element.62), channel_id=1, source_target_pairs={{8,12},{4,0},{9,13},{5,1},{10,14},{6,2},{11,15},{7,3},{24,28},{20,... | collective-permute-start | bytes 393224 | tf_op jit(solution)/shard_map/ppermute | solution.py:553
  24.1 11.8 %collective-permute-start.4 = (f32[2,128,128]{2,1,0:T(8,128)S(1)}, f32[2,128,128]{2,1,0:T(8,128)S(1)}, u32[]{:S(2)}, u32[]{:S(2)}) collective-permute-start(f32[2,128,128]{2,1,0:T(8,128)S(1)} %get-tuple-element.59), channel_id=1, source_target_pairs={{8,12},{4,0},{9,13},{5,1},{10,14},{6,2},{11,15},{7,3},{24,28},{20,... | collective-permute-start | bytes 393224 | tf_op jit(solution)/shard_map/ppermute | solution.py:553
  25.5 6.3 %collective-permute-start.9 = (f32[4,64]{1,0:T(4,128)S(1)}, f32[4,64]{1,0:T(4,128)S(1)}, u32[]{:S(2)}, u32[]{:S(2)}) collective-permute-start(f32[4,64]{1,0:T(4,128)S(1)} %add_add_fusion.refs_17_), channel_id=1, source_target_pairs={{0,12},{4,8},{8,4},{12,0},{1,13},{5,9},{9,5},{13,1},{2,14},{6,10},... | collective-permute-start | bytes 3080 | tf_op jit(solution)/shard_map/ppermute | solution.py:590
  28.0 5.3 %collective-permute-start.8 = (f32[4,64]{1,0:T(4,128)S(1)}, f32[4,64]{1,0:T(4,128)S(1)}, u32[]{:S(2)}, u32[]{:S(2)}) collective-permute-start(f32[4,64]{1,0:T(4,128)S(1)} %add_add_fusion.refs_17_), channel_id=1, source_target_pairs={{0,8},{4,12},{8,0},{12,4},{1,9},{5,13},{9,1},{13,5},{2,10},{6,14},... | collective-permute-start | bytes 3080 | tf_op jit(solution)/shard_map/ppermute | solution.py:590
  31.7 4.2 %collective-permute-start.7 = (f32[4,64]{1,0:T(4,128)S(1)}, f32[4,64]{1,0:T(4,128)S(1)}, u32[]{:S(2)}, u32[]{:S(2)}) collective-permute-start(f32[4,64]{1,0:T(4,128)S(1)} %add_add_fusion.refs_17_), channel_id=1, source_target_pairs={{0,4},{4,0},{8,12},{12,8},{1,5},{5,1},{9,13},{13,9},{2,6},{6,2},{1... | collective-permute-start | bytes 3080 | tf_op jit(solution)/shard_map/ppermute | solution.py:590
